TPU v7x, 32 devices: a whole 2x2x4 slice. The times are simulated.
32 devices in a mesh: seq: 4 (over y, core), fsdp: 8 (over z, x).
Axes of the slice: x: 2, y: 2, z: 4, core: 2. Of those that a mesh axis runs over, the one named last changes fastest.
Arguments:
- inputs: bfloat16 [16, 1024, 1152], P('fsdp', 'seq'), may hold values from -6 to 6
- cotangent: bfloat16 [16, 1024, 1152], P('fsdp', 'seq'), may hold values from -6 to 6
- segments: int32 [16, 1024], P('fsdp', 'seq'), may hold values from 0 to 2, as said below
- exits: int32 [16, 1024], P('fsdp', 'seq'), may hold values from 0 to 2, as said below
- confidence: float32 [16, 1024], P('fsdp', 'seq'), may hold values from 0.05 to 1
- attn_gain: bfloat16 [1152], P('fsdp'), may hold values from 0.099609375 to 1.8984375
- q_weight: bfloat16 [1152, 1024], P('fsdp'), may hold values from -0.1875 to 0.1875
- k_weight: bfloat16 [1152, 256], P('fsdp'), may hold values from -0.1875 to 0.1875
- v_weight: bfloat16 [1152, 256], P('fsdp'), may hold values from -0.1875 to 0.1875
- o_weight: bfloat16 [1024, 1152], P('fsdp'), may hold values from -1 to 1
- q_down: bfloat16 [1152, 256], P('fsdp'), may hold values from -0.1875 to 0.1875
- q_up: bfloat16 [256, 1024], P('fsdp'), may hold values from -0.1875 to 0.1875
- k_down: bfloat16 [1152, 256], P('fsdp'), may hold values from -0.1875 to 0.1875
- k_up: bfloat16 [256, 256], P('fsdp'), may hold values from -0.1875 to 0.1875
- v_down: bfloat16 [1152, 256], P('fsdp'), may hold values from -0.1875 to 0.1875
- v_up: bfloat16 [256, 256], P('fsdp'), may hold values from -0.1875 to 0.1875
- o_down: bfloat16 [1024, 256], P('fsdp'), may hold values from -1 to 1
- o_up: bfloat16 [256, 1152], P('fsdp'), may hold values from -0.1875 to 0.1875
- mlp_gain: bfloat16 [1152], P('fsdp'), may hold values from 0.099609375 to 1.8984375
- gate_weight: bfloat16 [1152, 6912], P('fsdp'), may hold values from -0.1875 to 0.1875
- up_weight: bfloat16 [1152, 6912], P('fsdp'), may hold values from -0.1875 to 0.1875
- down_weight: bfloat16 [6912, 1152], P('fsdp'), may hold values from -0.078125 to 0.078125
- gate_down: bfloat16 [1152, 256], P('fsdp'), may hold values from -0.1875 to 0.1875
- gate_up: bfloat16 [256, 6912], P('fsdp'), may hold values from -0.1875 to 0.1875
- up_down: bfloat16 [1152, 256], P('fsdp'), may hold values from -0.1875 to 0.1875
- up_up: bfloat16 [256, 6912], P('fsdp'), may hold values from -0.1875 to 0.1875
- down_down: bfloat16 [6912, 256], P('fsdp'), may hold values from -0.078125 to 0.078125
- down_up: bfloat16 [256, 1152], P('fsdp'), may hold values from -0.1875 to 0.1875
Outputs:
- outputs: bfloat16 [16, 1024, 1152], P('fsdp', 'seq')
- input_grad: bfloat16 [16, 1024, 1152], P('fsdp', 'seq')
- grad_attn_gain: float32 [1152], P('fsdp')
- grad_q_weight: float32 [1152, 1024], P('fsdp')
- grad_k_weight: float32 [1152, 256], P('fsdp')
- grad_v_weight: float32 [1152, 256], P('fsdp')
- grad_o_weight: float32 [1024, 1152], P('fsdp')
- grad_q_down: float32 [1152, 256], P('fsdp')
- grad_q_up: float32 [256, 1024], P('fsdp')
- grad_k_down: float32 [1152, 256], P('fsdp')
- grad_k_up: float32 [256, 256], P('fsdp')
- grad_v_down: float32 [1152, 256], P('fsdp')
- grad_v_up: float32 [256, 256], P('fsdp')
- grad_o_down: float32 [1024, 256], P('fsdp')
- grad_o_up: float32 [256, 1152], P('fsdp')
- grad_mlp_gain: float32 [1152], P('fsdp')
- grad_gate_weight: float32 [1152, 6912], P('fsdp')
- grad_up_weight: float32 [1152, 6912], P('fsdp')
- grad_down_weight: float32 [6912, 1152], P('fsdp')
- grad_gate_down: float32 [1152, 256], P('fsdp')
- grad_gate_up: float32 [256, 6912], P('fsdp')
- grad_up_down: float32 [1152, 256], P('fsdp')
- grad_up_up: float32 [256, 6912], P('fsdp')
- grad_down_down: float32 [6912, 256], P('fsdp')
- grad_down_up: float32 [256, 1152], P('fsdp')
- exit_counts: int32 [3], replicated
- mean_confidence: float32 [3], replicated
Inputs may be any that keep to these rules, and one draw needn't show every extreme that they name: `segments`: along each row, with places counted from 0, the document numbers never fall and take the values 0, 1, 2, each on at least one token; document 1 begins at a place from 1 to 128, and document 2 begins at a place from 896 to 1023. The first token of row r exits at depth r mod 3, so every depth is the exit depth of some token of the batch.
All inputs are finite; a program needn't handle non-finite values.
Results may differ from a plain program's by a relative error of at most 0.025.
Values may be sent and summed in bfloat16 or wider, within the bound.
A program may use at most 320 MiB of HBM per device.

v0:
```python
import jax
import jax.numpy as jnp
from jax import lax
from jax.sharding import PartitionSpec as P

H = 4
HD = 256
DEPTHS = 3
LOOP = 1


epsilon = 1e-06
rope_base = 10000.0
contract_rows = (((0,), (0,)), ((), ()))


def rms_norm(values, gain):
    return values * lax.rsqrt(jnp.mean(values * values, axis=-1, keepdims=True) + epsilon) * gain


def gated_unit(gate, up_linear_output):
    return jax.nn.gelu(gate, approximate=True) * up_linear_output


def rotate(values, positions, sign):
    half_width = values.shape[-1] // 2
    frequency = rope_base ** (-2.0 * jnp.arange(half_width, dtype=jnp.float32) / values.shape[-1])
    angles = sign * positions.astype(jnp.float32)[:, None] * frequency[None, :]
    cosine = jnp.cos(angles)[:, None, :]
    sine_part = jnp.sin(angles)[:, None, :]
    first_half = values[..., :half_width]
    second_half = values[..., half_width:]
    return jnp.concatenate(
        [
            first_half * cosine - second_half * sine_part,
            second_half * cosine + first_half * sine_part,
        ],
        axis=-1,
    )


def adapted_matrix(source, base_matrix, down_matrix, up_matrix):
    low_inner = jnp.dot(source, down_matrix, preferred_element_type=jnp.float32).astype(
        jnp.bfloat16
    )
    result = jnp.dot(source, base_matrix, preferred_element_type=jnp.float32)
    return (result + jnp.dot(low_inner, up_matrix, preferred_element_type=jnp.float32), low_inner)


def adapted_back(source, low_inner, grad_low, base_matrix, down_matrix, up_matrix):
    grad_base = lax.dot_general(source, grad_low, contract_rows, preferred_element_type=jnp.float32)
    gradient_up_linear = lax.dot_general(
        low_inner, grad_low, contract_rows, preferred_element_type=jnp.float32
    )
    grad_inner = jnp.dot(grad_low, up_matrix.T, preferred_element_type=jnp.float32).astype(
        jnp.bfloat16
    )
    grad_down = lax.dot_general(
        source, grad_inner, contract_rows, preferred_element_type=jnp.float32
    )
    grad_source = jnp.dot(grad_low, base_matrix.T, preferred_element_type=jnp.float32)
    grad_source = grad_source + jnp.dot(
        grad_inner, down_matrix.T, preferred_element_type=jnp.float32
    )
    return (grad_source, grad_base, grad_down, gradient_up_linear)


def unchanged(state_now):
    return state_now


def shards(
    inputs,
    cotangent,
    segments,
    exits,
    confidence,
    attn_gain,
    q_weight,
    k_weight,
    v_weight,
    o_weight,
    q_down,
    q_up,
    k_down,
    k_up,
    v_down,
    v_up,
    o_down,
    o_up,
    mlp_gain,
    gate_weight,
    up_weight,
    down_weight,
    gate_down,
    gate_up,
    up_down,
    up_up,
    down_down,
    down_up,
):
    n_seq = lax.axis_size("seq")
    row_count, group_len, model_width = inputs.shape
    tokens = row_count * group_len
    score_scale = HD ** (-0.5)
    places = lax.axis_index("seq") * group_len + jnp.arange(group_len, dtype=jnp.int32)
    token_places = jnp.tile(places, row_count)
    (
        gain_attn,
        query_base,
        key_base,
        value_base,
        output_base,
        query_down,
        query_up,
        key_down,
        key_up,
        value_down,
        value_up,
        output_down,
        output_up,
    ) = (
        lax.all_gather(attn_gain, "fsdp", axis=0, tiled=True),
        lax.all_gather(q_weight, "fsdp", axis=0, tiled=True),
        lax.all_gather(k_weight, "fsdp", axis=0, tiled=True),
        lax.all_gather(v_weight, "fsdp", axis=0, tiled=True),
        lax.all_gather(o_weight, "fsdp", axis=0, tiled=True),
        lax.all_gather(q_down, "fsdp", axis=0, tiled=True),
        lax.all_gather(q_up, "fsdp", axis=0, tiled=True),
        lax.all_gather(k_down, "fsdp", axis=0, tiled=True),
        lax.all_gather(k_up, "fsdp", axis=0, tiled=True),
        lax.all_gather(v_down, "fsdp", axis=0, tiled=True),
        lax.all_gather(v_up, "fsdp", axis=0, tiled=True),
        lax.all_gather(o_down, "fsdp", axis=0, tiled=True),
        lax.all_gather(o_up, "fsdp", axis=0, tiled=True),
    )
    resid = inputs.reshape(tokens, model_width).astype(jnp.float32)
    active = (exits.reshape(tokens) >= LOOP).astype(jnp.float32)[:, None]
    normed, norm_pull = jax.vjp(rms_norm, resid, gain_attn.astype(jnp.float32))
    normed_low = normed.astype(jnp.bfloat16)
    query_lin, query_inner = adapted_matrix(normed_low, query_base, query_down, query_up)
    key_lin, key_inner = adapted_matrix(normed_low, key_base, key_down, key_up)
    value_lin, value_inner = adapted_matrix(normed_low, value_base, value_down, value_up)
    queries = rotate(query_lin.reshape(tokens, H, HD), token_places, 1.0).astype(jnp.bfloat16)
    keys_rot = rotate(key_lin.reshape(tokens, 1, HD), token_places, 1.0).astype(jnp.bfloat16)
    keys_rot = keys_rot.reshape(row_count, group_len, HD)
    values_low = value_lin.astype(jnp.bfloat16).reshape(row_count, group_len, HD)
    query_rows = queries.reshape(row_count, group_len * H, HD)
    query_seg = jnp.repeat(segments, H, axis=1)
    query_place = jnp.repeat(places, H)
    seg_wire = segments.astype(jnp.bfloat16)

    def visible(piece_seg):
        count = piece_seg.shape[1]
        key_place = jnp.arange(count, dtype=jnp.int32)
        same_doc = query_seg[:, :, None] == piece_seg.astype(jnp.int32)[:, None, :]
        return same_doc & (key_place[None, None, :] <= query_place[None, :, None])

    start_state = (
        jnp.full((row_count, group_len * H), -1e30, jnp.float32),
        jnp.zeros((row_count, group_len * H), jnp.float32),
        jnp.zeros((row_count, group_len * H, HD), jnp.float32),
    )
    piece_keys = lax.all_gather(keys_rot, "seq", axis=1, tiled=True)
    piece_values = lax.all_gather(values_low, "seq", axis=1, tiled=True)
    piece_seg = lax.all_gather(seg_wire, "seq", axis=1, tiled=True)
    allowed = visible(piece_seg)

    def fold_work(state_in):
        row_top, totals, accum = state_in
        scores = (
            jnp.einsum("sqd,skd->sqk", query_rows, piece_keys, preferred_element_type=jnp.float32)
            * score_scale
        )
        scores = jnp.where(allowed, scores, -1e30)
        new_top = jnp.maximum(row_top, jnp.max(scores, axis=-1))
        weights = jnp.where(allowed, jnp.exp(scores - new_top[..., None]), 0.0)
        totals = jnp.sum(weights, axis=-1)
        accum = jnp.einsum(
            "sqk,skd->sqd",
            weights.astype(jnp.bfloat16),
            piece_values,
            preferred_element_type=jnp.float32,
        )
        return (new_top, totals, accum)

    row_top, totals, accum = lax.cond(jnp.any(allowed), fold_work, unchanged, start_state)
    log_total = row_top + jnp.log(totals)
    attn_f32 = accum / totals[..., None]
    attn_low = attn_f32.reshape(tokens, H * HD).astype(jnp.bfloat16)
    branch_attn, output_inner = adapted_matrix(attn_low, output_base, output_down, output_up)
    middle = resid + active * branch_attn
    (
        gain_mlp,
        gate_shared_weight,
        up_shared_weight,
        down_shared_weight,
        gate_adapter_lower,
        gate_adapter_raise,
        up_adapter_lower,
        up_adapter_raise,
        down_adapter_lower,
        down_adapter_raise,
    ) = (
        lax.all_gather(mlp_gain, "fsdp", axis=0, tiled=True),
        lax.all_gather(gate_weight, "fsdp", axis=0, tiled=True),
        lax.all_gather(up_weight, "fsdp", axis=0, tiled=True),
        lax.all_gather(down_weight, "fsdp", axis=0, tiled=True),
        lax.all_gather(gate_down, "fsdp", axis=0, tiled=True),
        lax.all_gather(gate_up, "fsdp", axis=0, tiled=True),
        lax.all_gather(up_down, "fsdp", axis=0, tiled=True),
        lax.all_gather(up_up, "fsdp", axis=0, tiled=True),
        lax.all_gather(down_down, "fsdp", axis=0, tiled=True),
        lax.all_gather(down_up, "fsdp", axis=0, tiled=True),
    )
    normed2, norm2_pull = jax.vjp(rms_norm, middle, gain_mlp.astype(jnp.float32))
    second_normed_reduced = normed2.astype(jnp.bfloat16)
    gate_linear_output, gate_projection_inner = adapted_matrix(
        second_normed_reduced, gate_shared_weight, gate_adapter_lower, gate_adapter_raise
    )
    up_linear_output, up_projection_inner = adapted_matrix(
        second_normed_reduced, up_shared_weight, up_adapter_lower, up_adapter_raise
    )
    hidden, unit_pull = jax.vjp(gated_unit, gate_linear_output, up_linear_output)
    hidden_reduced_precision = hidden.astype(jnp.bfloat16)
    feedforward_branch, down_projection_inner = adapted_matrix(
        hidden_reduced_precision, down_shared_weight, down_adapter_lower, down_adapter_raise
    )
    outputs = (
        (middle + active * feedforward_branch)
        .astype(jnp.bfloat16)
        .reshape(row_count, group_len, model_width)
    )
    grad_out = cotangent.reshape(tokens, model_width).astype(jnp.float32)
    gradient_feedforward_branch = (active * grad_out).astype(jnp.bfloat16)
    grad_hidden, g_down_base, g_down_down, g_down_up = adapted_back(
        hidden_reduced_precision,
        down_projection_inner,
        gradient_feedforward_branch,
        down_shared_weight,
        down_adapter_lower,
        down_adapter_raise,
    )
    gradient_gate_linear, gradient_up_linear = unit_pull(grad_hidden)
    gradient_gate_linear = gradient_gate_linear.astype(jnp.bfloat16)
    gradient_up_linear = gradient_up_linear.astype(jnp.bfloat16)
    grad_n2_gate, g_gate_base, g_gate_down, g_gate_up = adapted_back(
        second_normed_reduced,
        gate_projection_inner,
        gradient_gate_linear,
        gate_shared_weight,
        gate_adapter_lower,
        gate_adapter_raise,
    )
    grad_n2_up, g_up_base, g_up_down, g_up_up = adapted_back(
        second_normed_reduced,
        up_projection_inner,
        gradient_up_linear,
        up_shared_weight,
        up_adapter_lower,
        up_adapter_raise,
    )
    grad_mid_norm, g_mlp_gain = norm2_pull(grad_n2_gate + grad_n2_up)
    grad_mid = grad_out + grad_mid_norm
    mlp_shards = (
        lax.psum_scatter(
            g_mlp_gain.astype(jnp.bfloat16), "fsdp", scatter_dimension=0, tiled=True
        ).astype(jnp.float32),
        lax.psum_scatter(
            g_gate_base.astype(jnp.bfloat16), "fsdp", scatter_dimension=0, tiled=True
        ).astype(jnp.float32),
        lax.psum_scatter(
            g_up_base.astype(jnp.bfloat16), "fsdp", scatter_dimension=0, tiled=True
        ).astype(jnp.float32),
        lax.psum_scatter(
            g_down_base.astype(jnp.bfloat16), "fsdp", scatter_dimension=0, tiled=True
        ).astype(jnp.float32),
        lax.psum_scatter(
            g_gate_down.astype(jnp.bfloat16), "fsdp", scatter_dimension=0, tiled=True
        ).astype(jnp.float32),
        lax.psum_scatter(
            g_gate_up.astype(jnp.bfloat16), "fsdp", scatter_dimension=0, tiled=True
        ).astype(jnp.float32),
        lax.psum_scatter(
            g_up_down.astype(jnp.bfloat16), "fsdp", scatter_dimension=0, tiled=True
        ).astype(jnp.float32),
        lax.psum_scatter(
            g_up_up.astype(jnp.bfloat16), "fsdp", scatter_dimension=0, tiled=True
        ).astype(jnp.float32),
        lax.psum_scatter(
            g_down_down.astype(jnp.bfloat16), "fsdp", scatter_dimension=0, tiled=True
        ).astype(jnp.float32),
        lax.psum_scatter(
            g_down_up.astype(jnp.bfloat16), "fsdp", scatter_dimension=0, tiled=True
        ).astype(jnp.float32),
    )
    grad_branch_attn = (active * grad_mid).astype(jnp.bfloat16)
    grad_attn, g_o_base, g_o_down, g_o_up = adapted_back(
        attn_low, output_inner, grad_branch_attn, output_base, output_down, output_up
    )
    grad_attn_rows = grad_attn.astype(jnp.bfloat16).reshape(row_count, group_len * H, HD)
    row_dots = jnp.sum(grad_attn_rows.astype(jnp.float32) * attn_f32, axis=-1)
    full_len = group_len * n_seq
    back_state = (
        jnp.zeros((row_count, group_len * H, HD), jnp.float32),
        jnp.zeros((row_count, full_len, HD), jnp.float32),
        jnp.zeros((row_count, full_len, HD), jnp.float32),
    )
    back_piece_keys = lax.all_gather(keys_rot, "seq", axis=1, tiled=True)
    back_piece_values = lax.all_gather(values_low, "seq", axis=1, tiled=True)
    piece_seg = lax.all_gather(seg_wire, "seq", axis=1, tiled=True)
    back_allowed = visible(piece_seg)

    def back_work(state_in):
        scores = (
            jnp.einsum(
                "sqd,skd->sqk", query_rows, back_piece_keys, preferred_element_type=jnp.float32
            )
            * score_scale
        )
        probs = jnp.where(back_allowed, jnp.exp(scores - log_total[..., None]), 0.0)
        grad_probs = jnp.einsum(
            "sqd,skd->sqk", grad_attn_rows, back_piece_values, preferred_element_type=jnp.float32
        )
        grad_scores = (probs * (grad_probs - row_dots[..., None])).astype(jnp.bfloat16)
        grad_query = (
            jnp.einsum(
                "sqk,skd->sqd", grad_scores, back_piece_keys, preferred_element_type=jnp.float32
            )
            * score_scale
        )
        key_part = (
            jnp.einsum("sqk,sqd->skd", grad_scores, query_rows, preferred_element_type=jnp.float32)
            * score_scale
        )
        value_part = jnp.einsum(
            "sqk,sqd->skd",
            probs.astype(jnp.bfloat16),
            grad_attn_rows,
            preferred_element_type=jnp.float32,
        )
        return (grad_query, key_part, value_part)

    grad_query, grad_keys, grad_values = lax.cond(
        jnp.any(back_allowed), back_work, unchanged, back_state
    )
    grad_keys, grad_values = (
        lax.psum_scatter(
            grad_keys.astype(jnp.bfloat16), "seq", scatter_dimension=1, tiled=True
        ).astype(jnp.float32),
        lax.psum_scatter(
            grad_values.astype(jnp.bfloat16), "seq", scatter_dimension=1, tiled=True
        ).astype(jnp.float32),
    )
    grad_q_lin = (
        rotate(grad_query.reshape(tokens, H, HD), token_places, -1.0)
        .reshape(tokens, H * HD)
        .astype(jnp.bfloat16)
    )
    grad_k_lin = (
        rotate(grad_keys.reshape(tokens, 1, HD), token_places, -1.0)
        .reshape(tokens, HD)
        .astype(jnp.bfloat16)
    )
    grad_v_lin = grad_values.reshape(tokens, HD).astype(jnp.bfloat16)
    grad_n_query, g_q_base, g_q_down, g_q_up = adapted_back(
        normed_low, query_inner, grad_q_lin, query_base, query_down, query_up
    )
    grad_n_key, g_k_base, g_k_down, g_k_up = adapted_back(
        normed_low, key_inner, grad_k_lin, key_base, key_down, key_up
    )
    grad_n_value, g_v_base, g_v_down, g_v_up = adapted_back(
        normed_low, value_inner, grad_v_lin, value_base, value_down, value_up
    )
    grad_in_norm, g_attn_gain = norm_pull(grad_n_query + grad_n_key + grad_n_value)
    input_grad = (
        (grad_mid + grad_in_norm).astype(jnp.bfloat16).reshape(row_count, group_len, model_width)
    )
    attn_shards = (
        lax.psum_scatter(
            g_attn_gain.astype(jnp.bfloat16), "fsdp", scatter_dimension=0, tiled=True
        ).astype(jnp.float32),
        lax.psum_scatter(
            g_q_base.astype(jnp.bfloat16), "fsdp", scatter_dimension=0, tiled=True
        ).astype(jnp.float32),
        lax.psum_scatter(
            g_k_base.astype(jnp.bfloat16), "fsdp", scatter_dimension=0, tiled=True
        ).astype(jnp.float32),
        lax.psum_scatter(
            g_v_base.astype(jnp.bfloat16), "fsdp", scatter_dimension=0, tiled=True
        ).astype(jnp.float32),
        lax.psum_scatter(
            g_o_base.astype(jnp.bfloat16), "fsdp", scatter_dimension=0, tiled=True
        ).astype(jnp.float32),
        lax.psum_scatter(
            g_q_down.astype(jnp.bfloat16), "fsdp", scatter_dimension=0, tiled=True
        ).astype(jnp.float32),
        lax.psum_scatter(
            g_q_up.astype(jnp.bfloat16), "fsdp", scatter_dimension=0, tiled=True
        ).astype(jnp.float32),
        lax.psum_scatter(
            g_k_down.astype(jnp.bfloat16), "fsdp", scatter_dimension=0, tiled=True
        ).astype(jnp.float32),
        lax.psum_scatter(
            g_k_up.astype(jnp.bfloat16), "fsdp", scatter_dimension=0, tiled=True
        ).astype(jnp.float32),
        lax.psum_scatter(
            g_v_down.astype(jnp.bfloat16), "fsdp", scatter_dimension=0, tiled=True
        ).astype(jnp.float32),
        lax.psum_scatter(
            g_v_up.astype(jnp.bfloat16), "fsdp", scatter_dimension=0, tiled=True
        ).astype(jnp.float32),
        lax.psum_scatter(
            g_o_down.astype(jnp.bfloat16), "fsdp", scatter_dimension=0, tiled=True
        ).astype(jnp.float32),
        lax.psum_scatter(
            g_o_up.astype(jnp.bfloat16), "fsdp", scatter_dimension=0, tiled=True
        ).astype(jnp.float32),
    )
    summed = (
        lax.psum(attn_shards[0].astype(jnp.bfloat16), "seq").astype(jnp.float32),
        lax.psum(attn_shards[1].astype(jnp.bfloat16), "seq").astype(jnp.float32),
        lax.psum(attn_shards[2].astype(jnp.bfloat16), "seq").astype(jnp.float32),
        lax.psum(attn_shards[3].astype(jnp.bfloat16), "seq").astype(jnp.float32),
        lax.psum(attn_shards[4].astype(jnp.bfloat16), "seq").astype(jnp.float32),
        lax.psum(attn_shards[5].astype(jnp.bfloat16), "seq").astype(jnp.float32),
        lax.psum(attn_shards[6].astype(jnp.bfloat16), "seq").astype(jnp.float32),
        lax.psum(attn_shards[7].astype(jnp.bfloat16), "seq").astype(jnp.float32),
        lax.psum(attn_shards[8].astype(jnp.bfloat16), "seq").astype(jnp.float32),
        lax.psum(attn_shards[9].astype(jnp.bfloat16), "seq").astype(jnp.float32),
        lax.psum(attn_shards[10].astype(jnp.bfloat16), "seq").astype(jnp.float32),
        lax.psum(attn_shards[11].astype(jnp.bfloat16), "seq").astype(jnp.float32),
        lax.psum(attn_shards[12].astype(jnp.bfloat16), "seq").astype(jnp.float32),
        lax.psum(mlp_shards[0].astype(jnp.bfloat16), "seq").astype(jnp.float32),
        lax.psum(mlp_shards[1].astype(jnp.bfloat16), "seq").astype(jnp.float32),
        lax.psum(mlp_shards[2].astype(jnp.bfloat16), "seq").astype(jnp.float32),
        lax.psum(mlp_shards[3].astype(jnp.bfloat16), "seq").astype(jnp.float32),
        lax.psum(mlp_shards[4].astype(jnp.bfloat16), "seq").astype(jnp.float32),
        lax.psum(mlp_shards[5].astype(jnp.bfloat16), "seq").astype(jnp.float32),
        lax.psum(mlp_shards[6].astype(jnp.bfloat16), "seq").astype(jnp.float32),
        lax.psum(mlp_shards[7].astype(jnp.bfloat16), "seq").astype(jnp.float32),
        lax.psum(mlp_shards[8].astype(jnp.bfloat16), "seq").astype(jnp.float32),
        lax.psum(mlp_shards[9].astype(jnp.bfloat16), "seq").astype(jnp.float32),
    )
    depth_ids = jnp.arange(DEPTHS, dtype=jnp.int32)
    matches = (exits.reshape(tokens)[:, None] == depth_ids[None, :]).astype(jnp.float32)
    count_local = jnp.sum(matches, axis=0)
    conf_local = jnp.sum(matches * confidence.reshape(tokens)[:, None], axis=0)
    count_all, conf_all = lax.psum((count_local, conf_local), ("seq", "fsdp"))
    mean_confidence = conf_all / count_all
    return (
        outputs,
        input_grad,
        summed[0],
        summed[1],
        summed[2],
        summed[3],
        summed[4],
        summed[5],
        summed[6],
        summed[7],
        summed[8],
        summed[9],
        summed[10],
        summed[11],
        summed[12],
        summed[13],
        summed[14],
        summed[15],
        summed[16],
        summed[17],
        summed[18],
        summed[19],
        summed[20],
        summed[21],
        summed[22],
        count_all.astype(jnp.int32),
        mean_confidence,
    )


def solution(mesh):
    in_specs = (
        P("fsdp", "seq", None),
        P("fsdp", "seq", None),
        P("fsdp", "seq"),
        P("fsdp", "seq"),
        P("fsdp", "seq"),
        P("fsdp"),
        P("fsdp", None),
        P("fsdp", None),
        P("fsdp", None),
        P("fsdp", None),
        P("fsdp", None),
        P("fsdp", None),
        P("fsdp", None),
        P("fsdp", None),
        P("fsdp", None),
        P("fsdp", None),
        P("fsdp", None),
        P("fsdp", None),
        P("fsdp"),
        P("fsdp", None),
        P("fsdp", None),
        P("fsdp", None),
        P("fsdp", None),
        P("fsdp", None),
        P("fsdp", None),
        P("fsdp", None),
        P("fsdp", None),
        P("fsdp", None),
    )
    out_specs = (
        P("fsdp", "seq", None),
        P("fsdp", "seq", None),
        P("fsdp"),
        P("fsdp", None),
        P("fsdp", None),
        P("fsdp", None),
        P("fsdp", None),
        P("fsdp", None),
        P("fsdp", None),
        P("fsdp", None),
        P("fsdp", None),
        P("fsdp", None),
        P("fsdp", None),
        P("fsdp", None),
        P("fsdp", None),
        P("fsdp"),
        P("fsdp", None),
        P("fsdp", None),
        P("fsdp", None),
        P("fsdp", None),
        P("fsdp", None),
        P("fsdp", None),
        P("fsdp", None),
        P("fsdp", None),
        P("fsdp", None),
        P(),
        P(),
    )
    return jax.shard_map(shards, mesh=mesh, in_specs=in_specs, out_specs=out_specs, check_vma=False)
```

profile of v0, /device:TPU:0, one launch (start us, length us, event | category | flops | bytes accessed | tf_op | source)
XLA Modules:
  0.0 3613.9 jit_solution(12072195137469182479)
XLA Ops:
  11.7 24.0 all-reduce.6
  38.0 31.6 all_gather.88
  69.6 32.0 all_gather.87
  103.2 31.5 all_gather.86
  137.2 30.6 all_gather.92
  167.9 31.5 all_gather.91
  200.6 31.5 all_gather.90
  238.5 5.1 all_gather.81
  249.5 34.5 all_gather.85
  283.9 34.6 all_gather.95
  321.6 33.3 all_gather.84
  354.9 35.5 all_gather.96
  390.4 35.0 all_gather.102
  425.5 35.2 all_gather.99
  460.7 32.7 all_gather.106
  508.7 16.4 conditional.2
  537.9 9.4 fusion.84
  547.4 9.7 fusion.83
  557.1 9.1 fusion.86
  566.2 190.5 %all-gather.23.cloned.1.call-done = bf16[1152,6912]{1,0:T(8,128)(2,1)} async-done(((bf16[144,6912]{1,0:T(8,128)(2,1)}), bf16[1152,6912]{1,0:T(8,128)(2,1)}) %all-gather.23.cloned.1.call-update) | async-done | bytes 15925264 | tf_op jit(solution)/shard_map/all_gather | solution.py:207
  756.7 20.4 convolution_add_fusion.1
  777.1 197.2 %all-gather.27.cloned.1.call-done = bf16[6912,1152]{1,0:T(8,128)(2,1)} async-done(((bf16[864,1152]{1,0:T(8,128)(2,1)}), bf16[6912,1152]{1,0:T(8,128)(2,1)}) %all-gather.27.cloned.1.call-update) | async-done | bytes 15925264 | tf_op jit(solution)/shard_map/all_gather | solution.py:208
  974.3 25.8 convolution_add_fusion
  1000.1 191.7 %all-gather.19.cloned.1.call-done = bf16[1152,6912]{1,0:T(8,128)(2,1)} async-done(((bf16[144,6912]{1,0:T(8,128)(2,1)}), bf16[1152,6912]{1,0:T(8,128)(2,1)}) %all-gather.19.cloned.1.call-update) | async-done | bytes 15925264 | tf_op jit(solution)/shard_map/all_gather | solution.py:206
  1191.8 32.9 fusion.22
  1224.7 6.2 convolution_convert_fusion.22
  1237.5 16.6 convolution_add_fusion.3
  1254.1 16.3 multiply_reduce_fusion.1
  1276.7 38.7 %conditional.3 = (bf16[2,1024,256]{2,1,0:T(8,128)(2,1)}, bf16[2,1024,256]{2,1,0:T(8,128)(2,1)}, f32[512,4,128]{2,1,0:T(4,128)}, f32[512,4,128]{2,1,0:T(4,128)}) conditional(s32[]{:T(128)} %convert_element_type.401, () %tuple.37, (bf16[2,1024,256]{2,1,0:T(8,128)(2,1)}, bf16[2,1024,256]{2,1,0:T(8,128)(2,1)S(1)}, f32[2,1024]{1,0:T(2,128)}, ...), branch_computations={%region_8.9_spmd, %region_9.0_spmd} | conditional | flops 5392826368 | bytes 130081000 | solution.py:344
  1276.7 6.2 fusion.78
  1287.5 5.3 multiply_convert_fusion
  1307.6 7.4 fusion.9
  1335.7 6.2 convolution_convert_fusion.25
  1357.0 9.7 reduce-scatter.26.cloned.1.call-done
  1383.3 7.0 convolution_convert_fusion.5
  1390.4 7.0 convolution_convert_fusion.4
  1397.4 6.9 convolution_convert_fusion.3
  1404.4 14.5 convolution_convert_fusion.1
  1419.2 14.5 convolution_convert_fusion.2
  1433.8 15.2 convolution_convert_fusion
  1451.1 39.7 %all-reduce.4 = (f32[3]{0:T(128)}, f32[3]{0:T(128)}) all-reduce(f32[3]{0:T(128)} %get-tuple-element.147, f32[3]{0:T(128)} %get-tuple-element.146), channel_id=1, replica_groups=mesh['seq'=4,'fsdp'=8] {'seq','fsdp'}, use_global_device_ids=true, to_apply=%region_63.64 | all-reduce | flops 6 | bytes 48 | tf_op jit(solution)/shard_map/psum | solution.py:449
  1500.0 60.8 %reduce-scatter.58.cloned.1.call-done = bf16[144,256]{1,0:T(8,128)(2,1)} async-done(((bf16[1152,256]{1,0:T(8,128)(2,1)}), bf16[144,256]{1,0:T(8,128)(2,1)}) %reduce-scatter.58.cloned.1.call-update) | async-done | bytes 73744 | tf_op jit(solution)/shard_map/reduce_scatter | solution.py:278
  1560.8 64.6 %reduce-scatter.62.cloned.1.call-done = bf16[144,256]{1,0:T(8,128)(2,1)} async-done(((bf16[1152,256]{1,0:T(8,128)(2,1)}), bf16[144,256]{1,0:T(8,128)(2,1)}) %reduce-scatter.62.cloned.1.call-update) | async-done | bytes 73744 | tf_op jit(solution)/shard_map/reduce_scatter | solution.py:284
  1625.4 64.3 %reduce-scatter.50.cloned.1.call-done = bf16[32,1152]{1,0:T(8,128)(2,1)} async-done(((bf16[256,1152]{1,0:T(8,128)(2,1)}), bf16[32,1152]{1,0:T(8,128)(2,1)}) %reduce-scatter.50.cloned.1.call-update) | async-done | bytes 73744 | tf_op jit(solution)/shard_map/reduce_scatter | solution.py:416
  1689.7 64.6 %reduce-scatter.36.cloned.1.call-done = bf16[144,256]{1,0:T(8,128)(2,1)} async-done(((bf16[1152,256]{1,0:T(8,128)(2,1)}), bf16[144,256]{1,0:T(8,128)(2,1)}) %reduce-scatter.36.cloned.1.call-update) | async-done | bytes 73744 | tf_op jit(solution)/shard_map/reduce_scatter | solution.py:395
  1754.4 64.4 %reduce-scatter.68.cloned.1.call-done = bf16[32,1152]{1,0:T(8,128)(2,1)} async-done(((bf16[256,1152]{1,0:T(8,128)(2,1)}), bf16[32,1152]{1,0:T(8,128)(2,1)}) %reduce-scatter.68.cloned.1.call-update) | async-done | bytes 73744 | tf_op jit(solution)/shard_map/reduce_scatter | solution.py:293
  1818.8 64.7 %reduce-scatter.30.cloned.1.call-done = bf16[144,256]{1,0:T(8,128)(2,1)} async-done(((bf16[1152,256]{1,0:T(8,128)(2,1)}), bf16[144,256]{1,0:T(8,128)(2,1)}) %reduce-scatter.30.cloned.1.call-update) | async-done | bytes 73744 | tf_op jit(solution)/shard_map/reduce_scatter | solution.py:386
  1883.4 64.4 %reduce-scatter.40.cloned.1.call-done = bf16[144,256]{1,0:T(8,128)(2,1)} async-done(((bf16[1152,256]{1,0:T(8,128)(2,1)}), bf16[144,256]{1,0:T(8,128)(2,1)}) %reduce-scatter.40.cloned.1.call-update) | async-done | bytes 73744 | tf_op jit(solution)/shard_map/reduce_scatter | solution.py:401
  1947.8 64.8 %reduce-scatter.44.cloned.1.call-done = bf16[144,256]{1,0:T(8,128)(2,1)} async-done(((bf16[1152,256]{1,0:T(8,128)(2,1)}), bf16[144,256]{1,0:T(8,128)(2,1)}) %reduce-scatter.44.cloned.1.call-update) | async-done | bytes 73744 | tf_op jit(solution)/shard_map/reduce_scatter | solution.py:407
  2012.6 64.4 %reduce-scatter.32.cloned.1.call-done = bf16[144,256]{1,0:T(8,128)(2,1)} async-done(((bf16[1152,256]{1,0:T(8,128)(2,1)}), bf16[144,256]{1,0:T(8,128)(2,1)}) %reduce-scatter.32.cloned.1.call-update) | async-done | bytes 73744 | tf_op jit(solution)/shard_map/reduce_scatter | solution.py:389
  2077.0 71.8 %reduce-scatter.34.cloned.1.call-done = bf16[128,1152]{1,0:T(8,128)(2,1)} async-done(((bf16[1024,1152]{1,0:T(8,128)(2,1)}), bf16[128,1152]{1,0:T(8,128)(2,1)}) %reduce-scatter.34.cloned.1.call-update) | async-done | bytes 294928 | tf_op jit(solution)/shard_map/reduce_scatter | solution.py:392
  2148.9 72.0 %reduce-scatter.28.cloned.1.call-done = bf16[144,1024]{1,0:T(8,128)(2,1)} async-done(((bf16[1152,1024]{1,0:T(8,128)(2,1)}), bf16[144,1024]{1,0:T(8,128)(2,1)}) %reduce-scatter.28.cloned.1.call-update) | async-done | bytes 294928 | tf_op jit(solution)/shard_map/reduce_scatter | solution.py:383
  2220.9 82.5 %reduce-scatter.60.cloned.1.call-done = bf16[32,6912]{1,0:T(8,128)(2,1)} async-done(((bf16[256,6912]{1,0:T(8,128)(2,1)}), bf16[32,6912]{1,0:T(8,128)(2,1)}) %reduce-scatter.60.cloned.1.call-update) | async-done | bytes 442384 | tf_op jit(solution)/shard_map/reduce_scatter | solution.py:281
  2303.4 83.2 %reduce-scatter.64.cloned.1.call-done = bf16[32,6912]{1,0:T(8,128)(2,1)} async-done(((bf16[256,6912]{1,0:T(8,128)(2,1)}), bf16[32,6912]{1,0:T(8,128)(2,1)}) %reduce-scatter.64.cloned.1.call-update) | async-done | bytes 442384 | tf_op jit(solution)/shard_map/reduce_scatter | solution.py:287
  2386.6 83.4 %reduce-scatter.66.cloned.1.call-done = bf16[864,256]{1,0:T(8,128)(2,1)} async-done(((bf16[6912,256]{1,0:T(8,128)(2,1)}), bf16[864,256]{1,0:T(8,128)(2,1)}) %reduce-scatter.66.cloned.1.call-update) | async-done | bytes 442384 | tf_op jit(solution)/shard_map/reduce_scatter | solution.py:290
  2470.0 273.2 %reduce-scatter.54.cloned.1.call-done = bf16[144,6912]{1,0:T(8,128)(2,1)} async-done(((bf16[1152,6912]{1,0:T(8,128)(2,1)}), bf16[144,6912]{1,0:T(8,128)(2,1)}) %reduce-scatter.54.cloned.1.call-update) | async-done | bytes 1990672 | tf_op jit(solution)/shard_map/reduce_scatter | solution.py:272
  2743.2 272.7 %reduce-scatter.52.cloned.1.call-done = bf16[144,6912]{1,0:T(8,128)(2,1)} async-done(((bf16[1152,6912]{1,0:T(8,128)(2,1)}), bf16[144,6912]{1,0:T(8,128)(2,1)}) %reduce-scatter.52.cloned.1.call-update) | async-done | bytes 1990672 | tf_op jit(solution)/shard_map/reduce_scatter | solution.py:269
  3015.9 272.8 %reduce-scatter.56.cloned.1.call-done = bf16[864,1152]{1,0:T(8,128)(2,1)} async-done(((bf16[6912,1152]{1,0:T(8,128)(2,1)}), bf16[864,1152]{1,0:T(8,128)(2,1)}) %reduce-scatter.56.cloned.1.call-update) | async-done | bytes 1990672 | tf_op jit(solution)/shard_map/reduce_scatter | solution.py:275
  3288.7 17.5 fusion.30
  3315.4 20.4 all-reduce.5
  3343.4 9.6 reduce-scatter.42.cloned.1.call-done
  3353.0 64.0 %reduce-scatter.46.cloned.1.call-done = bf16[32,256]{1,0:T(8,128)(2,1)} async-done(((bf16[256,256]{1,0:T(8,128)(2,1)}), bf16[32,256]{1,0:T(8,128)(2,1)}) %reduce-scatter.46.cloned.1.call-update) | async-done | bytes 16400 | tf_op jit(solution)/shard_map/reduce_scatter | solution.py:410
  3417.0 11.0 all-reduce.7
  3430.3 155.6 %all-reduce.11.cloned.1.call-done = (bf16[144,1024]{1,0:T(8,128)(2,1)}, bf16[144,256]{1,0:T(8,128)(2,1)}, bf16[144,256]{1,0:T(8,128)(2,1)}, bf16[128,1152]{1,0:T...) async-done(((bf16[144,1024]{1,0:T(8,128)(2,1)}, ...) | async-done | bytes 8683536 | tf_op jit(solution)/shard_map/psum | solution.py:422
  (459 shorter events, 204.2 us)
Async XLA Ops:
  7.2 94.4 %copy-start = (bf16[2,256,1152]{2,1,0:T(8,128)(2,1)S(1)}, bf16[2,256,1152]{2,1,0:T(8,128)(2,1)}, u32[]{:S(2)}) copy-start(bf16[2,256,1152]{2,1,0:T(8,128)(2,1)} %param.32) | copy-start | bytes 3538948
  7.2 490.0 %all-gather.11.cloned.1.call-start = ((), (), s32[]{:S(2)}) async-start(), calls=%async_computation.23 | async-start | bytes 2654208 | tf_op jit(solution)/shard_map/all_gather | solution.py:124
  7.9 500.8 %all-gather.13.cloned.1.call-start = ((), (), s32[]{:S(2)}) async-start(), calls=%async_computation.24 | async-start | bytes 1310720 | tf_op jit(solution)/shard_map/all_gather | solution.py:164
  35.7 66.2 %copy-start.79 = (f32[1152]{0:T(1024)}, f32[1152]{0:T(1024)S(1)}, u32[]{:S(2)}) copy-start(f32[1152]{0:T(1024)S(1)} %convert_element_type.403) | copy-start | bytes 13828
  37.9 64.0 %copy-start.109 = (f32[1,2,2,128]{3,1,2,0:T(2,128)}, f32[1,2,2,128]{3,1,2,0:T(2,128)S(1)}, u32[]{:S(2)}) copy-start(f32[1,2,2,128]{3,1,2,0:T(2,128)S(1)} %copy.80) | copy-start | bytes 6148
  37.9 64.6 %copy-start.101 = (f32[512]{0:T(512)}, f32[512]{0:T(512)S(1)}, u32[]{:S(2)}) copy-start(f32[512]{0:T(512)S(1)} %rsqrt.23) | copy-start | bytes 6148
  69.5 33.0 copy-start.60
  69.5 65.7 %copy-start.113 = (f32[128]{0:T(128)}, f32[128]{0:T(128)S(1)}, u32[]{:S(2)}) copy-start(f32[128]{0:T(128)S(1)} %multiply_power_fusion) | copy-start | bytes 1540
  102.0 395.3 %copy-start.6 = (bf16[512,1152]{1,0:T(8,128)(2,1)}, bf16[512,1152]{1,0:T(8,128)(2,1)S(1)}, u32[]{:S(2)}) copy-start(bf16[512,1152]{1,0:T(8,128)(2,1)S(1)} %fusion.37) | copy-start | bytes 3538948
  134.7 64.7 %copy-start.14 = (bf16[1152,256]{1,0:T(8,128)(2,1)}, bf16[1152,256]{1,0:T(8,128)(2,1)S(1)}, u32[]{:S(2)}) copy-start(bf16[1152,256]{1,0:T(8,128)(2,1)S(1)} %all_gather.86) | copy-start | bytes 1769476
  137.2 371.5 %all-gather.15.cloned.1.call-start = ((), (), s32[]{:S(2)}) async-start(), calls=%async_computation.25 | async-start | bytes 1310720 | tf_op jit(solution)/shard_map/all_gather | solution.py:165
  167.9 32.0 copy-start.46
  199.4 33.9 copy-start.27
  233.3 297.4 %all-gather.17.cloned.1.call-start = ((), (), s32[]{:S(2)}) async-start(), calls=%async_computation.26 | async-start | bytes 2654208 | tf_op jit(solution)/shard_map/all_gather | solution.py:127
  233.9 304.0 %all-gather.25.cloned.1.call-start = ((), (), s32[]{:S(2)}) async-start(), calls=%async_computation.30 | async-start | bytes 3981312 | tf_op jit(solution)/shard_map/all_gather | solution.py:212
  234.5 312.9 %all-gather.21.cloned.1.call-start = ((), (), s32[]{:S(2)}) async-start(), calls=%async_computation.28 | async-start | bytes 3981312 | tf_op jit(solution)/shard_map/all_gather | solution.py:210
  235.1 322.0 %all-gather.29.cloned.1.call-start = ((), (), s32[]{:S(2)}) async-start(), calls=%async_computation.32 | async-start | bytes 3981312 | tf_op jit(solution)/shard_map/all_gather | solution.py:213
  235.8 520.9 %all-gather.23.cloned.1.call-start = ((), (), s32[]{:S(2)}) async-start(), calls=%async_computation.29 | async-start | bytes 17915904 | tf_op jit(solution)/shard_map/all_gather | solution.py:207
  236.6 737.7 %all-gather.27.cloned.1.call-start = ((), (), s32[]{:S(2)}) async-start(), calls=%async_computation.31 | async-start | bytes 17915904 | tf_op jit(solution)/shard_map/all_gather | solution.py:208
  237.3 954.4 %all-gather.19.cloned.1.call-start = ((), (), s32[]{:S(2)}) async-start(), calls=%async_computation.27 | async-start | bytes 17915904 | tf_op jit(solution)/shard_map/all_gather | solution.py:206
  237.9 1108.1 %reduce-scatter.24.cloned.1.call-start = ((), (), s32[]{:S(2)}) async-start(), calls=%async_computation.33 | async-start | bytes 1310720 | tf_op jit(solution)/shard_map/reduce_scatter | solution.py:348
  244.3 74.3 %copy-start.114 = (f32[128]{0:T(128)S(1)}, f32[128]{0:T(128)}, u32[]{:S(2)}) copy-start(f32[128]{0:T(128)} %copy-done.113) | copy-start | bytes 1540
  244.3 77.3 %copy-start.93 = (bf16[144,256]{1,0:T(8,128)(2,1)S(1)}, bf16[144,256]{1,0:T(8,128)(2,1)}, u32[]{:S(2)}) copy-start(bf16[144,256]{1,0:T(8,128)(2,1)} %param.42) | copy-start | bytes 221188
  249.3 72.2 %copy-start.110 = (s32[1,2,2,128]{3,1,2,0:T(2,128)}, s32[1,2,2,128]{3,1,2,0:T(2,128)S(1)}, u32[]{:S(2)}) copy-start(s32[1,2,2,128]{3,1,2,0:T(2,128)S(1)} %copy.79) | copy-start | bytes 6148
  249.4 285.9 %copy-start.81 = (f32[1152]{0:T(1024)}, f32[1152]{0:T(1024)S(1)}, u32[]{:S(2)}) copy-start(f32[1152]{0:T(1024)S(1)} %convert_element_type.414) | copy-start | bytes 13828
  249.4 72.1 %copy-start.106 = (f32[512]{0:T(512)}, f32[512]{0:T(512)S(1)}, u32[]{:S(2)}) copy-start(f32[512]{0:T(512)S(1)} %broadcast_multiply_fusion) | copy-start | bytes 6148
  249.4 285.0 %copy-start.103 = (f32[512]{0:T(512)}, f32[512]{0:T(512)S(1)}, u32[]{:S(2)}) copy-start(f32[512]{0:T(512)S(1)} %compare_convert_fusion) | copy-start | bytes 6148
  249.4 211.2 %copy-start.94 = (bf16[32,1152]{1,0:T(8,128)(2,1)S(1)}, bf16[32,1152]{1,0:T(8,128)(2,1)}, u32[]{:S(2)}) copy-start(bf16[32,1152]{1,0:T(8,128)(2,1)} %param.59) | copy-start | bytes 221188
  354.9 138.5 %copy-start.32 = (bf16[1152,256]{1,0:T(8,128)(2,1)}, bf16[1152,256]{1,0:T(8,128)(2,1)S(1)}, u32[]{:S(2)}) copy-start(bf16[1152,256]{1,0:T(8,128)(2,1)S(1)} %all_gather.84) | copy-start | bytes 1769476
  354.9 139.8 %copy-start.4 = (bf16[2,256,1152]{2,1,0:T(8,128)(2,1)S(1)}, bf16[2,256,1152]{2,1,0:T(8,128)(2,1)}, u32[]{:S(2)}) copy-start(bf16[2,256,1152]{2,1,0:T(8,128)(2,1)} %param.33) | copy-start | bytes 3538948
  535.2 12.1 copy-start.107
  536.8 655.0 %copy-start.44 = (bf16[512,1152]{1,0:T(8,128)(2,1)}, bf16[512,1152]{1,0:T(8,128)(2,1)S(1)}, u32[]{:S(2)}) copy-start(bf16[512,1152]{1,0:T(8,128)(2,1)S(1)} %multiply_convert_fusion.4) | copy-start | bytes 3538948
  566.2 408.1 %copy-start.17 = (bf16[512,1152]{1,0:T(8,128)(2,1)S(1)}, bf16[512,1152]{1,0:T(8,128)(2,1)}, u32[]{:S(2)}) copy-start(bf16[512,1152]{1,0:T(8,128)(2,1)} %copy-done.16) | copy-start | bytes 3538948
  1237.5 16.6 copy-start.3
  1237.5 16.6 copy-start.82
  1237.5 16.6 copy-start.98
  1254.1 16.4 copy-start.108
  1254.1 16.4 copy-start.5
  1254.1 16.4 copy-start.104
  1315.5 51.3 %reduce-scatter.26.cloned.1.call-start = ((), (), s32[]{:S(2)}) async-start(), calls=%async_computation.34 | async-start | bytes 1310720 | tf_op jit(solution)/shard_map/reduce_scatter | solution.py:351
  1316.0 184.0 %reduce-scatter.48.cloned.1.call-start = ((), (), s32[]{:S(2)}) async-start(), calls=%async_computation.45 | async-start | bytes 589824 | tf_op jit(solution)/shard_map/reduce_scatter | solution.py:413
  1318.6 181.4 %reduce-scatter.38.cloned.1.call-start = ((), (), s32[]{:S(2)}) async-start(), calls=%async_computation.40 | async-start | bytes 589824 | tf_op jit(solution)/shard_map/reduce_scatter | solution.py:398
  1324.0 236.8 %reduce-scatter.58.cloned.1.call-start = ((), (), s32[]{:S(2)}) async-start(), calls=%async_computation.50 | async-start | bytes 663552 | tf_op jit(solution)/shard_map/reduce_scatter | solution.py:278
  1326.4 299.1 %reduce-scatter.62.cloned.1.call-start = ((), (), s32[]{:S(2)}) async-start(), calls=%async_computation.52 | async-start | bytes 663552 | tf_op jit(solution)/shard_map/reduce_scatter | solution.py:284
  1328.7 361.0 %reduce-scatter.50.cloned.1.call-start = ((), (), s32[]{:S(2)}) async-start(), calls=%async_computation.46 | async-start | bytes 663552 | tf_op jit(solution)/shard_map/reduce_scatter | solution.py:416
  1331.7 422.7 %reduce-scatter.36.cloned.1.call-start = ((), (), s32[]{:S(2)}) async-start(), calls=%async_computation.39 | async-start | bytes 663552 | tf_op jit(solution)/shard_map/reduce_scatter | solution.py:395
  1335.6 483.1 %reduce-scatter.68.cloned.1.call-start = ((), (), s32[]{:S(2)}) async-start(), calls=%async_computation.55 | async-start | bytes 663552 | tf_op jit(solution)/shard_map/reduce_scatter | solution.py:293
  1343.9 539.5 %reduce-scatter.30.cloned.1.call-start = ((), (), s32[]{:S(2)}) async-start(), calls=%async_computation.36 | async-start | bytes 663552 | tf_op jit(solution)/shard_map/reduce_scatter | solution.py:386
  1352.3 595.5 %reduce-scatter.40.cloned.1.call-start = ((), (), s32[]{:S(2)}) async-start(), calls=%async_computation.41 | async-start | bytes 663552 | tf_op jit(solution)/shard_map/reduce_scatter | solution.py:401
  1357.0 655.6 %reduce-scatter.44.cloned.1.call-start = ((), (), s32[]{:S(2)}) async-start(), calls=%async_computation.43 | async-start | bytes 663552 | tf_op jit(solution)/shard_map/reduce_scatter | solution.py:407
  1371.3 705.8 %reduce-scatter.32.cloned.1.call-start = ((), (), s32[]{:S(2)}) async-start(), calls=%async_computation.37 | async-start | bytes 663552 | tf_op jit(solution)/shard_map/reduce_scatter | solution.py:389
  1374.0 774.9 %reduce-scatter.34.cloned.1.call-start = ((), (), s32[]{:S(2)}) async-start(), calls=%async_computation.38 | async-start | bytes 2654208 | tf_op jit(solution)/shard_map/reduce_scatter | solution.py:392
  1378.6 842.3 %reduce-scatter.28.cloned.1.call-start = ((), (), s32[]{:S(2)}) async-start(), calls=%async_computation.35 | async-start | bytes 2654208 | tf_op jit(solution)/shard_map/reduce_scatter | solution.py:383
  1383.3 920.1 %reduce-scatter.60.cloned.1.call-start = ((), (), s32[]{:S(2)}) async-start(), calls=%async_computation.51 | async-start | bytes 3981312 | tf_op jit(solution)/shard_map/reduce_scatter | solution.py:281
  1390.3 996.3 %reduce-scatter.64.cloned.1.call-start = ((), (), s32[]{:S(2)}) async-start(), calls=%async_computation.53 | async-start | bytes 3981312 | tf_op jit(solution)/shard_map/reduce_scatter | solution.py:287
  1397.4 1072.6 %reduce-scatter.66.cloned.1.call-start = ((), (), s32[]{:S(2)}) async-start(), calls=%async_computation.54 | async-start | bytes 3981312 | tf_op jit(solution)/shard_map/reduce_scatter | solution.py:290
  1404.3 1338.9 %reduce-scatter.54.cloned.1.call-start = ((), (), s32[]{:S(2)}) async-start(), calls=%async_computation.48 | async-start | bytes 17915904 | tf_op jit(solution)/shard_map/reduce_scatter | solution.py:272
  1418.9 1596.9 %reduce-scatter.52.cloned.1.call-start = ((), (), s32[]{:S(2)}) async-start(), calls=%async_computation.47 | async-start | bytes 17915904 | tf_op jit(solution)/shard_map/reduce_scatter | solution.py:269
  1433.7 1855.0 %reduce-scatter.56.cloned.1.call-start = ((), (), s32[]{:S(2)}) async-start(), calls=%async_computation.49 | async-start | bytes 17915904 | tf_op jit(solution)/shard_map/reduce_scatter | solution.py:275
  1449.0 1904.0 %reduce-scatter.42.cloned.1.call-start = ((), (), s32[]{:S(2)}) async-start(), calls=%async_computation.42 | async-start | bytes 147456 | tf_op jit(solution)/shard_map/reduce_scatter | solution.py:404
  1492.7 1924.2 %reduce-scatter.46.cloned.1.call-start = ((), (), s32[]{:S(2)}) async-start(), calls=%async_computation.44 | async-start | bytes 147456 | tf_op jit(solution)/shard_map/reduce_scatter | solution.py:410
  1496.7 2089.3 %all-reduce.11.cloned.1.call-start = ((), (), s32[]{:S(2)}) async-start(), calls=%async_computation.56 | async-start | bytes 17367040 | tf_op jit(solution)/shard_map/psum | solution.py:422
  3288.7 17.5 copy-start.21
  3288.7 17.5 copy-start.117
  (93 other events, 312.0 us)
Sparse Core Ops, SparseCore 0:
  10.2 57.1 all-gather.10
  137.3 14.0 all-gather.12
  233.5 14.4 all-gather.14
  250.0 60.0 all-gather.16
  312.1 79.4 all-gather.24
  393.7 77.8 all-gather.20
  473.8 64.9 all-gather.28
  541.0 215.6 all-gather.22
  758.9 215.3 all-gather.26
  976.4 215.3 all-gather.18
  1315.6 23.0 reduce-scatter.23
  1341.8 24.8 reduce-scatter.25
  1370.1 61.9 reduce-scatter.47
  1435.6 60.9 reduce-scatter.37
  1499.7 61.0 reduce-scatter.57
  1564.3 61.0 reduce-scatter.61
  1628.6 61.1 reduce-scatter.49
  1693.2 61.0 reduce-scatter.35
  1757.6 61.0 reduce-scatter.67
  1822.2 61.1 reduce-scatter.29
  1886.7 61.0 reduce-scatter.39
  1951.5 61.1 reduce-scatter.43
  2015.9 61.0 reduce-scatter.31
  2080.8 68.0 reduce-scatter.33
  2152.7 68.0 reduce-scatter.27
  2225.4 77.9 reduce-scatter.59
  2307.9 78.6 reduce-scatter.63
  2391.2 78.6 reduce-scatter.65
  2474.4 268.7 reduce-scatter.53
  2747.4 268.3 reduce-scatter.51
  3020.3 268.3 reduce-scatter.55
  3292.9 59.9 reduce-scatter.41
  3357.1 59.8 reduce-scatter.45
  3422.5 163.3 all-reduce.10
where the time goes:
time: 3620 us; the launch traced here: 3610 us
  waiting for transfers between devices  2610 us (72%)
  blocking collectives  530 us (15%)
  matrix products  347 us (10%)
  other arithmetic  64.5 us (2%)
  local copies, waits for them, and re-layouts  38.8 us (1%)
    reduce_scatter x1, waiting for transfers between devices, shards(): lax.psum_scatter(g_up_base.astype(jnp.bfloat16), 'fsdp', scatter_dimensio...  273 us
    reduce_scatter x1, waiting for transfers between devices, shards(): lax.psum_scatter(g_down_base.astype(jnp.bfloat16), 'fsdp', scatter_dimens...  273 us
    reduce_scatter x1, waiting for transfers between devices, shards(): lax.psum_scatter(g_gate_base.astype(jnp.bfloat16), 'fsdp', scatter_dimens...  273 us
    all_gather x1, waiting for transfers between devices, shards(): lax.all_gather(down_weight, 'fsdp', axis=0, tiled=True)  197 us
    all_gather x1, waiting for transfers between devices, shards(): lax.all_gather(gate_weight, 'fsdp', axis=0, tiled=True)  192 us
    all_gather x1, waiting for transfers between devices, shards(): lax.all_gather(up_weight, 'fsdp', axis=0, tiled=True)  191 us
    psum x1, waiting for transfers between devices, shards(): lax.psum(attn_shards[1].astype(jnp.bfloat16), 'seq').astype(jnp.float32)  156 us
    reduce_scatter x1, waiting for transfers between devices, shards(): lax.psum_scatter(g_down_down.astype(jnp.bfloat16), 'fsdp', scatter_dimens...  83.4 us
  transfers between devices with their start and end apart: 34, of which 24 were waited for; matrix products, arithmetic and copies ran while one was open for 8% of the time, Pallas kernels for 0%

commit v1 on v0

v1 whole, which is shorter than its diff:
```python
import jax
import jax.numpy as jnp
from jax import lax
from jax.sharding import PartitionSpec as P

H = 4
HD = 256
DEPTHS = 3
LOOP = 1
CORES = 2

epsilon = 1e-06
rope_base = 10000.0
low = jnp.bfloat16
wide = jnp.float32


def mul(left, right):
    return jnp.dot(left, right, preferred_element_type=wide)


def mul_t(left, right):
    return lax.dot_general(left, right, (((1,), (1,)), ((), ())), preferred_element_type=wide)


def t_mul(left, right):
    return lax.dot_general(left, right, (((0,), (0,)), ((), ())), preferred_element_type=wide)


def ring_order(count, width):
    if width < 2 or count % width or (count // width) % 2:
        return list(range(count))
    depth = count // width
    walk = [0]
    for z in range(depth):
        columns = range(1, width) if z % 2 == 0 else range(width - 1, 0, -1)
        walk += [z * width + x for x in columns]
    walk += [z * width for z in range(depth - 1, 0, -1)]
    return walk


class Ring:
    def __init__(self, count, width):
        self.count = count
        walk = ring_order(count, width)
        self.walk = jnp.array(walk, jnp.int32)
        place = [0] * count
        for spot, device in enumerate(walk):
            place[device] = spot
        self.spot = jnp.array(place, jnp.int32)[lax.axis_index("fsdp")]
        self.up = [(walk[i], walk[(i + 1) % count]) for i in range(count)]
        self.down = [(b, a) for a, b in self.up]

    def at(self, offset):
        return self.walk[lax.rem(self.spot + offset + self.count, self.count)]

    def gather(self, block, flip=False):
        ahead, back, sign = (self.down, self.up, 1) if flip else (self.up, self.down, -1)
        pieces = [(self.at(0), block)]
        first = second = block
        for step in range(1, self.count // 2 + 1):
            first = lax.ppermute(first, "fsdp", ahead)
            pieces.append((self.at(sign * step), first))
            if step <= (self.count - 1) // 2:
                second = lax.ppermute(second, "fsdp", back)
                pieces.append((self.at(-sign * step), second))
        return pieces

    def scatter(self, part, flip=False):
        ahead, back, sign = (self.down, self.up, -1) if flip else (self.up, self.down, 1)
        total = part(self.at(0))
        for way, side, steps in (
            (ahead, sign, self.count // 2),
            (back, -sign, (self.count - 1) // 2),
        ):
            moving = None
            for step in range(steps, 0, -1):
                term = part(self.at(side * step))
                if moving is not None:
                    term = term + moving.astype(wide)
                moving = lax.ppermute(term.astype(low), "fsdp", way)
            if moving is not None:
                total = total + moving.astype(wide)
        return total


class Group:
    def __init__(self, count):
        self.count = count
        self.chips = count // CORES
        me = lax.axis_index("seq")
        self.y, self.core = me // CORES, lax.rem(me, CORES)
        self.sibling = [(i, i ^ 1) for i in range(count)]
        self.order = [(k, c) for k in range(self.chips) for c in range(CORES)]

    def shift(self, k):
        n = self.chips
        return [(i, ((i // CORES + k) % n) * CORES + i % CORES) for i in range(self.count)]

    def index(self, k, c):
        return lax.rem(self.y + k, self.chips) * CORES + (self.core + c) % CORES

    def pieces(self, block):
        mine = [block] + [
            lax.ppermute(block, "seq", self.shift(-k)) for k in range(1, self.chips)
        ]
        out = []
        for piece in mine:
            out += [piece, lax.ppermute(piece, "seq", self.sibling)]
        return out

    def scatter(self, part):
        near = [part(k, 0) for k in range(self.chips)]
        far = [
            lax.ppermute(part(k, 1).astype(low), "seq", self.sibling) for k in range(self.chips)
        ]
        sums = [a + b.astype(wide) for a, b in zip(near, far, strict=True)]
        total = sums[0]
        for k in range(1, self.chips):
            total = total + lax.ppermute(sums[k].astype(low), "seq", self.shift(k)).astype(wide)
        return total

    def laid(self, pieces, axis, dtype):
        width = pieces[0].shape[axis]
        shape = list(pieces[0].shape)
        shape[axis] = width * self.count
        out = jnp.zeros(shape, dtype)
        for (k, c), piece in zip(self.order, pieces, strict=True):
            out = lax.dynamic_update_slice_in_dim(
                out, piece.astype(dtype), self.index(k, c) * width, axis
            )
        return out


def stacked(pieces, count):
    out = jnp.zeros((count,) + pieces[0][1].shape, pieces[0][1].dtype)
    for index, block in pieces:
        out = lax.dynamic_update_index_in_dim(out, block, index, 0)
    return out


def spread_sum(values, axis):
    count = lax.axis_size(axis)
    if count & (count - 1):
        return lax.psum(values, axis)
    step = 1
    while step < count:
        values = values + lax.ppermute(values, axis, [(i, i ^ step) for i in range(count)])
        step *= 2
    return values


def rope(values, cosine, sine):
    half = values.shape[-1] // 2
    first, second = values[..., :half], values[..., half:]
    cosine, sine = cosine[:, None, :], sine[:, None, :]
    return jnp.concatenate([first * cosine - second * sine, second * cosine + first * sine], axis=-1)


def gelu_parts(gate):
    scale = (2.0 / jnp.pi) ** 0.5
    cube = 0.044715
    curve = jnp.tanh(scale * (gate + cube * gate * gate * gate))
    value = 0.5 * gate * (1.0 + curve)
    slope = 0.5 * (1.0 + curve) + 0.5 * gate * (1.0 - curve * curve) * scale * (
        1.0 + 3.0 * cube * gate * gate
    )
    return value, slope


def shards(
    inputs,
    cotangent,
    segments,
    exits,
    confidence,
    attn_gain,
    q_weight,
    k_weight,
    v_weight,
    o_weight,
    q_down,
    q_up,
    k_down,
    k_up,
    v_down,
    v_up,
    o_down,
    o_up,
    mlp_gain,
    gate_weight,
    up_weight,
    down_weight,
    gate_down,
    gate_up,
    up_down,
    up_up,
    down_down,
    down_up,
):
    n_seq, n_f = lax.axis_size("seq"), lax.axis_size("fsdp")
    me = lax.axis_index("seq")
    ring = Ring(n_f, n_seq // CORES)
    group = Group(n_seq)
    rows, length, width = inputs.shape
    tokens = rows * length
    rank = q_down.shape[1]
    hq = q_weight.shape[1]
    ff = gate_weight.shape[1]
    own_rows = q_weight.shape[0]
    rank_rows = q_up.shape[0]
    o_rows = o_weight.shape[0]
    cut = ff // (n_f * n_seq)
    slab = n_f * cut
    scale = HD ** (-0.5)

    gain1 = attn_gain.astype(wide)[:, None]
    gain2 = mlp_gain.astype(wide)[:, None]

    def columns_of(array):
        part = array.shape[1] // n_seq
        return lax.dynamic_slice_in_dim(array, me * part, part, 1)

    def rows_of(array):
        part = array.shape[0] // n_seq
        return lax.dynamic_slice_in_dim(array, me * part, part, 0)

    def whole_by_columns(array):
        part = columns_of(array)
        mine = stacked(ring.gather(part), n_f).reshape(-1, part.shape[1])
        return group.laid(group.pieces(mine), 1, low)

    def whole_by_rows(array, flip=False):
        part = rows_of(array)
        mine = stacked(ring.gather(part, flip), n_f)
        return group.laid(group.pieces(mine), 1, low).reshape(-1, part.shape[1])

    def cut_columns(array):
        view = array.reshape(array.shape[0], n_f, n_seq, cut)
        return lax.dynamic_index_in_dim(view, me, 2, keepdims=False).reshape(-1, slab)

    side1 = jnp.concatenate(
        [
            part.astype(wide) * gain1
            for part in (q_weight, k_weight, v_weight, q_down, k_down, v_down)
        ]
        + [gate_down.astype(wide) * gain2],
        axis=1,
    ).astype(low)
    side1 = whole_by_columns(side1)
    ups = whole_by_rows(jnp.concatenate([q_up, k_up, v_up, o_up, down_up], axis=1), True)
    side_o = whole_by_rows(jnp.concatenate([o_weight, o_down], axis=1))
    up_adapter = whole_by_columns((up_down.astype(wide) * gain2).astype(low))

    kv = HD
    lin = hq + 2 * kv
    qkv_side = side1[:, : lin + 3 * rank]
    gate_adapter = side1[:, lin + 3 * rank :]
    q_raise, k_raise, v_raise = ups[:, :hq], ups[:, hq : hq + kv], ups[:, hq + kv : lin]
    o_raise, d_raise = ups[:, lin : lin + width], ups[:, lin + width :]

    raises = jnp.concatenate([cut_columns(gate_up), cut_columns(up_up)], axis=0)
    raises = stacked(ring.gather(raises, True), n_f)
    g_raise = raises[:, :rank_rows].reshape(-1, slab)
    u_raise = raises[:, rank_rows:].reshape(-1, slab)
    gate_own = cut_columns(gate_weight).astype(wide) + mul(gate_down, g_raise)
    up_own = cut_columns(up_weight).astype(wide) + mul(up_down, u_raise)
    gate_full = stacked(ring.gather((gate_own * gain2).astype(low)), n_f).reshape(-1, slab)
    up_full = stacked(ring.gather((up_own * gain2).astype(low), True), n_f).reshape(-1, slab)
    gate_own, up_own = gate_own.astype(low), up_own.astype(low)
    d_lower = rows_of(down_down)
    down_own = (rows_of(down_weight).astype(wide) + mul(d_lower, d_raise)).astype(low)
    down_full = stacked(ring.gather(down_own), n_f).reshape(slab, width)

    resid = inputs.reshape(tokens, width).astype(wide)
    active = (exits.reshape(tokens) >= LOOP).astype(wide)[:, None]
    cot = cotangent.reshape(tokens, width).astype(wide)
    g_mlp = group.pieces((active * cot).astype(low))
    g_mlp = jnp.concatenate(g_mlp, axis=0)
    places = me * length + jnp.arange(length, dtype=jnp.int32)
    frequency = rope_base ** (-2.0 * jnp.arange(HD // 2, dtype=wide) / HD)
    angles = jnp.tile(places, rows).astype(wide)[:, None] * frequency[None, :]
    cosine, sine = jnp.cos(angles), jnp.sin(angles)
    r1 = lax.rsqrt(jnp.mean(resid * resid, axis=-1, keepdims=True) + epsilon)
    unit1 = (resid * r1).astype(low)
    projected = mul(unit1, qkv_side)
    inner = projected[:, lin:].astype(low)
    q_inner, k_inner, v_inner = inner[:, :rank], inner[:, rank : 2 * rank], inner[:, 2 * rank :]
    q_lin = projected[:, :hq] + mul(q_inner, q_raise)
    k_lin = projected[:, hq : hq + kv] + mul(k_inner, k_raise)
    v_lin = projected[:, hq + kv : lin] + mul(v_inner, v_raise)
    queries = rope(q_lin.reshape(tokens, H, HD), cosine, sine).astype(low)
    queries = queries.reshape(rows, length, H, HD).transpose(0, 2, 1, 3)
    queries = queries.reshape(rows, H * length, HD)
    keys = rope(k_lin.reshape(tokens, 1, HD), cosine, sine).astype(low).reshape(rows, length, HD)
    values = v_lin.astype(low).reshape(rows, length, HD)
    both = group.pieces(jnp.concatenate([keys, values], axis=-1))
    both = jnp.concatenate(both, axis=1)
    keys, values = both[..., :HD], both[..., HD:]
    key_seg = jnp.concatenate(group.pieces(segments.astype(low)), axis=1).astype(jnp.int32)
    key_place = jnp.concatenate(
        [
            group.index(k, c) * length + jnp.arange(length, dtype=jnp.int32)
            for k, c in group.order
        ]
    )
    query_seg, query_place = jnp.tile(segments, (1, H)), jnp.tile(places, H)
    allowed = (query_seg[:, :, None] == key_seg[:, None, :]) & (
        key_place[None, None, :] <= query_place[None, :, None]
    )
    scores = (
        jnp.einsum("sqd,skd->sqk", queries, keys, preferred_element_type=wide) * scale
    )
    scores = jnp.where(allowed, scores, -1e30)
    top = jnp.max(scores, axis=-1, keepdims=True)
    weights = jnp.exp(scores - top)
    totals = jnp.sum(weights, axis=-1, keepdims=True)
    attn = (
        jnp.einsum("sqk,skd->sqd", weights.astype(low), values, preferred_element_type=wide)
        / totals
    )
    log_total = top + jnp.log(totals)

    def to_tokens(rows_heads):
        view = rows_heads.reshape(rows, H, length, HD).transpose(0, 2, 1, 3)
        return view.reshape(tokens, hq)

    def to_heads(flat):
        view = flat.reshape(rows, length, H, HD).transpose(0, 2, 1, 3)
        return view.reshape(rows, H * length, HD)

    attn_low = to_tokens(attn.astype(low))
    projected = mul(attn_low, side_o)
    o_inner = projected[:, width:].astype(low)
    mid = resid + active * (projected[:, :width] + mul(o_inner, o_raise))

    r2 = lax.rsqrt(jnp.mean(mid * mid, axis=-1, keepdims=True) + epsilon)
    unit2 = jnp.concatenate(group.pieces((mid * r2).astype(low)), axis=0)
    gate = mul(unit2, gate_full).astype(low)
    up = mul(unit2, up_full).astype(low)
    value, slope = gelu_parts(gate.astype(wide))
    hidden = (value * up.astype(wide)).astype(low)
    g_down = t_mul(hidden, g_mlp).astype(low)
    branch = mul(hidden, down_full)

    def token_block(array):
        def part(k, c):
            at = group.order.index((k, c)) * tokens
            return array[at : at + tokens]

        return part

    outputs = mid + active * group.scatter(token_block(branch))
    outputs = outputs.astype(low).reshape(rows, length, width)

    def ring_block(array, size):
        return lambda owner: lax.dynamic_slice_in_dim(array, owner * size, size, 0).astype(wide)

    g_down = ring.scatter(ring_block(g_down, cut), True).astype(low)
    g_hidden = mul_t(g_mlp, down_full)
    g_gate = (g_hidden * up.astype(wide) * slope).astype(low)
    g_up = (g_hidden * value).astype(low)
    e2 = mul_t(g_gate, gate_full) + mul_t(g_up, up_full)
    e2 = group.scatter(token_block(e2))
    g_mid = cot + r2 * e2 - mid * (r2 * r2 * r2 * jnp.mean(e2 * mid, axis=-1, keepdims=True))
    gg = t_mul(unit2, g_gate).astype(low)
    gu = t_mul(unit2, g_up).astype(low)
    gg_raise = t_mul(gate_adapter, gg).astype(low)
    gu_raise = t_mul(up_adapter, gu).astype(low)
    gg = ring.scatter(ring_block(gg, own_rows))
    gu = ring.scatter(ring_block(gu, own_rows), True)

    def raise_block(owner):
        return jnp.concatenate(
            [
                lax.dynamic_slice_in_dim(part, owner * rank_rows, rank_rows, 0)
                for part in (gg_raise, gu_raise)
            ],
            axis=0,
        ).astype(wide)

    g_raises = ring.scatter(raise_block).astype(low)

    mlp_small = jnp.concatenate(
        [
            mul_t((gg * gain2).astype(low), g_raise),
            mul_t((gu * gain2).astype(low), u_raise),
            jnp.broadcast_to(
                jnp.sum(
                    gg * gate_own.astype(wide) + gu * up_own.astype(wide), axis=1, keepdims=True
                ),
                (own_rows, 128),
            ),
        ],
        axis=1,
    )
    mlp_small = spread_sum(mlp_small, "seq")
    grad_gate_down, grad_up_down = mlp_small[:, :rank], mlp_small[:, rank : 2 * rank]
    grad_mlp_gain = mlp_small[:, 2 * rank]

    def back_columns(array):
        view = array.reshape(array.shape[0], n_f, cut)
        return group.laid(
            [piece[:, :, None, :] for piece in group.pieces(view)], 2, wide
        ).reshape(array.shape[0], ff)

    grad_gate_weight = back_columns((gg * gain2).astype(low))
    grad_up_weight = back_columns((gu * gain2).astype(low))
    g_raises = back_columns(g_raises)
    grad_gate_up, grad_up_up = g_raises[:rank_rows], g_raises[rank_rows:]
    down_rows = jnp.concatenate([g_down, mul_t(g_down, d_raise).astype(low)], axis=1)
    down_rows = group.laid(group.pieces(down_rows), 0, wide)
    grad_down_weight, grad_down_down = down_rows[:, :width], down_rows[:, width:]
    gd_raise = t_mul(d_lower, g_down).astype(low)

    g_branch = (active * g_mid).astype(low)
    g_inner = mul_t(g_branch, o_raise).astype(low)
    g_attn = mul_t(jnp.concatenate([g_branch, g_inner], axis=1), side_o).astype(low)
    g_o = t_mul(attn_low, g_branch).astype(low)
    go_raise = t_mul(o_inner, g_branch).astype(low)
    o_pack = jnp.concatenate(
        [
            g_o.reshape(n_f, o_rows, width),
            go_raise.reshape(n_f, rank_rows, width),
            gd_raise.reshape(n_f, rank_rows, width),
        ],
        axis=1,
    )

    def whole_sum_rows(pack, flip=False):
        part = pack.shape[1] // n_seq
        mine = group.scatter(
            lambda k, c: lax.dynamic_slice_in_dim(
                pack, group.index(k, c) * part, part, 1
            ).astype(wide)
        ).astype(low)
        done = ring.scatter(
            lambda owner: lax.dynamic_index_in_dim(mine, owner, 0, keepdims=False).astype(wide), flip
        ).astype(low)
        return group.laid(group.pieces(done), 0, wide)

    def whole_sum_columns(pack, flip=False):
        part = pack.shape[2] // n_seq
        mine = group.scatter(
            lambda k, c: lax.dynamic_slice_in_dim(
                pack, group.index(k, c) * part, part, 2
            ).astype(wide)
        ).astype(low)
        done = ring.scatter(
            lambda owner: lax.dynamic_index_in_dim(mine, owner, 0, keepdims=False).astype(wide), flip
        ).astype(low)
        return group.laid(group.pieces(done), 1, wide)

    o_pack = whole_sum_rows(o_pack)
    grad_o_weight = o_pack[:o_rows]
    grad_o_up = o_pack[o_rows : o_rows + rank_rows]
    grad_down_up = o_pack[o_rows + rank_rows :]
    grad_o_down = mul_t(grad_o_weight.astype(low), o_raise)

    g_heads = to_heads(g_attn)
    dots = jnp.sum(g_heads.astype(wide) * attn, axis=-1, keepdims=True)
    scores = (
        jnp.einsum("sqd,skd->sqk", queries, keys, preferred_element_type=wide) * scale
    )
    probs = jnp.where(allowed, jnp.exp(scores - log_total), 0.0)
    d_probs = jnp.einsum("sqd,skd->sqk", g_heads, values, preferred_element_type=wide)
    d_scores = (probs * (d_probs - dots)).astype(low)
    d_query = jnp.einsum("sqk,skd->sqd", d_scores, keys, preferred_element_type=wide) * scale
    d_key = jnp.einsum("sqk,sqd->skd", d_scores, queries, preferred_element_type=wide) * scale
    d_value = jnp.einsum("sqk,sqd->skd", probs.astype(low), g_heads, preferred_element_type=wide)
    d_both = jnp.concatenate([d_key, d_value], axis=-1)

    def key_block(k, c):
        at = group.order.index((k, c)) * length
        return d_both[:, at : at + length]

    d_both = group.scatter(key_block).reshape(tokens, 2 * HD)
    g_q = rope(to_tokens(d_query).reshape(tokens, H, HD), cosine, -sine)
    g_q = g_q.reshape(tokens, hq).astype(low)
    g_k = rope(d_both[:, None, :HD], cosine, -sine).reshape(tokens, HD).astype(low)
    g_v = d_both[:, HD:].astype(low)
    gi_q = mul_t(g_q, q_raise).astype(low)
    gi_k = mul_t(g_k, k_raise).astype(low)
    gi_v = mul_t(g_v, v_raise).astype(low)
    g_lin = jnp.concatenate([g_q, g_k, g_v], axis=1)
    e1 = mul_t(jnp.concatenate([g_lin, gi_q, gi_k, gi_v], axis=1), qkv_side)
    input_grad = g_mid + r1 * e1 - resid * (
        r1 * r1 * r1 * jnp.mean(e1 * resid, axis=-1, keepdims=True)
    )
    input_grad = input_grad.astype(low).reshape(rows, length, width)
    g_qkv = t_mul(unit1, g_lin).astype(low)
    gr_qkv = jnp.concatenate(
        [t_mul(q_inner, g_q), t_mul(k_inner, g_k), t_mul(v_inner, g_v)], axis=1
    ).astype(low)
    qkv_pack = jnp.concatenate(
        [g_qkv.reshape(n_f, own_rows, lin), gr_qkv.reshape(n_f, rank_rows, lin)], axis=1
    )
    qkv_pack = whole_sum_columns(qkv_pack, True)
    unit_grad = qkv_pack[:own_rows]
    grad_lin = unit_grad * gain1
    grad_q_weight, grad_k_weight, grad_v_weight = (
        grad_lin[:, :hq],
        grad_lin[:, hq : hq + kv],
        grad_lin[:, hq + kv :],
    )
    grad_q_up, grad_k_up, grad_v_up = (
        qkv_pack[own_rows:, :hq],
        qkv_pack[own_rows:, hq : hq + kv],
        qkv_pack[own_rows:, hq + kv :],
    )
    grad_q_down = mul_t(grad_q_weight.astype(low), q_raise)
    grad_k_down = mul_t(grad_k_weight.astype(low), k_raise)
    grad_v_down = mul_t(grad_v_weight.astype(low), v_raise)
    own_lin = jnp.concatenate(
        [
            q_weight.astype(wide) + mul(q_down, q_raise),
            k_weight.astype(wide) + mul(k_down, k_raise),
            v_weight.astype(wide) + mul(v_down, v_raise),
        ],
        axis=1,
    )
    grad_attn_gain = jnp.sum(unit_grad * own_lin, axis=1)

    depth_ids = jnp.arange(DEPTHS, dtype=jnp.int32)
    matches = (exits.reshape(tokens)[:, None] == depth_ids[None, :]).astype(wide)
    counted = jnp.concatenate(
        [jnp.sum(matches, axis=0), jnp.sum(matches * confidence.reshape(tokens)[:, None], axis=0)]
    )
    counted = spread_sum(spread_sum(counted, "seq"), "fsdp")
    mean_confidence = counted[DEPTHS:] / counted[:DEPTHS]
    return (
        outputs,
        input_grad,
        grad_attn_gain,
        grad_q_weight,
        grad_k_weight,
        grad_v_weight,
        grad_o_weight,
        grad_q_down,
        grad_q_up,
        grad_k_down,
        grad_k_up,
        grad_v_down,
        grad_v_up,
        grad_o_down,
        grad_o_up,
        grad_mlp_gain,
        grad_gate_weight,
        grad_up_weight,
        grad_down_weight,
        grad_gate_down,
        grad_gate_up,
        grad_up_down,
        grad_up_up,
        grad_down_down,
        grad_down_up,
        counted[:DEPTHS].astype(jnp.int32),
        mean_confidence,
    )


def solution(mesh):
    tokens3 = P("fsdp", "seq", None)
    tokens2 = P("fsdp", "seq")
    vector, matrix = P("fsdp"), P("fsdp", None)
    in_specs = (tokens3,) * 2 + (tokens2,) * 3 + (vector,) + (matrix,) * 12 + (vector,) + (matrix,) * 9
    out_specs = (
        (tokens3,) * 2 + (vector,) + (matrix,) * 12 + (vector,) + (matrix,) * 9 + (P(), P())
    )
    return jax.shard_map(shards, mesh=mesh, in_specs=in_specs, out_specs=out_specs, check_vma=False)
```

time: 3620 us -> 1430 us (0.40)
  waiting for transfers between devices: 2610 us -> 361 us
  blocking collectives: 530 us -> 0 us
  local copies, waits for them, and re-layouts: 38.8 us -> 500 us
  starting transfers between devices: 2.02 us -> 141 us
  matrix products: 347 us -> 235 us
  other arithmetic: 64.5 us -> 128 us
    reduce_scatter x23 -> x0, waiting for transfers between devices: 1870 us -> none  [the longest x1 273 us: shards(): lax.psum_scatter(g_up_base.astype(jnp.bfloat16), 'fsdp', scatter_dimensio...]
    all_gather x10 -> x0, waiting for transfers between devices: 579 us -> none  [the longest x1 197 us: shards(): lax.all_gather(down_weight, 'fsdp', axis=0, tiled=True)]
    all_gather x14 -> x0, blocking collectives: 435 us -> none  [the longest x1 35.5 us: shards(): lax.all_gather(o_up, 'fsdp', axis=0, tiled=True)]
    ppermute x0 -> x162, waiting for transfers between devices: none -> 361 us  [the longest x42 106 us: scatter(): moving = lax.ppermute(term.astype(low), 'fsdp', way)]
    dynamic_update_slice x0 -> x87, local copies, waits for them, and re-layouts: none -> 313 us  [the longest x28 268 us: laid(): lax.dynamic_update_slice_in_dim(out, piece.astype(dtype), self.index(k, c...]
    psum x1 -> x0, waiting for transfers between devices: 156 us -> none  [shards(): lax.psum(attn_shards[1].astype(jnp.bfloat16), 'seq').astype(jnp.float32)]
    ppermute x0 -> x162, starting transfers between devices: none -> 141 us  [the longest x42 43.8 us: scatter(): moving = lax.ppermute(term.astype(low), 'fsdp', way)]
    dot_general x70 -> x49, matrix products: 347 us -> 235 us  [the longest x16 78.7 us: mul_t(): lax.dot_general(left, right, (((1,), (1,)), ((), ())), preferred_element_...]
  transfers between devices with their start and end apart: 34 -> 162, of which waited for: 24 -> 70; matrix products, arithmetic and copies ran while one was open for 8% -> 54% of each run, Pallas kernels for 0% -> 0%
where the time goes in v1:
time: 1430 us; the launch traced here: 1410 us
  local copies, waits for them, and re-layouts  500 us (35%)
  waiting for transfers between devices  361 us (25%)
  matrix products  235 us (16%)
  starting transfers between devices  141 us (10%)
  other arithmetic  128 us (9%)
  between operations  43.3 us (3%)
    dynamic_update_slice x28, local copies, waits for them, and re-layouts, laid(): lax.dynamic_update_slice_in_dim(out, piece.astype(dtype), self.index(k, c...  268 us
    ppermute x42, waiting for transfers between devices, scatter(): moving = lax.ppermute(term.astype(low), 'fsdp', way)  106 us
    ppermute x32, waiting for transfers between devices, gather(): first = lax.ppermute(first, 'fsdp', ahead)  105 us
    dot_general x16, matrix products, mul_t(): lax.dot_general(left, right, (((1,), (1,)), ((), ())), preferred_element_...  78.7 us
    ppermute x14, waiting for transfers between devices, pieces(): lax.ppermute(block, 'seq', self.shift(-k))  77.4 us
    dot_general x15, matrix products, mul(): return jnp.dot(left, right, preferred_element_type=wide)  67.4 us
    dot_general x12, matrix products, t_mul(): lax.dot_general(left, right, (((0,), (0,)), ((), ())), preferred_element_...  65.8 us
    dynamic_update_slice x59, local copies, waits for them, and re-layouts, stacked(): out = lax.dynamic_update_index_in_dim(out, block, index, 0)  45 us
  transfers between devices with their start and end apart: 162, of which 70 were waited for; matrix products, arithmetic and copies ran while one was open for 54% of the time, Pallas kernels for 0%

profile of v1, /device:TPU:0, one launch (start us, length us, event | category | flops | bytes accessed | tf_op | source)
XLA Modules:
  0.0 1409.0 jit_solution(5232716179203602926)
XLA Ops:
  63.1 10.0 reshape.641
  73.0 9.9 reshape.648
  83.0 5.9 constant_dynamic-slice_fusion.27
  146.9 6.1 collective-permute-done.137
  181.5 4.3 dynamic_update_slice.415
  226.6 5.1 dynamic_update_slice.416
  231.7 6.4 collective-permute-done.145
  256.5 4.3 dynamic_update_slice.418
  288.8 5.2 collective-permute-done.44
  335.2 8.4 collective-permute-done.46
  347.3 8.4 collective-permute-done.60
  360.4 10.4 collective-permute-done.55
  374.6 9.5 collective-permute-done.48
  390.7 8.1 collective-permute-done.62
  403.6 7.0 collective-permute-done.57
  411.0 5.3 collective-permute-done.58
  430.0 8.8 collective-permute-done.24
  457.1 5.4 fusion.69
  476.7 10.7 collective-permute-done.52
  487.3 10.5 collective-permute-done.37
  502.9 13.1 convolution_convert_fusion
  515.9 17.4 %convolution_convert_fusion.1 = bf16[2048,1728]{0,1:T(8,128)(2,1)} fusion(bf16[1152,1728]{1,0:T(8,128)(2,1)} %bitcast.74, bf16[512,1152]{1,0:T(8,128)(2,1)} %collective-permute-done.38, bf16[512,1152]{1,0:T(8,128)(2,1)} %collective-permute-done.37, bf16[512,1152]{1,0:T(8,128)(2,1)} %collective-permute-done.36, bf16[512,1152]{1,0:T(8,128)(2,1)S(1)} %multiply_convert_fusion.3), kind=kOutput, calls=%fused_computation.28 | convolution fusion | flops 8176140288 | bytes 15777792 | tf_op jit(solution)/shard_map/dot_general | solution.py:19
  533.4 19.6 %fusion.196 = (bf16[2048,1152]{1,0:T(8,128)(2,1)}, f32[2048,1152]{1,0:T(8,128)}) fusion(bf16[1728,1152]{1,0:T(8,128)(2,1)} %bitcast.94, bf16[2048,1728]{0,1:T(8,128)(2,1)S(1)} %convolution_convert_fusion, bf16[2048,1728]{0,1:T(8,128)(2,1)} %convolution_convert_fusion.1), kind=kOutput, calls=%fused_computation.506 | convolution fusion | flops 8198553600 | bytes 32292864 | tf_op jit(solution)/shard_map/dot_general | solution.py:19
  553.0 28.2 %fusion.6 = (bf16[2048,1728]{0,1:T(8,128)(2,1)}, bf16[2048,1728]{0,1:T(8,128)(2,1)}) fusion(bf16[2048,1728]{0,1:T(8,128)(2,1)} %convolution_convert_fusion.1, bf16[2048,1728]{0,1:T(8,128)(2,1)} %copy-done.141, bf16[1728,1152]{1,0:T(8,128)(2,1)} %bitcast.94, bf16[512,1152]{1,0:T(8,128)(2,1)} %collective-permute-done.72, ...), kind=kOutput, calls=%fused_computation.15 | convolution fusion | flops 8261074944 | bytes 37011456 | tf_op jit(solution)/shard_map/dot_general | solution.py:23
  581.2 13.0 convolution_convert_fusion.4
  598.1 12.2 fusion.198
  610.3 11.0 convolution_convert_fusion.3
  632.3 21.9 %convolution_convert_fusion.5 = bf16[1728,1152]{1,0:T(8,128)(2,1)} fusion(bf16[512,1152]{1,0:T(8,128)(2,1)} %collective-permute-done.72, bf16[512,1152]{1,0:T(8,128)(2,1)} %collective-permute-done.71, bf16[512,1152]{1,0:T(8,128)(2,1)} %collective-permute-done.70, bf16[512,1152]{1,0:T(8,128)(2,1)} %fusion.30, bf16[2048,1728]{0,1:T(8,128)(2,1)} %copy-done.141, ...), kind=kOutput, calls=%fused_computation.32 | convolution fusion | flops 8217059328 | bytes 22855680 | tf_op jit(solution)/shard_map/dot_general | solution.py:27
  665.2 16.8 %fusion.195 = (bf16[2048,1152]{1,0:T(8,128)(2,1)S(1)}, f32[2048,1152]{1,0:T(8,128)}) fusion(f32[2048,1152]{1,0:T(8,128)} %fusion.198, bf16[2048,1728]{0,1:T(8,128)(2,1)} %get-tuple-element.49, bf16[1152,1728]{1,0:T(8,128)(2,1)} %bitcast.74), kind=kOutput, calls=%fused_computation.505 | convolution fusion | flops 8158445568 | bytes 34652160 | tf_op jit(solution)/shard_map/dot_general | solution.py:23
  688.3 18.7 %collective-permute-done.148 = bf16[64,1728]{0,1:T(8,128)(2,1)S(1)} collective-permute-done((bf16[64,1728]{0,1:T(8,128)(2,1)S(1)}, bf16[64,1728]{0,1:T(8,128)(2,1)S(1)}, u32[]{:S(2)}, u32[]{:S(2)}) %collective-permute-start.148) | collective-permute-done | bytes 221216 | tf_op jit(solution)/shard_map/ppermute | solution.py:81
  708.2 9.0 collective-permute-done.152
  724.2 13.5 collective-permute-done.149
  741.0 6.8 collective-permute-done.150
  751.0 7.0 dynamic_update_slice.419
  771.7 10.7 collective-permute-done.155
  785.4 9.8 dynamic_update_slice.420
  795.3 9.9 dynamic_update_slice.421
  814.0 9.8 dynamic_update_slice.422
  836.7 9.5 collective-permute-done.114
  853.2 9.4 collective-permute-done.124
  869.0 5.3 collective-permute-done.97
  882.7 16.4 %collective-permute-done.69 = bf16[512,1152]{1,0:T(8,128)(2,1)S(1)} collective-permute-done((bf16[512,1152]{1,0:T(8,128)(2,1)S(1)}, bf16[512,1152]{1,0:T(8,128)(2,1)S(1)}, u32[]{:S(2)}, u32[]{:S(2)}) %collective-permute-start.69) | collective-permute-done | bytes 1179680 | tf_op jit(solution)/shard_map/ppermute | solution.py:120
  900.8 4.7 multiply_convert_fusion.2
  917.0 6.7 fusion.21
  923.8 4.2 multiply_convert_fusion.1
  959.0 7.6 collective-permute-done.118
  977.2 4.4 reshape.699
  995.5 25.8 %dynamic_update_slice.399 = f32[144,8,4,216]{3,2,1,0:T(4,128)} dynamic-update-slice(f32[144,8,4,216]{3,2,1,0:T(4,128)} %broadcast.257.clone.1, f32[144,8,1,216]{3,2,1,0:T(1,128)} %reshape.700, s32[]{:T(128)} %constant.428.clone.1, s32[]{:T(128)} %constant.428.clone.1, s32[]{:T(128)S(6)} %select_n.654, s32[]{:T(128)} %constant.428.clone.1) | dynamic-update-slice | bytes 1990660 | tf_op jit(solution)/shard_map/dynamic_update_slice | solution.py:129
  1024.6 26.0 %dynamic_update_slice.395 = f32[144,8,4,216]{3,2,1,0:T(4,128)} dynamic-update-slice(f32[144,8,4,216]{3,2,1,0:T(4,128)} %broadcast.257.clone, f32[144,8,1,216]{3,2,1,0:T(1,128)} %reshape.699, s32[]{:T(128)} %constant.428.clone.1, s32[]{:T(128)} %constant.428.clone.1, s32[]{:T(128)S(6)} %select_n.654, s32[]{:T(128)} %constant.428.clone.1) | dynamic-update-slice | bytes 1990660 | tf_op jit(solution)/shard_map/dynamic_update_slice | solution.py:129
  1056.4 23.3 %collective-permute-done.132 = bf16[144,8,216]{2,1,0:T(8,128)(2,1)} collective-permute-done((bf16[144,8,216]{2,1,0:T(8,128)(2,1)}, bf16[144,8,216]{2,1,0:T(8,128)(2,1)}, u32[]{:S(2)}, u32[]{:S(2)}) %collective-permute-start.132) | collective-permute-done | bytes 497696 | tf_op jit(solution)/shard_map/ppermute | solution.py:105
  1082.0 12.7 collective-permute-done.129
  1104.9 25.8 %dynamic_update_slice.400 = f32[144,8,4,216]{3,2,1,0:T(4,128)} dynamic-update-slice(f32[144,8,4,216]{3,2,1,0:T(4,128)} %dynamic_update_slice.399, f32[144,8,1,216]{3,2,1,0:T(1,128)} %copy.153, s32[]{:T(128)} %constant.428.clone.1, s32[]{:T(128)} %constant.428.clone.1, s32[]{:T(128)S(6)} %select_n.655, s32[]{:T(128)} %constant.428.clone.1) | dynamic-update-slice | bytes 1990660 | tf_op jit(solution)/shard_map/dynamic_update_slice | solution.py:129
  1130.6 25.8 %dynamic_update_slice.401 = f32[144,8,4,216]{3,2,1,0:T(4,128)} dynamic-update-slice(f32[144,8,4,216]{3,2,1,0:T(4,128)} %dynamic_update_slice.400, f32[144,8,1,216]{3,2,1,0:T(1,128)} %copy.154, s32[]{:T(128)} %constant.428.clone.1, s32[]{:T(128)} %constant.428.clone.1, s32[]{:T(128)S(6)} %select_n.656, s32[]{:T(128)} %constant.428.clone.1) | dynamic-update-slice | bytes 1990660 | tf_op jit(solution)/shard_map/dynamic_update_slice | solution.py:129
  1156.4 25.8 %dynamic_update_slice.396 = f32[144,8,4,216]{3,2,1,0:T(4,128)} dynamic-update-slice(f32[144,8,4,216]{3,2,1,0:T(4,128)} %dynamic_update_slice.395, f32[144,8,1,216]{3,2,1,0:T(1,128)} %copy.149, s32[]{:T(128)} %constant.428.clone.1, s32[]{:T(128)} %constant.428.clone.1, s32[]{:T(128)S(6)} %select_n.655, s32[]{:T(128)} %constant.428.clone.1) | dynamic-update-slice | bytes 1990660 | tf_op jit(solution)/shard_map/dynamic_update_slice | solution.py:129
  1182.2 25.8 %dynamic_update_slice.397 = f32[144,8,4,216]{3,2,1,0:T(4,128)} dynamic-update-slice(f32[144,8,4,216]{3,2,1,0:T(4,128)} %dynamic_update_slice.396, f32[144,8,1,216]{3,2,1,0:T(1,128)} %copy.150, s32[]{:T(128)} %constant.428.clone.1, s32[]{:T(128)} %constant.428.clone.1, s32[]{:T(128)S(6)} %select_n.656, s32[]{:T(128)} %constant.428.clone.1) | dynamic-update-slice | bytes 1990660 | tf_op jit(solution)/shard_map/dynamic_update_slice | solution.py:129
  1214.5 4.9 collective-permute-done.127
  1224.0 6.2 collective-permute-done.78
  1256.7 5.9 fusion.43
  1292.0 25.9 %dynamic_update_slice.402 = f32[144,8,4,216]{3,2,1,0:T(4,128)} dynamic-update-slice(f32[144,8,4,216]{3,2,1,0:T(4,128)} %dynamic_update_slice.401, f32[144,8,1,216]{3,2,1,0:T(1,128)} %copy.155, s32[]{:T(128)} %constant.428.clone.1, s32[]{:T(128)} %constant.428.clone.1, s32[]{:T(128)S(6)} %select_n.657, s32[]{:T(128)} %constant.428.clone.1) | dynamic-update-slice | bytes 1990660 | tf_op jit(solution)/shard_map/dynamic_update_slice | solution.py:129
  1317.9 6.5 reshape.665
  1327.9 25.8 %dynamic_update_slice.398 = f32[144,8,4,216]{3,2,1,0:T(4,128)} dynamic-update-slice(f32[144,8,4,216]{3,2,1,0:T(4,128)} %dynamic_update_slice.397, f32[144,8,1,216]{3,2,1,0:T(1,128)} %copy.151, s32[]{:T(128)} %constant.428.clone.1, s32[]{:T(128)} %constant.428.clone.1, s32[]{:T(128)S(6)} %select_n.657, s32[]{:T(128)} %constant.428.clone.1) | dynamic-update-slice | bytes 1990660 | tf_op jit(solution)/shard_map/dynamic_update_slice | solution.py:129
  1353.7 6.5 reshape.663
  1367.8 4.3 slice.314
  1398.3 4.1 collective-permute-done.90
  (918 shorter events, 618.3 us)
Async XLA Ops:
  17.1 156.1 %collective-permute-start.13 = (bf16[8,3840]{1,0:T(8,128)(2,1)}, bf16[8,3840]{1,0:T(8,128)(2,1)}, u32[]{:S(2)}, u32[]{:S(2)}) collective-permute-start(bf16[8,3840]{1,0:T(8,128)(2,1)} %get-tuple-element.46), channel_id=1, source_target_pairs={{1,0},{3,1},{5,3},{7,5},{6,7},{4,6},{2,4},{0,2},{9,8},{11,9},{13,1... | collective-permute-start | bytes 184328 | tf_op jit(solution)/shard_map/ppermute | solution.py:62
  20.1 156.2 %collective-permute-start.14 = (bf16[8,3840]{1,0:T(8,128)(2,1)}, bf16[8,3840]{1,0:T(8,128)(2,1)}, u32[]{:S(2)}, u32[]{:S(2)}) collective-permute-start(bf16[8,3840]{1,0:T(8,128)(2,1)} %get-tuple-element.46), channel_id=1, source_target_pairs={{0,1},{1,3},{3,5},{5,7},{7,6},{6,4},{4,2},{2,0},{8,9},{9,11},{11,1... | collective-permute-start | bytes 184328 | tf_op jit(solution)/shard_map/ppermute | solution.py:65
  28.7 191.6 %collective-permute-start.39 = (bf16[64,1728]{1,0:T(8,128)(2,1)}, bf16[64,1728]{1,0:T(8,128)(2,1)}, u32[]{:S(2)}, u32[]{:S(2)}) collective-permute-start(bf16[64,1728]{1,0:T(8,128)(2,1)} %constant_dynamic-update-slice_fusion.5), channel_id=1, source_target_pairs={{1,0},{3,1},{5,3},{7,5},{6,7},{4,6},{2,4},{0,2},{9,8},{11,9},{13,1... | collective-permute-start | bytes 663560 | tf_op jit(solution)/shard_map/ppermute | solution.py:62
  31.7 111.2 %collective-permute-start.1 = (bf16[2,256]{1,0:T(2,128)(2,1)}, bf16[2,256]{1,0:T(2,128)(2,1)}, u32[]{:S(2)}, u32[]{:S(2)}) collective-permute-start(bf16[2,256]{1,0:T(2,128)(2,1)} %convert_element_type.898), channel_id=1, source_target_pairs={{0,16},{8,24},{16,0},{24,8},{1,17},{9,25},{17,1},{25,9},{2,18},{10... | collective-permute-start | bytes 3080 | tf_op jit(solution)/shard_map/ppermute | solution.py:105
  34.0 93.1 %collective-permute-start.157 = (f32[6]{0:T(128)}, f32[6]{0:T(128)}, u32[]{:S(2)}, u32[]{:S(2)}) collective-permute-start(f32[6]{0:T(128)} %pad_maximum_fusion.13), channel_id=1, source_target_pairs={{0,8},{8,0},{16,24},{24,16},{1,9},{9,1},{17,25},{25,17},{2,10},{10... | collective-permute-start | bytes 80 | tf_op jit(solution)/shard_map/ppermute | solution.py:148
  144.2 78.5 %collective-permute-start.40 = (bf16[64,1728]{1,0:T(8,128)(2,1)}, bf16[64,1728]{1,0:T(8,128)(2,1)}, u32[]{:S(2)}, u32[]{:S(2)}) collective-permute-start(bf16[64,1728]{1,0:T(8,128)(2,1)} %constant_dynamic-update-slice_fusion.5), channel_id=1, source_target_pairs={{0,1},{1,3},{3,5},{5,7},{7,6},{6,4},{4,2},{2,0},{8,9},{9,11},{11,1... | collective-permute-start | bytes 663560 | tf_op jit(solution)/shard_map/ppermute | solution.py:65
  180.2 35.7 %collective-permute-start.3 = (bf16[144,640]{1,0:T(8,128)(2,1)}, bf16[144,640]{1,0:T(8,128)(2,1)}, u32[]{:S(2)}, u32[]{:S(2)}) collective-permute-start(bf16[144,640]{1,0:T(8,128)(2,1)} %get-tuple-element.48), channel_id=1, source_target_pairs={{0,1},{1,3},{3,5},{5,7},{7,6},{6,4},{4,2},{2,0},{8,9},{9,11},{11,1... | collective-permute-start | bytes 552968 | tf_op jit(solution)/shard_map/ppermute | solution.py:62
  185.8 31.7 %collective-permute-start.4 = (bf16[144,640]{1,0:T(8,128)(2,1)}, bf16[144,640]{1,0:T(8,128)(2,1)S(1)}, u32[]{:S(2)}, u32[]{:S(2)}) collective-permute-start(bf16[144,640]{1,0:T(8,128)(2,1)} %get-tuple-element.48), channel_id=1, source_target_pairs={{1,0},{3,1},{5,3},{7,5},{6,7},{4,6},{2,4},{0,2},{9,8},{11,9},{13,1... | collective-permute-start | bytes 552968 | tf_op jit(solution)/shard_map/ppermute | solution.py:65
  215.3 159.2 %collective-permute-start.71 = (bf16[512,1152]{1,0:T(8,128)(2,1)}, bf16[512,1152]{1,0:T(8,128)(2,1)}, u32[]{:S(2)}, u32[]{:S(2)}) collective-permute-start(bf16[512,1152]{1,0:T(8,128)(2,1)} %fusion.30), channel_id=1, source_target_pairs={{0,16},{8,24},{16,0},{24,8},{1,17},{9,25},{17,1},{25,9},{2,18},{10... | collective-permute-start | bytes 3538952 | tf_op jit(solution)/shard_map/ppermute | solution.py:105
  220.2 25.7 %collective-permute-start.30 = (bf16[32,1408]{1,0:T(8,128)(2,1)}, bf16[32,1408]{1,0:T(8,128)(2,1)}, u32[]{:S(2)}, u32[]{:S(2)}) collective-permute-start(bf16[32,1408]{1,0:T(8,128)(2,1)} %collective-permute-done.28), channel_id=1, source_target_pairs={{0,1},{1,3},{3,5},{5,7},{7,6},{6,4},{4,2},{2,0},{8,9},{9,11},{11,1... | collective-permute-start | bytes 270344 | tf_op jit(solution)/shard_map/ppermute | solution.py:62
  222.7 20.7 %collective-permute-start.19 = (bf16[8,3840]{1,0:T(8,128)(2,1)S(1)}, bf16[8,3840]{1,0:T(8,128)(2,1)S(1)}, u32[]{:S(2)}, u32[]{:S(2)}) collective-permute-start(bf16[8,3840]{1,0:T(8,128)(2,1)S(1)} %collective-permute-done.17), channel_id=1, source_target_pairs={{1,0},{3,1},{5,3},{7,5},{6,7},{4,6},{2,4},{0,2},{9,8},{11,9},{13,1... | collective-permute-start | bytes 184328 | tf_op jit(solution)/shard_map/ppermute | solution.py:62
  225.0 23.4 %collective-permute-start.31 = (bf16[32,1408]{1,0:T(8,128)(2,1)}, bf16[32,1408]{1,0:T(8,128)(2,1)}, u32[]{:S(2)}, u32[]{:S(2)}) collective-permute-start(bf16[32,1408]{1,0:T(8,128)(2,1)} %collective-permute-done.29), channel_id=1, source_target_pairs={{1,0},{3,1},{5,3},{7,5},{6,7},{4,6},{2,4},{0,2},{9,8},{11,9},{13,1... | collective-permute-start | bytes 270344 | tf_op jit(solution)/shard_map/ppermute | solution.py:65
  238.1 22.7 %collective-permute-start.5 = (bf16[144,640]{1,0:T(8,128)(2,1)}, bf16[144,640]{1,0:T(8,128)(2,1)}, u32[]{:S(2)}, u32[]{:S(2)}) collective-permute-start(bf16[144,640]{1,0:T(8,128)(2,1)} %collective-permute-done.3), channel_id=1, source_target_pairs={{0,1},{1,3},{3,5},{5,7},{7,6},{6,4},{4,2},{2,0},{8,9},{9,11},{11,1... | collective-permute-start | bytes 552968 | tf_op jit(solution)/shard_map/ppermute | solution.py:62
  260.8 40.3 %collective-permute-start.20 = (bf16[8,8,3840]{2,1,0:T(8,128)(2,1)}, bf16[8,8,3840]{2,1,0:T(8,128)(2,1)S(1)}, u32[]{:S(2)}, u32[]{:S(2)}) collective-permute-start(bf16[8,8,3840]{2,1,0:T(8,128)(2,1)} %bitcast_dynamic-update-slice_fusion.48), channel_id=1, source_target_pairs={{0,8},{8,0},{16,24},{24,16},{1,9},{9,1},{17,25},{25,17},{2,10},{10... | collective-permute-start | bytes 1474568 | tf_op jit(solution)/shard_map/ppermute | solution.py:109
  262.4 40.3 %collective-permute-start.21 = (bf16[8,8,3840]{2,1,0:T(8,128)(2,1)}, bf16[8,8,3840]{2,1,0:T(8,128)(2,1)S(1)}, u32[]{:S(2)}, u32[]{:S(2)}) collective-permute-start(bf16[8,8,3840]{2,1,0:T(8,128)(2,1)} %bitcast_dynamic-update-slice_fusion.48), channel_id=1, source_target_pairs={{0,16},{8,24},{16,0},{24,8},{1,17},{9,25},{17,1},{25,9},{2,18},{10... | collective-permute-start | bytes 1474568 | tf_op jit(solution)/shard_map/ppermute | solution.py:105
  265.2 49.8 %collective-permute-start.33 = (bf16[8,32,1408]{2,1,0:T(8,128)(2,1)S(1)}, bf16[8,32,1408]{2,1,0:T(8,128)(2,1)S(1)}, u32[]{:S(2)}, u32[]{:S(2)}) collective-permute-start(bf16[8,32,1408]{2,1,0:T(8,128)(2,1)S(1)} %bitcast_dynamic-update-slice_fusion.40), channel_id=1, source_target_pairs={{0,8},{8,0},{16,24},{24,16},{1,9},{9,1},{17,25},{25,17},{2,10},{10... | collective-permute-start | bytes 2162696 | tf_op jit(solution)/shard_map/ppermute | solution.py:109
  302.7 84.5 %collective-permute-start.10 = (bf16[1152,640]{1,0:T(8,128)(2,1)}, bf16[1152,640]{1,0:T(8,128)(2,1)S(1)}, u32[]{:S(2)}, u32[]{:S(2)}) collective-permute-start(bf16[1152,640]{1,0:T(8,128)(2,1)} %bitcast.25), channel_id=1, source_target_pairs={{0,8},{8,0},{16,24},{24,16},{1,9},{9,1},{17,25},{25,17},{2,10},{10... | collective-permute-start | bytes 4423688 | tf_op jit(solution)/shard_map/ppermute | solution.py:109
  307.1 81.7 %collective-permute-start.11 = (bf16[1152,640]{1,0:T(8,128)(2,1)}, bf16[1152,640]{1,0:T(8,128)(2,1)S(1)}, u32[]{:S(2)}, u32[]{:S(2)}) collective-permute-start(bf16[1152,640]{1,0:T(8,128)(2,1)} %bitcast.25), channel_id=1, source_target_pairs={{0,16},{8,24},{16,0},{24,8},{1,17},{9,25},{17,1},{25,9},{2,18},{10... | collective-permute-start | bytes 4423688 | tf_op jit(solution)/shard_map/ppermute | solution.py:105
  374.5 178.5 %collective-permute-start.70 = (bf16[512,1152]{1,0:T(8,128)(2,1)}, bf16[512,1152]{1,0:T(8,128)(2,1)}, u32[]{:S(2)}, u32[]{:S(2)}) collective-permute-start(bf16[512,1152]{1,0:T(8,128)(2,1)} %fusion.30), channel_id=1, source_target_pairs={{0,8},{8,0},{16,24},{24,16},{1,9},{9,1},{17,25},{25,17},{2,10},{10... | collective-permute-start | bytes 3538952 | tf_op jit(solution)/shard_map/ppermute | solution.py:109
  384.1 168.9 %collective-permute-start.72 = (bf16[512,1152]{1,0:T(8,128)(2,1)}, bf16[512,1152]{1,0:T(8,128)(2,1)}, u32[]{:S(2)}, u32[]{:S(2)}) collective-permute-start(bf16[512,1152]{1,0:T(8,128)(2,1)} %collective-permute-done.71), channel_id=1, source_target_pairs={{0,8},{8,0},{16,24},{24,16},{1,9},{9,1},{17,25},{25,17},{2,10},{10... | collective-permute-start | bytes 3538952 | tf_op jit(solution)/shard_map/ppermute | solution.py:109
  388.9 21.7 %collective-permute-start.57 = (bf16[144,1728]{1,0:T(8,128)(2,1)S(1)}, bf16[144,1728]{1,0:T(8,128)(2,1)S(1)}, u32[]{:S(2)}, u32[]{:S(2)}) collective-permute-start(bf16[144,1728]{1,0:T(8,128)(2,1)S(1)} %collective-permute-done.55), channel_id=1, source_target_pairs={{1,0},{3,1},{5,3},{7,5},{6,7},{4,6},{2,4},{0,2},{9,8},{11,9},{13,1... | collective-permute-start | bytes 1493000 | tf_op jit(solution)/shard_map/ppermute | solution.py:62
  419.7 50.2 %collective-permute-start.64 = (bf16[216,1152]{1,0:T(8,128)(2,1)}, bf16[216,1152]{1,0:T(8,128)(2,1)}, u32[]{:S(2)}, u32[]{:S(2)}) collective-permute-start(bf16[216,1152]{1,0:T(8,128)(2,1)} %collective-permute-done.62), channel_id=1, source_target_pairs={{0,1},{1,3},{3,5},{5,7},{7,6},{6,4},{4,2},{2,0},{8,9},{9,11},{11,1... | collective-permute-start | bytes 1493000 | tf_op jit(solution)/shard_map/ppermute | solution.py:62
  446.2 26.5 %collective-permute-start.65 = (bf16[216,1152]{1,0:T(8,128)(2,1)}, bf16[216,1152]{1,0:T(8,128)(2,1)}, u32[]{:S(2)}, u32[]{:S(2)}) collective-permute-start(bf16[216,1152]{1,0:T(8,128)(2,1)} %collective-permute-done.63), channel_id=1, source_target_pairs={{1,0},{3,1},{5,3},{7,5},{6,7},{4,6},{2,4},{0,2},{9,8},{11,9},{13,1... | collective-permute-start | bytes 1493000 | tf_op jit(solution)/shard_map/ppermute | solution.py:65
  447.7 27.4 %collective-permute-start.59 = (bf16[144,1728]{1,0:T(8,128)(2,1)S(1)}, bf16[144,1728]{1,0:T(8,128)(2,1)S(1)}, u32[]{:S(2)}, u32[]{:S(2)}) collective-permute-start(bf16[144,1728]{1,0:T(8,128)(2,1)S(1)} %copy-done.86), channel_id=1, source_target_pairs={{1,0},{3,1},{5,3},{7,5},{6,7},{4,6},{2,4},{0,2},{9,8},{11,9},{13,1... | collective-permute-start | bytes 1493000 | tf_op jit(solution)/shard_map/ppermute | solution.py:62
  469.9 27.9 %collective-permute-start.37 = (bf16[512,1152]{1,0:T(8,128)(2,1)S(1)}, bf16[512,1152]{1,0:T(8,128)(2,1)}, u32[]{:S(2)}, u32[]{:S(2)}) collective-permute-start(bf16[512,1152]{1,0:T(8,128)(2,1)S(1)} %multiply_convert_fusion.3), channel_id=1, source_target_pairs={{0,16},{8,24},{16,0},{24,8},{1,17},{9,25},{17,1},{25,9},{2,18},{10... | collective-permute-start | bytes 3538952 | tf_op jit(solution)/shard_map/ppermute | solution.py:105
  475.1 23.6 %collective-permute-start.66 = (bf16[216,1152]{1,0:T(8,128)(2,1)}, bf16[216,1152]{1,0:T(8,128)(2,1)S(1)}, u32[]{:S(2)}, u32[]{:S(2)}) collective-permute-start(bf16[216,1152]{1,0:T(8,128)(2,1)} %collective-permute-done.64), channel_id=1, source_target_pairs={{0,1},{1,3},{3,5},{5,7},{7,6},{6,4},{4,2},{2,0},{8,9},{9,11},{11,1... | collective-permute-start | bytes 1493000 | tf_op jit(solution)/shard_map/ppermute | solution.py:62
  628.8 55.7 %collective-permute-start.147 = (bf16[64,1728]{0,1:T(8,128)(2,1)}, bf16[64,1728]{0,1:T(8,128)(2,1)}, u32[]{:S(2)}, u32[]{:S(2)}) collective-permute-start(bf16[64,1728]{0,1:T(8,128)(2,1)} %pad_maximum_fusion.10), channel_id=1, source_target_pairs={{0,1},{1,3},{3,5},{5,7},{7,6},{6,4},{4,2},{2,0},{8,9},{9,11},{11,1... | collective-permute-start | bytes 663560 | tf_op jit(solution)/shard_map/ppermute | solution.py:81
  630.4 55.9 %collective-permute-start.151 = (bf16[64,1728]{0,1:T(8,128)(2,1)}, bf16[64,1728]{0,1:T(8,128)(2,1)}, u32[]{:S(2)}, u32[]{:S(2)}) collective-permute-start(bf16[64,1728]{0,1:T(8,128)(2,1)} %pad_maximum_fusion.11), channel_id=1, source_target_pairs={{1,0},{3,1},{5,3},{7,5},{6,7},{4,6},{2,4},{0,2},{9,8},{11,9},{13,1... | collective-permute-start | bytes 663560 | tf_op jit(solution)/shard_map/ppermute | solution.py:81
  656.4 61.6 %collective-permute-start.92 = (bf16[216,1152]{1,0:T(8,128)(2,1)}, bf16[216,1152]{1,0:T(8,128)(2,1)}, u32[]{:S(2)}, u32[]{:S(2)}) collective-permute-start(bf16[216,1152]{1,0:T(8,128)(2,1)} %get-tuple-element.70), channel_id=1, source_target_pairs={{1,0},{3,1},{5,3},{7,5},{6,7},{4,6},{2,4},{0,2},{9,8},{11,9},{13,1... | collective-permute-start | bytes 1493000 | tf_op jit(solution)/shard_map/ppermute | solution.py:81
  657.9 191.6 %collective-permute-start.96 = (bf16[216,1152]{1,0:T(8,128)(2,1)}, bf16[216,1152]{1,0:T(8,128)(2,1)}, u32[]{:S(2)}, u32[]{:S(2)}) collective-permute-start(bf16[216,1152]{1,0:T(8,128)(2,1)} %get-tuple-element.71), channel_id=1, source_target_pairs={{0,1},{1,3},{3,5},{5,7},{7,6},{6,4},{4,2},{2,0},{8,9},{9,11},{11,1... | collective-permute-start | bytes 1493000 | tf_op jit(solution)/shard_map/ppermute | solution.py:81
  660.5 60.3 %collective-permute-start.119 = (bf16[144,1728]{1,0:T(8,128)(2,1)S(1)}, bf16[144,1728]{1,0:T(8,128)(2,1)S(1)}, u32[]{:S(2)}, u32[]{:S(2)}) collective-permute-start(bf16[144,1728]{1,0:T(8,128)(2,1)S(1)} %get-tuple-element.62), channel_id=1, source_target_pairs={{1,0},{3,1},{5,3},{7,5},{6,7},{4,6},{2,4},{0,2},{9,8},{11,9},{13,1... | collective-permute-start | bytes 1493000 | tf_op jit(solution)/shard_map/ppermute | solution.py:81
  684.5 147.4 %collective-permute-start.123 = (bf16[144,1728]{1,0:T(8,128)(2,1)}, bf16[144,1728]{1,0:T(8,128)(2,1)}, u32[]{:S(2)}, u32[]{:S(2)}) collective-permute-start(bf16[144,1728]{1,0:T(8,128)(2,1)} %get-tuple-element.63), channel_id=1, source_target_pairs={{0,1},{1,3},{3,5},{5,7},{7,6},{6,4},{4,2},{2,0},{8,9},{9,11},{11,1... | collective-permute-start | bytes 1493000 | tf_op jit(solution)/shard_map/ppermute | solution.py:81
  686.4 20.6 %collective-permute-start.148 = (bf16[64,1728]{0,1:T(8,128)(2,1)S(1)}, bf16[64,1728]{0,1:T(8,128)(2,1)S(1)}, u32[]{:S(2)}, u32[]{:S(2)}) collective-permute-start(bf16[64,1728]{0,1:T(8,128)(2,1)S(1)} %add_convert_fusion.26), channel_id=1, source_target_pairs={{0,1},{1,3},{3,5},{5,7},{7,6},{6,4},{4,2},{2,0},{8,9},{9,11},{11,1... | collective-permute-start | bytes 663560 | tf_op jit(solution)/shard_map/ppermute | solution.py:81
  717.2 22.2 %collective-permute-start.112 = (bf16[144,1728]{1,0:T(8,128)(2,1)S(1)}, bf16[144,1728]{1,0:T(8,128)(2,1)S(1)}, u32[]{:S(2)}, u32[]{:S(2)}) collective-permute-start(bf16[144,1728]{1,0:T(8,128)(2,1)S(1)} %get-tuple-element.66), channel_id=1, source_target_pairs={{0,1},{1,3},{3,5},{5,7},{7,6},{6,4},{4,2},{2,0},{8,9},{9,11},{11,1... | collective-permute-start | bytes 1493000 | tf_op jit(solution)/shard_map/ppermute | solution.py:81
  741.0 64.2 %collective-permute-start.68 = (bf16[512,1152]{1,0:T(8,128)(2,1)}, bf16[512,1152]{1,0:T(8,128)(2,1)}, u32[]{:S(2)}, u32[]{:S(2)}) collective-permute-start(bf16[512,1152]{1,0:T(8,128)(2,1)} %get-tuple-element.57), channel_id=1, source_target_pairs={{0,8},{8,0},{16,24},{24,16},{1,9},{9,1},{17,25},{25,17},{2,10},{10... | collective-permute-start | bytes 3538952 | tf_op jit(solution)/shard_map/ppermute | solution.py:115
  762.1 46.3 %collective-permute-start.74 = (bf16[512,1152]{1,0:T(8,128)(2,1)}, bf16[512,1152]{1,0:T(8,128)(2,1)}, u32[]{:S(2)}, u32[]{:S(2)}) collective-permute-start(bf16[512,1152]{1,0:T(8,128)(2,1)} %get-tuple-element.55), channel_id=1, source_target_pairs={{0,8},{8,0},{16,24},{24,16},{1,9},{9,1},{17,25},{25,17},{2,10},{10... | collective-permute-start | bytes 3538952 | tf_op jit(solution)/shard_map/ppermute | solution.py:115
  782.4 53.6 %collective-permute-start.116 = (bf16[144,1728]{1,0:T(8,128)(2,1)}, bf16[144,1728]{1,0:T(8,128)(2,1)}, u32[]{:S(2)}, u32[]{:S(2)}) collective-permute-start(bf16[144,1728]{1,0:T(8,128)(2,1)} %get-tuple-element.67), channel_id=1, source_target_pairs={{1,0},{3,1},{5,3},{7,5},{6,7},{4,6},{2,4},{0,2},{9,8},{11,9},{13,1... | collective-permute-start | bytes 1493000 | tf_op jit(solution)/shard_map/ppermute | solution.py:81
  805.1 75.9 %collective-permute-start.67 = (bf16[512,1152]{1,0:T(8,128)(2,1)}, bf16[512,1152]{1,0:T(8,128)(2,1)}, u32[]{:S(2)}, u32[]{:S(2)}) collective-permute-start(bf16[512,1152]{1,0:T(8,128)(2,1)} %get-tuple-element.56), channel_id=1, source_target_pairs={{0,8},{8,0},{16,24},{24,16},{1,9},{9,1},{17,25},{25,17},{2,10},{10... | collective-permute-start | bytes 3538952 | tf_op jit(solution)/shard_map/ppermute | solution.py:115
  832.0 44.8 %collective-permute-start.73 = (bf16[512,1152]{1,0:T(8,128)(2,1)S(1)}, bf16[512,1152]{1,0:T(8,128)(2,1)S(1)}, u32[]{:S(2)}, u32[]{:S(2)}) collective-permute-start(bf16[512,1152]{1,0:T(8,128)(2,1)S(1)} %copy-done.65), channel_id=1, source_target_pairs={{0,8},{8,0},{16,24},{24,16},{1,9},{9,1},{17,25},{25,17},{2,10},{10... | collective-permute-start | bytes 3538952 | tf_op jit(solution)/shard_map/ppermute | solution.py:115
  846.2 32.0 %collective-permute-start.75 = (bf16[512,1152]{1,0:T(8,128)(2,1)S(1)}, bf16[512,1152]{1,0:T(8,128)(2,1)S(1)}, u32[]{:S(2)}, u32[]{:S(2)}) collective-permute-start(bf16[512,1152]{1,0:T(8,128)(2,1)S(1)} %copy-done.67), channel_id=1, source_target_pairs={{0,16},{8,24},{16,0},{24,8},{1,17},{9,25},{17,1},{25,9},{2,18},{10... | collective-permute-start | bytes 3538952 | tf_op jit(solution)/shard_map/ppermute | solution.py:120
  865.9 33.1 %collective-permute-start.69 = (bf16[512,1152]{1,0:T(8,128)(2,1)S(1)}, bf16[512,1152]{1,0:T(8,128)(2,1)S(1)}, u32[]{:S(2)}, u32[]{:S(2)}) collective-permute-start(bf16[512,1152]{1,0:T(8,128)(2,1)S(1)} %copy-done.66), channel_id=1, source_target_pairs={{0,16},{8,24},{16,0},{24,8},{1,17},{9,25},{17,1},{25,9},{2,18},{10... | collective-permute-start | bytes 3538952 | tf_op jit(solution)/shard_map/ppermute | solution.py:120
  874.3 80.0 %collective-permute-start.95 = (bf16[216,1152]{1,0:T(8,128)(2,1)S(1)}, bf16[216,1152]{1,0:T(8,128)(2,1)}, u32[]{:S(2)}, u32[]{:S(2)}) collective-permute-start(bf16[216,1152]{1,0:T(8,128)(2,1)S(1)} %get-tuple-element.68), channel_id=1, source_target_pairs={{1,0},{3,1},{5,3},{7,5},{6,7},{4,6},{2,4},{0,2},{9,8},{11,9},{13,1... | collective-permute-start | bytes 1493000 | tf_op jit(solution)/shard_map/ppermute | solution.py:81
  876.7 81.7 %collective-permute-start.122 = (bf16[144,1728]{1,0:T(8,128)(2,1)}, bf16[144,1728]{1,0:T(8,128)(2,1)}, u32[]{:S(2)}, u32[]{:S(2)}) collective-permute-start(bf16[144,1728]{1,0:T(8,128)(2,1)} %get-tuple-element.60), channel_id=1, source_target_pairs={{1,0},{3,1},{5,3},{7,5},{6,7},{4,6},{2,4},{0,2},{9,8},{11,9},{13,1... | collective-permute-start | bytes 1493000 | tf_op jit(solution)/shard_map/ppermute | solution.py:81
  878.3 80.8 %collective-permute-start.115 = (bf16[144,1728]{1,0:T(8,128)(2,1)}, bf16[144,1728]{1,0:T(8,128)(2,1)S(1)}, u32[]{:S(2)}, u32[]{:S(2)}) collective-permute-start(bf16[144,1728]{1,0:T(8,128)(2,1)} %get-tuple-element.64), channel_id=1, source_target_pairs={{0,1},{1,3},{3,5},{5,7},{7,6},{6,4},{4,2},{2,0},{8,9},{9,11},{11,1... | collective-permute-start | bytes 1493000 | tf_op jit(solution)/shard_map/ppermute | solution.py:81
  881.1 74.0 %collective-permute-start.98 = (bf16[216,1152]{1,0:T(8,128)(2,1)}, bf16[216,1152]{1,0:T(8,128)(2,1)}, u32[]{:S(2)}, u32[]{:S(2)}) collective-permute-start(bf16[216,1152]{1,0:T(8,128)(2,1)} %add_convert_fusion.16), channel_id=1, source_target_pairs={{0,1},{1,3},{3,5},{5,7},{7,6},{6,4},{4,2},{2,0},{8,9},{9,11},{11,1... | collective-permute-start | bytes 1493000 | tf_op jit(solution)/shard_map/ppermute | solution.py:81
  899.0 60.0 %collective-permute-start.125 = (bf16[144,1728]{1,0:T(8,128)(2,1)}, bf16[144,1728]{1,0:T(8,128)(2,1)}, u32[]{:S(2)}, u32[]{:S(2)}) collective-permute-start(bf16[144,1728]{1,0:T(8,128)(2,1)} %add_convert_fusion.5), channel_id=1, source_target_pairs={{0,1},{1,3},{3,5},{5,7},{7,6},{6,4},{4,2},{2,0},{8,9},{9,11},{11,1... | collective-permute-start | bytes 1493000 | tf_op jit(solution)/shard_map/ppermute | solution.py:81
  955.0 97.6 %collective-permute-start.77 = (bf16[2,256,512]{2,1,0:T(8,128)(2,1)}, bf16[2,256,512]{2,1,0:T(8,128)(2,1)}, u32[]{:S(2)}, u32[]{:S(2)}) collective-permute-start(bf16[2,256,512]{2,1,0:T(8,128)(2,1)} %get-tuple-element.84), channel_id=1, source_target_pairs={{0,8},{8,0},{16,24},{24,16},{1,9},{9,1},{17,25},{25,17},{2,10},{10... | collective-permute-start | bytes 1572872 | tf_op jit(solution)/shard_map/ppermute | solution.py:115
  958.4 265.5 %collective-permute-start.76 = (bf16[2,256,512]{2,1,0:T(8,128)(2,1)}, bf16[2,256,512]{2,1,0:T(8,128)(2,1)}, u32[]{:S(2)}, u32[]{:S(2)}) collective-permute-start(bf16[2,256,512]{2,1,0:T(8,128)(2,1)} %get-tuple-element.83), channel_id=1, source_target_pairs={{0,8},{8,0},{16,24},{24,16},{1,9},{9,1},{17,25},{25,17},{2,10},{10... | collective-permute-start | bytes 1572872 | tf_op jit(solution)/shard_map/ppermute | solution.py:115
  971.0 79.6 %collective-permute-start.126 = (f32[144,640]{1,0:T(8,128)}, f32[144,640]{1,0:T(8,128)}, u32[]{:S(2)}, u32[]{:S(2)}) collective-permute-start(f32[144,640]{1,0:T(8,128)} %pad_maximum_fusion.12), channel_id=1, source_target_pairs={{0,8},{8,0},{16,24},{24,16},{1,9},{9,1},{17,25},{25,17},{2,10},{10... | collective-permute-start | bytes 1105928 | tf_op jit(solution)/shard_map/ppermute | solution.py:148
  984.4 223.6 %collective-permute-start.134 = (bf16[216,1408]{1,0:T(8,128)(2,1)}, bf16[216,1408]{1,0:T(8,128)(2,1)}, u32[]{:S(2)}, u32[]{:S(2)}) collective-permute-start(bf16[216,1408]{1,0:T(8,128)(2,1)} %pad_maximum_fusion.8), channel_id=1, source_target_pairs={{0,8},{8,0},{16,24},{24,16},{1,9},{9,1},{17,25},{25,17},{2,10},{10... | collective-permute-start | bytes 1824776 | tf_op jit(solution)/shard_map/ppermute | solution.py:109
  984.9 70.2 %collective-permute-start.131 = (bf16[144,8,216]{2,1,0:T(8,128)(2,1)}, bf16[144,8,216]{2,1,0:T(8,128)(2,1)}, u32[]{:S(2)}, u32[]{:S(2)}) collective-permute-start(bf16[144,8,216]{2,1,0:T(8,128)(2,1)} %reshape.664), channel_id=1, source_target_pairs={{0,8},{8,0},{16,24},{24,16},{1,9},{9,1},{17,25},{25,17},{2,10},{10... | collective-permute-start | bytes 1493000 | tf_op jit(solution)/shard_map/ppermute | solution.py:109
  1050.6 160.5 %collective-permute-start.135 = (bf16[216,1408]{1,0:T(8,128)(2,1)}, bf16[216,1408]{1,0:T(8,128)(2,1)}, u32[]{:S(2)}, u32[]{:S(2)}) collective-permute-start(bf16[216,1408]{1,0:T(8,128)(2,1)} %pad_maximum_fusion.8), channel_id=1, source_target_pairs={{0,16},{8,24},{16,0},{24,8},{1,17},{9,25},{17,1},{25,9},{2,18},{10... | collective-permute-start | bytes 1824776 | tf_op jit(solution)/shard_map/ppermute | solution.py:105
  1052.7 27.0 %collective-permute-start.132 = (bf16[144,8,216]{2,1,0:T(8,128)(2,1)}, bf16[144,8,216]{2,1,0:T(8,128)(2,1)}, u32[]{:S(2)}, u32[]{:S(2)}) collective-permute-start(bf16[144,8,216]{2,1,0:T(8,128)(2,1)} %reshape.664), channel_id=1, source_target_pairs={{0,16},{8,24},{16,0},{24,8},{1,17},{9,25},{17,1},{25,9},{2,18},{10... | collective-permute-start | bytes 1493000 | tf_op jit(solution)/shard_map/ppermute | solution.py:105
  1055.1 26.6 %collective-permute-start.128 = (bf16[144,8,216]{2,1,0:T(8,128)(2,1)S(1)}, bf16[144,8,216]{2,1,0:T(8,128)(2,1)S(1)}, u32[]{:S(2)}, u32[]{:S(2)}) collective-permute-start(bf16[144,8,216]{2,1,0:T(8,128)(2,1)S(1)} %copy-done.81), channel_id=1, source_target_pairs={{0,8},{8,0},{16,24},{24,16},{1,9},{9,1},{17,25},{25,17},{2,10},{10... | collective-permute-start | bytes 1493000 | tf_op jit(solution)/shard_map/ppermute | solution.py:109
  1081.8 139.0 %collective-permute-start.100 = (bf16[8,48,1152]{2,1,0:T(8,128)(2,1)}, bf16[8,48,1152]{2,1,0:T(8,128)(2,1)}, u32[]{:S(2)}, u32[]{:S(2)}) collective-permute-start(bf16[8,48,1152]{2,1,0:T(8,128)(2,1)} %get-tuple-element.73), channel_id=1, source_target_pairs={{0,8},{8,0},{16,24},{24,16},{1,9},{9,1},{17,25},{25,17},{2,10},{10... | collective-permute-start | bytes 2654216 | tf_op jit(solution)/shard_map/ppermute | solution.py:115
  1094.7 167.9 %collective-permute-start.99 = (bf16[8,48,1152]{2,1,0:T(8,128)(2,1)}, bf16[8,48,1152]{2,1,0:T(8,128)(2,1)}, u32[]{:S(2)}, u32[]{:S(2)}) collective-permute-start(bf16[8,48,1152]{2,1,0:T(8,128)(2,1)} %get-tuple-element.72), channel_id=1, source_target_pairs={{0,8},{8,0},{16,24},{24,16},{1,9},{9,1},{17,25},{25,17},{2,10},{10... | collective-permute-start | bytes 2654216 | tf_op jit(solution)/shard_map/ppermute | solution.py:115
  1219.4 56.4 %collective-permute-start.133 = (bf16[144,8,216]{2,1,0:T(8,128)(2,1)}, bf16[144,8,216]{2,1,0:T(8,128)(2,1)}, u32[]{:S(2)}, u32[]{:S(2)}) collective-permute-start(bf16[144,8,216]{2,1,0:T(8,128)(2,1)} %collective-permute-done.132), channel_id=1, source_target_pairs={{0,8},{8,0},{16,24},{24,16},{1,9},{9,1},{17,25},{25,17},{2,10},{10... | collective-permute-start | bytes 1493000 | tf_op jit(solution)/shard_map/ppermute | solution.py:109
  1220.8 66.1 %collective-permute-start.130 = (bf16[144,8,216]{2,1,0:T(8,128)(2,1)}, bf16[144,8,216]{2,1,0:T(8,128)(2,1)}, u32[]{:S(2)}, u32[]{:S(2)}) collective-permute-start(bf16[144,8,216]{2,1,0:T(8,128)(2,1)} %collective-permute-done.129), channel_id=1, source_target_pairs={{0,8},{8,0},{16,24},{24,16},{1,9},{9,1},{17,25},{25,17},{2,10},{10... | collective-permute-start | bytes 1493000 | tf_op jit(solution)/shard_map/ppermute | solution.py:109
  1223.9 141.7 %collective-permute-start.136 = (bf16[216,1408]{1,0:T(8,128)(2,1)}, bf16[216,1408]{1,0:T(8,128)(2,1)}, u32[]{:S(2)}, u32[]{:S(2)}) collective-permute-start(bf16[216,1408]{1,0:T(8,128)(2,1)} %collective-permute-done.135), channel_id=1, source_target_pairs={{0,8},{8,0},{16,24},{24,16},{1,9},{9,1},{17,25},{25,17},{2,10},{10... | collective-permute-start | bytes 1824776 | tf_op jit(solution)/shard_map/ppermute | solution.py:109
  1230.2 32.5 %collective-permute-start.101 = (bf16[8,48,1152]{2,1,0:T(8,128)(2,1)}, bf16[8,48,1152]{2,1,0:T(8,128)(2,1)}, u32[]{:S(2)}, u32[]{:S(2)}) collective-permute-start(bf16[8,48,1152]{2,1,0:T(8,128)(2,1)} %add_convert_fusion.3), channel_id=1, source_target_pairs={{0,16},{8,24},{16,0},{24,8},{1,17},{9,25},{17,1},{25,9},{2,18},{10... | collective-permute-start | bytes 2654216 | tf_op jit(solution)/shard_map/ppermute | solution.py:120
  1279.9 82.6 %collective-permute-start.79 = (bf16[8,176,384]{2,1,0:T(8,128)(2,1)}, bf16[8,176,384]{2,1,0:T(8,128)(2,1)}, u32[]{:S(2)}, u32[]{:S(2)}) collective-permute-start(bf16[8,176,384]{2,1,0:T(8,128)(2,1)} %get-tuple-element.58), channel_id=1, source_target_pairs={{0,8},{8,0},{16,24},{24,16},{1,9},{9,1},{17,25},{25,17},{2,10},{10... | collective-permute-start | bytes 3244040 | tf_op jit(solution)/shard_map/ppermute | solution.py:115
  1282.5 80.0 %collective-permute-start.81 = (bf16[8,176,384]{2,1,0:T(8,128)(2,1)}, bf16[8,176,384]{2,1,0:T(8,128)(2,1)}, u32[]{:S(2)}, u32[]{:S(2)}) collective-permute-start(bf16[8,176,384]{2,1,0:T(8,128)(2,1)} %add_convert_fusion.1), channel_id=1, source_target_pairs={{0,16},{8,24},{16,0},{24,8},{1,17},{9,25},{17,1},{25,9},{2,18},{10... | collective-permute-start | bytes 3244040 | tf_op jit(solution)/shard_map/ppermute | solution.py:120
  1285.5 74.8 %collective-permute-start.105 = (bf16[48,1152]{1,0:T(8,128)(2,1)S(1)}, bf16[48,1152]{1,0:T(8,128)(2,1)}, u32[]{:S(2)}, u32[]{:S(2)}) collective-permute-start(bf16[48,1152]{1,0:T(8,128)(2,1)S(1)} %get-tuple-element.113), channel_id=1, source_target_pairs={{0,1},{1,3},{3,5},{5,7},{7,6},{6,4},{4,2},{2,0},{8,9},{9,11},{11,1... | collective-permute-start | bytes 331784 | tf_op jit(solution)/shard_map/ppermute | solution.py:81
  1286.9 73.3 %collective-permute-start.108 = (bf16[48,1152]{1,0:T(8,128)(2,1)S(1)}, bf16[48,1152]{1,0:T(8,128)(2,1)}, u32[]{:S(2)}, u32[]{:S(2)}) collective-permute-start(bf16[48,1152]{1,0:T(8,128)(2,1)S(1)} %fusion.132), channel_id=1, source_target_pairs={{1,0},{3,1},{5,3},{7,5},{6,7},{4,6},{2,4},{0,2},{9,8},{11,9},{13,1... | collective-permute-start | bytes 331784 | tf_op jit(solution)/shard_map/ppermute | solution.py:81
  (242 other events, 3894.4 us)

commit v2 on v1

v2 whole, which is shorter than its diff:
```python
import jax
import jax.numpy as jnp
from jax import lax
from jax.experimental import pallas as pl
from jax.experimental.pallas import tpu as pltpu
from jax.sharding import PartitionSpec as P

H = 4
HD = 256
DEPTHS = 3
LOOP = 1
CORES = 2

epsilon = 1e-06
rope_base = 10000.0
low = jnp.bfloat16
wide = jnp.float32


def mul(left, right):
    return jnp.dot(left, right, preferred_element_type=wide)


def mul_t(left, right):
    return lax.dot_general(left, right, (((1,), (1,)), ((), ())), preferred_element_type=wide)


def t_mul(left, right):
    return lax.dot_general(left, right, (((0,), (0,)), ((), ())), preferred_element_type=wide)


def ring_order(count, width):
    if width < 2 or count % width or (count // width) % 2:
        return list(range(count))
    depth = count // width
    walk = [0]
    for z in range(depth):
        columns = range(1, width) if z % 2 == 0 else range(width - 1, 0, -1)
        walk += [z * width + x for x in columns]
    walk += [z * width for z in range(depth - 1, 0, -1)]
    return walk


MESH = pl.DeviceIdType.MESH
ANY = pl.BlockSpec(memory_space=pl.ANY)
VMEM = pl.BlockSpec(memory_space=pltpu.VMEM)


def pick(index, table):
    result = jnp.int32(table[0])
    for spot, value in enumerate(table):
        if spot:
            result = jnp.where(index == spot, jnp.int32(value), result)
    return result


class Places:
    def __init__(self, n_f, n_seq):
        self.n_f, self.n_seq, self.chips = n_f, n_seq, n_seq // CORES
        self.walk = ring_order(n_f, n_seq // CORES)
        spots = [0] * n_f
        for spot, device in enumerate(self.walk):
            spots[device] = spot
        self.f, self.me = lax.axis_index("fsdp"), lax.axis_index("seq")
        self.spot = pick(self.f, spots)
        self.y, self.core = self.me // CORES, lax.rem(self.me, CORES)

    def at(self, offset):
        return pick(lax.rem(self.spot + offset + self.n_f, self.n_f), self.walk)

    def seq(self, k, c):
        return lax.rem(self.y + k + self.chips, self.chips) * CORES + lax.rem(
            self.core + c, CORES
        )

    def greet(self, ring):
        barrier = pltpu.get_barrier_semaphore()
        friends = [{"seq": self.seq(0, 1)}]
        friends += [{"seq": self.seq(k, 0)} for k in range(1, self.chips)]
        if ring:
            friends += [{"fsdp": self.at(1)}, {"fsdp": self.at(-1)}]
        for friend in friends:
            pl.semaphore_signal(barrier, inc=1, device_id=friend, device_id_type=MESH)
        pl.semaphore_wait(barrier, len(friends))


def remote(source, target, send, receive, device):
    return pltpu.make_async_remote_copy(
        src_ref=source,
        dst_ref=target,
        send_sem=send,
        recv_sem=receive,
        device_id=device,
        device_id_type=MESH,
    )


def params(number):
    return pltpu.CompilerParams(
        collective_id=number, has_side_effects=True, vmem_limit_bytes=56 * 2**20
    )


def ring_steps(n_f):
    order = []
    for step in range(1, n_f // 2 + 1):
        order.append((step, 1))
        if step <= (n_f - 1) // 2:
            order.append((step, -1))
    return order


def gather_whole(blocks, number, n_f, n_seq):
    count = len(blocks)
    chips = n_seq // CORES
    steps = ring_steps(n_f)

    def body(*refs):
        ins, outs = refs[:count], refs[count : 2 * count]
        local, ring_s, ring_r, y_s, y_r, core_s, core_r = refs[2 * count :]
        here = Places(n_f, n_seq)
        started = []

        def share(ref, spot):
            width = ref.shape[-1] // n_seq
            return (slice(None), pl.ds(pl.multiple_of(spot * width, 128), width))

        copies = []
        for j in range(count):
            copy = pltpu.make_async_copy(ins[j], outs[j].at[here.f], local.at[j])
            copy.start()
            copies.append(copy)
        here.greet(True)

        def forward(j, step, way):
            owner = here.at(-way * (step - 1))
            mine = share(ins[j], here.me)
            source = ins[j].at[mine] if step == 1 else outs[j].at[(owner, *mine)]
            at = steps.index((step, way))
            copy = remote(
                source,
                outs[j].at[(owner, *mine)],
                ring_s.at[j, at],
                ring_r.at[j, at],
                {"fsdp": here.at(way)},
            )
            copy.start()
            started.append(copy)

        def landed(j, step, way):
            owner = here.at(-way * step)
            mine = share(ins[j], here.me)
            at = steps.index((step, way))
            block = outs[j].at[(owner, *mine)]
            remote(block, block, ring_s.at[j, at], ring_r.at[j, at], {"fsdp": here.at(way)}).wait_recv()
            return owner

        def to_core(j, at, k, owner):
            block = outs[j].at[(owner, *share(ins[j], here.seq(k, 0)))]
            copy = remote(
                block, block, core_s.at[j, at, k], core_r.at[j, at, k], {"seq": here.seq(0, 1)}
            )
            copy.start()
            started.append(copy)

        for j in range(count):
            for way in (1, -1):
                forward(j, 1, way)
        for at, (step, way) in enumerate(steps):
            for j in range(count):
                owner = landed(j, step, way)
                if (step + 1, way) in steps:
                    forward(j, step + 1, way)
                block = outs[j].at[(owner, *share(ins[j], here.me))]
                for k in range(1, chips):
                    copy = remote(
                        block, block, y_s.at[j, at, k], y_r.at[j, at, k], {"seq": here.seq(-k, 0)}
                    )
                    copy.start()
                    started.append(copy)
                to_core(j, at, 0, owner)
        for at, (step, way) in enumerate(steps):
            owner = here.at(-way * step)
            for j in range(count):
                for k in range(1, chips):
                    block = outs[j].at[(owner, *share(ins[j], here.seq(k, 0)))]
                    remote(
                        block, block, y_s.at[j, at, k], y_r.at[j, at, k], {"seq": here.seq(-k, 0)}
                    ).wait_recv()
                    to_core(j, at, k, owner)
        for at, (step, way) in enumerate(steps):
            owner = here.at(-way * step)
            for j in range(count):
                for k in range(chips):
                    block = outs[j].at[(owner, *share(ins[j], here.seq(k, 1)))]
                    remote(
                        block, block, core_s.at[j, at, k], core_r.at[j, at, k], {"seq": here.seq(0, 1)}
                    ).wait_recv()
        for copy in started:
            copy.wait_send()
        for copy in copies:
            copy.wait()

    sems = pltpu.SemaphoreType.DMA
    return pl.pallas_call(
        body,
        out_shape=tuple(jax.ShapeDtypeStruct((n_f,) + b.shape, b.dtype) for b in blocks),
        in_specs=[ANY] * count,
        out_specs=(ANY,) * count,
        scratch_shapes=[sems((count,))]
        + [sems((count, len(steps)))] * 2
        + [sems((count, len(steps), chips))] * 4,
        compiler_params=params(number),
    )(*blocks)


def gather_group(block, number, n_seq):
    rows = block.shape[0]
    chips = n_seq // CORES
    parts = 4 if rows % 64 == 0 else 1
    size = rows // parts

    def body(x, out, local, y_s, y_r, core_s, core_r):
        here = Places(1, n_seq)
        own = pltpu.make_async_copy(x, out.at[0], local)
        own.start()
        here.greet(False)
        started = []

        def to_core(source, k, part):
            cut = pl.ds(part * size, size)
            copy = remote(
                source.at[cut],
                out.at[k * CORES + 1, cut],
                core_s.at[k, part],
                core_r.at[k, part],
                {"seq": here.seq(0, 1)},
            )
            copy.start()
            started.append(copy)

        def over(k, part):
            cut = pl.ds(part * size, size)
            return remote(
                x.at[cut],
                out.at[k * CORES, cut],
                y_s.at[k, part],
                y_r.at[k, part],
                {"seq": here.seq(-k, 0)},
            )

        for part in range(parts):
            for k in range(1, chips):
                copy = over(k, part)
                copy.start()
                started.append(copy)
            to_core(x, 0, part)
        for part in range(parts):
            for k in range(1, chips):
                over(k, part).wait_recv()
                to_core(out.at[k * CORES], k, part)
        for part in range(parts):
            for k in range(chips):
                cut = pl.ds(part * size, size)
                block = out.at[k * CORES + 1, cut]
                remote(
                    block, block, core_s.at[k, part], core_r.at[k, part], {"seq": here.seq(0, 1)}
                ).wait_recv()
        for copy in started:
            copy.wait_send()
        own.wait()

    sems = pltpu.SemaphoreType.DMA
    return pl.pallas_call(
        body,
        out_shape=jax.ShapeDtypeStruct((n_seq,) + block.shape, block.dtype),
        in_specs=[ANY],
        out_specs=ANY,
        scratch_shapes=[sems(())] + [sems((chips, parts))] * 4,
        compiler_params=params(number),
    )(block)


def scatter_group(terms, number):
    n_seq, rows, columns = terms.shape
    chips = n_seq // CORES
    parts = 4 if rows % 64 == 0 else 1
    size = rows // parts

    def body(x, out, near, sums, far, y_s, y_r, core_s, core_r):
        here = Places(1, n_seq)
        here.greet(False)
        started = []

        def cross(k, part):
            cut = pl.ds(part * size, size)
            return remote(
                x.at[k * CORES + 1, cut],
                near.at[k, cut],
                core_s.at[k, part],
                core_r.at[k, part],
                {"seq": here.seq(0, 1)},
            )

        def over(k, part):
            cut = pl.ds(part * size, size)
            return remote(
                sums.at[k, cut],
                far.at[k, cut],
                y_s.at[k, part],
                y_r.at[k, part],
                {"seq": here.seq(k, 0)},
            )

        for k in [*range(1, chips), 0]:
            for part in range(parts):
                copy = cross(k, part)
                copy.start()
                started.append(copy)
        for k in range(1, chips):
            for part in range(parts):
                cut = pl.ds(part * size, size)
                cross(k, part).wait_recv()
                total = x[k * CORES, cut, :].astype(wide) + near[k, cut, :].astype(wide)
                sums[k, cut, :] = total.astype(low)
                copy = over(k, part)
                copy.start()
                started.append(copy)
        for part in range(parts):
            cut = pl.ds(part * size, size)
            cross(0, part).wait_recv()
            out[cut, :] = x[0, cut, :].astype(wide) + near[0, cut, :].astype(wide)
        for part in range(parts):
            cut = pl.ds(part * size, size)
            for k in range(1, chips):
                over(k, part).wait_recv()
                out[cut, :] = out[cut, :] + far[k, cut, :].astype(wide)
        for copy in started:
            copy.wait_send()

    sems = pltpu.SemaphoreType.DMA
    buffer = pltpu.VMEM((chips, rows, columns), low)
    return pl.pallas_call(
        body,
        out_shape=jax.ShapeDtypeStruct((rows, columns), wide),
        in_specs=[VMEM],
        out_specs=VMEM,
        scratch_shapes=[buffer] * 3 + [sems((chips, parts))] * 4,
        compiler_params=params(number),
    )(terms)


def scatter_whole(packs, number, n_seq):
    wanted = [pack.shape[2] for pack in packs]
    gaps = [-count % (128 * n_seq) for count in wanted]
    packs = [
        jnp.pad(pack, ((0, 0), (0, 0), (0, gap))) if gap else pack
        for pack, gap in zip(packs, gaps, strict=True)
    ]
    n_f, count = packs[0].shape[0], len(packs)
    chips = n_seq // CORES
    widths = [pack.shape[2] // n_seq for pack in packs]
    steps = ring_steps(n_f)
    offsets = [way * step for step, way in reversed(steps)] + [0]
    last = {way: max(step for step, w in steps if w == way) for way in (1, -1)}

    def body(*refs):
        xs, outs = refs[:count], refs[count : 2 * count]
        buffers, sem = refs[2 * count : 7 * count], refs[7 * count :]
        nears, sums, fars, terms, moves = (
            buffers[i * count : (i + 1) * count] for i in range(5)
        )
        core_s, core_r, y_s, y_r, ring_s, ring_r, over_s, over_r, side_s, side_r = sem
        here = Places(n_f, n_seq)
        here.greet(True)
        started = []

        def share(j, spot):
            return pl.ds(pl.multiple_of(spot * widths[j], 128), widths[j])

        def cross(j, i, k):
            owner = here.at(offsets[i])
            return remote(
                xs[j].at[owner, :, share(j, here.seq(k, 1))],
                nears[j].at[i, k],
                core_s.at[j, i, k],
                core_r.at[j, i, k],
                {"seq": here.seq(0, 1)},
            )

        def over(j, i, k):
            return remote(
                sums[j].at[i, k],
                fars[j].at[i, k],
                y_s.at[j, i, k],
                y_r.at[j, i, k],
                {"seq": here.seq(k, 0)},
            )

        def hop(j, step, way):
            at = steps.index((step, way))
            return remote(
                terms[j].at[at],
                moves[j].at[at],
                ring_s.at[j, at],
                ring_r.at[j, at],
                {"fsdp": here.at(way)},
            )

        def go(copy):
            copy.start()
            started.append(copy)

        for i in range(n_f):
            for j in range(count):
                for k in [*range(1, chips), 0]:
                    go(cross(j, i, k))
        for i in range(n_f):
            owner = here.at(offsets[i])
            for j in range(count):
                for k in range(1, chips):
                    cross(j, i, k).wait_recv()
                    mine = xs[j][owner, :, share(j, here.seq(k, 0))].astype(wide)
                    sums[j][i, k] = (mine + nears[j][i, k].astype(wide)).astype(low)
                    go(over(j, i, k))
        for i in range(n_f):
            owner = here.at(offsets[i])
            for j in range(count):
                cross(j, i, 0).wait_recv()
                total = xs[j][owner, :, share(j, here.me)].astype(wide)
                total = total + nears[j][i, 0].astype(wide)
                for k in range(1, chips):
                    over(j, i, k).wait_recv()
                    total = total + fars[j][i, k].astype(wide)
                if offsets[i]:
                    step, way = abs(offsets[i]), 1 if offsets[i] > 0 else -1
                    if step < last[way]:
                        hop(j, step + 1, way).wait_recv()
                        total = total + moves[j][steps.index((step + 1, way))].astype(wide)
                    terms[j][steps.index((step, way))] = total.astype(low)
                    go(hop(j, step, way))
                else:
                    for way in (1, -1):
                        if last[way] >= 1:
                            hop(j, 1, way).wait_recv()
                            total = total + moves[j][steps.index((1, way))].astype(wide)
                    outs[j][:, share(j, here.me)] = total.astype(low)

        def swap(j, k, spot):
            block = outs[j].at[:, share(j, spot)]
            return remote(block, block, over_s.at[j, k], over_r.at[j, k], {"seq": here.seq(-k, 0)})

        def side(j, k, spot):
            block = outs[j].at[:, share(j, spot)]
            return remote(block, block, side_s.at[j, k], side_r.at[j, k], {"seq": here.seq(0, 1)})

        for j in range(count):
            for k in range(1, chips):
                go(swap(j, k, here.me))
            go(side(j, 0, here.me))
        for j in range(count):
            for k in range(1, chips):
                swap(j, k, here.seq(k, 0)).wait_recv()
                go(side(j, k, here.seq(k, 0)))
        for j in range(count):
            for k in range(chips):
                side(j, k, here.seq(k, 1)).wait_recv()
        for copy in started:
            copy.wait_send()

    sems = pltpu.SemaphoreType.DMA
    shapes = [(pack.shape[1], width) for pack, width in zip(packs, widths, strict=True)]
    full = [pltpu.VMEM((n_f, chips, *shape), low) for shape in shapes]
    ring = [pltpu.VMEM((len(steps), *shape), low) for shape in shapes]
    results = pl.pallas_call(
        body,
        out_shape=tuple(jax.ShapeDtypeStruct(pack.shape[1:], low) for pack in packs),
        in_specs=[VMEM] * count,
        out_specs=(VMEM,) * count,
        scratch_shapes=full * 3
        + ring * 2
        + [sems((count, n_f, chips))] * 4
        + [sems((count, len(steps)))] * 2
        + [sems((count, chips))] * 4,
        compiler_params=params(number),
    )(*packs)
    return [result[:, :size] for result, size in zip(results, wanted, strict=True)]


class Ring:
    def __init__(self, count, width):
        self.count = count
        walk = ring_order(count, width)
        self.walk = jnp.array(walk, jnp.int32)
        place = [0] * count
        for spot, device in enumerate(walk):
            place[device] = spot
        self.spot = jnp.array(place, jnp.int32)[lax.axis_index("fsdp")]
        self.up = [(walk[i], walk[(i + 1) % count]) for i in range(count)]
        self.down = [(b, a) for a, b in self.up]

    def at(self, offset):
        return self.walk[lax.rem(self.spot + offset + self.count, self.count)]

    def hop(self, block, way):
        return lax.ppermute(block, "fsdp", self.up if way > 0 else self.down)


class Gathering:
    def __init__(self, ring, block, buffers, keep):
        self.ring, self.buffers, self.keep = ring, buffers, keep
        self.step, self.steps = 0, ring.count // 2
        self.moving = (block, block)
        self.new = [(0, block)]

    def advance(self):
        self.settle()
        if self.step == self.steps:
            return
        self.step += 1
        first, second = self.moving
        if self.step < self.steps:
            self.moving = (self.ring.hop(first, 1), self.ring.hop(second, -1))
            self.new = [(-self.step, self.moving[0]), (self.step, self.moving[1])]
        else:
            half = first.shape[1] // 256 * 128
            self.moving = (
                self.ring.hop(first[:, :half], 1),
                self.ring.hop(second[:, half:], -1),
            )
            self.new = [(self.step, jnp.concatenate(self.moving, axis=1))]

    def settle(self):
        for offset, block in self.new:
            self.buffers = self.keep(self.buffers, self.ring.at(offset), block)
        self.new = []

    def done(self):
        while self.step < self.steps:
            self.advance()
        self.settle()
        return self.buffers

    def live(self):
        return (self.moving, self.buffers, [block for _, block in self.new])

    def restore(self, live):
        self.moving, self.buffers, blocks = live
        self.new = [(offset, block) for (offset, _), block in zip(self.new, blocks, strict=True)]


class Scattering:
    def __init__(self, ring, part):
        self.ring, self.part = ring, part
        self.step, self.steps = 0, ring.count // 2
        self.moving = ()

    def advance(self):
        if self.step == self.steps:
            return
        self.step += 1
        offset = self.steps - self.step + 1
        if self.step == 1:
            term = self.part(self.ring.at(offset))
            self.half = term.shape[1] // 256 * 128
            ahead, back = term[:, : self.half], term[:, self.half :]
        else:
            ahead, back = self.joined(offset)
        self.moving = (
            self.ring.hop(ahead.astype(low), 1),
            self.ring.hop(back.astype(low), -1),
        )

    def joined(self, offset):
        ahead, back = self.part(self.ring.at(offset)), self.part(self.ring.at(-offset))
        first, second = (block.astype(wide) for block in self.moving)
        if self.step == 2:
            first = jnp.pad(first, ((0, 0), (0, ahead.shape[1] - self.half)))
            second = jnp.pad(second, ((0, 0), (self.half, 0)))
        return ahead + first, back + second

    def done(self):
        while self.step < self.steps:
            self.advance()
        total = self.part(self.ring.at(0))
        for block in self.moving:
            total = total + block.astype(wide)
        return total

    def live(self):
        return self.moving

    def restore(self, live):
        self.moving = live


def tie(movers, values):
    lives, values = lax.optimization_barrier(([mover.live() for mover in movers], values))
    for mover, live in zip(movers, lives, strict=True):
        mover.restore(live)
    return values


class Group:
    def __init__(self, count):
        self.count = count
        self.chips = count // CORES
        me = lax.axis_index("seq")
        self.y, self.core = me // CORES, lax.rem(me, CORES)
        self.sibling = [(i, i ^ 1) for i in range(count)]
        self.order = [(k, c) for k in range(self.chips) for c in range(CORES)]

    def shift(self, k):
        n = self.chips
        return [(i, ((i // CORES + k) % n) * CORES + i % CORES) for i in range(self.count)]

    def index(self, k, c):
        return lax.rem(self.y + k, self.chips) * CORES + (self.core + c) % CORES

    def over(self, block):
        return [block] + [
            lax.ppermute(block, "seq", self.shift(-k)) for k in range(1, self.chips)
        ]

    def across(self, blocks):
        out = []
        for block in blocks:
            out += [block, lax.ppermute(block, "seq", self.sibling)]
        return out

    def cross(self, terms):
        return [
            lax.ppermute(terms[k * CORES + 1], "seq", self.sibling) for k in range(self.chips)
        ]

    def send(self, sums):
        return [
            lax.ppermute(sums[k].astype(low), "seq", self.shift(k)) for k in range(1, self.chips)
        ]

    def laid(self, pieces, axis, dtype):
        width = pieces[0].shape[axis]
        shape = list(pieces[0].shape)
        shape[axis] = width * self.count
        out = jnp.zeros(shape, dtype)
        for (k, c), piece in zip(self.order, pieces, strict=True):
            out = lax.dynamic_update_slice_in_dim(
                out, piece.astype(dtype), self.index(k, c) * width, axis
            )
        return out


class Summing:
    def __init__(self, values, axes):
        self.values = values
        self.steps = [
            (axis, 1 << bit)
            for axis in axes
            for bit in range((lax.axis_size(axis) - 1).bit_length())
        ]
        assert all(lax.axis_size(axis) & (lax.axis_size(axis) - 1) == 0 for axis in axes)

    def advance(self):
        if self.steps:
            axis, step = self.steps.pop(0)
            pairs = [(i, i ^ step) for i in range(lax.axis_size(axis))]
            self.values = self.values + lax.ppermute(self.values, axis, pairs)

    def done(self):
        while self.steps:
            self.advance()
        return self.values

    def live(self):
        return self.values

    def restore(self, live):
        self.values = live


def cut_columns(weights, raises, gains, n_f, n_seq, slab):
    rows, ff = weights[0].shape
    rank_rows = raises[0].shape[0]
    block, cut = ff // n_f, ff // (n_f * n_seq)

    def body(gain_ref, w0, w1, r0, r1, out):
        me = lax.axis_index("seq")

        def run(ref, spot):
            runs = [
                ref[:, f * block + spot * cut : f * block + (spot + 1) * cut] for f in range(n_f)
            ]
            gap = slab - n_f * cut
            if gap:
                runs.append(jnp.zeros((ref.shape[0], gap), ref.dtype))
            return jnp.concatenate(runs, axis=1)

        for spot in range(n_seq):

            @pl.when(me == spot)
            def _():
                for side, (weight, raised) in enumerate(((w0, r0), (w1, r1))):
                    at = side * slab
                    out[:rank_rows, at : at + slab] = run(raised, spot)
                    scaled = run(weight, spot).astype(wide) * gain_ref[...]
                    out[rank_rows:, at : at + slab] = scaled.astype(low)

    return pl.pallas_call(
        body,
        out_shape=jax.ShapeDtypeStruct((rank_rows + rows, 2 * slab), low),
        compiler_params=pltpu.CompilerParams(vmem_limit_bytes=48 * 2**20),
    )(gains, *weights, *raises)


def place_columns(pieces, gains, n_f, n_seq, rank_rows, ff, slab):
    rows = pieces.shape[1] - rank_rows
    cut = ff // (n_f * n_seq)
    chips = n_seq // CORES

    def body(gain_ref, x, w0, w1, r0, r1):
        me = lax.axis_index("seq")
        y, core = me // CORES, lax.rem(me, CORES)

        def spot_of(spot):
            ahead = lax.rem(spot // CORES - y + chips, chips)
            return ahead * CORES + lax.rem(spot % CORES + core, CORES)

        def fill(out, first, count, at, gain):
            whole = [x[spot_of(spot), first : first + count, at : at + slab] for spot in range(n_seq)]
            runs = [
                whole[spot][:, f * cut : (f + 1) * cut] for f in range(n_f) for spot in range(n_seq)
            ]
            result = jnp.concatenate(runs, axis=1).astype(wide)
            out[...] = result if gain is None else result * gain

        for side, (weight, raised) in enumerate(((w0, r0), (w1, r1))):
            fill(raised, 0, rank_rows, side * slab, None)
            fill(weight, rank_rows, rows, side * slab, gain_ref[...])

    return pl.pallas_call(
        body,
        out_shape=(jax.ShapeDtypeStruct((rows, ff), wide),) * 2
        + (jax.ShapeDtypeStruct((rank_rows, ff), wide),) * 2,
        compiler_params=pltpu.CompilerParams(vmem_limit_bytes=56 * 2**20),
    )(gains, pieces)


def rope(values, cosine, sine):
    half = values.shape[-1] // 2
    first, second = values[..., :half], values[..., half:]
    cosine, sine = cosine[:, None, :], sine[:, None, :]
    return jnp.concatenate([first * cosine - second * sine, second * cosine + first * sine], axis=-1)


def gelu_parts(gate):
    scale = (2.0 / jnp.pi) ** 0.5
    cube = 0.044715
    curve = jnp.tanh(scale * (gate + cube * gate * gate * gate))
    value = 0.5 * gate * (1.0 + curve)
    slope = 0.5 * (1.0 + curve) + 0.5 * gate * (1.0 - curve * curve) * scale * (
        1.0 + 3.0 * cube * gate * gate
    )
    return value, slope


def shards(
    inputs,
    cotangent,
    segments,
    exits,
    confidence,
    attn_gain,
    q_weight,
    k_weight,
    v_weight,
    o_weight,
    q_down,
    q_up,
    k_down,
    k_up,
    v_down,
    v_up,
    o_down,
    o_up,
    mlp_gain,
    gate_weight,
    up_weight,
    down_weight,
    gate_down,
    gate_up,
    up_down,
    up_up,
    down_down,
    down_up,
):
    n_seq, n_f = lax.axis_size("seq"), lax.axis_size("fsdp")
    me = lax.axis_index("seq")
    ring = Ring(n_f, n_seq // CORES)
    group = Group(n_seq)
    rows, length, width = inputs.shape
    tokens = rows * length
    rank = q_down.shape[1]
    hq = q_weight.shape[1]
    ff = gate_weight.shape[1]
    own_rows = q_weight.shape[0]
    rank_rows = q_up.shape[0]
    o_rows = o_weight.shape[0]
    cut = ff // (n_f * n_seq)
    slab = -(-n_f * cut // 128) * 128
    scale = HD ** (-0.5)

    gain1 = attn_gain.astype(wide)[:, None]
    gain2 = mlp_gain.astype(wide)[:, None]

    def rows_of(array):
        part = array.shape[0] // n_seq
        return lax.dynamic_slice_in_dim(array, me * part, part, 0)

    def side_by_side(parts):
        total = sum(part.shape[1] for part in parts)
        gap = -total % (128 * n_seq)
        if gap:
            parts = [*parts, jnp.zeros((parts[0].shape[0], gap), low)]
        return jnp.concatenate(parts, axis=1)

    side1 = side_by_side(
        [
            (part.astype(wide) * gain1).astype(low)
            for part in (q_weight, k_weight, v_weight, q_down, k_down, v_down)
        ]
        + [(part.astype(wide) * gain2).astype(low) for part in (gate_down, up_down)]
    )
    ups = side_by_side([q_up, k_up, v_up, o_up, down_up])
    side_o = side_by_side([o_weight, o_down])

    def keep_slab(buffers, owner, block):
        raised, gates, raises = buffers
        put = lax.dynamic_update_index_in_dim
        return (
            put(raised, block[:rank_rows], owner, 0),
            put(gates, block[rank_rows:, :slab], owner, 0),
            put(raises, block[rank_rows:, slab:], owner, 0),
        )

    def keep_down(buffers, owner, block):
        return (lax.dynamic_update_index_in_dim(buffers[0], block, owner, 0),)

    slabs = Gathering(
        ring,
        cut_columns((gate_weight, up_weight), (gate_up, up_up), gain2, n_f, n_seq, slab),
        (
            jnp.zeros((n_f, rank_rows, 2 * slab), low),
            jnp.zeros((n_f, own_rows, slab), low),
            jnp.zeros((n_f, own_rows, slab), low),
        ),
        keep_slab,
    )
    d_lower = rows_of(down_down)
    downs = Gathering(
        ring,
        jnp.concatenate([rows_of(down_weight), d_lower], axis=1),
        (jnp.zeros((n_f, cut, width + rank), low),),
        keep_down,
    )

    depth_ids = jnp.arange(DEPTHS, dtype=jnp.int32)
    matches = (exits.reshape(tokens)[:, None] == depth_ids[None, :]).astype(wide)
    counted = Summing(
        jnp.concatenate(
            [jnp.sum(matches, axis=0), jnp.sum(matches * confidence.reshape(tokens)[:, None], axis=0)]
        ),
        ("seq", "fsdp"),
    )
    resid = inputs.reshape(tokens, width).astype(wide)
    active = (exits.reshape(tokens) >= LOOP).astype(wide)[:, None]
    cot = cotangent.reshape(tokens, width).astype(wide)
    g_mlp = (active * cot).astype(low)
    places = me * length + jnp.arange(length, dtype=jnp.int32)
    frequency = rope_base ** (-2.0 * jnp.arange(HD // 2, dtype=wide) / HD)
    angles = jnp.tile(places, rows).astype(wide)[:, None] * frequency[None, :]
    cosine, sine = jnp.cos(angles), jnp.sin(angles)
    r1 = lax.rsqrt(jnp.mean(resid * resid, axis=-1, keepdims=True) + epsilon)
    unit1 = (resid * r1).astype(low)

    slabs.advance()
    downs.advance()
    seg_pieces = group.over(segments.astype(low))
    whole = gather_whole((side1, ups, side_o), 0, n_f, n_seq)
    whole, seg_pieces, unit1, cosine, sine = tie(
        (slabs, downs), (whole, seg_pieces, unit1, cosine, sine)
    )
    side1, ups, side_o = (part.reshape(-1, part.shape[2]) for part in whole)
    kv = HD
    lin = hq + 2 * kv
    qkv_side = side1[:, : lin + 3 * rank]
    gate_adapter = side1[:, lin + 3 * rank : lin + 4 * rank]
    up_adapter = side1[:, lin + 4 * rank : lin + 5 * rank]
    side_o = side_o[:, : width + rank]
    q_raise, k_raise, v_raise = ups[:, :hq], ups[:, hq : hq + kv], ups[:, hq + kv : lin]
    o_raise, d_raise = ups[:, lin : lin + width], ups[:, lin + width : lin + 2 * width]

    slabs.advance()
    seg_pieces = group.across(seg_pieces)
    projected = mul(unit1, qkv_side)
    inner = projected[:, lin:].astype(low)
    q_inner, k_inner, v_inner = inner[:, :rank], inner[:, rank : 2 * rank], inner[:, 2 * rank :]
    q_lin = projected[:, :hq] + mul(q_inner, q_raise)
    k_lin = projected[:, hq : hq + kv] + mul(k_inner, k_raise)
    v_lin = projected[:, hq + kv : lin] + mul(v_inner, v_raise)
    queries = rope(q_lin.reshape(tokens, H, HD), cosine, sine).astype(low)
    queries = queries.reshape(rows, length, H, HD).transpose(0, 2, 1, 3)
    queries = queries.reshape(rows, H * length, HD)
    keys = rope(k_lin.reshape(tokens, 1, HD), cosine, sine).astype(low).reshape(tokens, HD)
    values = v_lin.astype(low)
    both = gather_group(jnp.concatenate([keys, values], axis=-1), 2, n_seq)
    both, queries, seg_pieces, inner = tie((slabs,), (both, queries, seg_pieces, inner))
    q_inner, k_inner, v_inner = inner[:, :rank], inner[:, rank : 2 * rank], inner[:, 2 * rank :]

    slabs.advance()
    g_mlp = group.over(g_mlp)
    both = both.reshape(n_seq, rows, length, 2 * HD)
    both = both.transpose(1, 0, 2, 3).reshape(rows, n_seq * length, 2 * HD)
    keys, values = both[..., :HD], both[..., HD:]
    key_seg = jnp.concatenate(seg_pieces, axis=1).astype(jnp.int32)
    key_place = jnp.concatenate(
        [
            group.index(k, c) * length + jnp.arange(length, dtype=jnp.int32)
            for k, c in group.order
        ]
    )
    query_seg, query_place = jnp.tile(segments, (1, H)), jnp.tile(places, H)
    allowed = (query_seg[:, :, None] == key_seg[:, None, :]) & (
        key_place[None, None, :] <= query_place[None, :, None]
    )
    scores = (
        jnp.einsum("sqd,skd->sqk", queries, keys, preferred_element_type=wide) * scale
    )
    scores = jnp.where(allowed, scores, -1e30)
    top = jnp.max(scores, axis=-1, keepdims=True)
    weights = jnp.exp(scores - top)
    totals = jnp.sum(weights, axis=-1, keepdims=True)
    attn = (
        jnp.einsum("sqk,skd->sqd", weights.astype(low), values, preferred_element_type=wide)
        / totals
    )
    log_total = top + jnp.log(totals)

    def to_tokens(rows_heads):
        view = rows_heads.reshape(rows, H, length, HD).transpose(0, 2, 1, 3)
        return view.reshape(tokens, hq)

    def to_heads(flat):
        view = flat.reshape(rows, length, H, HD).transpose(0, 2, 1, 3)
        return view.reshape(rows, H * length, HD)

    attn_low = to_tokens(attn.astype(low))
    projected = mul(attn_low, side_o)
    o_inner = projected[:, width:].astype(low)
    mid = resid + active * (projected[:, :width] + mul(o_inner, o_raise))
    r2 = lax.rsqrt(jnp.mean(mid * mid, axis=-1, keepdims=True) + epsilon)
    unit2 = (mid * r2).astype(low)
    unit2, mid, r2, g_mlp, attn, attn_low, o_inner, log_total = tie(
        (slabs, counted), (unit2, mid, r2, g_mlp, attn, attn_low, o_inner, log_total)
    )

    slabs.advance()
    downs.advance()
    counted.advance()
    g_mlp = group.across(g_mlp)
    unit2 = gather_group(unit2, 3, n_seq).reshape(-1, width)
    unit2, g_mlp = tie((slabs, downs, counted), (unit2, g_mlp))
    g_mlp = jnp.concatenate(g_mlp, axis=0)

    downs.advance()
    counted.advance()
    raised, gate_full, up_full = slabs.done()
    raised = raised.reshape(rank, 2 * slab)
    g_raise, u_raise = raised[:, :slab], raised[:, slab:]
    gate_full = (gate_full.reshape(width, slab).astype(wide) + mul(gate_adapter, g_raise)).astype(low)
    up_full = (up_full.reshape(width, slab).astype(wide) + mul(up_adapter, u_raise)).astype(low)
    gate = mul(unit2, gate_full).astype(low)
    up = mul(unit2, up_full).astype(low)
    value, slope = gelu_parts(gate.astype(wide))
    hidden = (value * up.astype(wide)).astype(low)[:, : n_f * cut]
    hidden, gate, up = tie((downs, counted), (hidden, gate, up))

    downs.advance()
    counted.advance()
    g_down = t_mul(hidden, g_mlp).astype(low)
    g_down, g_mlp = tie((downs, counted), (g_down, g_mlp))

    def ring_block(array, size):
        return lambda owner: lax.dynamic_slice_in_dim(array, owner * size, size, 0).astype(wide)

    down_sums = Scattering(ring, ring_block(g_down, cut))
    down_sums.advance()
    counted.advance()
    (down_raw,) = downs.done()
    down_raw = down_raw.reshape(n_f * cut, width + rank)
    down_full = (down_raw[:, :width].astype(wide) + mul(down_raw[:, width:], d_raise)).astype(low)
    padded = jnp.pad(down_full, ((0, slab - n_f * cut), (0, 0)))
    g_hidden = mul_t(g_mlp, padded)
    value, slope = gelu_parts(gate.astype(wide))
    g_gate = (g_hidden * up.astype(wide) * slope).astype(low)
    g_up = (g_hidden * value).astype(low)
    g_gate, g_up, down_full = tie((down_sums, counted), (g_gate, g_up, down_full))

    down_sums.advance()
    counted.advance()
    branch = mul(hidden, down_full).astype(low)
    branch, g_gate, g_up = tie((down_sums, counted), (branch, g_gate, g_up))

    down_sums.advance()
    terms = [branch[i * tokens : (i + 1) * tokens] for i in range(n_seq)]
    near = group.cross(terms)
    gg = t_mul(unit2, g_gate).astype(low)
    gu = t_mul(unit2, g_up).astype(low)
    gg_raise = t_mul(gate_adapter, gg).astype(low)
    gu_raise = t_mul(up_adapter, gu).astype(low)
    near, gg, gu, gg_raise, gu_raise, g_gate, g_up = tie(
        (down_sums,), (near, gg, gu, gg_raise, gu_raise, g_gate, g_up)
    )

    def slab_block(owner):
        return jnp.concatenate(
            [
                jnp.concatenate(
                    [
                        lax.dynamic_slice_in_dim(part, owner * size, size, 0)
                        for part in (raised, weight)
                        for size in (part.shape[0] // n_f,)
                    ],
                    axis=0,
                )
                for raised, weight in ((gg_raise, gg), (gu_raise, gu))
            ],
            axis=1,
        ).astype(wide)

    slab_sums = Scattering(ring, slab_block)
    slab_sums.advance()
    down_sums.advance()
    sums = [
        terms[k * CORES].astype(wide) + near[k].astype(wide) for k in range(n_seq // CORES)
    ]
    far = group.send(sums)
    e2 = (mul_t(g_gate, gate_full) + mul_t(g_up, up_full)).astype(low)
    e2, far, own_branch = tie((slab_sums, down_sums), (e2, far, sums[0]))
    for block in far:
        own_branch = own_branch + block.astype(wide)
    outputs = (mid + active * own_branch).astype(low).reshape(rows, length, width)

    slab_sums.advance()
    e2 = scatter_group(e2.reshape(n_seq, tokens, width), 5)
    g_down = down_sums.done().astype(low)
    down_rows = jnp.concatenate([g_down, mul_t(g_down, d_raise).astype(low)], axis=1)
    gd_raise = t_mul(d_lower, g_down).astype(low)
    e2, down_rows, gd_raise = tie((slab_sums,), (e2, down_rows, gd_raise))

    slab_sums.advance()
    down_rows = group.over(down_rows)
    g_mid = cot + r2 * e2 - mid * (r2 * r2 * r2 * jnp.mean(e2 * mid, axis=-1, keepdims=True))
    g_branch = (active * g_mid).astype(low)
    g_inner = mul_t(g_branch, o_raise).astype(low)
    g_attn = mul_t(jnp.concatenate([g_branch, g_inner], axis=1), side_o).astype(low)
    g_o = t_mul(attn_low, g_branch).astype(low)
    go_raise = t_mul(o_inner, g_branch).astype(low)
    o_pack = jnp.concatenate(
        [
            g_o.reshape(n_f, o_rows, width),
            go_raise.reshape(n_f, rank_rows, width),
            gd_raise.reshape(n_f, rank_rows, width),
        ],
        axis=1,
    )
    g_heads = to_heads(g_attn)
    dots = jnp.sum(g_heads.astype(wide) * attn, axis=-1, keepdims=True)
    scores = (
        jnp.einsum("sqd,skd->sqk", queries, keys, preferred_element_type=wide) * scale
    )
    probs = jnp.where(allowed, jnp.exp(scores - log_total), 0.0)
    d_probs = jnp.einsum("sqd,skd->sqk", g_heads, values, preferred_element_type=wide)
    d_scores = (probs * (d_probs - dots)).astype(low)
    d_query = jnp.einsum("sqk,skd->sqd", d_scores, keys, preferred_element_type=wide) * scale
    d_key = jnp.einsum("sqk,sqd->skd", d_scores, queries, preferred_element_type=wide) * scale
    d_value = jnp.einsum("sqk,sqd->skd", probs.astype(low), g_heads, preferred_element_type=wide)
    d_both = jnp.concatenate([d_key, d_value], axis=-1)
    d_both = d_both.astype(low).reshape(rows, n_seq, length, 2 * HD)
    d_both = scatter_group(d_both.transpose(1, 0, 2, 3).reshape(n_seq, tokens, 2 * HD), 8)
    d_both, d_query, o_pack, g_mid, down_rows = tie(
        (slab_sums,), (d_both, d_query, o_pack, g_mid, down_rows)
    )

    slab_sums.advance()
    down_rows = group.across(down_rows)
    g_q = rope(to_tokens(d_query).reshape(tokens, H, HD), cosine, -sine)
    g_q = g_q.reshape(tokens, hq).astype(low)
    g_k = rope(d_both[:, None, :HD], cosine, -sine).reshape(tokens, HD).astype(low)
    g_v = d_both[:, HD:].astype(low)
    gi_q = mul_t(g_q, q_raise).astype(low)
    gi_k = mul_t(g_k, k_raise).astype(low)
    gi_v = mul_t(g_v, v_raise).astype(low)
    g_lin = jnp.concatenate([g_q, g_k, g_v], axis=1)
    e1 = mul_t(jnp.concatenate([g_lin, gi_q, gi_k, gi_v], axis=1), qkv_side)
    input_grad = g_mid + r1 * e1 - resid * (
        r1 * r1 * r1 * jnp.mean(e1 * resid, axis=-1, keepdims=True)
    )
    input_grad = input_grad.astype(low).reshape(rows, length, width)
    g_qkv = t_mul(unit1, g_lin).astype(low)
    gr_qkv = jnp.concatenate(
        [t_mul(q_inner, g_q), t_mul(k_inner, g_k), t_mul(v_inner, g_v)], axis=1
    ).astype(low)
    qkv_pack = jnp.concatenate(
        [g_qkv.reshape(n_f, own_rows, lin), gr_qkv.reshape(n_f, rank_rows, lin)], axis=1
    )
    packs = scatter_whole((qkv_pack, o_pack), 6, n_seq)
    packs, down_rows = tie((slab_sums,), (packs, down_rows))
    qkv_pack, o_pack = (pack.astype(wide) for pack in packs)
    down_rows = group.laid(down_rows, 0, wide)
    grad_down_weight, grad_down_down = down_rows[:, :width], down_rows[:, width:]

    grad_o_weight = o_pack[:o_rows]
    grad_o_up = o_pack[o_rows : o_rows + rank_rows]
    grad_down_up = o_pack[o_rows + rank_rows :]
    grad_o_down = mul_t(packs[1][:o_rows], o_raise)
    unit_grad = qkv_pack[:own_rows]
    grad_lin = unit_grad * gain1
    grad_q_weight, grad_k_weight, grad_v_weight = (
        grad_lin[:, :hq],
        grad_lin[:, hq : hq + kv],
        grad_lin[:, hq + kv :],
    )
    grad_q_up, grad_k_up, grad_v_up = (
        qkv_pack[own_rows:, :hq],
        qkv_pack[own_rows:, hq : hq + kv],
        qkv_pack[own_rows:, hq + kv :],
    )
    grad_q_down = mul_t(grad_q_weight.astype(low), q_raise)
    grad_k_down = mul_t(grad_k_weight.astype(low), k_raise)
    grad_v_down = mul_t(grad_v_weight.astype(low), v_raise)
    own_lin = jnp.concatenate(
        [
            q_weight.astype(wide) + mul(q_down, q_raise),
            k_weight.astype(wide) + mul(k_down, k_raise),
            v_weight.astype(wide) + mul(v_down, v_raise),
        ],
        axis=1,
    )
    grad_attn_gain = jnp.sum(unit_grad * own_lin, axis=1)

    g_slab = slab_sums.done()
    unit_grad = g_slab[rank_rows:]
    own_full = [
        lax.dynamic_slice_in_dim(full, lax.axis_index("fsdp") * own_rows, own_rows, 0)
        for full in (gate_full, up_full)
    ]
    merged = jnp.concatenate(own_full, axis=1).astype(wide)
    weight_grad = (unit_grad * gain2).astype(low)
    mlp_small = Summing(
        jnp.concatenate(
            [
                mul_t(weight_grad[:, :slab], g_raise),
                mul_t(weight_grad[:, slab:], u_raise),
                jnp.broadcast_to(
                    jnp.sum(unit_grad * merged, axis=1, keepdims=True) / gain2, (own_rows, 128)
                ),
            ],
            axis=1,
        ),
        ("seq",),
    )
    slab_pieces = gather_group(g_slab.astype(low), 7, n_seq)
    mlp_small = mlp_small.done()
    grad_gate_down, grad_up_down = mlp_small[:, :rank], mlp_small[:, rank : 2 * rank]
    grad_mlp_gain = mlp_small[:, 2 * rank]
    grad_gate_weight, grad_up_weight, grad_gate_up, grad_up_up = place_columns(
        slab_pieces, gain2, n_f, n_seq, rank_rows, ff, slab
    )

    counted = counted.done()
    mean_confidence = counted[DEPTHS:] / counted[:DEPTHS]
    return (
        outputs,
        input_grad,
        grad_attn_gain,
        grad_q_weight,
        grad_k_weight,
        grad_v_weight,
        grad_o_weight,
        grad_q_down,
        grad_q_up,
        grad_k_down,
        grad_k_up,
        grad_v_down,
        grad_v_up,
        grad_o_down,
        grad_o_up,
        grad_mlp_gain,
        grad_gate_weight,
        grad_up_weight,
        grad_down_weight,
        grad_gate_down,
        grad_gate_up,
        grad_up_down,
        grad_up_up,
        grad_down_down,
        grad_down_up,
        counted[:DEPTHS].astype(jnp.int32),
        mean_confidence,
    )


def solution(mesh):
    tokens3 = P("fsdp", "seq", None)
    tokens2 = P("fsdp", "seq")
    vector, matrix = P("fsdp"), P("fsdp", None)
    in_specs = (tokens3,) * 2 + (tokens2,) * 3 + (vector,) + (matrix,) * 12 + (vector,) + (matrix,) * 9
    out_specs = (
        (tokens3,) * 2 + (vector,) + (matrix,) * 12 + (vector,) + (matrix,) * 9 + (P(), P())
    )
    return jax.shard_map(shards, mesh=mesh, in_specs=in_specs, out_specs=out_specs, check_vma=False)
```

time: 1430 us -> 837 us (0.59); the launches traced: 1410 us -> 832 us
  local copies, waits for them, and re-layouts: 500 us -> 109 us
  waiting for transfers between devices: 361 us -> 29.6 us
  Pallas kernels: 0 us -> 297 us
  starting transfers between devices: 141 us -> 48.9 us
  other arithmetic: 128 us -> 86.3 us
    ppermute x162 -> x51, waiting for transfers between devices: 361 us -> 29.6 us  [the longest x1 10.4 us: send(): lax.ppermute(sums[k].astype(low), 'seq', self.shift(k))]
    pallas_call x0 -> x9, Pallas kernels: none -> 297 us  [the longest x3 93.8 us: gather_group(): pl.pallas_call(body, out_shape=jax.ShapeDtypeStruct((n_seq,) + block.shap...]
    dynamic_update_slice x87 -> x24, local copies, waits for them, and re-layouts: 313 us -> 39.1 us  [the longest x8 15.7 us: keep_slab(): put(raises, block[rank_rows:, slab:], owner, 0)]
    ppermute x162 -> x51, starting transfers between devices: 141 us -> 48.9 us  [the longest x32 36.1 us: hop(): return lax.ppermute(block, 'fsdp', self.up if way > 0 else self.down)]
    reshape x10 -> x0, local copies, waits for them, and re-layouts: 43.1 us -> none  [the longest x4 25.1 us: cut_columns(): view = array.reshape(array.shape[0], n_f, n_seq, cut)]
    convert_element_type x14 -> x0, local copies, waits for them, and re-layouts: 33 us -> none  [the longest x12 27.5 us: laid(): piece.astype(dtype)]
    convert_element_type x50 -> x18, other arithmetic: 61.4 us -> 33.6 us  [the longest x1 9.16 us: shards(): hidden = (value * up.astype(wide)).astype(low)[:, :n_f * cut]]
    dot_general x12, matrix products: 65.8 us -> 47.9 us  [t_mul(): lax.dot_general(left, right, (((0,), (0,)), ((), ())), preferred_element_...]
  transfers between devices with their start and end apart: 162 -> 51, of which waited for: 70 -> 4; matrix products, arithmetic and copies ran while one was open for 54% -> 37% of each run, Pallas kernels for 0% -> 36%
where the time goes in v2:
time: 837 us; the launch traced here: 832 us
  Pallas kernels  297 us (35%)
  matrix products  221 us (26%)
  local copies, waits for them, and re-layouts  109 us (13%)
  other arithmetic  86.3 us (10%)
  starting transfers between devices  48.9 us (6%)
  between operations  40 us (5%)
  waiting for transfers between devices  29.6 us (4%)
    pallas_call x3, Pallas kernels, gather_group(): pl.pallas_call(body, out_shape=jax.ShapeDtypeStruct((n_seq,) + block.shap...  93.8 us
    dot_general x16, matrix products, mul_t(): lax.dot_general(left, right, (((1,), (1,)), ((), ())), preferred_element_...  75.3 us
    dot_general x15, matrix products, mul(): return jnp.dot(left, right, preferred_element_type=wide)  75.2 us
    pallas_call x1, Pallas kernels, gather_whole(): pl.pallas_call(body, out_shape=tuple((jax.ShapeDtypeStruct((n_f,) + b.sha...  69.4 us
    pallas_call x1, Pallas kernels, scatter_whole(): pl.pallas_call(body, out_shape=tuple((jax.ShapeDtypeStruct(pack.shape[1:]...  67.8 us
    pallas_call x2, Pallas kernels, scatter_group(): pl.pallas_call(body, out_shape=jax.ShapeDtypeStruct((rows, columns), wide...  56.7 us
    dot_general x12, matrix products, t_mul(): lax.dot_general(left, right, (((0,), (0,)), ((), ())), preferred_element_...  47.9 us
    ppermute x32, starting transfers between devices, hop(): return lax.ppermute(block, 'fsdp', self.up if way > 0 else self.down)  36.1 us
  transfers between devices with their start and end apart: 51, of which 4 were waited for; matrix products, arithmetic and copies ran while one was open for 37% of the time, Pallas kernels for 36%

profile of v2, /device:TPU:0, one launch (start us, length us, event | category | flops | bytes accessed | tf_op | source)
XLA Modules:
  0.0 831.8 jit_solution(4510954401866676473)
XLA Ops:
  7.4 3.0 collective-permute-start
  26.6 2.4 broadcast.175.clone
  29.8 2.3 broadcast.175.clone.1
  32.9 2.5 broadcast_in_dim.169
  78.8 2.6 fusion.43
  81.4 69.4 %shard_map.494 = (bf16[8,144,3072]{2,1,0:T(8,128)(2,1)}, bf16[8,32,4096]{2,1,0:T(8,128)(2,1)}, bf16[8,128,1536]{2,1,0:T(8,128)(2,1)}) custom-call(bf16[144,3072]{1,0:T(8,128)(2,1)} %constant_dynamic-update-slice_fusion.refs_0_, bf16[32,4096]{1,0:T(8,128)(2,1)} %copy-done.102, bf16[128,1536]{1,0:T(8,128)(2,1)} %maximum_maximum_fusion.1.refs_2_), custom_call_target="tpu_custom_call" | custom-call | tf_op jit(solution)/shard_map/pallas_call | solution.py:205
  152.5 6.2 fusion.176
  163.2 2.1 collective-permute-start.6
  165.3 3.2 reshape.395
  173.0 2.2 bitcast_dynamic-update-slice_fusion.19
  175.5 2.4 bitcast_dynamic-update-slice_fusion.6
  179.8 2.3 bitcast_dynamic-update-slice_fusion.18
  188.3 17.3 %shard_map.495 = bf16[4,512,512]{2,1,0:T(8,128)(2,1)} custom-call(bf16[512,512]{1,0:T(8,128)(2,1)} %pad_maximum_fusion.9.x), custom_call_target="tpu_custom_call" | custom-call | tf_op jit(solution)/shard_map/pallas_call | solution.py:274
  210.2 2.7 fusion.28
  212.8 3.4 fusion.21
  216.3 5.3 fusion.177
  229.2 2.3 bitcast_dynamic-update-slice_fusion.15
  232.7 2.4 bitcast_dynamic-update-slice_fusion.14
  247.6 2.3 bitcast_dynamic-update-slice_fusion.11
  250.0 9.0 %collective-permute-done.12 = bf16[176,1792]{1,0:T(8,128)(2,1)S(1)} collective-permute-done((bf16[176,1792]{1,0:T(8,128)(2,1)S(1)}, bf16[176,1792]{1,0:T(8,128)(2,1)S(1)}, u32[]{:S(2)}, u32[]{:S(2)}) %collective-permute-start.12) | collective-permute-done | bytes 630816 | tf_op jit(solution)/shard_map/ppermute | solution.py:506
  260.7 2.2 bitcast_dynamic-update-slice_fusion.10
  263.0 37.1 %shard_map.496 = bf16[4,512,1152]{2,1,0:T(8,128)(2,1)} custom-call(bf16[512,1152]{1,0:T(8,128)(2,1)} %multiply_convert_fusion.2.x), custom_call_target="tpu_custom_call" | custom-call | tf_op jit(solution)/shard_map/pallas_call | solution.py:274
  301.5 4.1 fusion.18
  305.6 5.1 fusion.19
  310.7 18.0 %fusion.178 = (f32[2048,1792]{0,1:T(8,128)}, bf16[2048,1792]{0,1:T(8,128)(2,1)}) fusion(bf16[2048,1152]{1,0:T(8,128)(2,1)} %bitcast.317, bf16[1152,1792]{1,0:T(8,128)(2,1)S(1)} %fusion.18), kind=kOutput, calls=%fused_computation.401 | convolution fusion | flops 8463056896 | bytes 30867456 | tf_op jit(solution)/shard_map/dot_general | solution.py:21
  328.7 14.1 %convolution_convert_fusion.1 = bf16[2048,1792]{0,1:T(8,128)(2,1)} fusion(bf16[2048,1152]{1,0:T(8,128)(2,1)} %bitcast.318, bf16[1152,1792]{1,0:T(8,128)(2,1)S(1)} %fusion.19), kind=kOutput, calls=%fused_computation.40 | convolution fusion | flops 8459386880 | bytes 16187392 | tf_op jit(solution)/shard_map/dot_general | solution.py:21
  347.2 11.1 %multiply_add_fusion = f32[2048,1792]{0,1:T(8,128)} fusion(bf16[2048,1792]{0,1:T(8,128)(2,1)} %get-tuple-element.242), kind=kLoop, calls=%fused_computation.7 | loop fusion | flops 18350080 | bytes 22020096 | tf_op jit(solution)/shard_map/add | solution.py:758
  361.9 2.1 copy-done.104
  364.0 9.2 %fusion.14 = bf16[2048,1728]{0,1:T(8,128)(2,1)S(1)} fusion(f32[2048,1792]{0,1:T(8,128)S(1)} %bitcast.301, f32[2048,1792]{0,1:T(8,128)} %multiply_add_fusion, bf16[2048,1792]{0,1:T(8,128)(2,1)} %convolution_convert_fusion.1), kind=kLoop, calls=%fused_computation.23 | loop fusion | flops 24772608 | bytes 42467328 | tf_op jit(solution)/shard_map/convert_element_type | solution.py:984
  373.2 2.5 bitcast_dynamic-update-slice_fusion.4
  375.8 3.7 bitcast_dynamic-update-slice_fusion.3
  385.2 9.5 %convolution_convert_fusion.6 = bf16[1728,1152]{1,0:T(8,128)(2,1)S(1)} fusion(bf16[2048,1728]{0,1:T(8,128)(2,1)S(1)} %fusion.14, bf16[2048,1152]{1,0:T(8,128)(2,1)S(1)} %copy-done.105), kind=kOutput, calls=%fused_computation.45 | convolution fusion | flops 8155717632 | bytes 15777792 | tf_op jit(solution)/shard_map/dot_general | solution.py:29
  400.3 6.0 fusion.20
  406.3 25.1 %fusion.8 = (bf16[2048,1792]{0,1:T(8,128)(2,1)}, bf16[2048,1792]{0,1:T(8,128)(2,1)}) fusion(bf16[2048,1792]{0,1:T(8,128)(2,1)S(1)} %bitcast.314, bf16[2048,1792]{0,1:T(8,128)(2,1)} %convolution_convert_fusion.1, bf16[2048,1152]{1,0:T(8,128)(2,1)} %copy-done.104, bf16[1728,1152]{1,0:T(8,128)(2,1)} %fusion.20), kind=kOutput, calls=%fused_computation.16 | convolution fusion | flops 8547467264 | bytes 38060032 | tf_op jit(solution)/shard_map/dot_general | solution.py:25
  435.4 12.2 %convolution_convert_fusion = bf16[2048,1152]{1,0:T(8,128)(2,1)S(1)} fusion(bf16[2048,1728]{0,1:T(8,128)(2,1)S(1)} %bitcast.316, bf16[1728,1152]{1,0:T(8,128)(2,1)} %fusion.20), kind=kOutput, calls=%fused_computation.39 | convolution fusion | flops 8156086272 | bytes 15777792 | tf_op jit(solution)/shard_map/dot_general | solution.py:21
  451.6 13.1 %convolution_convert_fusion.5 = bf16[1152,1792]{1,0:T(8,128)(2,1)S(1)} fusion(bf16[2048,1152]{1,0:T(8,128)(2,1)} %bitcast.319, bf16[2048,1792]{0,1:T(8,128)(2,1)} %get-tuple-element.260), kind=kOutput, calls=%fused_computation.44 | convolution fusion | flops 8457781248 | bytes 16187392 | tf_op jit(solution)/shard_map/dot_general | solution.py:29
  464.7 12.6 %convolution_convert_fusion.4 = bf16[1152,1792]{1,0:T(8,128)(2,1)S(1)} fusion(bf16[2048,1152]{1,0:T(8,128)(2,1)S(1)} %bitcast.322, bf16[2048,1792]{0,1:T(8,128)(2,1)} %get-tuple-element.261), kind=kOutput, calls=%fused_computation.43 | convolution fusion | flops 8457781248 | bytes 16187392 | tf_op jit(solution)/shard_map/dot_general | solution.py:29
  477.3 2.5 convolution_convert_fusion.11
  480.3 2.5 convolution_convert_fusion.10
  493.3 14.3 %fusion.180 = f32[2048,1152]{1,0:T(8,128)} fusion(bf16[2048,1792]{0,1:T(8,128)(2,1)} %get-tuple-element.261, bf16[1152,1792]{1,0:T(8,128)(2,1)S(1)} %copy-done.27), kind=kOutput, calls=%fused_computation.403 | convolution fusion | flops 8455716864 | bytes 20905984 | tf_op jit(solution)/shard_map/dot_general | solution.py:25
  511.4 14.9 %add_convert_fusion = bf16[2048,1152]{1,0:T(8,128)(2,1)} fusion(f32[2048,1152]{1,0:T(8,128)} %fusion.180, bf16[2048,1792]{0,1:T(8,128)(2,1)} %get-tuple-element.260, bf16[1152,1792]{1,0:T(8,128)(2,1)S(1)} %copy-done.25), kind=kOutput, calls=%fused_computation.30 | convolution fusion | flops 8460435456 | bytes 25624576 | tf_op jit(solution)/shard_map/dot_general | solution.py:25
  526.3 10.4 %collective-permute-done.39 = bf16[512,1152]{1,0:T(8,128)(2,1)S(1)} collective-permute-done((bf16[512,1152]{1,0:T(8,128)(2,1)S(1)}, bf16[512,1152]{1,0:T(8,128)(2,1)S(1)}, u32[]{:S(2)}, u32[]{:S(2)}) %collective-permute-start.39) | collective-permute-done | bytes 1179680 | tf_op jit(solution)/shard_map/ppermute | solution.py:638
  541.7 34.0 %shard_map.497 = f32[512,1152]{1,0:T(8,128)} custom-call(bf16[4,512,1152]{2,1,0:T(8,128)(2,1)} %bitcast.323), custom_call_target="tpu_custom_call" | custom-call | tf_op jit(solution)/shard_map/pallas_call | solution.py:343
  580.2 2.6 add_convert_fusion.4
  584.5 2.7 add_convert_fusion.3
  587.6 2.7 multiply_convert_fusion.1
  590.9 2.8 fusion.55
  598.0 5.3 fusion.58
  603.4 4.2 multiply_convert_fusion
  609.9 2.1 pad_maximum_fusion
  614.9 22.6 %shard_map.498 = f32[512,512]{1,0:T(8,128)} custom-call(bf16[4,512,512]{2,1,0:T(8,128)(2,1)} %bitcast.308), custom_call_target="tpu_custom_call" | custom-call | tf_op jit(solution)/shard_map/pallas_call | solution.py:343
  637.5 3.9 convolution_multiply_fusion
  644.4 2.7 convolution_convert_fusion.15
  658.3 6.7 fusion.46
  665.1 2.8 add_convert_fusion.2
  669.3 2.7 add_convert_fusion.1
  675.4 2.6 pad.45.refs_1_
  678.2 2.2 maximum_maximum_fusion.refs_0_
  680.4 67.8 %shard_map.499 = (bf16[176,1536]{1,0:T(8,128)(2,1)}, bf16[192,1536]{1,0:T(8,128)(2,1)}) custom-call(bf16[8,176,1536]{2,1,0:T(8,128)(2,1)} %maximum_maximum_fusion.refs_0_, bf16[8,192,1536]{2,1,0:T(8,128)(2,1)} %pad.45.refs_1_), custom_call_target="tpu_custom_call" | custom-call | tf_op jit(solution)/shard_map/pallas_call | solution.py:475
  752.6 3.3 fusion.168
  767.5 2.2 slice.441
  770.7 39.4 %shard_map.500.x = bf16[4,176,3584]{2,1,0:T(8,128)(2,1)} custom-call(bf16[176,3584]{1,0:T(8,128)(2,1)} %get-tuple-element.307.x), custom_call_target="tpu_custom_call" | custom-call | tf_op jit(solution)/shard_map/pallas_call | solution.py:274
  810.1 8.4 %shard_map.501 = (f32[144,6912]{1,0:T(8,128)}, f32[144,6912]{1,0:T(8,128)}, f32[32,6912]{1,0:T(8,128)}, f32[32,6912]{1,0:T(8,128)}) custom-call(f32[144,1]{1,0:T(8,128)} %copy-done.4, bf16[4,176,3584]{2,1,0:T(8,128)(2,1)} %shard_map.500.x), custom_call_target="tpu_custom_call" | custom-call | tf_op jit(solution)/shard_map/pallas_call | solution.py:740
  821.2 9.0 %collective-permute-done.50 = f32[144,640]{1,0:T(8,128)S(1)} collective-permute-done((f32[144,640]{1,0:T(8,128)S(1)}, f32[144,640]{1,0:T(8,128)S(1)}, u32[]{:S(2)}, u32[]{:S(2)}) %collective-permute-start.50) | collective-permute-done | bytes 368672 | tf_op jit(solution)/shard_map/ppermute | solution.py:667
  (622 shorter events, 181.9 us)
Async XLA Ops:
  1.5 40.1 %copy-start.135 = (f32[144]{0:T(256)}, f32[144]{0:T(256)S(1)}, u32[]{:S(2)}) copy-start(f32[144]{0:T(256)S(1)} %convert_element_type.469) | copy-start | bytes 1732
  7.4 145.0 %collective-permute-start = (bf16[176,3584]{1,0:T(8,128)(2,1)S(1)}, bf16[176,3584]{1,0:T(8,128)(2,1)}, u32[]{:S(2)}, u32[]{:S(2)}) collective-permute-start(bf16[176,3584]{1,0:T(8,128)(2,1)S(1)} %shard_map.493), channel_id=1, source_target_pairs={{0,1},{1,3},{3,5},{5,7},{7,6},{6,4},{4,2},{2,0},{8,9},{9,11},{11,1... | collective-permute-start | bytes 3784712 | tf_op jit(solution)/shard_map/ppermute | solution.py:506
  10.4 142.1 %collective-permute-start.1 = (bf16[176,3584]{1,0:T(8,128)(2,1)S(1)}, bf16[176,3584]{1,0:T(8,128)(2,1)}, u32[]{:S(2)}, u32[]{:S(2)}) collective-permute-start(bf16[176,3584]{1,0:T(8,128)(2,1)S(1)} %shard_map.493), channel_id=1, source_target_pairs={{1,0},{3,1},{5,3},{7,5},{6,7},{4,6},{2,4},{0,2},{9,8},{11,9},{13,1... | collective-permute-start | bytes 3784712 | tf_op jit(solution)/shard_map/ppermute | solution.py:506
  13.2 139.3 %collective-permute-start.2 = (bf16[216,1408]{1,0:T(8,128)(2,1)}, bf16[216,1408]{1,0:T(8,128)(2,1)}, u32[]{:S(2)}, u32[]{:S(2)}) collective-permute-start(bf16[216,1408]{1,0:T(8,128)(2,1)} %pad_maximum_fusion.6), channel_id=1, source_target_pairs={{0,1},{1,3},{3,5},{5,7},{7,6},{6,4},{4,2},{2,0},{8,9},{9,11},{11,1... | collective-permute-start | bytes 1824776 | tf_op jit(solution)/shard_map/ppermute | solution.py:506
  15.1 137.4 %collective-permute-start.3 = (bf16[216,1408]{1,0:T(8,128)(2,1)}, bf16[216,1408]{1,0:T(8,128)(2,1)}, u32[]{:S(2)}, u32[]{:S(2)}) collective-permute-start(bf16[216,1408]{1,0:T(8,128)(2,1)} %pad_maximum_fusion.6), channel_id=1, source_target_pairs={{1,0},{3,1},{5,3},{7,5},{6,7},{4,6},{2,4},{0,2},{9,8},{11,9},{13,1... | collective-permute-start | bytes 1824776 | tf_op jit(solution)/shard_map/ppermute | solution.py:506
  15.4 135.4 %collective-permute-start.4 = (bf16[2,256]{1,0:T(2,128)(2,1)S(1)}, bf16[2,256]{1,0:T(2,128)(2,1)}, u32[]{:S(2)}, u32[]{:S(2)}) collective-permute-start(bf16[2,256]{1,0:T(2,128)(2,1)S(1)} %convert_element_type.487), channel_id=1, source_target_pairs={{0,16},{8,24},{16,0},{24,8},{1,17},{9,25},{17,1},{25,9},{2,18},{10... | collective-permute-start | bytes 3080 | tf_op jit(solution)/shard_map/ppermute | solution.py:622
  25.7 199.6 %copy-start.133 = (f32[512]{0:T(512)}, f32[512]{0:T(512)S(1)}, u32[]{:S(2)}) copy-start(f32[512]{0:T(512)S(1)} %compare_convert_fusion) | copy-start | bytes 6148
  44.6 123.9 %copy-start.20 = (f32[512,128]{1,0:T(8,128)}, f32[512,128]{1,0:T(8,128)S(1)}, u32[]{:S(2)}) copy-start(f32[512,128]{1,0:T(8,128)S(1)} %get-tuple-element.179) | copy-start | bytes 786436
  44.6 142.9 %copy-start.22 = (f32[512,128]{1,0:T(8,128)}, f32[512,128]{1,0:T(8,128)S(1)}, u32[]{:S(2)}) copy-start(f32[512,128]{1,0:T(8,128)S(1)} %get-tuple-element.180) | copy-start | bytes 786436
  74.2 142.0 %copy-start.126 = (s32[1,2,4,256]{3,1,2,0:T(2,128)}, s32[1,2,4,256]{3,1,2,0:T(2,128)S(1)}, u32[]{:S(2)}) copy-start(s32[1,2,4,256]{3,1,2,0:T(2,128)S(1)} %copy.127) | copy-start | bytes 24580
  150.8 89.9 %collective-permute-start.11 = (bf16[512,1152]{1,0:T(8,128)(2,1)}, bf16[512,1152]{1,0:T(8,128)(2,1)}, u32[]{:S(2)}, u32[]{:S(2)}) collective-permute-start(bf16[512,1152]{1,0:T(8,128)(2,1)} %fusion.43), channel_id=1, source_target_pairs={{0,16},{8,24},{16,0},{24,8},{1,17},{9,25},{17,1},{25,9},{2,18},{10... | collective-permute-start | bytes 3538952 | tf_op jit(solution)/shard_map/ppermute | solution.py:622
  162.9 42.7 %collective-permute-start.5 = (bf16[176,3584]{1,0:T(8,128)(2,1)}, bf16[176,3584]{1,0:T(8,128)(2,1)}, u32[]{:S(2)}, u32[]{:S(2)}) collective-permute-start(bf16[176,3584]{1,0:T(8,128)(2,1)} %collective-permute-done), channel_id=1, source_target_pairs={{0,1},{1,3},{3,5},{5,7},{7,6},{6,4},{4,2},{2,0},{8,9},{9,11},{11,1... | collective-permute-start | bytes 3784712 | tf_op jit(solution)/shard_map/ppermute | solution.py:506
  163.2 42.4 %collective-permute-start.6 = (bf16[176,3584]{1,0:T(8,128)(2,1)}, bf16[176,3584]{1,0:T(8,128)(2,1)}, u32[]{:S(2)}, u32[]{:S(2)}) collective-permute-start(bf16[176,3584]{1,0:T(8,128)(2,1)} %collective-permute-done.1), channel_id=1, source_target_pairs={{1,0},{3,1},{5,3},{7,5},{6,7},{4,6},{2,4},{0,2},{9,8},{11,9},{13,1... | collective-permute-start | bytes 3784712 | tf_op jit(solution)/shard_map/ppermute | solution.py:506
  170.8 34.8 %collective-permute-start.7 = (bf16[2,256]{1,0:T(2,128)(2,1)S(1)}, bf16[2,256]{1,0:T(2,128)(2,1)S(1)}, u32[]{:S(2)}, u32[]{:S(2)}) collective-permute-start(bf16[2,256]{1,0:T(2,128)(2,1)S(1)} %convert_element_type.487), channel_id=1, source_target_pairs={{0,8},{8,0},{16,24},{24,16},{1,9},{9,1},{17,25},{25,17},{2,10},{10... | collective-permute-start | bytes 3080 | tf_op jit(solution)/shard_map/ppermute | solution.py:628
  170.9 34.7 %collective-permute-start.8 = (bf16[2,256]{1,0:T(2,128)(2,1)}, bf16[2,256]{1,0:T(2,128)(2,1)S(1)}, u32[]{:S(2)}, u32[]{:S(2)}) collective-permute-start(bf16[2,256]{1,0:T(2,128)(2,1)} %collective-permute-done.4), channel_id=1, source_target_pairs={{0,8},{8,0},{16,24},{24,16},{1,9},{9,1},{17,25},{25,17},{2,10},{10... | collective-permute-start | bytes 3080 | tf_op jit(solution)/shard_map/ppermute | solution.py:628
  187.5 47.5 %copy-start.48 = (bf16[512,768]{1,0:T(8,128)(2,1)}, bf16[512,768]{1,0:T(8,128)(2,1)S(1)}, u32[]{:S(2)}) copy-start(bf16[512,768]{1,0:T(8,128)(2,1)S(1)} %slice.406) | copy-start | bytes 2359300
  205.6 35.1 %collective-permute-start.9 = (bf16[176,3584]{1,0:T(8,128)(2,1)}, bf16[176,3584]{1,0:T(8,128)(2,1)}, u32[]{:S(2)}, u32[]{:S(2)}) collective-permute-start(bf16[176,3584]{1,0:T(8,128)(2,1)} %collective-permute-done.5), channel_id=1, source_target_pairs={{0,1},{1,3},{3,5},{5,7},{7,6},{6,4},{4,2},{2,0},{8,9},{9,11},{11,1... | collective-permute-start | bytes 3784712 | tf_op jit(solution)/shard_map/ppermute | solution.py:506
  205.9 34.8 %collective-permute-start.10 = (bf16[176,3584]{1,0:T(8,128)(2,1)}, bf16[176,3584]{1,0:T(8,128)(2,1)}, u32[]{:S(2)}, u32[]{:S(2)}) collective-permute-start(bf16[176,3584]{1,0:T(8,128)(2,1)} %collective-permute-done.6), channel_id=1, source_target_pairs={{1,0},{3,1},{5,3},{7,5},{6,7},{4,6},{2,4},{0,2},{9,8},{11,9},{13,1... | collective-permute-start | bytes 3784712 | tf_op jit(solution)/shard_map/ppermute | solution.py:506
  241.9 17.2 %collective-permute-start.12 = (bf16[176,1792]{1,0:T(8,128)(2,1)S(1)}, bf16[176,1792]{1,0:T(8,128)(2,1)S(1)}, u32[]{:S(2)}, u32[]{:S(2)}) collective-permute-start(bf16[176,1792]{1,0:T(8,128)(2,1)S(1)} %slice.331), channel_id=1, source_target_pairs={{0,1},{1,3},{3,5},{5,7},{7,6},{6,4},{4,2},{2,0},{8,9},{9,11},{11,1... | collective-permute-start | bytes 1892360 | tf_op jit(solution)/shard_map/ppermute | solution.py:506
  243.2 56.9 %collective-permute-start.13 = (bf16[176,1792]{1,0:T(8,128)(2,1)S(1)}, bf16[176,1792]{1,0:T(8,128)(2,1)S(1)}, u32[]{:S(2)}, u32[]{:S(2)}) collective-permute-start(bf16[176,1792]{1,0:T(8,128)(2,1)S(1)} %slice.332), channel_id=1, source_target_pairs={{1,0},{3,1},{5,3},{7,5},{6,7},{4,6},{2,4},{0,2},{9,8},{11,9},{13,1... | collective-permute-start | bytes 1892360 | tf_op jit(solution)/shard_map/ppermute | solution.py:506
  245.1 4.7 collective-permute-start.16
  245.1 55.1 %collective-permute-start.17 = (bf16[512,1152]{1,0:T(8,128)(2,1)S(1)}, bf16[512,1152]{1,0:T(8,128)(2,1)S(1)}, u32[]{:S(2)}, u32[]{:S(2)}) collective-permute-start(bf16[512,1152]{1,0:T(8,128)(2,1)S(1)} %copy-done.28), channel_id=1, source_target_pairs={{0,8},{8,0},{16,24},{24,16},{1,9},{9,1},{17,25},{25,17},{2,10},{10... | collective-permute-start | bytes 3538952 | tf_op jit(solution)/shard_map/ppermute | solution.py:628
  245.6 54.6 %collective-permute-start.18 = (bf16[512,1152]{1,0:T(8,128)(2,1)}, bf16[512,1152]{1,0:T(8,128)(2,1)S(1)}, u32[]{:S(2)}, u32[]{:S(2)}) collective-permute-start(bf16[512,1152]{1,0:T(8,128)(2,1)} %collective-permute-done.11), channel_id=1, source_target_pairs={{0,8},{8,0},{16,24},{24,16},{1,9},{9,1},{17,25},{25,17},{2,10},{10... | collective-permute-start | bytes 3538952 | tf_op jit(solution)/shard_map/ppermute | solution.py:628
  249.8 50.4 %collective-permute-start.14 = (bf16[216,1408]{1,0:T(8,128)(2,1)}, bf16[216,1408]{1,0:T(8,128)(2,1)}, u32[]{:S(2)}, u32[]{:S(2)}) collective-permute-start(bf16[216,1408]{1,0:T(8,128)(2,1)} %collective-permute-done.2), channel_id=1, source_target_pairs={{0,1},{1,3},{3,5},{5,7},{7,6},{6,4},{4,2},{2,0},{8,9},{9,11},{11,1... | collective-permute-start | bytes 1824776 | tf_op jit(solution)/shard_map/ppermute | solution.py:506
  259.0 41.2 %collective-permute-start.15 = (bf16[216,1408]{1,0:T(8,128)(2,1)}, bf16[216,1408]{1,0:T(8,128)(2,1)}, u32[]{:S(2)}, u32[]{:S(2)}) collective-permute-start(bf16[216,1408]{1,0:T(8,128)(2,1)} %collective-permute-done.3), channel_id=1, source_target_pairs={{1,0},{3,1},{5,3},{7,5},{6,7},{4,6},{2,4},{0,2},{9,8},{11,9},{13,1... | collective-permute-start | bytes 1824776 | tf_op jit(solution)/shard_map/ppermute | solution.py:506
  305.6 38.1 %copy-start.24 = (bf16[1152,1792]{1,0:T(8,128)(2,1)}, bf16[1152,1792]{1,0:T(8,128)(2,1)S(1)}, u32[]{:S(2)}) copy-start(bf16[1152,1792]{1,0:T(8,128)(2,1)S(1)} %fusion.18) | copy-start | bytes 12386308
  344.5 34.9 %collective-permute-start.19 = (bf16[216,1408]{1,0:T(8,128)(2,1)}, bf16[216,1408]{1,0:T(8,128)(2,1)}, u32[]{:S(2)}, u32[]{:S(2)}) collective-permute-start(bf16[216,1408]{1,0:T(8,128)(2,1)} %collective-permute-done.14), channel_id=1, source_target_pairs={{0,1},{1,3},{3,5},{5,7},{7,6},{6,4},{4,2},{2,0},{8,9},{9,11},{11,1... | collective-permute-start | bytes 1824776 | tf_op jit(solution)/shard_map/ppermute | solution.py:506
  345.0 34.4 %collective-permute-start.20 = (bf16[216,1408]{1,0:T(8,128)(2,1)}, bf16[216,1408]{1,0:T(8,128)(2,1)S(1)}, u32[]{:S(2)}, u32[]{:S(2)}) collective-permute-start(bf16[216,1408]{1,0:T(8,128)(2,1)} %collective-permute-done.15), channel_id=1, source_target_pairs={{1,0},{3,1},{5,3},{7,5},{6,7},{4,6},{2,4},{0,2},{9,8},{11,9},{13,1... | collective-permute-start | bytes 1824776 | tf_op jit(solution)/shard_map/ppermute | solution.py:506
  346.7 32.7 %collective-permute-start.21 = (f32[6]{0:T(128)S(1)}, f32[6]{0:T(128)S(1)}, u32[]{:S(2)}, u32[]{:S(2)}) collective-permute-start(f32[6]{0:T(128)S(1)} %add.664), channel_id=1, source_target_pairs={{0,16},{8,24},{16,0},{24,8},{1,17},{9,25},{17,1},{25,9},{2,18},{10... | collective-permute-start | bytes 80 | tf_op jit(solution)/shard_map/ppermute | solution.py:667
  380.6 15.1 %collective-permute-start.22 = (bf16[216,640]{1,0:T(8,128)(2,1)S(1)}, bf16[216,640]{1,0:T(8,128)(2,1)S(1)}, u32[]{:S(2)}, u32[]{:S(2)}) collective-permute-start(bf16[216,640]{1,0:T(8,128)(2,1)S(1)} %slice.347), channel_id=1, source_target_pairs={{0,1},{1,3},{3,5},{5,7},{7,6},{6,4},{4,2},{2,0},{8,9},{9,11},{11,1... | collective-permute-start | bytes 829448 | tf_op jit(solution)/shard_map/ppermute | solution.py:506
  381.2 14.5 %collective-permute-start.23 = (bf16[216,768]{1,0:T(8,128)(2,1)S(1)}, bf16[216,768]{1,0:T(8,128)(2,1)S(1)}, u32[]{:S(2)}, u32[]{:S(2)}) collective-permute-start(bf16[216,768]{1,0:T(8,128)(2,1)S(1)} %slice.348), channel_id=1, source_target_pairs={{1,0},{3,1},{5,3},{7,5},{6,7},{4,6},{2,4},{0,2},{9,8},{11,9},{13,1... | collective-permute-start | bytes 995336 | tf_op jit(solution)/shard_map/ppermute | solution.py:506
  382.8 12.9 %collective-permute-start.24 = (f32[6]{0:T(128)S(1)}, f32[6]{0:T(128)S(1)}, u32[]{:S(2)}, u32[]{:S(2)}) collective-permute-start(f32[6]{0:T(128)S(1)} %add.665), channel_id=1, source_target_pairs={{0,1},{1,0},{2,3},{3,2},{4,5},{5,4},{6,7},{7,6},{8,9},{9,8},{10,11... | collective-permute-start | bytes 80 | tf_op jit(solution)/shard_map/ppermute | solution.py:667
  394.7 96.0 %copy-start.38 = (bf16[1728,1152]{1,0:T(8,128)(2,1)}, bf16[1728,1152]{1,0:T(8,128)(2,1)S(1)}, u32[]{:S(2)}) copy-start(bf16[1728,1152]{1,0:T(8,128)(2,1)S(1)} %convolution_convert_fusion.6) | copy-start | bytes 11943940
  395.8 35.6 %collective-permute-start.25 = (bf16[216,512]{1,0:T(8,128)(2,1)S(1)}, bf16[216,512]{1,0:T(8,128)(2,1)S(1)}, u32[]{:S(2)}, u32[]{:S(2)}) collective-permute-start(bf16[216,512]{1,0:T(8,128)(2,1)S(1)} %constant_dynamic-slice_fusion), channel_id=1, source_target_pairs={{0,1},{1,3},{3,5},{5,7},{7,6},{6,4},{4,2},{2,0},{8,9},{9,11},{11,1... | collective-permute-start | bytes 663560 | tf_op jit(solution)/shard_map/ppermute | solution.py:506
  397.4 34.0 %collective-permute-start.26 = (bf16[216,640]{1,0:T(8,128)(2,1)S(1)}, bf16[216,640]{1,0:T(8,128)(2,1)S(1)}, u32[]{:S(2)}, u32[]{:S(2)}) collective-permute-start(bf16[216,640]{1,0:T(8,128)(2,1)S(1)} %dynamic-slice.1), channel_id=1, source_target_pairs={{1,0},{3,1},{5,3},{7,5},{6,7},{4,6},{2,4},{0,2},{9,8},{11,9},{13,1... | collective-permute-start | bytes 829448 | tf_op jit(solution)/shard_map/ppermute | solution.py:506
  398.4 33.0 %collective-permute-start.27 = (f32[6]{0:T(128)S(1)}, f32[6]{0:T(128)S(1)}, u32[]{:S(2)}, u32[]{:S(2)}) collective-permute-start(f32[6]{0:T(128)S(1)} %add.674), channel_id=1, source_target_pairs={{0,2},{1,3},{2,0},{3,1},{4,6},{5,7},{6,4},{7,5},{8,10},{9,11},{10,... | collective-permute-start | bytes 80 | tf_op jit(solution)/shard_map/ppermute | solution.py:667
  431.6 16.0 %collective-permute-start.28 = (bf16[216,1152]{1,0:T(8,128)(2,1)S(1)}, bf16[216,1152]{1,0:T(8,128)(2,1)S(1)}, u32[]{:S(2)}, u32[]{:S(2)}) collective-permute-start(bf16[216,1152]{1,0:T(8,128)(2,1)S(1)} %get-tuple-element.340), channel_id=1, source_target_pairs={{0,1},{1,3},{3,5},{5,7},{7,6},{6,4},{4,2},{2,0},{8,9},{9,11},{11,1... | collective-permute-start | bytes 1493000 | tf_op jit(solution)/shard_map/ppermute | solution.py:506
  433.7 13.9 %collective-permute-start.29 = (bf16[216,1152]{1,0:T(8,128)(2,1)S(1)}, bf16[216,1152]{1,0:T(8,128)(2,1)S(1)}, u32[]{:S(2)}, u32[]{:S(2)}) collective-permute-start(bf16[216,1152]{1,0:T(8,128)(2,1)S(1)} %get-tuple-element.339), channel_id=1, source_target_pairs={{1,0},{3,1},{5,3},{7,5},{6,7},{4,6},{2,4},{0,2},{9,8},{11,9},{13,1... | collective-permute-start | bytes 1493000 | tf_op jit(solution)/shard_map/ppermute | solution.py:506
  433.7 13.9 %collective-permute-start.30 = (f32[6]{0:T(128)S(1)}, f32[6]{0:T(128)S(1)}, u32[]{:S(2)}, u32[]{:S(2)}) collective-permute-start(f32[6]{0:T(128)S(1)} %add.678), channel_id=1, source_target_pairs={{0,4},{1,5},{2,6},{3,7},{4,0},{5,1},{6,2},{7,3},{8,12},{9,13},{10,... | collective-permute-start | bytes 80 | tf_op jit(solution)/shard_map/ppermute | solution.py:667
  448.6 34.1 %collective-permute-start.31 = (bf16[216,1152]{1,0:T(8,128)(2,1)}, bf16[216,1152]{1,0:T(8,128)(2,1)S(1)}, u32[]{:S(2)}, u32[]{:S(2)}) collective-permute-start(bf16[216,1152]{1,0:T(8,128)(2,1)} %get-tuple-element.338), channel_id=1, source_target_pairs={{0,1},{1,3},{3,5},{5,7},{7,6},{6,4},{4,2},{2,0},{8,9},{9,11},{11,1... | collective-permute-start | bytes 1493000 | tf_op jit(solution)/shard_map/ppermute | solution.py:506
  450.5 32.2 %collective-permute-start.32 = (bf16[216,1152]{1,0:T(8,128)(2,1)S(1)}, bf16[216,1152]{1,0:T(8,128)(2,1)S(1)}, u32[]{:S(2)}, u32[]{:S(2)}) collective-permute-start(bf16[216,1152]{1,0:T(8,128)(2,1)S(1)} %get-tuple-element.337), channel_id=1, source_target_pairs={{1,0},{3,1},{5,3},{7,5},{6,7},{4,6},{2,4},{0,2},{9,8},{11,9},{13,1... | collective-permute-start | bytes 1493000 | tf_op jit(solution)/shard_map/ppermute | solution.py:506
  451.0 31.8 %collective-permute-start.33 = (bf16[512,1152]{1,0:T(8,128)(2,1)S(1)}, bf16[512,1152]{1,0:T(8,128)(2,1)S(1)}, u32[]{:S(2)}, u32[]{:S(2)}) collective-permute-start(bf16[512,1152]{1,0:T(8,128)(2,1)S(1)} %get-tuple-element.318), channel_id=1, source_target_pairs={{0,8},{8,0},{16,24},{24,16},{1,9},{9,1},{17,25},{25,17},{2,10},{10... | collective-permute-start | bytes 3538952 | tf_op jit(solution)/shard_map/ppermute | solution.py:633
  451.1 31.7 %collective-permute-start.34 = (bf16[512,1152]{1,0:T(8,128)(2,1)S(1)}, bf16[512,1152]{1,0:T(8,128)(2,1)}, u32[]{:S(2)}, u32[]{:S(2)}) collective-permute-start(bf16[512,1152]{1,0:T(8,128)(2,1)S(1)} %get-tuple-element.317), channel_id=1, source_target_pairs={{0,8},{8,0},{16,24},{24,16},{1,9},{9,1},{17,25},{25,17},{2,10},{10... | collective-permute-start | bytes 3538952 | tf_op jit(solution)/shard_map/ppermute | solution.py:633
  488.6 37.7 %collective-permute-start.35 = (bf16[176,1792]{1,0:T(8,128)(2,1)S(1)}, bf16[176,1792]{1,0:T(8,128)(2,1)S(1)}, u32[]{:S(2)}, u32[]{:S(2)}) collective-permute-start(bf16[176,1792]{1,0:T(8,128)(2,1)S(1)} %pad_maximum_fusion.4), channel_id=1, source_target_pairs={{0,1},{1,3},{3,5},{5,7},{7,6},{6,4},{4,2},{2,0},{8,9},{9,11},{11,1... | collective-permute-start | bytes 1892360 | tf_op jit(solution)/shard_map/ppermute | solution.py:506
  490.6 35.7 %collective-permute-start.36 = (bf16[176,1792]{1,0:T(8,128)(2,1)S(1)}, bf16[176,1792]{1,0:T(8,128)(2,1)S(1)}, u32[]{:S(2)}, u32[]{:S(2)}) collective-permute-start(bf16[176,1792]{1,0:T(8,128)(2,1)S(1)} %pad_maximum_fusion.5), channel_id=1, source_target_pairs={{1,0},{3,1},{5,3},{7,5},{6,7},{4,6},{2,4},{0,2},{9,8},{11,9},{13,1... | collective-permute-start | bytes 1892360 | tf_op jit(solution)/shard_map/ppermute | solution.py:506
  491.0 35.3 %collective-permute-start.37 = (bf16[216,1152]{1,0:T(8,128)(2,1)S(1)}, bf16[216,1152]{1,0:T(8,128)(2,1)S(1)}, u32[]{:S(2)}, u32[]{:S(2)}) collective-permute-start(bf16[216,1152]{1,0:T(8,128)(2,1)S(1)} %get-tuple-element.336), channel_id=1, source_target_pairs={{0,1},{1,3},{3,5},{5,7},{7,6},{6,4},{4,2},{2,0},{8,9},{9,11},{11,1... | collective-permute-start | bytes 1493000 | tf_op jit(solution)/shard_map/ppermute | solution.py:506
  493.0 33.3 %collective-permute-start.38 = (bf16[216,1152]{1,0:T(8,128)(2,1)S(1)}, bf16[216,1152]{1,0:T(8,128)(2,1)S(1)}, u32[]{:S(2)}, u32[]{:S(2)}) collective-permute-start(bf16[216,1152]{1,0:T(8,128)(2,1)S(1)} %get-tuple-element.335), channel_id=1, source_target_pairs={{1,0},{3,1},{5,3},{7,5},{6,7},{4,6},{2,4},{0,2},{9,8},{11,9},{13,1... | collective-permute-start | bytes 1493000 | tf_op jit(solution)/shard_map/ppermute | solution.py:506
  509.7 27.1 %collective-permute-start.39 = (bf16[512,1152]{1,0:T(8,128)(2,1)S(1)}, bf16[512,1152]{1,0:T(8,128)(2,1)S(1)}, u32[]{:S(2)}, u32[]{:S(2)}) collective-permute-start(bf16[512,1152]{1,0:T(8,128)(2,1)S(1)} %get-tuple-element.316), channel_id=1, source_target_pairs={{0,16},{8,24},{16,0},{24,8},{1,17},{9,25},{17,1},{25,9},{2,18},{10... | collective-permute-start | bytes 3538952 | tf_op jit(solution)/shard_map/ppermute | solution.py:638
  538.1 40.8 %collective-permute-start.40 = (bf16[176,3584]{1,0:T(8,128)(2,1)}, bf16[176,3584]{1,0:T(8,128)(2,1)}, u32[]{:S(2)}, u32[]{:S(2)}) collective-permute-start(bf16[176,3584]{1,0:T(8,128)(2,1)} %add_convert_fusion.6), channel_id=1, source_target_pairs={{0,1},{1,3},{3,5},{5,7},{7,6},{6,4},{4,2},{2,0},{8,9},{9,11},{11,1... | collective-permute-start | bytes 3784712 | tf_op jit(solution)/shard_map/ppermute | solution.py:506
  541.0 37.9 %collective-permute-start.41 = (bf16[176,3584]{1,0:T(8,128)(2,1)}, bf16[176,3584]{1,0:T(8,128)(2,1)}, u32[]{:S(2)}, u32[]{:S(2)}) collective-permute-start(bf16[176,3584]{1,0:T(8,128)(2,1)} %add_convert_fusion.5), channel_id=1, source_target_pairs={{1,0},{3,1},{5,3},{7,5},{6,7},{4,6},{2,4},{0,2},{9,8},{11,9},{13,1... | collective-permute-start | bytes 3784712 | tf_op jit(solution)/shard_map/ppermute | solution.py:506
  541.7 36.0 %copy-start.63 = (bf16[216,256]{1,0:T(8,128)(2,1)S(1)}, bf16[216,256]{1,0:T(8,128)(2,1)}, u32[]{:S(2)}) copy-start(bf16[216,256]{1,0:T(8,128)(2,1)} %copy-done.62) | copy-start | bytes 331780
  582.8 58.7 %collective-permute-start.42 = (bf16[176,3584]{1,0:T(8,128)(2,1)}, bf16[176,3584]{1,0:T(8,128)(2,1)}, u32[]{:S(2)}, u32[]{:S(2)}) collective-permute-start(bf16[176,3584]{1,0:T(8,128)(2,1)} %add_convert_fusion.4), channel_id=1, source_target_pairs={{0,1},{1,3},{3,5},{5,7},{7,6},{6,4},{4,2},{2,0},{8,9},{9,11},{11,1... | collective-permute-start | bytes 3784712 | tf_op jit(solution)/shard_map/ppermute | solution.py:506
  587.2 54.3 %collective-permute-start.43 = (bf16[176,3584]{1,0:T(8,128)(2,1)}, bf16[176,3584]{1,0:T(8,128)(2,1)}, u32[]{:S(2)}, u32[]{:S(2)}) collective-permute-start(bf16[176,3584]{1,0:T(8,128)(2,1)} %add_convert_fusion.3), channel_id=1, source_target_pairs={{1,0},{3,1},{5,3},{7,5},{6,7},{4,6},{2,4},{0,2},{9,8},{11,9},{13,1... | collective-permute-start | bytes 3784712 | tf_op jit(solution)/shard_map/ppermute | solution.py:506
  609.8 31.7 %collective-permute-start.44 = (bf16[216,1408]{1,0:T(8,128)(2,1)S(1)}, bf16[216,1408]{1,0:T(8,128)(2,1)}, u32[]{:S(2)}, u32[]{:S(2)}) collective-permute-start(bf16[216,1408]{1,0:T(8,128)(2,1)S(1)} %pad_maximum_fusion.8), channel_id=1, source_target_pairs={{0,16},{8,24},{16,0},{24,8},{1,17},{9,25},{17,1},{25,9},{2,18},{10... | collective-permute-start | bytes 1824776 | tf_op jit(solution)/shard_map/ppermute | solution.py:622
  667.9 84.7 %collective-permute-start.45 = (bf16[176,3584]{1,0:T(8,128)(2,1)}, bf16[176,3584]{1,0:T(8,128)(2,1)}, u32[]{:S(2)}, u32[]{:S(2)}) collective-permute-start(bf16[176,3584]{1,0:T(8,128)(2,1)} %add_convert_fusion.2), channel_id=1, source_target_pairs={{0,1},{1,3},{3,5},{5,7},{7,6},{6,4},{4,2},{2,0},{8,9},{9,11},{11,1... | collective-permute-start | bytes 3784712 | tf_op jit(solution)/shard_map/ppermute | solution.py:506
  672.0 80.6 %collective-permute-start.46 = (bf16[176,3584]{1,0:T(8,128)(2,1)}, bf16[176,3584]{1,0:T(8,128)(2,1)}, u32[]{:S(2)}, u32[]{:S(2)}) collective-permute-start(bf16[176,3584]{1,0:T(8,128)(2,1)} %add_convert_fusion.1), channel_id=1, source_target_pairs={{1,0},{3,1},{5,3},{7,5},{6,7},{4,6},{2,4},{0,2},{9,8},{11,9},{13,1... | collective-permute-start | bytes 3784712 | tf_op jit(solution)/shard_map/ppermute | solution.py:506
  680.4 68.9 %copy-start.44 = (bf16[216,1408]{1,0:T(8,128)(2,1)S(1)}, bf16[216,1408]{1,0:T(8,128)(2,1)}, u32[]{:S(2)}) copy-start(bf16[216,1408]{1,0:T(8,128)(2,1)} %copy-done.43) | copy-start | bytes 1824772
  680.4 69.5 %copy-start.132 = (f32[1,2,2,128]{3,1,2,0:T(2,128)S(1)}, f32[1,2,2,128]{3,1,2,0:T(2,128)}, u32[]{:S(2)}) copy-start(f32[1,2,2,128]{3,1,2,0:T(2,128)} %copy-done.131) | copy-start | bytes 6148
  680.4 69.5 %copy-start.13 = (f32[512,1152]{1,0:T(8,128)S(1)}, f32[512,1152]{1,0:T(8,128)}, u32[]{:S(2)}) copy-start(f32[512,1152]{1,0:T(8,128)} %get-tuple-element.281) | copy-start | bytes 7077892
  749.3 2.3 collective-permute-start.47
  749.8 2.7 collective-permute-start.48
  762.9 56.5 %collective-permute-start.49 = (f32[144,640]{1,0:T(8,128)S(1)}, f32[144,640]{1,0:T(8,128)S(1)}, u32[]{:S(2)}, u32[]{:S(2)}) collective-permute-start(f32[144,640]{1,0:T(8,128)S(1)} %pad_maximum_fusion.10), channel_id=1, source_target_pairs={{0,8},{8,0},{16,24},{24,16},{1,9},{9,1},{17,25},{25,17},{2,10},{10... | collective-permute-start | bytes 1105928 | tf_op jit(solution)/shard_map/ppermute | solution.py:667
  765.8 52.6 %copy-start.46 = (f32[144,1024]{1,0:T(8,128)}, f32[144,1024]{1,0:T(8,128)S(1)}, u32[]{:S(2)}) copy-start(f32[144,1024]{1,0:T(8,128)S(1)} %slice.429) | copy-start | bytes 1769476
  819.5 10.7 %collective-permute-start.50 = (f32[144,640]{1,0:T(8,128)S(1)}, f32[144,640]{1,0:T(8,128)S(1)}, u32[]{:S(2)}, u32[]{:S(2)}) collective-permute-start(f32[144,640]{1,0:T(8,128)S(1)} %fusion.167), channel_id=1, source_target_pairs={{0,16},{8,24},{16,0},{24,8},{1,17},{9,25},{17,1},{25,9},{2,18},{10... | collective-permute-start | bytes 1105928 | tf_op jit(solution)/shard_map/ppermute | solution.py:667
  (149 other events, 1063.2 us)

commit v3 on v2

--- a/solution.py
+++ b/solution.py
@@ -95,6 +95,12 @@
     )
 
 
+def brief(us):
+    return pl.CostEstimate(
+        flops=int(us * 1.0e9), bytes_accessed=int(us * 1.0e6), transcendentals=0
+    )
+
+
 def params(number):
     return pltpu.CompilerParams(
         collective_id=number, has_side_effects=True, vmem_limit_bytes=56 * 2**20
@@ -110,10 +116,43 @@
     return order
 
 
-def gather_whole(blocks, number, n_f, n_seq):
+def pack_small(gain1, gain2, attention, lower, raises, raises2, outward, n_seq):
+    groups = [(attention, gain1), (raises, None), (outward, None), (raises2, None), (lower, gain2)]
+    shares = (CORES, CORES, n_seq, n_seq, n_seq)
+
+    def body(*refs):
+        refs = list(refs)
+        for (parts, gain), out in zip(groups, refs[-len(groups) :], strict=True):
+            factor = None if gain is None else refs.pop(0)[...]
+            at = 0
+            for part in parts:
+                block = refs.pop(0)[...]
+                if factor is not None:
+                    block = (block.astype(wide) * factor).astype(low)
+                out[:, at : at + part.shape[1]] = block
+                at += part.shape[1]
+            if at < out.shape[1]:
+                out[:, at:] = jnp.zeros((out.shape[0], out.shape[1] - at), low)
+
+    sizes = []
+    for (parts, _), ways in zip(groups, shares, strict=True):
+        total = sum(part.shape[1] for part in parts)
+        sizes.append((parts[0].shape[0], total + -total % (128 * ways)))
+    operands = []
+    for parts, gain in groups:
+        operands += ([] if gain is None else [gain]) + list(parts)
+    return pl.pallas_call(
+        body,
+        out_shape=tuple(jax.ShapeDtypeStruct(size, low) for size in sizes),
+        compiler_params=pltpu.CompilerParams(vmem_limit_bytes=48 * 2**20),
+    )(*operands)
+
+
+def gather_whole(blocks, spread, number, n_f, n_seq):
     count = len(blocks)
     chips = n_seq // CORES
     steps = ring_steps(n_f)
+    order = [j for j in range(count) if spread[j]] + [j for j in range(count) if not spread[j]]
 
     def body(*refs):
         ins, outs = refs[:count], refs[count : 2 * count]
@@ -121,9 +160,13 @@
         here = Places(n_f, n_seq)
         started = []
 
-        def share(ref, spot):
-            width = ref.shape[-1] // n_seq
+        def share(j, k, c):
+            spot = here.seq(k, c) if spread[j] else lax.rem(here.core + c, CORES)
+            width = ins[j].shape[-1] // (n_seq if spread[j] else CORES)
             return (slice(None), pl.ds(pl.multiple_of(spot * width, 128), width))
+
+        def far(j):
+            return range(1, chips if spread[j] else 1)
 
         copies = []
         for j in range(count):
@@ -132,9 +175,12 @@
             copies.append(copy)
         here.greet(True)
 
+        def flip(j):
+            return 1 if j == 0 else -1
+
         def forward(j, step, way):
-            owner = here.at(-way * (step - 1))
-            mine = share(ins[j], here.me)
+            owner = here.at(-flip(j) * way * (step - 1))
+            mine = share(j, 0, 0)
             source = ins[j].at[mine] if step == 1 else outs[j].at[(owner, *mine)]
             at = steps.index((step, way))
             copy = remote(
@@ -142,37 +188,36 @@
                 outs[j].at[(owner, *mine)],
                 ring_s.at[j, at],
                 ring_r.at[j, at],
-                {"fsdp": here.at(way)},
+                {"fsdp": here.at(flip(j) * way)},
             )
             copy.start()
             started.append(copy)
 
         def landed(j, step, way):
-            owner = here.at(-way * step)
-            mine = share(ins[j], here.me)
+            owner = here.at(-flip(j) * way * step)
             at = steps.index((step, way))
-            block = outs[j].at[(owner, *mine)]
-            remote(block, block, ring_s.at[j, at], ring_r.at[j, at], {"fsdp": here.at(way)}).wait_recv()
+            block = outs[j].at[(owner, *share(j, 0, 0))]
+            remote(block, block, ring_s.at[j, at], ring_r.at[j, at], {"fsdp": here.at(flip(j) * way)}).wait_recv()
             return owner
 
         def to_core(j, at, k, owner):
-            block = outs[j].at[(owner, *share(ins[j], here.seq(k, 0)))]
+            block = outs[j].at[(owner, *share(j, k, 0))]
             copy = remote(
                 block, block, core_s.at[j, at, k], core_r.at[j, at, k], {"seq": here.seq(0, 1)}
             )
             copy.start()
             started.append(copy)
 
-        for j in range(count):
+        for j in order:
             for way in (1, -1):
                 forward(j, 1, way)
         for at, (step, way) in enumerate(steps):
-            for j in range(count):
+            for j in order:
                 owner = landed(j, step, way)
                 if (step + 1, way) in steps:
                     forward(j, step + 1, way)
-                block = outs[j].at[(owner, *share(ins[j], here.me))]
-                for k in range(1, chips):
+                block = outs[j].at[(owner, *share(j, 0, 0))]
+                for k in far(j):
                     copy = remote(
                         block, block, y_s.at[j, at, k], y_r.at[j, at, k], {"seq": here.seq(-k, 0)}
                     )
@@ -180,19 +225,19 @@
                     started.append(copy)
                 to_core(j, at, 0, owner)
         for at, (step, way) in enumerate(steps):
-            owner = here.at(-way * step)
-            for j in range(count):
-                for k in range(1, chips):
-                    block = outs[j].at[(owner, *share(ins[j], here.seq(k, 0)))]
+            for j in order:
+                owner = here.at(-flip(j) * way * step)
+                for k in far(j):
+                    block = outs[j].at[(owner, *share(j, k, 0))]
                     remote(
                         block, block, y_s.at[j, at, k], y_r.at[j, at, k], {"seq": here.seq(-k, 0)}
                     ).wait_recv()
                     to_core(j, at, k, owner)
         for at, (step, way) in enumerate(steps):
-            owner = here.at(-way * step)
-            for j in range(count):
-                for k in range(chips):
-                    block = outs[j].at[(owner, *share(ins[j], here.seq(k, 1)))]
+            for j in order:
+                owner = here.at(-flip(j) * way * step)
+                for k in [0, *far(j)]:
+                    block = outs[j].at[(owner, *share(j, k, 1))]
                     remote(
                         block, block, core_s.at[j, at, k], core_r.at[j, at, k], {"seq": here.seq(0, 1)}
                     ).wait_recv()
@@ -350,51 +395,61 @@
     )(terms)
 
 
-def scatter_whole(packs, number, n_seq):
+def scatter_whole(packs, block, small, number, n_seq):
     wanted = [pack.shape[2] for pack in packs]
-    gaps = [-count % (128 * n_seq) for count in wanted]
+    gaps = [-count % (128 * CORES) for count in wanted]
     packs = [
         jnp.pad(pack, ((0, 0), (0, 0), (0, gap))) if gap else pack
         for pack, gap in zip(packs, gaps, strict=True)
     ]
     n_f, count = packs[0].shape[0], len(packs)
     chips = n_seq // CORES
-    widths = [pack.shape[2] // n_seq for pack in packs]
+    widths = [pack.shape[2] // CORES for pack in packs]
     steps = ring_steps(n_f)
     offsets = [way * step for step, way in reversed(steps)] + [0]
     last = {way: max(step for step, w in steps if w == way) for way in (1, -1)}
 
     def body(*refs):
-        xs, outs = refs[:count], refs[count : 2 * count]
-        buffers, sem = refs[2 * count : 7 * count], refs[7 * count :]
-        nears, sums, fars, terms, moves = (
-            buffers[i * count : (i + 1) * count] for i in range(5)
-        )
-        core_s, core_r, y_s, y_r, ring_s, ring_r, over_s, over_r, side_s, side_r = sem
+        refs = list(refs)
+
+        def take(n):
+            taken, refs[:] = refs[:n], refs[n:]
+            return taken
+
+        xs = take(count)
+        block_in, small_in = take(2)
+        outs = take(count)
+        block_out, small_out = take(2)
+        nears, terms, moves, parts = (take(count) for _ in range(4))
+        (smalls,) = take(1)
+        core_s, core_r, ring_s, ring_r, y_s, y_r, side_s, side_r = take(8)
+        local, far_s, far_r, near_s, near_r = take(5)
         here = Places(n_f, n_seq)
+        own = pltpu.make_async_copy(block_in, block_out.at[0], local)
+        own.start()
+        smalls[here.me] = small_in[...]
         here.greet(True)
         started = []
 
+        def flip(j):
+            return 1 if j == 0 else -1
+
+        def go(copy):
+            copy.start()
+            started.append(copy)
+
         def share(j, spot):
             return pl.ds(pl.multiple_of(spot * widths[j], 128), widths[j])
 
-        def cross(j, i, k):
-            owner = here.at(offsets[i])
+        other = lax.rem(here.core + 1, CORES)
+
+        def cross(j, i):
             return remote(
-                xs[j].at[owner, :, share(j, here.seq(k, 1))],
-                nears[j].at[i, k],
-                core_s.at[j, i, k],
-                core_r.at[j, i, k],
+                xs[j].at[here.at(flip(j) * offsets[i]), :, share(j, other)],
+                nears[j].at[i],
+                core_s.at[j, i],
+                core_r.at[j, i],
                 {"seq": here.seq(0, 1)},
-            )
-
-        def over(j, i, k):
-            return remote(
-                sums[j].at[i, k],
-                fars[j].at[i, k],
-                y_s.at[j, i, k],
-                y_r.at[j, i, k],
-                {"seq": here.seq(k, 0)},
             )
 
         def hop(j, step, way):
@@ -404,34 +459,49 @@
                 moves[j].at[at],
                 ring_s.at[j, at],
                 ring_r.at[j, at],
-                {"fsdp": here.at(way)},
-            )
-
-        def go(copy):
-            copy.start()
-            started.append(copy)
-
+                {"fsdp": here.at(flip(j) * way)},
+            )
+
+        def far_block(k):
+            return remote(
+                block_in, block_out.at[k * CORES], far_s.at[k], far_r.at[k], {"seq": here.seq(-k, 0)}
+            )
+
+        def near_block(k):
+            source = block_in if k == 0 else block_out.at[k * CORES]
+            return remote(
+                source,
+                block_out.at[k * CORES + 1],
+                near_s.at[k],
+                near_r.at[k],
+                {"seq": here.seq(0, 1)},
+            )
+
+        def far_small(k, spot):
+            slot = smalls.at[spot]
+            return remote(
+                slot, slot, far_s.at[chips + k], far_r.at[chips + k], {"seq": here.seq(-k, 0)}
+            )
+
+        def near_small(k, spot):
+            slot = smalls.at[spot]
+            return remote(
+                slot, slot, near_s.at[chips + k], near_r.at[chips + k], {"seq": here.seq(0, 1)}
+            )
+
+        for k in range(1, chips):
+            go(far_small(k, here.me))
+            go(far_block(k))
         for i in range(n_f):
             for j in range(count):
-                for k in [*range(1, chips), 0]:
-                    go(cross(j, i, k))
+                go(cross(j, i))
+        go(near_small(0, here.me))
+        go(near_block(0))
         for i in range(n_f):
-            owner = here.at(offsets[i])
             for j in range(count):
-                for k in range(1, chips):
-                    cross(j, i, k).wait_recv()
-                    mine = xs[j][owner, :, share(j, here.seq(k, 0))].astype(wide)
-                    sums[j][i, k] = (mine + nears[j][i, k].astype(wide)).astype(low)
-                    go(over(j, i, k))
-        for i in range(n_f):
-            owner = here.at(offsets[i])
-            for j in range(count):
-                cross(j, i, 0).wait_recv()
-                total = xs[j][owner, :, share(j, here.me)].astype(wide)
-                total = total + nears[j][i, 0].astype(wide)
-                for k in range(1, chips):
-                    over(j, i, k).wait_recv()
-                    total = total + fars[j][i, k].astype(wide)
+                cross(j, i).wait_recv()
+                total = xs[j][here.at(flip(j) * offsets[i]), :, share(j, here.core)].astype(wide)
+                total = total + nears[j][i].astype(wide)
                 if offsets[i]:
                     step, way = abs(offsets[i]), 1 if offsets[i] > 0 else -1
                     if step < last[way]:
@@ -444,116 +514,201 @@
                         if last[way] >= 1:
                             hop(j, 1, way).wait_recv()
                             total = total + moves[j][steps.index((1, way))].astype(wide)
-                    outs[j][:, share(j, here.me)] = total.astype(low)
+                    parts[j][here.y] = total.astype(low)
 
         def swap(j, k, spot):
-            block = outs[j].at[:, share(j, spot)]
-            return remote(block, block, over_s.at[j, k], over_r.at[j, k], {"seq": here.seq(-k, 0)})
-
-        def side(j, k, spot):
-            block = outs[j].at[:, share(j, spot)]
-            return remote(block, block, side_s.at[j, k], side_r.at[j, k], {"seq": here.seq(0, 1)})
+            slot = parts[j].at[spot]
+            return remote(slot, slot, y_s.at[j, k], y_r.at[j, k], {"seq": here.seq(-k, 0)})
+
+        def side(j, core):
+            columns = outs[j].at[:, share(j, core)]
+            return remote(columns, columns, side_s.at[j], side_r.at[j], {"seq": here.seq(0, 1)})
 
         for j in range(count):
             for k in range(1, chips):
-                go(swap(j, k, here.me))
-            go(side(j, 0, here.me))
+                go(swap(j, k, here.y))
+        for k in range(1, chips):
+            far_small(k, here.seq(k, 0)).wait_recv()
+            go(near_small(k, here.seq(k, 0)))
+            far_block(k).wait_recv()
+            go(near_block(k))
         for j in range(count):
             for k in range(1, chips):
-                swap(j, k, here.seq(k, 0)).wait_recv()
-                go(side(j, k, here.seq(k, 0)))
+                swap(j, k, lax.rem(here.y + k, chips)).wait_recv()
+            total = parts[j][0].astype(wide)
+            for y in range(1, chips):
+                total = total + parts[j][y].astype(wide)
+            outs[j][:, share(j, here.core)] = total.astype(low)
+            go(side(j, here.core))
+        for k in range(chips):
+            near_small(k, here.seq(k, 1)).wait_recv()
+        total = smalls[0].astype(wide)
+        for spot in range(1, n_seq):
+            total = total + smalls[spot].astype(wide)
+        small_out[...] = total
+        for k in range(chips):
+            near_block(k).wait_recv()
         for j in range(count):
-            for k in range(chips):
-                side(j, k, here.seq(k, 1)).wait_recv()
+            side(j, other).wait_recv()
         for copy in started:
             copy.wait_send()
+        own.wait()
 
     sems = pltpu.SemaphoreType.DMA
     shapes = [(pack.shape[1], width) for pack, width in zip(packs, widths, strict=True)]
-    full = [pltpu.VMEM((n_f, chips, *shape), low) for shape in shapes]
+    near = [pltpu.VMEM((n_f, *shape), low) for shape in shapes]
     ring = [pltpu.VMEM((len(steps), *shape), low) for shape in shapes]
+    part = [pltpu.VMEM((chips, *shape), low) for shape in shapes]
     results = pl.pallas_call(
         body,
-        out_shape=tuple(jax.ShapeDtypeStruct(pack.shape[1:], low) for pack in packs),
-        in_specs=[VMEM] * count,
-        out_specs=(VMEM,) * count,
-        scratch_shapes=full * 3
+        out_shape=tuple(jax.ShapeDtypeStruct(pack.shape[1:], low) for pack in packs)
+        + (
+            jax.ShapeDtypeStruct((n_seq, *block.shape), low),
+            jax.ShapeDtypeStruct(small.shape, wide),
+        ),
+        in_specs=[VMEM] * count + [ANY, VMEM],
+        out_specs=(VMEM,) * count + (ANY, VMEM),
+        scratch_shapes=near
         + ring * 2
-        + [sems((count, n_f, chips))] * 4
+        + part
+        + [pltpu.VMEM((n_seq, *small.shape), low)]
+        + [sems((count, n_f))] * 2
         + [sems((count, len(steps)))] * 2
-        + [sems((count, chips))] * 4,
+        + [sems((count, chips))] * 2
+        + [sems((count,))] * 2
+        + [sems(())]
+        + [sems((2 * chips,))] * 4,
         compiler_params=params(number),
-    )(*packs)
-    return [result[:, :size] for result, size in zip(results, wanted, strict=True)]
+    )(*packs, block, small)
+    sums = [result[:, :size] for result, size in zip(results[:count], wanted, strict=True)]
+    return sums, results[count], results[count + 1]
+
+
+def ring_terms(sides, outs, n_f, n_seq, dtype):
+    flat, spots = [], []
+    left = 0
+    for side in sides:
+        top = 0
+        for part in side:
+            flat.append(part)
+            spots.append((top, left))
+            top += part.shape[1]
+        left += side[0].shape[2]
+    moved = [block for _, _, _, came in outs for block, _ in came]
+
+    def body(*refs):
+        parts, moves = refs[: len(flat)], list(refs[len(flat) : len(flat) + len(moved)])
+        results = refs[len(flat) + len(moved) : len(flat) + len(moved) + len(outs)]
+        scratch, sem = refs[len(flat) + len(moved) + len(outs) : -1], refs[-1]
+        here = Places(n_f, n_seq)
+        copies = []
+        for i, (offset, first, stop, _) in enumerate(outs):
+            owner = here.at(offset)
+            for at, (part, (above, before)) in enumerate(zip(parts, spots, strict=True)):
+                start, end = max(first, before), min(stop, before + part.shape[2])
+                if start < end:
+                    copies.append(
+                        pltpu.make_async_copy(
+                            part.at[owner, :, start - before : end - before],
+                            scratch[i].at[
+                                above : above + part.shape[1], start - first : end - first
+                            ],
+                            sem.at[i, at],
+                        )
+                    )
+        for copy in copies:
+            copy.start()
+        for copy in copies:
+            copy.wait()
+        for i, (_, first, stop, came) in enumerate(outs):
+            edges = sorted(
+                {first, stop}
+                | {c for _, c in came}
+                | {c + block.shape[1] for block, c in came}
+            )
+            here_moves = [(moves.pop(0), c) for _, c in came]
+            for start, end in zip(edges, edges[1:]):
+                total = scratch[i][:, start - first : end - first].astype(wide)
+                for ref, c in here_moves:
+                    if c <= start and end <= c + ref.shape[1]:
+                        total = total + ref[:, start - c : end - c].astype(wide)
+                results[i][:, start - first : end - first] = total.astype(dtype)
+
+    rows = sum(part.shape[1] for part in sides[0])
+    shapes = [(rows, stop - first) for _, first, stop, _ in outs]
+    return pl.pallas_call(
+        body,
+        out_shape=tuple(jax.ShapeDtypeStruct(shape, dtype) for shape in shapes),
+        in_specs=[ANY] * len(flat) + [VMEM] * len(moved),
+        out_specs=(VMEM,) * len(outs),
+        scratch_shapes=[pltpu.VMEM(shape, low) for shape in shapes]
+        + [pltpu.SemaphoreType.DMA((len(outs), len(flat)))],
+        cost_estimate=brief(1),
+        compiler_params=pltpu.CompilerParams(vmem_limit_bytes=32 * 2**20),
+    )(*flat, *moved)
 
 
 class Ring:
     def __init__(self, count, width):
         self.count = count
         walk = ring_order(count, width)
-        self.walk = jnp.array(walk, jnp.int32)
-        place = [0] * count
-        for spot, device in enumerate(walk):
-            place[device] = spot
-        self.spot = jnp.array(place, jnp.int32)[lax.axis_index("fsdp")]
         self.up = [(walk[i], walk[(i + 1) % count]) for i in range(count)]
         self.down = [(b, a) for a, b in self.up]
 
-    def at(self, offset):
-        return self.walk[lax.rem(self.spot + offset + self.count, self.count)]
-
     def hop(self, block, way):
         return lax.ppermute(block, "fsdp", self.up if way > 0 else self.down)
 
 
 class Gathering:
-    def __init__(self, ring, block, buffers, keep):
-        self.ring, self.buffers, self.keep = ring, buffers, keep
+    def __init__(self, ring, block):
+        self.ring = ring
         self.step, self.steps = 0, ring.count // 2
         self.moving = (block, block)
-        self.new = [(0, block)]
+        self.places = [(0, 0)]
+        self.blocks = [block]
 
     def advance(self):
-        self.settle()
         if self.step == self.steps:
             return
         self.step += 1
         first, second = self.moving
         if self.step < self.steps:
             self.moving = (self.ring.hop(first, 1), self.ring.hop(second, -1))
-            self.new = [(-self.step, self.moving[0]), (self.step, self.moving[1])]
+            self.places += [(-self.step, 0), (self.step, 0)]
         else:
             half = first.shape[1] // 256 * 128
             self.moving = (
                 self.ring.hop(first[:, :half], 1),
                 self.ring.hop(second[:, half:], -1),
             )
-            self.new = [(self.step, jnp.concatenate(self.moving, axis=1))]
-
-    def settle(self):
-        for offset, block in self.new:
-            self.buffers = self.keep(self.buffers, self.ring.at(offset), block)
-        self.new = []
+            self.places += [(self.step, 0), (self.step, half)]
+        self.blocks += list(self.moving)
 
     def done(self):
         while self.step < self.steps:
             self.advance()
-        self.settle()
-        return self.buffers
+        return [
+            (offset, block, column)
+            for (offset, column), block in zip(self.places, self.blocks, strict=True)
+        ]
 
     def live(self):
-        return (self.moving, self.buffers, [block for _, block in self.new])
+        return (self.moving, self.blocks)
 
     def restore(self, live):
-        self.moving, self.buffers, blocks = live
-        self.new = [(offset, block) for (offset, _), block in zip(self.new, blocks, strict=True)]
+        self.moving, self.blocks = live
 
 
 class Scattering:
-    def __init__(self, ring, part):
-        self.ring, self.part = ring, part
+    def __init__(self, ring, sides, n_seq):
+        self.ring, self.sides, self.n_seq = ring, sides, n_seq
+        self.width = sum(side[0].shape[2] for side in sides)
+        self.half = self.width // 256 * 128
         self.step, self.steps = 0, ring.count // 2
         self.moving = ()
+
+    def terms(self, outs, dtype):
+        return ring_terms(self.sides, outs, self.ring.count, self.n_seq, dtype)
 
     def advance(self):
         if self.step == self.steps:
@@ -561,30 +716,23 @@
         self.step += 1
         offset = self.steps - self.step + 1
         if self.step == 1:
-            term = self.part(self.ring.at(offset))
-            self.half = term.shape[1] // 256 * 128
-            ahead, back = term[:, : self.half], term[:, self.half :]
+            outs = [(offset, 0, self.half, []), (offset, self.half, self.width, [])]
         else:
-            ahead, back = self.joined(offset)
-        self.moving = (
-            self.ring.hop(ahead.astype(low), 1),
-            self.ring.hop(back.astype(low), -1),
-        )
-
-    def joined(self, offset):
-        ahead, back = self.part(self.ring.at(offset)), self.part(self.ring.at(-offset))
-        first, second = (block.astype(wide) for block in self.moving)
-        if self.step == 2:
-            first = jnp.pad(first, ((0, 0), (0, ahead.shape[1] - self.half)))
-            second = jnp.pad(second, ((0, 0), (self.half, 0)))
-        return ahead + first, back + second
-
-    def done(self):
+            ahead, back = self.moving
+            right = self.half if self.step == 2 else 0
+            outs = [
+                (offset, 0, self.width, [(ahead, 0)]),
+                (-offset, 0, self.width, [(back, right)]),
+            ]
+        ahead, back = self.terms(outs, low)
+        self.moving = (self.ring.hop(ahead, 1), self.ring.hop(back, -1))
+
+    def done(self, dtype):
         while self.step < self.steps:
             self.advance()
-        total = self.part(self.ring.at(0))
-        for block in self.moving:
-            total = total + block.astype(wide)
+        right = self.half if self.steps == 1 else 0
+        ahead, back = self.moving
+        (total,) = self.terms([(0, 0, self.width, [(ahead, 0), (back, right)])], dtype)
         return total
 
     def live(self):
@@ -627,6 +775,9 @@
         for block in blocks:
             out += [block, lax.ppermute(block, "seq", self.sibling)]
         return out
+
+    def swap(self, block):
+        return lax.ppermute(block, "seq", self.sibling)
 
     def cross(self, terms):
         return [
@@ -745,22 +896,262 @@
     )(gains, pieces)
 
 
-def rope(values, cosine, sine):
-    half = values.shape[-1] // 2
-    first, second = values[..., :half], values[..., half:]
-    cosine, sine = cosine[:, None, :], sine[:, None, :]
-    return jnp.concatenate([first * cosine - second * sine, second * cosine + first * sine], axis=-1)
-
-
 def gelu_parts(gate):
     scale = (2.0 / jnp.pi) ** 0.5
     cube = 0.044715
-    curve = jnp.tanh(scale * (gate + cube * gate * gate * gate))
-    value = 0.5 * gate * (1.0 + curve)
-    slope = 0.5 * (1.0 + curve) + 0.5 * gate * (1.0 - curve * curve) * scale * (
-        1.0 + 3.0 * cube * gate * gate
-    )
+    square = gate * gate
+    half = 0.5 * jnp.tanh(gate * (scale + scale * cube * square)) + 0.5
+    value = gate * half
+    slope = half + value * (1.0 - half) * (2.0 * scale + 6.0 * scale * cube * square)
     return value, slope
+
+
+def attention(queries, both, mask, rows):
+    n_seq, tokens, _ = both.shape
+    length = tokens // rows
+    scale = HD ** (-0.5)
+
+    def body(q, kv, hidden, out, log_total):
+        for r in range(rows):
+            at = slice(r * length, (r + 1) * length)
+            keys = kv[:, at, :HD].reshape(n_seq * length, HD)
+            values = kv[:, at, HD:].reshape(n_seq * length, HD)
+            for h in range(H):
+                head = slice(h * HD, (h + 1) * HD)
+                scores = mul_t(q[at, head], keys) * scale + hidden[r]
+                top = jnp.max(scores, axis=-1, keepdims=True)
+                weights = jnp.exp(scores - top)
+                total = jnp.sum(weights, axis=-1, keepdims=True)
+                out[at, head] = (mul(weights.astype(low), values) / total).astype(low)
+                log_total[r, h] = top + jnp.log(total)
+
+    return pl.pallas_call(
+        body,
+        out_shape=(
+            jax.ShapeDtypeStruct(queries.shape, low),
+            jax.ShapeDtypeStruct((rows, H, length, 1), wide),
+        ),
+        cost_estimate=brief(2),
+        compiler_params=pltpu.CompilerParams(vmem_limit_bytes=48 * 2**20),
+    )(queries, both, mask)
+
+
+def attention_back(queries, both, mask, log_total, out, g_out, cosine, sine, rows):
+    n_seq, tokens, _ = both.shape
+    length = tokens // rows
+    scale = HD ** (-0.5)
+    half = HD // 2
+
+    def body(q, kv, hidden, logs, o, g, cos, sin, g_q, g_both):
+        for r in range(rows):
+            at = slice(r * length, (r + 1) * length)
+            keys = kv[:, at, :HD].reshape(n_seq * length, HD)
+            values = kv[:, at, HD:].reshape(n_seq * length, HD)
+            d_keys = d_values = None
+            for h in range(H):
+                head = slice(h * HD, (h + 1) * HD)
+                scores = mul_t(q[at, head], keys) * scale + hidden[r]
+                probs = jnp.exp(scores - logs[r, h])
+                grad = g[at, head]
+                dots = jnp.sum(
+                    grad.astype(wide) * o[at, head].astype(wide), axis=-1, keepdims=True
+                )
+                d_scores = (probs * (mul_t(grad, values) - dots)).astype(low)
+                d_query = mul(d_scores, keys) * scale
+                first, second = d_query[:, :half], d_query[:, half:]
+                c, s = cos[at, :], sin[at, :]
+                turned = jnp.concatenate([first * c + second * s, second * c - first * s], axis=1)
+                g_q[at, head] = turned.astype(low)
+                d_key = t_mul(d_scores, q[at, head])
+                d_value = t_mul(probs.astype(low), grad)
+                d_keys = d_key if d_keys is None else d_keys + d_key
+                d_values = d_value if d_values is None else d_values + d_value
+            g_both[:, at, :HD] = (d_keys * scale).astype(low).reshape(n_seq, length, HD)
+            g_both[:, at, HD:] = d_values.astype(low).reshape(n_seq, length, HD)
+
+    return pl.pallas_call(
+        body,
+        out_shape=(
+            jax.ShapeDtypeStruct(queries.shape, low),
+            jax.ShapeDtypeStruct(both.shape, low),
+        ),
+        cost_estimate=brief(3),
+        compiler_params=pltpu.CompilerParams(vmem_limit_bytes=56 * 2**20),
+    )(queries, both, mask, log_total, out, g_out, cosine, sine)
+
+
+def landing(items, buffers, rows_first, sem, here):
+    copies = []
+    for at, (offset, ref, column) in enumerate(items):
+        owner = here.at(offset)
+        first = 0
+        for part, buffer in enumerate(buffers):
+            count = rows_first[part]
+            copies.append(
+                pltpu.make_async_copy(
+                    ref.at[first : first + count],
+                    buffer.at[owner, :, column : column + ref.shape[1]],
+                    sem.at[at, part],
+                )
+            )
+            first += count
+    for copy in copies:
+        copy.start()
+    for copy in copies:
+        copy.wait()
+
+
+def mlp_forward(
+    items, tokens2, adapters, before, part, n_f, n_seq, rank_rows, own_rows, slab
+):
+    count, width = tokens2.shape
+    rank = rank_rows * n_f
+    tile = 256 if slab % 256 == 0 else 128
+    chunk = 512
+    first, stop = part
+    wanted = []
+    for side in range(2):
+        start, end = side * slab + first * tile, side * slab + stop * tile
+        for at, (offset, block, column) in enumerate(items):
+            low_end, high_end = max(start, column), min(end, column + block.shape[1])
+            if low_end < high_end:
+                wanted.append((at, offset, low_end - column, high_end - column, side, low_end - start))
+    adapters = [a.reshape(n_f, own_rows, rank) for a in adapters]
+
+    def body(x, lower_g, lower_u, *refs):
+        blocks, refs = refs[: len(items)], refs[len(items) + len(before) :]
+        hidden, back_g, back_u, full_g, full_u, raised_g, raised_u = refs[:7]
+        raises, weights, merged, sem = refs[7:]
+        here = Places(n_f, n_seq)
+        step = pl.program_id(0)
+
+        @pl.when(step == 0)
+        def _():
+            copies = []
+            for number, (at, offset, start, end, side, column) in enumerate(wanted):
+                owner = here.at(offset)
+                for which, (buffer, rows) in enumerate(
+                    (
+                        (raises, slice(0, rank_rows)),
+                        (weights, slice(rank_rows, rank_rows + own_rows)),
+                    )
+                ):
+                    copies.append(
+                        pltpu.make_async_copy(
+                            blocks[at].at[rows, start:end],
+                            buffer.at[side, owner, :, column : column + end - start],
+                            sem.at[number, which],
+                        )
+                    )
+            for copy in copies:
+                copy.start()
+            for copy in copies:
+                copy.wait()
+
+        for side, (lower, full, raised) in enumerate(
+            ((lower_g, full_g, raised_g), (lower_u, full_u, raised_u))
+        ):
+            columns = pl.ds(pl.multiple_of(step * tile, 128), tile)
+            up_matrix = raises[side, :, :, columns].reshape(rank, tile)
+            raised[...] = up_matrix
+            for f in range(n_f):
+                total = weights[side, f, :, columns].astype(wide) + mul(lower[f], up_matrix)
+                total = total.astype(low)
+                full[f] = total
+                merged[side, f * own_rows : (f + 1) * own_rows, :] = total
+
+        def some(i, carry):
+            at = pl.ds(pl.multiple_of(i * chunk, chunk), chunk)
+            gate = mul(x[at, :], merged[0])
+            up = mul(x[at, :], merged[1])
+            value, slope = gelu_parts(gate)
+            hidden[at, :] = (value * up).astype(low)
+            back_g[at, :] = (up * slope).astype(low)
+            back_u[at, :] = value.astype(low)
+            return carry
+
+        lax.fori_loop(0, count // chunk, some, 0, unroll=True)
+
+    by_column = pl.BlockSpec((count, tile), lambda j: (0, j + first))
+    by_weight = pl.BlockSpec((n_f, own_rows, tile), lambda j: (0, 0, j + first))
+    by_raise = pl.BlockSpec((rank, tile), lambda j: (0, j + first))
+    return pl.pallas_call(
+        body,
+        grid=(stop - first,),
+        out_shape=(jax.ShapeDtypeStruct((count, slab), low),) * 3
+        + (jax.ShapeDtypeStruct((n_f, own_rows, slab), low),) * 2
+        + (jax.ShapeDtypeStruct((rank, slab), low),) * 2,
+        in_specs=[VMEM] * 3 + [ANY] * (len(items) + len(before)),
+        input_output_aliases={3 + len(items) + i: i for i in range(len(before))},
+        out_specs=(by_column,) * 3 + (by_weight,) * 2 + (by_raise,) * 2,
+        scratch_shapes=[
+            pltpu.VMEM((2, n_f, rank_rows, (stop - first) * tile), low),
+            pltpu.VMEM((2, n_f, own_rows, (stop - first) * tile), low),
+            pltpu.VMEM((2, width, tile), low),
+            pltpu.SemaphoreType.DMA((len(wanted), 2)),
+        ],
+        cost_estimate=brief(3),
+        compiler_params=pltpu.CompilerParams(vmem_limit_bytes=56 * 2**20),
+    )(tokens2, *adapters, *(block for _, block, _ in items), *before)
+
+
+def mlp_backward(items, d_raise, g_tokens, back_g, back_u, n_f, n_seq, cut, slab):
+    count, width = g_tokens.shape
+    rank = d_raise.shape[0]
+    tile = 256 if slab % 256 == 0 else 128
+    chunk = 512
+    offsets = [(offset, column) for offset, _, column in items]
+
+    def body(g, raised, mul_g, mul_u, *refs):
+        blocks = refs[: len(items)]
+        grad_g, grad_u, full, raw, merged, sem = refs[len(items) :]
+        here = Places(n_f, n_seq)
+        step = pl.program_id(0)
+
+        @pl.when(step == 0)
+        def _():
+            landing(
+                [(o, ref, c) for (o, c), ref in zip(offsets, blocks, strict=True)],
+                (raw,),
+                (cut,),
+                sem,
+                here,
+            )
+            for f in range(n_f):
+                merged[f * cut : (f + 1) * cut, :] = raw[f, :, :width].astype(wide) + mul(
+                    raw[f, :, width:], raised[...]
+                )
+            if slab > n_f * cut:
+                merged[n_f * cut :, :] = jnp.zeros((slab - n_f * cut, width), wide)
+
+        weight = merged[pl.ds(pl.multiple_of(step * tile, tile), tile), :].astype(low)
+        full[...] = weight
+
+        def some(i, carry):
+            at = pl.ds(pl.multiple_of(i * chunk, chunk), chunk)
+            g_hidden = mul_t(g[at, :], weight)
+            grad_g[at, :] = (g_hidden * mul_g[at, :].astype(wide)).astype(low)
+            grad_u[at, :] = (g_hidden * mul_u[at, :].astype(wide)).astype(low)
+            return carry
+
+        lax.fori_loop(0, count // chunk, some, 0, unroll=True)
+
+    by_column = pl.BlockSpec((count, tile), lambda j: (0, j))
+    return pl.pallas_call(
+        body,
+        grid=(slab // tile,),
+        out_shape=(jax.ShapeDtypeStruct((count, slab), low),) * 2
+        + (jax.ShapeDtypeStruct((slab, width), low),),
+        in_specs=[VMEM] * 2 + [by_column] * 2 + [ANY] * len(items),
+        out_specs=(by_column,) * 2 + (pl.BlockSpec((tile, width), lambda j: (j, 0)),),
+        scratch_shapes=[
+            pltpu.VMEM((n_f, cut, width + rank), low),
+            pltpu.VMEM((slab, width), wide),
+            pltpu.SemaphoreType.DMA((len(items), 1)),
+        ],
+        cost_estimate=brief(3),
+        compiler_params=pltpu.CompilerParams(vmem_limit_bytes=56 * 2**20),
+    )(g_tokens, d_raise, back_g, back_u, *(block for _, block, _ in items))
 
 
 def shards(
@@ -816,52 +1207,22 @@
         part = array.shape[0] // n_seq
         return lax.dynamic_slice_in_dim(array, me * part, part, 0)
 
-    def side_by_side(parts):
-        total = sum(part.shape[1] for part in parts)
-        gap = -total % (128 * n_seq)
-        if gap:
-            parts = [*parts, jnp.zeros((parts[0].shape[0], gap), low)]
-        return jnp.concatenate(parts, axis=1)
-
-    side1 = side_by_side(
-        [
-            (part.astype(wide) * gain1).astype(low)
-            for part in (q_weight, k_weight, v_weight, q_down, k_down, v_down)
-        ]
-        + [(part.astype(wide) * gain2).astype(low) for part in (gate_down, up_down)]
-    )
-    ups = side_by_side([q_up, k_up, v_up, o_up, down_up])
-    side_o = side_by_side([o_weight, o_down])
-
-    def keep_slab(buffers, owner, block):
-        raised, gates, raises = buffers
-        put = lax.dynamic_update_index_in_dim
-        return (
-            put(raised, block[:rank_rows], owner, 0),
-            put(gates, block[rank_rows:, :slab], owner, 0),
-            put(raises, block[rank_rows:, slab:], owner, 0),
-        )
-
-    def keep_down(buffers, owner, block):
-        return (lax.dynamic_update_index_in_dim(buffers[0], block, owner, 0),)
+    small_blocks = pack_small(
+        gain1,
+        gain2,
+        (q_weight, k_weight, v_weight, q_down, k_down, v_down),
+        (gate_down, up_down),
+        (q_up, k_up, v_up),
+        (o_up, down_up),
+        (o_weight, o_down),
+        n_seq,
+    )
 
     slabs = Gathering(
-        ring,
-        cut_columns((gate_weight, up_weight), (gate_up, up_up), gain2, n_f, n_seq, slab),
-        (
-            jnp.zeros((n_f, rank_rows, 2 * slab), low),
-            jnp.zeros((n_f, own_rows, slab), low),
-            jnp.zeros((n_f, own_rows, slab), low),
-        ),
-        keep_slab,
+        ring, cut_columns((gate_weight, up_weight), (gate_up, up_up), gain2, n_f, n_seq, slab)
     )
     d_lower = rows_of(down_down)
-    downs = Gathering(
-        ring,
-        jnp.concatenate([rows_of(down_weight), d_lower], axis=1),
-        (jnp.zeros((n_f, cut, width + rank), low),),
-        keep_down,
-    )
+    downs = Gathering(ring, jnp.concatenate([rows_of(down_weight), d_lower], axis=1))
 
     depth_ids = jnp.arange(DEPTHS, dtype=jnp.int32)
     matches = (exits.reshape(tokens)[:, None] == depth_ids[None, :]).astype(wide)
@@ -883,21 +1244,18 @@
     unit1 = (resid * r1).astype(low)
 
     slabs.advance()
-    downs.advance()
     seg_pieces = group.over(segments.astype(low))
-    whole = gather_whole((side1, ups, side_o), 0, n_f, n_seq)
-    whole, seg_pieces, unit1, cosine, sine = tie(
-        (slabs, downs), (whole, seg_pieces, unit1, cosine, sine)
-    )
-    side1, ups, side_o = (part.reshape(-1, part.shape[2]) for part in whole)
+    whole = gather_whole(small_blocks, (False, False, True, True, True), 0, n_f, n_seq)
+    whole, seg_pieces, unit1, cosine, sine, g_mlp = tie(
+        (slabs, downs), (whole, seg_pieces, unit1, cosine, sine, g_mlp)
+    )
+    qkv_side, ups, side_o, ups2, adapters = (part.reshape(-1, part.shape[2]) for part in whole)
     kv = HD
     lin = hq + 2 * kv
-    qkv_side = side1[:, : lin + 3 * rank]
-    gate_adapter = side1[:, lin + 3 * rank : lin + 4 * rank]
-    up_adapter = side1[:, lin + 4 * rank : lin + 5 * rank]
+    gate_adapter, up_adapter = adapters[:, :rank], adapters[:, rank : 2 * rank]
     side_o = side_o[:, : width + rank]
     q_raise, k_raise, v_raise = ups[:, :hq], ups[:, hq : hq + kv], ups[:, hq + kv : lin]
-    o_raise, d_raise = ups[:, lin : lin + width], ups[:, lin + width : lin + 2 * width]
+    o_raise, d_raise = ups2[:, :width], ups2[:, width : 2 * width]
 
     slabs.advance()
     seg_pieces = group.across(seg_pieces)
@@ -907,20 +1265,20 @@
     q_lin = projected[:, :hq] + mul(q_inner, q_raise)
     k_lin = projected[:, hq : hq + kv] + mul(k_inner, k_raise)
     v_lin = projected[:, hq + kv : lin] + mul(v_inner, v_raise)
-    queries = rope(q_lin.reshape(tokens, H, HD), cosine, sine).astype(low)
-    queries = queries.reshape(rows, length, H, HD).transpose(0, 2, 1, 3)
-    queries = queries.reshape(rows, H * length, HD)
-    keys = rope(k_lin.reshape(tokens, 1, HD), cosine, sine).astype(low).reshape(tokens, HD)
+    half = HD // 2
+
+    def rope(values):
+        parts = []
+        for at in range(0, values.shape[1], HD):
+            first, second = values[:, at : at + half], values[:, at + half : at + HD]
+            parts += [first * cosine - second * sine, second * cosine + first * sine]
+        return jnp.concatenate(parts, axis=1)
+
+    queries = rope(q_lin).astype(low)
+    keys = rope(k_lin).astype(low)
     values = v_lin.astype(low)
-    both = gather_group(jnp.concatenate([keys, values], axis=-1), 2, n_seq)
-    both, queries, seg_pieces, inner = tie((slabs,), (both, queries, seg_pieces, inner))
-    q_inner, k_inner, v_inner = inner[:, :rank], inner[:, rank : 2 * rank], inner[:, 2 * rank :]
-
-    slabs.advance()
-    g_mlp = group.over(g_mlp)
-    both = both.reshape(n_seq, rows, length, 2 * HD)
-    both = both.transpose(1, 0, 2, 3).reshape(rows, n_seq * length, 2 * HD)
-    keys, values = both[..., :HD], both[..., HD:]
+    both = jnp.concatenate([keys, values], axis=-1)
+    both = gather_group(both, 2, n_seq)
     key_seg = jnp.concatenate(seg_pieces, axis=1).astype(jnp.int32)
     key_place = jnp.concatenate(
         [
@@ -928,141 +1286,152 @@
             for k, c in group.order
         ]
     )
-    query_seg, query_place = jnp.tile(segments, (1, H)), jnp.tile(places, H)
-    allowed = (query_seg[:, :, None] == key_seg[:, None, :]) & (
-        key_place[None, None, :] <= query_place[None, :, None]
-    )
-    scores = (
-        jnp.einsum("sqd,skd->sqk", queries, keys, preferred_element_type=wide) * scale
-    )
-    scores = jnp.where(allowed, scores, -1e30)
-    top = jnp.max(scores, axis=-1, keepdims=True)
-    weights = jnp.exp(scores - top)
-    totals = jnp.sum(weights, axis=-1, keepdims=True)
-    attn = (
-        jnp.einsum("sqk,skd->sqd", weights.astype(low), values, preferred_element_type=wide)
-        / totals
-    )
-    log_total = top + jnp.log(totals)
-
-    def to_tokens(rows_heads):
-        view = rows_heads.reshape(rows, H, length, HD).transpose(0, 2, 1, 3)
-        return view.reshape(tokens, hq)
-
-    def to_heads(flat):
-        view = flat.reshape(rows, length, H, HD).transpose(0, 2, 1, 3)
-        return view.reshape(rows, H * length, HD)
-
-    attn_low = to_tokens(attn.astype(low))
+    allowed = (segments[:, :, None] == key_seg[:, None, :]) & (
+        key_place[None, None, :] <= places[None, :, None]
+    )
+    mask = jnp.where(allowed, 0.0, -1e30).astype(wide)
+    both, queries, mask, inner, g_mlp = tie((slabs,), (both, queries, mask, inner, g_mlp))
+    q_inner, k_inner, v_inner = inner[:, :rank], inner[:, rank : 2 * rank], inner[:, 2 * rank :]
+
+    slabs.advance()
+    g_mlp = group.over(g_mlp)
+    attn_low, log_total = attention(queries, both, mask, rows)
     projected = mul(attn_low, side_o)
     o_inner = projected[:, width:].astype(low)
     mid = resid + active * (projected[:, :width] + mul(o_inner, o_raise))
     r2 = lax.rsqrt(jnp.mean(mid * mid, axis=-1, keepdims=True) + epsilon)
     unit2 = (mid * r2).astype(low)
-    unit2, mid, r2, g_mlp, attn, attn_low, o_inner, log_total = tie(
-        (slabs, counted), (unit2, mid, r2, g_mlp, attn, attn_low, o_inner, log_total)
+    unit2, mid, r2, g_mlp, attn_low, o_inner, log_total = tie(
+        (slabs,), (unit2, mid, r2, g_mlp, attn_low, o_inner, log_total)
     )
 
     slabs.advance()
     downs.advance()
-    counted.advance()
+    unit2 = gather_group(unit2, 3, n_seq).reshape(-1, width)
+    unit2, g_mlp = tie((slabs, downs), (unit2, g_mlp))
+
+    downs.advance()
     g_mlp = group.across(g_mlp)
-    unit2 = gather_group(unit2, 3, n_seq).reshape(-1, width)
-    unit2, g_mlp = tie((slabs, downs, counted), (unit2, g_mlp))
-    g_mlp = jnp.concatenate(g_mlp, axis=0)
-
+    tiles = slab // (256 if slab % 256 == 0 else 128)
+    arrived = slabs.done()
+
+    def forward(first, stop, before):
+        return mlp_forward(
+            arrived,
+            unit2,
+            (gate_adapter, up_adapter),
+            before,
+            (first, stop),
+            n_f,
+            n_seq,
+            rank_rows,
+            own_rows,
+            slab,
+        )
+
+    half_way = forward(0, (tiles + 1) // 2, ())
+    half_way, g_mlp = tie((downs,), (half_way, g_mlp))
     downs.advance()
     counted.advance()
-    raised, gate_full, up_full = slabs.done()
-    raised = raised.reshape(rank, 2 * slab)
-    g_raise, u_raise = raised[:, :slab], raised[:, slab:]
-    gate_full = (gate_full.reshape(width, slab).astype(wide) + mul(gate_adapter, g_raise)).astype(low)
-    up_full = (up_full.reshape(width, slab).astype(wide) + mul(up_adapter, u_raise)).astype(low)
-    gate = mul(unit2, gate_full).astype(low)
-    up = mul(unit2, up_full).astype(low)
-    value, slope = gelu_parts(gate.astype(wide))
-    hidden = (value * up.astype(wide)).astype(low)[:, : n_f * cut]
-    hidden, gate, up = tie((downs, counted), (hidden, gate, up))
+    hidden, back_g, back_u, gate_full, up_full, g_raise, u_raise = forward(
+        (tiles + 1) // 2, tiles, half_way
+    )
+    hidden, back_g, back_u, g_mlp = tie((downs, counted), (hidden, back_g, back_u, g_mlp))
+    g_mlp = jnp.concatenate(g_mlp, axis=0)
 
     downs.advance()
     counted.advance()
     g_down = t_mul(hidden, g_mlp).astype(low)
-    g_down, g_mlp = tie((downs, counted), (g_down, g_mlp))
-
-    def ring_block(array, size):
-        return lambda owner: lax.dynamic_slice_in_dim(array, owner * size, size, 0).astype(wide)
-
-    down_sums = Scattering(ring, ring_block(g_down, cut))
+    g_down, g_mlp, back_g, back_u = tie((downs, counted), (g_down, g_mlp, back_g, back_u))
+
+    down_sums = Scattering(ring, [[g_down[: n_f * cut].reshape(n_f, cut, width)]], n_seq)
+
     down_sums.advance()
     counted.advance()
-    (down_raw,) = downs.done()
-    down_raw = down_raw.reshape(n_f * cut, width + rank)
-    down_full = (down_raw[:, :width].astype(wide) + mul(down_raw[:, width:], d_raise)).astype(low)
-    padded = jnp.pad(down_full, ((0, slab - n_f * cut), (0, 0)))
-    g_hidden = mul_t(g_mlp, padded)
-    value, slope = gelu_parts(gate.astype(wide))
-    g_gate = (g_hidden * up.astype(wide) * slope).astype(low)
-    g_up = (g_hidden * value).astype(low)
+    g_gate, g_up, down_full = mlp_backward(
+        downs.done(), d_raise, g_mlp, back_g, back_u, n_f, n_seq, cut, slab
+    )
     g_gate, g_up, down_full = tie((down_sums, counted), (g_gate, g_up, down_full))
 
     down_sums.advance()
     counted.advance()
-    branch = mul(hidden, down_full).astype(low)
-    branch, g_gate, g_up = tie((down_sums, counted), (branch, g_gate, g_up))
-
+    gg = t_mul(unit2, g_gate).astype(low)
+    gg_raise = t_mul(gate_adapter, gg).astype(low)
+    gg, gg_raise, g_gate, g_up, unit2 = tie(
+        (down_sums, counted), (gg, gg_raise, g_gate, g_up, unit2)
+    )
     down_sums.advance()
-    terms = [branch[i * tokens : (i + 1) * tokens] for i in range(n_seq)]
-    near = group.cross(terms)
-    gg = t_mul(unit2, g_gate).astype(low)
     gu = t_mul(unit2, g_up).astype(low)
-    gg_raise = t_mul(gate_adapter, gg).astype(low)
     gu_raise = t_mul(up_adapter, gu).astype(low)
-    near, gg, gu, gg_raise, gu_raise, g_gate, g_up = tie(
-        (down_sums,), (near, gg, gu, gg_raise, gu_raise, g_gate, g_up)
-    )
-
-    def slab_block(owner):
-        return jnp.concatenate(
-            [
-                jnp.concatenate(
-                    [
-                        lax.dynamic_slice_in_dim(part, owner * size, size, 0)
-                        for part in (raised, weight)
-                        for size in (part.shape[0] // n_f,)
-                    ],
-                    axis=0,
-                )
-                for raised, weight in ((gg_raise, gg), (gu_raise, gu))
-            ],
-            axis=1,
-        ).astype(wide)
-
-    slab_sums = Scattering(ring, slab_block)
+    gg, gu, gg_raise, gu_raise, g_gate, g_up = tie(
+        (down_sums,), (gg, gu, gg_raise, gu_raise, g_gate, g_up)
+    )
+    slab_sums = Scattering(
+        ring,
+        [
+            [part.reshape(n_f, -1, slab) for part in side]
+            for side in ((gg_raise, gg), (gu_raise, gu))
+        ],
+        n_seq,
+    )
+    chips = range(n_seq // CORES)
+    here_tokens = CORES * tokens
+
+    def token_gradient(at):
+        result = mul_t(g_gate[at], gate_full.reshape(width, slab))
+        return (result + mul_t(g_up[at], up_full.reshape(width, slab))).astype(low)
+
     slab_sums.advance()
-    down_sums.advance()
-    sums = [
-        terms[k * CORES].astype(wide) + near[k].astype(wide) for k in range(n_seq // CORES)
-    ]
-    far = group.send(sums)
-    e2 = (mul_t(g_gate, gate_full) + mul_t(g_up, up_full)).astype(low)
-    e2, far, own_branch = tie((slab_sums, down_sums), (e2, far, sums[0]))
-    for block in far:
-        own_branch = own_branch + block.astype(wide)
-    outputs = (mid + active * own_branch).astype(low).reshape(rows, length, width)
-
-    slab_sums.advance()
-    e2 = scatter_group(e2.reshape(n_seq, tokens, width), 5)
-    g_down = down_sums.done().astype(low)
+    e2_there = token_gradient(slice(here_tokens, None))
+    g_down = down_sums.done(low)
     down_rows = jnp.concatenate([g_down, mul_t(g_down, d_raise).astype(low)], axis=1)
     gd_raise = t_mul(d_lower, g_down).astype(low)
-    e2, down_rows, gd_raise = tie((slab_sums,), (e2, down_rows, gd_raise))
+    e2_there, g_gate, g_up, down_rows, gd_raise = tie(
+        (slab_sums,), (e2_there, g_gate, g_up, down_rows, gd_raise)
+    )
 
     slab_sums.advance()
+    there = [e2_there[i * tokens : (i + 1) * tokens] for i in range(n_seq - CORES)]
+    e2_near = [group.swap(there[(k - 1) * CORES + 1]) for k in chips[1:]]
     down_rows = group.over(down_rows)
+    e2_here = token_gradient(slice(0, here_tokens))
+    e2_here, e2_near, hidden, down_rows = tie((slab_sums,), (e2_here, e2_near, hidden, down_rows))
+
+    slab_sums.advance()
+    e2_sums = [
+        there[(k - 1) * CORES].astype(wide) + e2_near[k - 1].astype(wide) for k in chips[1:]
+    ]
+    e2_far = group.send([None, *e2_sums])
+    e2_own = group.swap(e2_here[tokens:])
+    branch = mul(hidden, down_full).astype(low)
+    branch, e2_far, e2_own, e2_here = tie((slab_sums,), (branch, e2_far, e2_own, e2_here))
+    terms = [branch[i * tokens : (i + 1) * tokens] for i in range(n_seq)]
+    e2 = e2_here[:tokens].astype(wide) + e2_own.astype(wide)
+    for block in e2_far:
+        e2 = e2 + block.astype(wide)
+
+    slab_sums.advance()
+    near = group.cross(terms)
     g_mid = cot + r2 * e2 - mid * (r2 * r2 * r2 * jnp.mean(e2 * mid, axis=-1, keepdims=True))
     g_branch = (active * g_mid).astype(low)
     g_inner = mul_t(g_branch, o_raise).astype(low)
     g_attn = mul_t(jnp.concatenate([g_branch, g_inner], axis=1), side_o).astype(low)
+    sums = [terms[k * CORES].astype(wide) + near[k].astype(wide) for k in chips]
+    g_attn, sums, g_mid, g_branch, down_rows = tie(
+        (slab_sums,), (g_attn, sums, g_mid, g_branch, down_rows)
+    )
+
+    middle = tokens // 2
+    down_rows = group.across(down_rows)
+    far_first = group.send([block[:middle] for block in sums])
+    g_q, d_terms = attention_back(
+        queries, both, mask, log_total, attn_low, g_attn, cosine, sine, rows
+    )
+    d_terms, g_q, g_mid, g_branch, down_rows, sums, far_first = tie(
+        (), (d_terms, g_q, g_mid, g_branch, down_rows, sums, far_first)
+    )
+
+    d_near = group.cross([d_terms[i] for i in range(n_seq)])
     g_o = t_mul(attn_low, g_branch).astype(low)
     go_raise = t_mul(o_inner, g_branch).astype(low)
     o_pack = jnp.concatenate(
@@ -1073,29 +1442,21 @@
         ],
         axis=1,
     )
-    g_heads = to_heads(g_attn)
-    dots = jnp.sum(g_heads.astype(wide) * attn, axis=-1, keepdims=True)
-    scores = (
-        jnp.einsum("sqd,skd->sqk", queries, keys, preferred_element_type=wide) * scale
-    )
-    probs = jnp.where(allowed, jnp.exp(scores - log_total), 0.0)
-    d_probs = jnp.einsum("sqd,skd->sqk", g_heads, values, preferred_element_type=wide)
-    d_scores = (probs * (d_probs - dots)).astype(low)
-    d_query = jnp.einsum("sqk,skd->sqd", d_scores, keys, preferred_element_type=wide) * scale
-    d_key = jnp.einsum("sqk,sqd->skd", d_scores, queries, preferred_element_type=wide) * scale
-    d_value = jnp.einsum("sqk,sqd->skd", probs.astype(low), g_heads, preferred_element_type=wide)
-    d_both = jnp.concatenate([d_key, d_value], axis=-1)
-    d_both = d_both.astype(low).reshape(rows, n_seq, length, 2 * HD)
-    d_both = scatter_group(d_both.transpose(1, 0, 2, 3).reshape(n_seq, tokens, 2 * HD), 8)
-    d_both, d_query, o_pack, g_mid, down_rows = tie(
-        (slab_sums,), (d_both, d_query, o_pack, g_mid, down_rows)
-    )
-
-    slab_sums.advance()
-    down_rows = group.across(down_rows)
-    g_q = rope(to_tokens(d_query).reshape(tokens, H, HD), cosine, -sine)
-    g_q = g_q.reshape(tokens, hq).astype(low)
-    g_k = rope(d_both[:, None, :HD], cosine, -sine).reshape(tokens, HD).astype(low)
+    d_sums = [d_terms[k * CORES].astype(wide) + d_near[k].astype(wide) for k in chips]
+    d_far = group.send(d_sums)
+    d_far, g_q, d_both, o_pack, down_rows, sums = tie(
+        (), (d_far, g_q, d_sums[0], o_pack, down_rows, sums)
+    )
+
+    far = group.send([block[middle:] for block in sums])
+    down_rows = group.laid(down_rows, 0, wide)
+    grad_down_weight, grad_down_down = down_rows[:, :width], down_rows[:, width:]
+    for block in d_far:
+        d_both = d_both + block.astype(wide)
+    first, second = d_both[:, :half], d_both[:, half:HD]
+    g_k = jnp.concatenate(
+        [first * cosine + second * sine, second * cosine - first * sine], axis=1
+    ).astype(low)
     g_v = d_both[:, HD:].astype(low)
     gi_q = mul_t(g_q, q_raise).astype(low)
     gi_k = mul_t(g_k, k_raise).astype(low)
@@ -1113,11 +1474,35 @@
     qkv_pack = jnp.concatenate(
         [g_qkv.reshape(n_f, own_rows, lin), gr_qkv.reshape(n_f, rank_rows, lin)], axis=1
     )
-    packs = scatter_whole((qkv_pack, o_pack), 6, n_seq)
-    packs, down_rows = tie((slab_sums,), (packs, down_rows))
+    qkv_pack, o_pack, grad_down_weight, grad_down_down, input_grad, far, own_branch = tie(
+        (), (qkv_pack, o_pack, grad_down_weight, grad_down_down, input_grad, far, sums[0])
+    )
+    for first, second in zip(far_first, far, strict=True):
+        own_branch = own_branch + jnp.concatenate([first, second], axis=0).astype(wide)
+    outputs = (mid + active * own_branch).astype(low).reshape(rows, length, width)
+
+    g_slab = slab_sums.done(wide)
+    unit_grad = g_slab[rank_rows:]
+    own_full = [
+        lax.dynamic_index_in_dim(full, lax.axis_index("fsdp"), 0, False)
+        for full in (gate_full, up_full)
+    ]
+    merged = jnp.concatenate(own_full, axis=1).astype(wide)
+    weight_grad = (unit_grad * gain2).astype(low)
+    mlp_small = jnp.concatenate(
+        [
+            mul_t(weight_grad[:, :slab], g_raise),
+            mul_t(weight_grad[:, slab:], u_raise),
+            jnp.broadcast_to(
+                jnp.sum(unit_grad * merged, axis=1, keepdims=True) / gain2, (own_rows, 128)
+            ),
+        ],
+        axis=1,
+    ).astype(low)
+    packs, slab_pieces, mlp_small = scatter_whole(
+        (qkv_pack, o_pack), g_slab.astype(low), mlp_small, 6, n_seq
+    )
     qkv_pack, o_pack = (pack.astype(wide) for pack in packs)
-    down_rows = group.laid(down_rows, 0, wide)
-    grad_down_weight, grad_down_down = down_rows[:, :width], down_rows[:, width:]
 
     grad_o_weight = o_pack[:o_rows]
     grad_o_up = o_pack[o_rows : o_rows + rank_rows]
@@ -1148,29 +1533,6 @@
     )
     grad_attn_gain = jnp.sum(unit_grad * own_lin, axis=1)
 
-    g_slab = slab_sums.done()
-    unit_grad = g_slab[rank_rows:]
-    own_full = [
-        lax.dynamic_slice_in_dim(full, lax.axis_index("fsdp") * own_rows, own_rows, 0)
-        for full in (gate_full, up_full)
-    ]
-    merged = jnp.concatenate(own_full, axis=1).astype(wide)
-    weight_grad = (unit_grad * gain2).astype(low)
-    mlp_small = Summing(
-        jnp.concatenate(
-            [
-                mul_t(weight_grad[:, :slab], g_raise),
-                mul_t(weight_grad[:, slab:], u_raise),
-                jnp.broadcast_to(
-                    jnp.sum(unit_grad * merged, axis=1, keepdims=True) / gain2, (own_rows, 128)
-                ),
-            ],
-            axis=1,
-        ),
-        ("seq",),
-    )
-    slab_pieces = gather_group(g_slab.astype(low), 7, n_seq)
-    mlp_small = mlp_small.done()
     grad_gate_down, grad_up_down = mlp_small[:, :rank], mlp_small[:, rank : 2 * rank]
     grad_mlp_gain = mlp_small[:, 2 * rank]
     grad_gate_weight, grad_up_weight, grad_gate_up, grad_up_up = place_columns(

time: 837 us -> 629 us (0.75)
  matrix products: 221 us -> 128 us
  local copies, waits for them, and re-layouts: 109 us -> 45.9 us
  other arithmetic: 86.3 us -> 40.5 us
  waiting for transfers between devices: 29.6 us -> 72.4 us
  between operations: 40 us -> 3.18 us
  Pallas kernels: 297 us -> 276 us
    dot_general x15 -> x10, matrix products: 75.2 us -> 29.5 us  [mul(): return jnp.dot(left, right, preferred_element_type=wide)]
    pallas_call x3 -> x2, Pallas kernels: 93.8 us -> 54.4 us  [gather_group(): pl.pallas_call(body, out_shape=jax.ShapeDtypeStruct((n_seq,) + block.shap...]
    dynamic_update_slice x24 -> x0, local copies, waits for them, and re-layouts: 39.1 us -> none  [the longest x8 15.7 us: keep_slab(): put(raises, block[rank_rows:, slab:], owner, 0)]
    pallas_call x2 -> x16, Pallas kernels: 56.7 us -> 88.5 us  [the longest x2 40.6 us: mlp_forward(): pl.pallas_call(body, grid=(stop - first,), out_shape=(jax.ShapeDtypeStruc...]
    convert_element_type x14 -> x4, other arithmetic: 29.9 us -> 5.59 us  [the longest x1 2.51 us: shards(): (mid + active * own_branch).astype(low).reshape(rows, length, width)]
    dot_general x6 -> x0, matrix products: 22.7 us -> none  [the longest x1 5.32 us: shards(): jnp.einsum('sqk,skd->sqd', weights.astype(low), values, preferred_element...]
    dot_general x16 -> x17, matrix products: 75.3 us -> 56.3 us  [mul_t(): lax.dot_general(left, right, (((1,), (1,)), ((), ())), preferred_element_...]
    ppermute x32, waiting for transfers between devices: 9.09 us -> 27.4 us  [hop(): return lax.ppermute(block, 'fsdp', self.up if way > 0 else self.down)]
  transfers between devices with their start and end apart: 51 -> 56, of which waited for: 4 -> 16; matrix products, arithmetic and copies ran while one was open for 37% -> 26% of each run, Pallas kernels for 36% -> 32%
where the time goes in v3:
time: 629 us; the launch traced here: 619 us
  Pallas kernels  276 us (44%)
  matrix products  128 us (20%)
  waiting for transfers between devices  72.4 us (12%)
  starting transfers between devices  52.7 us (8%)
  local copies, waits for them, and re-layouts  45.9 us (7%)
  other arithmetic  40.5 us (6%)
    pallas_call x1, Pallas kernels, scatter_whole(): pl.pallas_call(body, out_shape=tuple((jax.ShapeDtypeStruct(pack.shape[1:]...  63.1 us
    pallas_call x1, Pallas kernels, gather_whole(): pl.pallas_call(body, out_shape=tuple((jax.ShapeDtypeStruct((n_f,) + b.sha...  61.1 us
    dot_general x17, matrix products, mul_t(): lax.dot_general(left, right, (((1,), (1,)), ((), ())), preferred_element_...  56.3 us
    pallas_call x2, Pallas kernels, gather_group(): pl.pallas_call(body, out_shape=jax.ShapeDtypeStruct((n_seq,) + block.shap...  54.4 us
    dot_general x12, matrix products, t_mul(): lax.dot_general(left, right, (((0,), (0,)), ((), ())), preferred_element_...  42.5 us
    pallas_call x2, Pallas kernels, mlp_forward(): pl.pallas_call(body, grid=(stop - first,), out_shape=(jax.ShapeDtypeStruc...  40.6 us
    ppermute x32, starting transfers between devices, hop(): return lax.ppermute(block, 'fsdp', self.up if way > 0 else self.down)  35.9 us
    dot_general x10, matrix products, mul(): return jnp.dot(left, right, preferred_element_type=wide)  29.5 us
  transfers between devices with their start and end apart: 56, of which 16 were waited for; matrix products, arithmetic and copies ran while one was open for 26% of the time, Pallas kernels for 32%

profile of v3, /device:TPU:0, one launch (start us, length us, event | category | flops | bytes accessed | tf_op | source)
XLA Modules:
  0.0 619.1 jit_solution(11167373489517966506)
XLA Ops:
  8.0 3.0 collective-permute-start
  11.1 2.0 collective-permute-start.2
  17.1 2.0 pad_maximum_fusion.1.refs_0_
  28.2 61.1 %shard_map.477 = (bf16[8,144,2304]{2,1,0:T(8,128)(2,1)}, bf16[8,32,1536]{2,1,0:T(8,128)(2,1)}, bf16[8,128,1536]{2,1,0:T(8,128)(2,1)}, bf16[8,32,2560]{2,1,0:T(8,128)(2,1)}, bf16[8,144,512]{2,1,0:T(8,128)(2,1)}) custom-call(bf16[144,2304]{1,0:T(8,128)(2,1)} %copy-done.8, bf16[32,1536]{1,0:T(8,128)(2,1)} %copy-done.20, bf16[128,1536]{1,0:T(8,128)(2,1)} %copy-done.11, ...), custom_call_target="tpu_custom_call" | custom-call | tf_op jit(solution)/shard_map/pallas_call | solution.py:250
  89.3 6.2 fusion.105
  102.0 17.3 %shard_map.478.kv = bf16[4,512,512]{2,1,0:T(8,128)(2,1)} custom-call(bf16[512,512]{1,0:T(8,128)(2,1)} %pad_maximum_fusion.3.x), custom_call_target="tpu_custom_call" | custom-call | tf_op jit(solution)/shard_map/pallas_call | solution.py:319
  119.3 1.8 and_select_fusion.hidden
  121.1 6.7 %collective-permute-done.3.refs_3_ = bf16[176,3584]{1,0:T(8,128)(2,1)S(1)} collective-permute-done((bf16[176,3584]{1,0:T(8,128)(2,1)}, bf16[176,3584]{1,0:T(8,128)(2,1)S(1)}, u32[]{:S(2)}, u32[]{:S(2)}) %collective-permute-start.3) | collective-permute-done | bytes 1261600 | tf_op jit(solution)/shard_map/ppermute | solution.py:659
  132.1 5.2 shard_map.479
  137.4 4.4 fusion.10
  142.5 1.9 multiply_reduce_fusion.1
  145.9 12.1 %collective-permute-done.9 = bf16[512,1152]{1,0:T(8,128)(2,1)S(1)} collective-permute-done((bf16[512,1152]{1,0:T(8,128)(2,1)S(1)}, bf16[512,1152]{1,0:T(8,128)(2,1)S(1)}, u32[]{:S(2)}, u32[]{:S(2)}) %collective-permute-start.9) | collective-permute-done | bytes 1179680 | tf_op jit(solution)/shard_map/ppermute | solution.py:770
  160.4 1.6 collective-permute-start.10
  163.4 1.6 collective-permute-start.12
  166.8 37.1 %shard_map.480 = bf16[4,512,1152]{2,1,0:T(8,128)(2,1)} custom-call(bf16[512,1152]{1,0:T(8,128)(2,1)} %multiply_convert_fusion.1.x), custom_call_target="tpu_custom_call" | custom-call | tf_op jit(solution)/shard_map/pallas_call | solution.py:319
  205.7 1.6 collective-permute-start.14
  210.0 22.4 %shard_map.481 = (bf16[2048,1792]{1,0:T(8,128)(2,1)}, bf16[2048,1792]{1,0:T(8,128)(2,1)}, bf16[2048,1792]{1,0:T(8,128)(2,1)}, bf16[8,144,1792]{2,1,0:T(8,128)(2,...) custom-call(bf16[2048,1152]{1,0:T(8,128)(2,1)} %bitcast.146, ...), custom_call_target="tpu_custom_call" | custom-call | flops 3000000000 | bytes 3000000 | tf_op jit(solution)/shard_map/pallas_call | solution.py:1078
  233.6 1.6 collective-permute-start.18
  236.4 1.9 slice.348.raised
  238.4 18.2 %shard_map.482 = (bf16[2048,1792]{1,0:T(8,128)(2,1)}, bf16[2048,1792]{1,0:T(8,128)(2,1)}, bf16[2048,1792]{1,0:T(8,128)(2,1)}, bf16[8,144,1792]{2,1,0:T(8,128)(2,...) custom-call(bf16[2048,1152]{1,0:T(8,128)(2,1)} %bitcast.147, ...), custom_call_target="tpu_custom_call", output_to_operand_aliasing={{0}: (12, {}), {1}: (13, {}), {2}: (14, {}), {3}: (15, {}),... | custom-call | flops 3000000000 | bytes 3000000 | tf_op jit(solution)/shard_map/pallas_call | solution.py:1078
  256.6 1.9 dynamic-slice_bitcast_fusion
  260.1 1.8 collective-permute-start.21
  261.9 1.7 constant_dynamic-update-slice_fusion.2
  264.0 10.0 %convolution_convert_fusion = bf16[1792,1152]{1,0:T(8,128)(2,1)S(1)} fusion(bf16[2048,1792]{1,0:T(8,128)(2,1)S(1)} %copy-done.48, bf16[2048,1152]{1,0:T(8,128)(2,1)S(1)} %constant_dynamic-update-slice_fusion.g), kind=kOutput, calls=%fused_computation | convolution fusion | flops 8457781248 | bytes 16187392 | tf_op jit(solution)/shard_map/dot_general | solution.py:29
  274.1 1.6 collective-permute-start.26
  276.2 1.6 collective-permute-start.25
  278.3 23.0 %shard_map.484 = (bf16[2048,1792]{1,0:T(8,128)(2,1)}, bf16[2048,1792]{1,0:T(8,128)(2,1)}, bf16[1792,1152]{1,0:T(8,128)(2,1)}) custom-call(bf16[2048,1152]{1,0:T(8,128)(2,1)} %copy-done.47, bf16[256,1152]{1,0:T(8,128)(2,1)} %slice.348.raised, bf16[2048,1792]{1,0:T(8,128)(2,1)} %get-tuple-element.399.mul_g, bf16[2048,1792]{1,0:T(8,128)(2,1)} %get-tuple-element.400.mul_u, ...), custom_call_target="tpu_custom_call" | custom-call | flops 3000000000 | bytes 3000000 | tf_op jit(solution)/shard_map/pallas_call | solution.py:1140
  302.6 1.8 collective-permute-start.28
  304.4 13.6 %convolution_convert_fusion.4 = bf16[1152,1792]{1,0:T(8,128)(2,1)S(1)} fusion(bf16[2048,1152]{1,0:T(8,128)(2,1)} %bitcast.148, bf16[2048,1792]{1,0:T(8,128)(2,1)} %get-tuple-element.447), kind=kOutput, calls=%fused_computation.4 | convolution fusion | flops 8457781248 | bytes 16187392 | tf_op jit(solution)/shard_map/dot_general | solution.py:29
  318.0 1.6 collective-permute-start.29
  322.6 2.0 collective-permute-start.31
  324.7 9.8 %convolution_convert_fusion.3 = bf16[1152,1792]{1,0:T(8,128)(2,1)S(1)} fusion(bf16[2048,1152]{1,0:T(8,128)(2,1)S(1)} %bitcast.151, bf16[2048,1792]{1,0:T(8,128)(2,1)S(1)} %bitcast.209), kind=kOutput, calls=%fused_computation.3 | convolution fusion | flops 8457781248 | bytes 16187392 | tf_op jit(solution)/shard_map/dot_general | solution.py:29
  336.9 2.0 collective-permute-start.35
  340.1 2.2 collective-permute-start.33
  342.3 9.3 %fusion.3 = f32[1024,1152]{1,0:T(8,128)} fusion(bf16[1152,1792]{1,0:T(8,128)(2,1)S(1)} %bitcast.173, bf16[2048,1792]{1,0:T(8,128)(2,1)} %get-tuple-element.448), kind=kOutput, calls=%fused_computation.12 | convolution fusion | flops 4227858432 | bytes 12517376 | tf_op jit(solution)/shard_map/dot_general | solution.py:25
  351.7 9.8 %add_convert_fusion.1 = bf16[1024,1152]{1,0:T(8,128)(2,1)} fusion(f32[1024,1152]{1,0:T(8,128)} %fusion.3, bf16[1152,1792]{1,0:T(8,128)(2,1)S(1)} %bitcast.172, bf16[2048,1792]{1,0:T(8,128)(2,1)} %get-tuple-element.447), kind=kOutput, calls=%fused_computation.6 | convolution fusion | flops 4230217728 | bytes 14876672 | tf_op jit(solution)/shard_map/dot_general | solution.py:25
  366.4 2.4 collective-permute-start.37
  368.8 9.3 %fusion = f32[1024,1152]{1,0:T(8,128)} fusion(bf16[1152,1792]{1,0:T(8,128)(2,1)S(1)} %bitcast.174, bf16[2048,1792]{1,0:T(8,128)(2,1)} %get-tuple-element.448), kind=kOutput, calls=%fused_computation.9 | convolution fusion | flops 4227858432 | bytes 12517376 | tf_op jit(solution)/shard_map/dot_general | solution.py:25
  380.4 9.6 %add_convert_fusion = bf16[1024,1152]{1,0:T(8,128)(2,1)S(1)} fusion(f32[1024,1152]{1,0:T(8,128)} %fusion, bf16[1152,1792]{1,0:T(8,128)(2,1)} %bitcast.171, bf16[2048,1792]{1,0:T(8,128)(2,1)} %get-tuple-element.447), kind=kOutput, calls=%fused_computation.5 | convolution fusion | flops 4230217728 | bytes 14876672 | tf_op jit(solution)/shard_map/dot_general | solution.py:25
  390.0 5.7 collective-permute-done.39
  395.7 1.9 add_convert_fusion.3
  400.2 1.9 collective-permute-start.41
  402.3 13.5 %convolution_convert_fusion.2 = bf16[2048,1152]{1,0:T(8,128)(2,1)} fusion(bf16[2048,1792]{1,0:T(8,128)(2,1)S(1)} %bitcast.166, bf16[1792,1152]{1,0:T(8,128)(2,1)} %get-tuple-element.456), kind=kOutput, calls=%fused_computation.2 | convolution fusion | flops 8458076160 | bytes 16187392 | tf_op jit(solution)/shard_map/dot_general | solution.py:21
  415.8 9.5 %collective-permute-done.42 = bf16[512,1152]{1,0:T(8,128)(2,1)S(1)} collective-permute-done((bf16[512,1152]{1,0:T(8,128)(2,1)S(1)}, bf16[512,1152]{1,0:T(8,128)(2,1)S(1)}, u32[]{:S(2)}, u32[]{:S(2)}) %collective-permute-start.42) | collective-permute-done | bytes 1179680 | tf_op jit(solution)/shard_map/ppermute | solution.py:789
  425.3 3.9 collective-permute-done.40.refs_4_
  431.9 1.9 collective-permute-start.55
  433.8 2.6 collective-permute-done.55
  441.2 1.8 convert_add_fusion.1
  443.4 2.4 multiply_convert_fusion
  445.8 2.0 convolution_convert_fusion.14
  447.9 4.6 fusion.26.g
  452.5 1.7 convert_add_fusion.2
  454.1 13.1 %collective-permute-done.44.refs_4_ = bf16[176,3584]{1,0:T(8,128)(2,1)S(1)} collective-permute-done((bf16[176,3584]{1,0:T(8,128)(2,1)S(1)}, bf16[176,3584]{1,0:T(8,128)(2,1)S(1)}, u32[]{:S(2)}, u32[]{:S(2)}) %collective-permute-start.44) | collective-permute-done | bytes 1261600 | tf_op jit(solution)/shard_map/ppermute | solution.py:659
  473.3 11.3 %shard_map.493 = (bf16[512,1024]{1,0:T(8,128)(2,1)}, bf16[4,512,512]{2,1,0:T(8,128)(2,1)}) custom-call(bf16[512,1024]{1,0:T(8,128)(2,1)} %copy-done.29, bf16[4,512,512]{2,1,0:T(8,128)(2,1)} %shard_map.478.kv, f32[2,256,1024]{2,1,0:T(8,128)} %and_select_fusion.hidden, f32[2,4,256,1]{3,2,1,0:T(8,128)} %copy-done.32, bf16[512,1024]{1,0:T(8,128)(2,1)} %copy-done.30, ...), custom_call_target="tpu_custom_call" | custom-call | flops 3000000000 | bytes 3000000 | tf_op jit(solution)/shard_map/pallas_call | solution.py:972
  492.3 12.0 %collective-permute-done.52 = bf16[512,512]{1,0:T(8,128)(2,1)S(1)} collective-permute-done((bf16[512,512]{1,0:T(8,128)(2,1)S(1)}, bf16[512,512]{1,0:T(8,128)(2,1)S(1)}, u32[]{:S(2)}, u32[]{:S(2)}) %collective-permute-start.52) | collective-permute-done | bytes 524320 | tf_op jit(solution)/shard_map/ppermute | solution.py:789
  507.8 2.1 convolution_convert_fusion.1
  510.5 3.3 fusion.15
  521.5 2.2 slice.353
  524.6 2.4 maximum_maximum_fusion.refs_0_
  529.3 2.2 pad.4.refs_1_
  531.5 63.1 %shard_map.495 = (bf16[176,1536]{1,0:T(8,128)(2,1)}, bf16[192,1280]{1,0:T(8,128)(2,1)}, bf16[4,176,3584]{2,1,0:T(8,128)(2,1)}, f32[144,640]{1,0:T(8,128)}) custom-call(bf16[8,176,1536]{2,1,0:T(8,128)(2,1)} %maximum_maximum_fusion.refs_0_, bf16[8,192,1280]{2,1,0:T(8,128)(2,1)} %pad.4.refs_1_, bf16[176,3584]{1,0:T(8,128)(2,1)} %convert_element_type.306.refs_2_, ...), custom_call_target="tpu_custom_call" | custom-call | tf_op jit(solution)/shard_map/pallas_call | solution.py:562
  596.8 2.3 fusion.43
  605.0 8.4 %shard_map.496 = (f32[144,6912]{1,0:T(8,128)}, f32[144,6912]{1,0:T(8,128)}, f32[32,6912]{1,0:T(8,128)}, f32[32,6912]{1,0:T(8,128)}) custom-call(f32[144,1]{1,0:T(8,128)} %copy-done.7, bf16[4,176,3584]{2,1,0:T(8,128)(2,1)} %get-tuple-element.515.x), custom_call_target="tpu_custom_call" | custom-call | tf_op jit(solution)/shard_map/pallas_call | solution.py:891
  616.1 2.5 add_convert_fusion.2
  (470 shorter events, 113.3 us)
Async XLA Ops:
  8.0 81.3 %collective-permute-start = (bf16[176,3584]{1,0:T(8,128)(2,1)S(1)}, bf16[176,3584]{1,0:T(8,128)(2,1)}, u32[]{:S(2)}, u32[]{:S(2)}) collective-permute-start(bf16[176,3584]{1,0:T(8,128)(2,1)S(1)} %shard_map.475.refs_0_), channel_id=1, source_target_pairs={{0,1},{1,3},{3,5},{5,7},{7,6},{6,4},{4,2},{2,0},{8,9},{9,11},{11,1... | collective-permute-start | bytes 3784712 | tf_op jit(solution)/shard_map/ppermute | solution.py:659
  11.0 78.3 %collective-permute-start.1 = (bf16[176,3584]{1,0:T(8,128)(2,1)S(1)}, bf16[176,3584]{1,0:T(8,128)(2,1)}, u32[]{:S(2)}, u32[]{:S(2)}) collective-permute-start(bf16[176,3584]{1,0:T(8,128)(2,1)S(1)} %shard_map.475.refs_0_), channel_id=1, source_target_pairs={{1,0},{3,1},{5,3},{7,5},{6,7},{4,6},{2,4},{0,2},{9,8},{11,9},{13,1... | collective-permute-start | bytes 3784712 | tf_op jit(solution)/shard_map/ppermute | solution.py:659
  11.1 78.2 %collective-permute-start.2 = (bf16[2,256]{1,0:T(2,128)(2,1)S(1)}, bf16[2,256]{1,0:T(2,128)(2,1)S(1)}, u32[]{:S(2)}, u32[]{:S(2)}) collective-permute-start(bf16[2,256]{1,0:T(2,128)(2,1)S(1)} %convert_element_type.247), channel_id=1, source_target_pairs={{0,16},{8,24},{16,0},{24,8},{1,17},{9,25},{17,1},{25,9},{2,18},{10... | collective-permute-start | bytes 3080 | tf_op jit(solution)/shard_map/ppermute | solution.py:770
  20.1 79.8 %copy-start.35 = (f32[512,128]{1,0:T(8,128)}, f32[512,128]{1,0:T(8,128)S(1)}, u32[]{:S(2)}) copy-start(f32[512,128]{1,0:T(8,128)S(1)} %get-tuple-element.294.sin) | copy-start | bytes 786436
  20.1 79.8 %copy-start.37 = (f32[512,128]{1,0:T(8,128)}, f32[512,128]{1,0:T(8,128)S(1)}, u32[]{:S(2)}) copy-start(f32[512,128]{1,0:T(8,128)S(1)} %get-tuple-element.293.cos) | copy-start | bytes 786436
  21.1 121.4 %copy-start.101 = (f32[512]{0:T(512)}, f32[512]{0:T(512)S(1)}, u32[]{:S(2)}) copy-start(f32[512]{0:T(512)S(1)} %compare_convert_fusion) | copy-start | bytes 6148
  24.2 107.0 %copy-start.54 = (bf16[512,1152]{1,0:T(8,128)(2,1)}, bf16[512,1152]{1,0:T(8,128)(2,1)S(1)}, u32[]{:S(2)}) copy-start(bf16[512,1152]{1,0:T(8,128)(2,1)S(1)} %fusion.12) | copy-start | bytes 3538948
  96.2 23.1 %collective-permute-start.5 = (bf16[2,256]{1,0:T(2,128)(2,1)S(1)}, bf16[2,256]{1,0:T(2,128)(2,1)S(1)}, u32[]{:S(2)}, u32[]{:S(2)}) collective-permute-start(bf16[2,256]{1,0:T(2,128)(2,1)S(1)} %convert_element_type.247), channel_id=1, source_target_pairs={{0,8},{8,0},{16,24},{24,16},{1,9},{9,1},{17,25},{25,17},{2,10},{10... | collective-permute-start | bytes 3080 | tf_op jit(solution)/shard_map/ppermute | solution.py:776
  96.8 22.5 %collective-permute-start.6 = (bf16[2,256]{1,0:T(2,128)(2,1)S(1)}, bf16[2,256]{1,0:T(2,128)(2,1)S(1)}, u32[]{:S(2)}, u32[]{:S(2)}) collective-permute-start(bf16[2,256]{1,0:T(2,128)(2,1)S(1)} %collective-permute-done.2), channel_id=1, source_target_pairs={{0,8},{8,0},{16,24},{24,16},{1,9},{9,1},{17,25},{25,17},{2,10},{10... | collective-permute-start | bytes 3080 | tf_op jit(solution)/shard_map/ppermute | solution.py:776
  97.5 30.3 %collective-permute-start.3 = (bf16[176,3584]{1,0:T(8,128)(2,1)}, bf16[176,3584]{1,0:T(8,128)(2,1)S(1)}, u32[]{:S(2)}, u32[]{:S(2)}) collective-permute-start(bf16[176,3584]{1,0:T(8,128)(2,1)} %collective-permute-done.refs_1_), channel_id=1, source_target_pairs={{0,1},{1,3},{3,5},{5,7},{7,6},{6,4},{4,2},{2,0},{8,9},{9,11},{11,1... | collective-permute-start | bytes 3784712 | tf_op jit(solution)/shard_map/ppermute | solution.py:659
  99.0 30.2 %collective-permute-start.4 = (bf16[176,3584]{1,0:T(8,128)(2,1)}, bf16[176,3584]{1,0:T(8,128)(2,1)S(1)}, u32[]{:S(2)}, u32[]{:S(2)}) collective-permute-start(bf16[176,3584]{1,0:T(8,128)(2,1)} %collective-permute-done.1.refs_2_), channel_id=1, source_target_pairs={{1,0},{3,1},{5,3},{7,5},{6,7},{4,6},{2,4},{0,2},{9,8},{11,9},{13,1... | collective-permute-start | bytes 3784712 | tf_op jit(solution)/shard_map/ppermute | solution.py:659
  129.2 29.0 %collective-permute-start.7 = (bf16[176,3584]{1,0:T(8,128)(2,1)S(1)}, bf16[176,3584]{1,0:T(8,128)(2,1)S(1)}, u32[]{:S(2)}, u32[]{:S(2)}) collective-permute-start(bf16[176,3584]{1,0:T(8,128)(2,1)S(1)} %collective-permute-done.3.refs_3_), channel_id=1, source_target_pairs={{0,1},{1,3},{3,5},{5,7},{7,6},{6,4},{4,2},{2,0},{8,9},{9,11},{11,1... | collective-permute-start | bytes 3784712 | tf_op jit(solution)/shard_map/ppermute | solution.py:659
  130.8 28.7 %collective-permute-start.8 = (bf16[176,3584]{1,0:T(8,128)(2,1)S(1)}, bf16[176,3584]{1,0:T(8,128)(2,1)S(1)}, u32[]{:S(2)}, u32[]{:S(2)}) collective-permute-start(bf16[176,3584]{1,0:T(8,128)(2,1)S(1)} %collective-permute-done.4.refs_4_), channel_id=1, source_target_pairs={{1,0},{3,1},{5,3},{7,5},{6,7},{4,6},{2,4},{0,2},{9,8},{11,9},{13,1... | collective-permute-start | bytes 3784712 | tf_op jit(solution)/shard_map/ppermute | solution.py:659
  131.3 26.6 %collective-permute-start.9 = (bf16[512,1152]{1,0:T(8,128)(2,1)S(1)}, bf16[512,1152]{1,0:T(8,128)(2,1)S(1)}, u32[]{:S(2)}, u32[]{:S(2)}) collective-permute-start(bf16[512,1152]{1,0:T(8,128)(2,1)S(1)} %fusion.12), channel_id=1, source_target_pairs={{0,16},{8,24},{16,0},{24,8},{1,17},{9,25},{17,1},{25,9},{2,18},{10... | collective-permute-start | bytes 3538952 | tf_op jit(solution)/shard_map/ppermute | solution.py:770
  160.4 43.5 %collective-permute-start.10 = (bf16[176,1792]{1,0:T(8,128)(2,1)}, bf16[176,1792]{1,0:T(8,128)(2,1)S(1)}, u32[]{:S(2)}, u32[]{:S(2)}) collective-permute-start(bf16[176,1792]{1,0:T(8,128)(2,1)} %slice.268), channel_id=1, source_target_pairs={{0,1},{1,3},{3,5},{5,7},{7,6},{6,4},{4,2},{2,0},{8,9},{9,11},{11,1... | collective-permute-start | bytes 1892360 | tf_op jit(solution)/shard_map/ppermute | solution.py:659
  162.9 41.1 %collective-permute-start.11 = (bf16[176,1792]{1,0:T(8,128)(2,1)}, bf16[176,1792]{1,0:T(8,128)(2,1)S(1)}, u32[]{:S(2)}, u32[]{:S(2)}) collective-permute-start(bf16[176,1792]{1,0:T(8,128)(2,1)} %slice.269), channel_id=1, source_target_pairs={{1,0},{3,1},{5,3},{7,5},{6,7},{4,6},{2,4},{0,2},{9,8},{11,9},{13,1... | collective-permute-start | bytes 1892360 | tf_op jit(solution)/shard_map/ppermute | solution.py:659
  163.4 40.6 %collective-permute-start.12 = (bf16[216,1408]{1,0:T(8,128)(2,1)}, bf16[216,1408]{1,0:T(8,128)(2,1)}, u32[]{:S(2)}, u32[]{:S(2)}) collective-permute-start(bf16[216,1408]{1,0:T(8,128)(2,1)} %pad_maximum_fusion.1.refs_0_), channel_id=1, source_target_pairs={{0,1},{1,3},{3,5},{5,7},{7,6},{6,4},{4,2},{2,0},{8,9},{9,11},{11,1... | collective-permute-start | bytes 1824776 | tf_op jit(solution)/shard_map/ppermute | solution.py:659
  164.9 39.0 %collective-permute-start.13 = (bf16[216,1408]{1,0:T(8,128)(2,1)}, bf16[216,1408]{1,0:T(8,128)(2,1)}, u32[]{:S(2)}, u32[]{:S(2)}) collective-permute-start(bf16[216,1408]{1,0:T(8,128)(2,1)} %pad_maximum_fusion.1.refs_0_), channel_id=1, source_target_pairs={{1,0},{3,1},{5,3},{7,5},{6,7},{4,6},{2,4},{0,2},{9,8},{11,9},{13,1... | collective-permute-start | bytes 1824776 | tf_op jit(solution)/shard_map/ppermute | solution.py:659
  165.6 1.1 collective-permute-start.20
  204.0 28.4 %collective-permute-start.16 = (bf16[512,1152]{1,0:T(8,128)(2,1)S(1)}, bf16[512,1152]{1,0:T(8,128)(2,1)}, u32[]{:S(2)}, u32[]{:S(2)}) collective-permute-start(bf16[512,1152]{1,0:T(8,128)(2,1)S(1)} %copy-done.55), channel_id=1, source_target_pairs={{0,8},{8,0},{16,24},{24,16},{1,9},{9,1},{17,25},{25,17},{2,10},{10... | collective-permute-start | bytes 3538952 | tf_op jit(solution)/shard_map/ppermute | solution.py:776
  204.3 28.2 %collective-permute-start.17 = (bf16[512,1152]{1,0:T(8,128)(2,1)S(1)}, bf16[512,1152]{1,0:T(8,128)(2,1)S(1)}, u32[]{:S(2)}, u32[]{:S(2)}) collective-permute-start(bf16[512,1152]{1,0:T(8,128)(2,1)S(1)} %copy-done.78), channel_id=1, source_target_pairs={{0,8},{8,0},{16,24},{24,16},{1,9},{9,1},{17,25},{25,17},{2,10},{10... | collective-permute-start | bytes 3538952 | tf_op jit(solution)/shard_map/ppermute | solution.py:776
  205.7 26.7 %collective-permute-start.14 = (bf16[216,1408]{1,0:T(8,128)(2,1)}, bf16[216,1408]{1,0:T(8,128)(2,1)S(1)}, u32[]{:S(2)}, u32[]{:S(2)}) collective-permute-start(bf16[216,1408]{1,0:T(8,128)(2,1)} %collective-permute-done.12.refs_1_), channel_id=1, source_target_pairs={{0,1},{1,3},{3,5},{5,7},{7,6},{6,4},{4,2},{2,0},{8,9},{9,11},{11,1... | collective-permute-start | bytes 1824776 | tf_op jit(solution)/shard_map/ppermute | solution.py:659
  207.3 25.2 %collective-permute-start.15 = (bf16[216,1408]{1,0:T(8,128)(2,1)}, bf16[216,1408]{1,0:T(8,128)(2,1)}, u32[]{:S(2)}, u32[]{:S(2)}) collective-permute-start(bf16[216,1408]{1,0:T(8,128)(2,1)} %collective-permute-done.13.refs_2_), channel_id=1, source_target_pairs={{1,0},{3,1},{5,3},{7,5},{6,7},{4,6},{2,4},{0,2},{9,8},{11,9},{13,1... | collective-permute-start | bytes 1824776 | tf_op jit(solution)/shard_map/ppermute | solution.py:659
  233.6 24.9 %collective-permute-start.18 = (bf16[216,1408]{1,0:T(8,128)(2,1)S(1)}, bf16[216,1408]{1,0:T(8,128)(2,1)S(1)}, u32[]{:S(2)}, u32[]{:S(2)}) collective-permute-start(bf16[216,1408]{1,0:T(8,128)(2,1)S(1)} %collective-permute-done.14.refs_3_), channel_id=1, source_target_pairs={{0,1},{1,3},{3,5},{5,7},{7,6},{6,4},{4,2},{2,0},{8,9},{9,11},{11,1... | collective-permute-start | bytes 1824776 | tf_op jit(solution)/shard_map/ppermute | solution.py:659
  235.2 23.3 %collective-permute-start.19 = (bf16[216,1408]{1,0:T(8,128)(2,1)}, bf16[216,1408]{1,0:T(8,128)(2,1)S(1)}, u32[]{:S(2)}, u32[]{:S(2)}) collective-permute-start(bf16[216,1408]{1,0:T(8,128)(2,1)} %collective-permute-done.15.refs_4_), channel_id=1, source_target_pairs={{1,0},{3,1},{5,3},{7,5},{6,7},{4,6},{2,4},{0,2},{9,8},{11,9},{13,1... | collective-permute-start | bytes 1824776 | tf_op jit(solution)/shard_map/ppermute | solution.py:659
  258.6 15.4 %collective-permute-start.23 = (f32[6]{0:T(128)S(1)}, f32[6]{0:T(128)S(1)}, u32[]{:S(2)}, u32[]{:S(2)}) collective-permute-start(f32[6]{0:T(128)S(1)} %fusion.144), channel_id=1, source_target_pairs={{0,16},{8,24},{16,0},{24,8},{1,17},{9,25},{17,1},{25,9},{2,18},{10... | collective-permute-start | bytes 80 | tf_op jit(solution)/shard_map/ppermute | solution.py:818
  259.5 14.5 %collective-permute-start.22 = (bf16[216,768]{1,0:T(8,128)(2,1)S(1)}, bf16[216,768]{1,0:T(8,128)(2,1)S(1)}, u32[]{:S(2)}, u32[]{:S(2)}) collective-permute-start(bf16[216,768]{1,0:T(8,128)(2,1)S(1)} %slice.273), channel_id=1, source_target_pairs={{1,0},{3,1},{5,3},{7,5},{6,7},{4,6},{2,4},{0,2},{9,8},{11,9},{13,1... | collective-permute-start | bytes 995336 | tf_op jit(solution)/shard_map/ppermute | solution.py:659
  260.1 14.0 %collective-permute-start.21 = (bf16[216,640]{1,0:T(8,128)(2,1)S(1)}, bf16[216,640]{1,0:T(8,128)(2,1)S(1)}, u32[]{:S(2)}, u32[]{:S(2)}) collective-permute-start(bf16[216,640]{1,0:T(8,128)(2,1)S(1)} %slice.272), channel_id=1, source_target_pairs={{0,1},{1,3},{3,5},{5,7},{7,6},{6,4},{4,2},{2,0},{8,9},{9,11},{11,1... | collective-permute-start | bytes 829448 | tf_op jit(solution)/shard_map/ppermute | solution.py:659
  274.1 27.2 %collective-permute-start.26 = (f32[6]{0:T(128)S(1)}, f32[6]{0:T(128)S(1)}, u32[]{:S(2)}, u32[]{:S(2)}) collective-permute-start(f32[6]{0:T(128)S(1)} %add.259), channel_id=1, source_target_pairs={{0,1},{1,0},{2,3},{3,2},{4,5},{5,4},{6,7},{7,6},{8,9},{9,8},{10,11... | collective-permute-start | bytes 80 | tf_op jit(solution)/shard_map/ppermute | solution.py:818
  276.2 25.1 %collective-permute-start.25 = (bf16[216,640]{1,0:T(8,128)(2,1)S(1)}, bf16[216,640]{1,0:T(8,128)(2,1)S(1)}, u32[]{:S(2)}, u32[]{:S(2)}) collective-permute-start(bf16[216,640]{1,0:T(8,128)(2,1)S(1)} %get-tuple-element.396), channel_id=1, source_target_pairs={{1,0},{3,1},{5,3},{7,5},{6,7},{4,6},{2,4},{0,2},{9,8},{11,9},{13,1... | collective-permute-start | bytes 829448 | tf_op jit(solution)/shard_map/ppermute | solution.py:659
  277.8 23.4 %collective-permute-start.24 = (bf16[216,512]{1,0:T(8,128)(2,1)S(1)}, bf16[216,512]{1,0:T(8,128)(2,1)S(1)}, u32[]{:S(2)}, u32[]{:S(2)}) collective-permute-start(bf16[216,512]{1,0:T(8,128)(2,1)S(1)} %get-tuple-element.395), channel_id=1, source_target_pairs={{0,1},{1,3},{3,5},{5,7},{7,6},{6,4},{4,2},{2,0},{8,9},{9,11},{11,1... | collective-permute-start | bytes 663560 | tf_op jit(solution)/shard_map/ppermute | solution.py:659
  302.1 19.5 %collective-permute-start.27 = (bf16[216,1152]{1,0:T(8,128)(2,1)S(1)}, bf16[216,1152]{1,0:T(8,128)(2,1)S(1)}, u32[]{:S(2)}, u32[]{:S(2)}) collective-permute-start(bf16[216,1152]{1,0:T(8,128)(2,1)S(1)} %get-tuple-element.415), channel_id=1, source_target_pairs={{0,1},{1,3},{3,5},{5,7},{7,6},{6,4},{4,2},{2,0},{8,9},{9,11},{11,1... | collective-permute-start | bytes 1493000 | tf_op jit(solution)/shard_map/ppermute | solution.py:659
  302.6 19.0 %collective-permute-start.28 = (bf16[216,1152]{1,0:T(8,128)(2,1)S(1)}, bf16[216,1152]{1,0:T(8,128)(2,1)S(1)}, u32[]{:S(2)}, u32[]{:S(2)}) collective-permute-start(bf16[216,1152]{1,0:T(8,128)(2,1)S(1)} %get-tuple-element.416), channel_id=1, source_target_pairs={{1,0},{3,1},{5,3},{7,5},{6,7},{4,6},{2,4},{0,2},{9,8},{11,9},{13,1... | collective-permute-start | bytes 1493000 | tf_op jit(solution)/shard_map/ppermute | solution.py:659
  318.0 3.6 collective-permute-start.29
  322.6 13.3 %collective-permute-start.30 = (bf16[216,1152]{1,0:T(8,128)(2,1)S(1)}, bf16[216,1152]{1,0:T(8,128)(2,1)S(1)}, u32[]{:S(2)}, u32[]{:S(2)}) collective-permute-start(bf16[216,1152]{1,0:T(8,128)(2,1)S(1)} %get-tuple-element.422), channel_id=1, source_target_pairs={{0,1},{1,3},{3,5},{5,7},{7,6},{6,4},{4,2},{2,0},{8,9},{9,11},{11,1... | collective-permute-start | bytes 1493000 | tf_op jit(solution)/shard_map/ppermute | solution.py:659
  322.6 13.2 %collective-permute-start.31 = (bf16[216,1152]{1,0:T(8,128)(2,1)S(1)}, bf16[216,1152]{1,0:T(8,128)(2,1)S(1)}, u32[]{:S(2)}, u32[]{:S(2)}) collective-permute-start(bf16[216,1152]{1,0:T(8,128)(2,1)S(1)} %get-tuple-element.423), channel_id=1, source_target_pairs={{1,0},{3,1},{5,3},{7,5},{6,7},{4,6},{2,4},{0,2},{9,8},{11,9},{13,1... | collective-permute-start | bytes 1493000 | tf_op jit(solution)/shard_map/ppermute | solution.py:659
  336.8 24.6 %collective-permute-start.34 = (bf16[216,1152]{1,0:T(8,128)(2,1)S(1)}, bf16[216,1152]{1,0:T(8,128)(2,1)S(1)}, u32[]{:S(2)}, u32[]{:S(2)}) collective-permute-start(bf16[216,1152]{1,0:T(8,128)(2,1)S(1)} %get-tuple-element.441), channel_id=1, source_target_pairs={{0,1},{1,3},{3,5},{5,7},{7,6},{6,4},{4,2},{2,0},{8,9},{9,11},{11,1... | collective-permute-start | bytes 1493000 | tf_op jit(solution)/shard_map/ppermute | solution.py:659
  336.9 24.5 %collective-permute-start.35 = (bf16[216,1152]{1,0:T(8,128)(2,1)S(1)}, bf16[216,1152]{1,0:T(8,128)(2,1)S(1)}, u32[]{:S(2)}, u32[]{:S(2)}) collective-permute-start(bf16[216,1152]{1,0:T(8,128)(2,1)S(1)} %get-tuple-element.442), channel_id=1, source_target_pairs={{1,0},{3,1},{5,3},{7,5},{6,7},{4,6},{2,4},{0,2},{9,8},{11,9},{13,1... | collective-permute-start | bytes 1493000 | tf_op jit(solution)/shard_map/ppermute | solution.py:659
  340.0 25.5 %collective-permute-start.32 = (bf16[176,1792]{1,0:T(8,128)(2,1)S(1)}, bf16[176,1792]{1,0:T(8,128)(2,1)S(1)}, u32[]{:S(2)}, u32[]{:S(2)}) collective-permute-start(bf16[176,1792]{1,0:T(8,128)(2,1)S(1)} %get-tuple-element.433), channel_id=1, source_target_pairs={{0,1},{1,3},{3,5},{5,7},{7,6},{6,4},{4,2},{2,0},{8,9},{9,11},{11,1... | collective-permute-start | bytes 1892360 | tf_op jit(solution)/shard_map/ppermute | solution.py:659
  340.1 25.4 %collective-permute-start.33 = (bf16[176,1792]{1,0:T(8,128)(2,1)S(1)}, bf16[176,1792]{1,0:T(8,128)(2,1)S(1)}, u32[]{:S(2)}, u32[]{:S(2)}) collective-permute-start(bf16[176,1792]{1,0:T(8,128)(2,1)S(1)} %get-tuple-element.434), channel_id=1, source_target_pairs={{1,0},{3,1},{5,3},{7,5},{6,7},{4,6},{2,4},{0,2},{9,8},{11,9},{13,1... | collective-permute-start | bytes 1892360 | tf_op jit(solution)/shard_map/ppermute | solution.py:659
  366.2 29.4 %collective-permute-start.36 = (bf16[176,3584]{1,0:T(8,128)(2,1)S(1)}, bf16[176,3584]{1,0:T(8,128)(2,1)S(1)}, u32[]{:S(2)}, u32[]{:S(2)}) collective-permute-start(bf16[176,3584]{1,0:T(8,128)(2,1)S(1)} %get-tuple-element.445), channel_id=1, source_target_pairs={{0,1},{1,3},{3,5},{5,7},{7,6},{6,4},{4,2},{2,0},{8,9},{9,11},{11,1... | collective-permute-start | bytes 3784712 | tf_op jit(solution)/shard_map/ppermute | solution.py:659
  366.4 29.3 %collective-permute-start.37 = (bf16[176,3584]{1,0:T(8,128)(2,1)S(1)}, bf16[176,3584]{1,0:T(8,128)(2,1)S(1)}, u32[]{:S(2)}, u32[]{:S(2)}) collective-permute-start(bf16[176,3584]{1,0:T(8,128)(2,1)S(1)} %get-tuple-element.446), channel_id=1, source_target_pairs={{1,0},{3,1},{5,3},{7,5},{6,7},{4,6},{2,4},{0,2},{9,8},{11,9},{13,1... | collective-permute-start | bytes 3784712 | tf_op jit(solution)/shard_map/ppermute | solution.py:659
  379.2 16.5 %collective-permute-start.38 = (bf16[512,1152]{1,0:T(8,128)(2,1)}, bf16[512,1152]{1,0:T(8,128)(2,1)}, u32[]{:S(2)}, u32[]{:S(2)}) collective-permute-start(bf16[512,1152]{1,0:T(8,128)(2,1)} %slice.280), channel_id=1, source_target_pairs={{0,8},{8,0},{16,24},{24,16},{1,9},{9,1},{17,25},{25,17},{2,10},{10... | collective-permute-start | bytes 3538952 | tf_op jit(solution)/shard_map/ppermute | solution.py:780
  379.2 16.5 %collective-permute-start.39 = (bf16[216,1408]{1,0:T(8,128)(2,1)}, bf16[216,1408]{1,0:T(8,128)(2,1)}, u32[]{:S(2)}, u32[]{:S(2)}) collective-permute-start(bf16[216,1408]{1,0:T(8,128)(2,1)} %pad_maximum_fusion.2), channel_id=1, source_target_pairs={{0,16},{8,24},{16,0},{24,8},{1,17},{9,25},{17,1},{25,9},{2,18},{10... | collective-permute-start | bytes 1824776 | tf_op jit(solution)/shard_map/ppermute | solution.py:770
  397.6 27.7 %collective-permute-start.42 = (bf16[512,1152]{1,0:T(8,128)(2,1)S(1)}, bf16[512,1152]{1,0:T(8,128)(2,1)S(1)}, u32[]{:S(2)}, u32[]{:S(2)}) collective-permute-start(bf16[512,1152]{1,0:T(8,128)(2,1)S(1)} %add_convert_fusion.3), channel_id=1, source_target_pairs={{0,16},{8,24},{16,0},{24,8},{1,17},{9,25},{17,1},{25,9},{2,18},{10... | collective-permute-start | bytes 3538952 | tf_op jit(solution)/shard_map/ppermute | solution.py:789
  400.0 29.1 %collective-permute-start.40 = (bf16[176,3584]{1,0:T(8,128)(2,1)S(1)}, bf16[176,3584]{1,0:T(8,128)(2,1)S(1)}, u32[]{:S(2)}, u32[]{:S(2)}) collective-permute-start(bf16[176,3584]{1,0:T(8,128)(2,1)S(1)} %get-tuple-element.453), channel_id=1, source_target_pairs={{0,1},{1,3},{3,5},{5,7},{7,6},{6,4},{4,2},{2,0},{8,9},{9,11},{11,1... | collective-permute-start | bytes 3784712 | tf_op jit(solution)/shard_map/ppermute | solution.py:659
  400.2 29.0 %collective-permute-start.41 = (bf16[176,3584]{1,0:T(8,128)(2,1)S(1)}, bf16[176,3584]{1,0:T(8,128)(2,1)S(1)}, u32[]{:S(2)}, u32[]{:S(2)}) collective-permute-start(bf16[176,3584]{1,0:T(8,128)(2,1)S(1)} %get-tuple-element.454), channel_id=1, source_target_pairs={{1,0},{3,1},{5,3},{7,5},{6,7},{4,6},{2,4},{0,2},{9,8},{11,9},{13,1... | collective-permute-start | bytes 3784712 | tf_op jit(solution)/shard_map/ppermute | solution.py:659
  402.2 23.1 %collective-permute-start.43 = (bf16[512,1152]{1,0:T(8,128)(2,1)S(1)}, bf16[512,1152]{1,0:T(8,128)(2,1)S(1)}, u32[]{:S(2)}, u32[]{:S(2)}) collective-permute-start(bf16[512,1152]{1,0:T(8,128)(2,1)S(1)} %slice.282), channel_id=1, source_target_pairs={{0,8},{8,0},{16,24},{24,16},{1,9},{9,1},{17,25},{25,17},{2,10},{10... | collective-permute-start | bytes 3538952 | tf_op jit(solution)/shard_map/ppermute | solution.py:780
  430.6 10.5 %collective-permute-start.47 = (bf16[512,1152]{1,0:T(8,128)(2,1)S(1)}, bf16[512,1152]{1,0:T(8,128)(2,1)}, u32[]{:S(2)}, u32[]{:S(2)}) collective-permute-start(bf16[512,1152]{1,0:T(8,128)(2,1)S(1)} %slice.287), channel_id=1, source_target_pairs={{0,8},{8,0},{16,24},{24,16},{1,9},{9,1},{17,25},{25,17},{2,10},{10... | collective-permute-start | bytes 3538952 | tf_op jit(solution)/shard_map/ppermute | solution.py:784
  431.9 4.5 collective-permute-start.55
  438.2 29.0 %collective-permute-start.44 = (bf16[176,3584]{1,0:T(8,128)(2,1)S(1)}, bf16[176,3584]{1,0:T(8,128)(2,1)S(1)}, u32[]{:S(2)}, u32[]{:S(2)}) collective-permute-start(bf16[176,3584]{1,0:T(8,128)(2,1)S(1)} %get-tuple-element.461), channel_id=1, source_target_pairs={{0,1},{1,3},{3,5},{5,7},{7,6},{6,4},{4,2},{2,0},{8,9},{9,11},{11,1... | collective-permute-start | bytes 3784712 | tf_op jit(solution)/shard_map/ppermute | solution.py:659
  439.0 28.8 %collective-permute-start.45 = (bf16[176,3584]{1,0:T(8,128)(2,1)S(1)}, bf16[176,3584]{1,0:T(8,128)(2,1)S(1)}, u32[]{:S(2)}, u32[]{:S(2)}) collective-permute-start(bf16[176,3584]{1,0:T(8,128)(2,1)S(1)} %get-tuple-element.462), channel_id=1, source_target_pairs={{1,0},{3,1},{5,3},{7,5},{6,7},{4,6},{2,4},{0,2},{9,8},{11,9},{13,1... | collective-permute-start | bytes 3784712 | tf_op jit(solution)/shard_map/ppermute | solution.py:659
  442.9 9.5 %collective-permute-start.46 = (bf16[512,1152]{1,0:T(8,128)(2,1)S(1)}, bf16[512,1152]{1,0:T(8,128)(2,1)S(1)}, u32[]{:S(2)}, u32[]{:S(2)}) collective-permute-start(bf16[512,1152]{1,0:T(8,128)(2,1)S(1)} %get-tuple-element.534), channel_id=1, source_target_pairs={{0,8},{8,0},{16,24},{24,16},{1,9},{9,1},{17,25},{25,17},{2,10},{10... | collective-permute-start | bytes 3538952 | tf_op jit(solution)/shard_map/ppermute | solution.py:784
  468.7 15.9 %collective-permute-start.50 = (bf16[256,1152]{1,0:T(8,128)(2,1)}, bf16[256,1152]{1,0:T(8,128)(2,1)}, u32[]{:S(2)}, u32[]{:S(2)}) collective-permute-start(bf16[256,1152]{1,0:T(8,128)(2,1)} %slice.528), channel_id=1, source_target_pairs={{0,16},{8,24},{16,0},{24,8},{1,17},{9,25},{17,1},{25,9},{2,18},{10... | collective-permute-start | bytes 1769480 | tf_op jit(solution)/shard_map/ppermute | solution.py:789
  470.0 14.6 %collective-permute-start.48 = (bf16[216,1408]{1,0:T(8,128)(2,1)}, bf16[216,1408]{1,0:T(8,128)(2,1)}, u32[]{:S(2)}, u32[]{:S(2)}) collective-permute-start(bf16[216,1408]{1,0:T(8,128)(2,1)} %pad_maximum_fusion.2), channel_id=1, source_target_pairs={{0,8},{8,0},{16,24},{24,16},{1,9},{9,1},{17,25},{25,17},{2,10},{10... | collective-permute-start | bytes 1824776 | tf_op jit(solution)/shard_map/ppermute | solution.py:776
  470.0 14.6 %collective-permute-start.49 = (bf16[216,1408]{1,0:T(8,128)(2,1)}, bf16[216,1408]{1,0:T(8,128)(2,1)}, u32[]{:S(2)}, u32[]{:S(2)}) collective-permute-start(bf16[216,1408]{1,0:T(8,128)(2,1)} %collective-permute-done.39), channel_id=1, source_target_pairs={{0,8},{8,0},{16,24},{24,16},{1,9},{9,1},{17,25},{25,17},{2,10},{10... | collective-permute-start | bytes 1824776 | tf_op jit(solution)/shard_map/ppermute | solution.py:776
  485.9 4.1 collective-permute-start.51
  486.0 4.1 collective-permute-start.53
  490.4 14.0 %collective-permute-start.52 = (bf16[512,512]{1,0:T(8,128)(2,1)S(1)}, bf16[512,512]{1,0:T(8,128)(2,1)S(1)}, u32[]{:S(2)}, u32[]{:S(2)}) collective-permute-start(bf16[512,512]{1,0:T(8,128)(2,1)S(1)} %get-tuple-element.538), channel_id=1, source_target_pairs={{0,16},{8,24},{16,0},{24,8},{1,17},{9,25},{17,1},{25,9},{2,18},{10... | collective-permute-start | bytes 1572872 | tf_op jit(solution)/shard_map/ppermute | solution.py:789
  513.9 14.5 %collective-permute-start.54 = (bf16[256,1152]{1,0:T(8,128)(2,1)S(1)}, bf16[256,1152]{1,0:T(8,128)(2,1)S(1)}, u32[]{:S(2)}, u32[]{:S(2)}) collective-permute-start(bf16[256,1152]{1,0:T(8,128)(2,1)S(1)} %slice.527), channel_id=1, source_target_pairs={{0,16},{8,24},{16,0},{24,8},{1,17},{9,25},{17,1},{25,9},{2,18},{10... | collective-permute-start | bytes 1769480 | tf_op jit(solution)/shard_map/ppermute | solution.py:789
  531.5 64.3 %copy-start.69 = (f32[144,1024]{1,0:T(8,128)S(1)}, f32[144,1024]{1,0:T(8,128)}, u32[]{:S(2)}) copy-start(f32[144,1024]{1,0:T(8,128)} %fusion.32) | copy-start | bytes 1769476
  531.5 64.3 %copy-start.87 = (f32[144,256]{1,0:T(8,128)S(1)}, f32[144,256]{1,0:T(8,128)}, u32[]{:S(2)}) copy-start(f32[144,256]{1,0:T(8,128)} %fusion.36) | copy-start | bytes 442372
  531.5 64.3 %copy-start.88 = (f32[144,256]{1,0:T(8,128)S(1)}, f32[144,256]{1,0:T(8,128)}, u32[]{:S(2)}) copy-start(f32[144,256]{1,0:T(8,128)} %fusion.37) | copy-start | bytes 442372
  531.5 64.3 %copy-start.105 = (f32[144]{0:T(256)S(1)}, f32[144]{0:T(256)}, u32[]{:S(2)}) copy-start(f32[144]{0:T(256)} %copy-done.104) | copy-start | bytes 1732
  (114 other events, 894.4 us)

commit v4 on v3

--- a/solution.py
+++ b/solution.py
@@ -462,6 +462,10 @@
                 {"fsdp": here.at(flip(j) * way)},
             )
 
+        def swap(j, k, spot):
+            slot = parts[j].at[spot]
+            return remote(slot, slot, y_s.at[j, k], y_r.at[j, k], {"seq": here.seq(-k, 0)})
+
         def far_block(k):
             return remote(
                 block_in, block_out.at[k * CORES], far_s.at[k], far_r.at[k], {"seq": here.seq(-k, 0)}
@@ -515,18 +519,13 @@
                             hop(j, 1, way).wait_recv()
                             total = total + moves[j][steps.index((1, way))].astype(wide)
                     parts[j][here.y] = total.astype(low)
-
-        def swap(j, k, spot):
-            slot = parts[j].at[spot]
-            return remote(slot, slot, y_s.at[j, k], y_r.at[j, k], {"seq": here.seq(-k, 0)})
+                    for k in range(1, chips):
+                        go(swap(j, k, here.y))
 
         def side(j, core):
             columns = outs[j].at[:, share(j, core)]
             return remote(columns, columns, side_s.at[j], side_r.at[j], {"seq": here.seq(0, 1)})
 
-        for j in range(count):
-            for k in range(1, chips):
-                go(swap(j, k, here.y))
         for k in range(1, chips):
             far_small(k, here.seq(k, 0)).wait_recv()
             go(near_small(k, here.seq(k, 0)))
@@ -906,6 +905,45 @@
     return value, slope
 
 
+def project(unit, side, ups, cosine, sine, hq, rank):
+    tokens = unit.shape[0]
+    lin = hq + 2 * HD
+    half = HD // 2
+
+    def body(x, weights, raises, cos, sin, queries, both, inner):
+        low_inner = mul(x[...], weights[:, lin:]).astype(low)
+        inner[...] = low_inner
+
+        def head(at, own):
+            columns = slice(at, at + HD)
+            return mul(x[...], weights[:, columns]) + mul(
+                low_inner[:, own * rank : (own + 1) * rank], raises[:, columns]
+            )
+
+        def turned(values):
+            first, second = values[:, :half], values[:, half:]
+            c, s = cos[...], sin[...]
+            return jnp.concatenate(
+                [first * c - second * s, second * c + first * s], axis=1
+            ).astype(low)
+
+        for at in range(0, hq, HD):
+            queries[:, at : at + HD] = turned(head(at, 0))
+        both[:, :HD] = turned(head(hq, 1))
+        both[:, HD:] = head(hq + HD, 2).astype(low)
+
+    return pl.pallas_call(
+        body,
+        out_shape=(
+            jax.ShapeDtypeStruct((tokens, hq), low),
+            jax.ShapeDtypeStruct((tokens, 2 * HD), low),
+            jax.ShapeDtypeStruct((tokens, 3 * rank), low),
+        ),
+        cost_estimate=brief(2),
+        compiler_params=pltpu.CompilerParams(vmem_limit_bytes=48 * 2**20),
+    )(unit, side, ups, cosine, sine)
+
+
 def attention(queries, both, mask, rows):
     n_seq, tokens, _ = both.shape
     length = tokens // rows
@@ -978,6 +1016,76 @@
         cost_estimate=brief(3),
         compiler_params=pltpu.CompilerParams(vmem_limit_bytes=56 * 2**20),
     )(queries, both, mask, log_total, out, g_out, cosine, sine)
+
+
+def by_owner(out, first, product, n_f):
+    rows = product.shape[0] // n_f
+    for f in range(n_f):
+        out[f, first : first + rows, :] = product[f * rows : (f + 1) * rows].astype(low)
+    return first + rows
+
+
+def output_gradients(attn, inner, g_branch, ready, n_f):
+    columns = g_branch.shape[1]
+    sizes = [part.shape[-2] if part.ndim == 3 else part.shape[1] // n_f for part in (attn, inner, ready)]
+
+    def body(a, b, g, done, out):
+        first = by_owner(out, 0, t_mul(a[...], g[...]), n_f)
+        first = by_owner(out, first, t_mul(b[...], g[...]), n_f)
+        out[:, first:, :] = done[...]
+
+    return pl.pallas_call(
+        body,
+        out_shape=jax.ShapeDtypeStruct((n_f, sum(sizes), columns), low),
+        cost_estimate=brief(2),
+        compiler_params=pltpu.CompilerParams(vmem_limit_bytes=40 * 2**20),
+    )(attn, inner, g_branch, ready)
+
+
+def query_gradients(unit, inner, g_q, raises, side, hq, rank, n_f):
+    tokens, width = unit.shape
+    lin = hq + 2 * HD
+    rows = width // n_f + rank // n_f
+
+    def body(x, low_inner, g, ups, weights, e1, out):
+        g_inner = mul_t(g[...], ups[:, :hq]).astype(low)
+        e1[...] = mul_t(g[...], weights[:, :hq]) + mul_t(g_inner, weights[:, lin : lin + rank])
+        first = by_owner(out, 0, t_mul(x[...], g[...]), n_f)
+        by_owner(out, first, t_mul(low_inner[...], g[...]), n_f)
+
+    return pl.pallas_call(
+        body,
+        out_shape=(
+            jax.ShapeDtypeStruct((tokens, width), wide),
+            jax.ShapeDtypeStruct((n_f, rows, hq), low),
+        ),
+        cost_estimate=brief(2),
+        compiler_params=pltpu.CompilerParams(vmem_limit_bytes=48 * 2**20),
+    )(unit, inner, g_q, raises, side)
+
+
+def lay_rows(pieces, cut_at, n_seq):
+    rows, columns = pieces[0].shape
+    chips = n_seq // CORES
+
+    def body(*refs):
+        me = lax.axis_index("seq")
+        y, core = me // CORES, lax.rem(me, CORES)
+        for at, ref in enumerate(refs[:n_seq]):
+            spot = lax.rem(y + at // CORES, chips) * CORES + lax.rem(core + at % CORES, CORES)
+            refs[n_seq][spot] = ref[:, :cut_at].astype(wide)
+            refs[n_seq + 1][spot] = ref[:, cut_at:].astype(wide)
+
+    results = pl.pallas_call(
+        body,
+        out_shape=(
+            jax.ShapeDtypeStruct((n_seq, rows, cut_at), wide),
+            jax.ShapeDtypeStruct((n_seq, rows, columns - cut_at), wide),
+        ),
+        cost_estimate=brief(1),
+        compiler_params=pltpu.CompilerParams(vmem_limit_bytes=32 * 2**20),
+    )(*pieces)
+    return [result.reshape(n_seq * rows, -1) for result in results]
 
 
 def landing(items, buffers, rows_first, sem, here):
@@ -1259,25 +1367,8 @@
 
     slabs.advance()
     seg_pieces = group.across(seg_pieces)
-    projected = mul(unit1, qkv_side)
-    inner = projected[:, lin:].astype(low)
-    q_inner, k_inner, v_inner = inner[:, :rank], inner[:, rank : 2 * rank], inner[:, 2 * rank :]
-    q_lin = projected[:, :hq] + mul(q_inner, q_raise)
-    k_lin = projected[:, hq : hq + kv] + mul(k_inner, k_raise)
-    v_lin = projected[:, hq + kv : lin] + mul(v_inner, v_raise)
     half = HD // 2
-
-    def rope(values):
-        parts = []
-        for at in range(0, values.shape[1], HD):
-            first, second = values[:, at : at + half], values[:, at + half : at + HD]
-            parts += [first * cosine - second * sine, second * cosine + first * sine]
-        return jnp.concatenate(parts, axis=1)
-
-    queries = rope(q_lin).astype(low)
-    keys = rope(k_lin).astype(low)
-    values = v_lin.astype(low)
-    both = jnp.concatenate([keys, values], axis=-1)
+    queries, both, inner = project(unit1, qkv_side, ups, cosine, sine, hq, rank)
     both = gather_group(both, 2, n_seq)
     key_seg = jnp.concatenate(seg_pieces, axis=1).astype(jnp.int32)
     key_place = jnp.concatenate(
@@ -1416,41 +1507,33 @@
     g_branch = (active * g_mid).astype(low)
     g_inner = mul_t(g_branch, o_raise).astype(low)
     g_attn = mul_t(jnp.concatenate([g_branch, g_inner], axis=1), side_o).astype(low)
+    g_attn, terms, near, g_mid, g_branch, down_rows = tie(
+        (slab_sums,), (g_attn, terms, near, g_mid, g_branch, down_rows)
+    )
+
+    down_rows = group.across(down_rows)
     sums = [terms[k * CORES].astype(wide) + near[k].astype(wide) for k in chips]
-    g_attn, sums, g_mid, g_branch, down_rows = tie(
-        (slab_sums,), (g_attn, sums, g_mid, g_branch, down_rows)
-    )
-
     middle = tokens // 2
-    down_rows = group.across(down_rows)
     far_first = group.send([block[:middle] for block in sums])
     g_q, d_terms = attention_back(
         queries, both, mask, log_total, attn_low, g_attn, cosine, sine, rows
     )
-    d_terms, g_q, g_mid, g_branch, down_rows, sums, far_first = tie(
-        (), (d_terms, g_q, g_mid, g_branch, down_rows, sums, far_first)
+    o_pack = output_gradients(
+        attn_low, o_inner, g_branch, gd_raise.reshape(n_f, rank_rows, width), n_f
+    )
+    d_terms, g_q, g_mid, o_pack, down_rows, sums, far_first = tie(
+        (), (d_terms, g_q, g_mid, o_pack, down_rows, sums, far_first)
     )
 
     d_near = group.cross([d_terms[i] for i in range(n_seq)])
-    g_o = t_mul(attn_low, g_branch).astype(low)
-    go_raise = t_mul(o_inner, g_branch).astype(low)
-    o_pack = jnp.concatenate(
-        [
-            g_o.reshape(n_f, o_rows, width),
-            go_raise.reshape(n_f, rank_rows, width),
-            gd_raise.reshape(n_f, rank_rows, width),
-        ],
-        axis=1,
-    )
     d_sums = [d_terms[k * CORES].astype(wide) + d_near[k].astype(wide) for k in chips]
     d_far = group.send(d_sums)
-    d_far, g_q, d_both, o_pack, down_rows, sums = tie(
-        (), (d_far, g_q, d_sums[0], o_pack, down_rows, sums)
-    )
-
-    far = group.send([block[middle:] for block in sums])
-    down_rows = group.laid(down_rows, 0, wide)
-    grad_down_weight, grad_down_down = down_rows[:, :width], down_rows[:, width:]
+    e1, q_pack = query_gradients(unit1, q_inner, g_q, ups, qkv_side, hq, rank, n_f)
+    grad_down_weight, grad_down_down = lay_rows(down_rows, width, n_seq)
+    d_far, e1, d_both, q_pack, grad_down_weight, grad_down_down = tie(
+        (), (d_far, e1, d_sums[0], q_pack, grad_down_weight, grad_down_down)
+    )
+
     for block in d_far:
         d_both = d_both + block.astype(wide)
     first, second = d_both[:, :half], d_both[:, half:HD]
@@ -1458,28 +1541,25 @@
         [first * cosine + second * sine, second * cosine - first * sine], axis=1
     ).astype(low)
     g_v = d_both[:, HD:].astype(low)
-    gi_q = mul_t(g_q, q_raise).astype(low)
     gi_k = mul_t(g_k, k_raise).astype(low)
     gi_v = mul_t(g_v, v_raise).astype(low)
-    g_lin = jnp.concatenate([g_q, g_k, g_v], axis=1)
-    e1 = mul_t(jnp.concatenate([g_lin, gi_q, gi_k, gi_v], axis=1), qkv_side)
+    g_kv = jnp.concatenate([g_k, g_v], axis=1)
+    e1 = e1 + mul_t(g_kv, qkv_side[:, hq:lin])
+    e1 = e1 + mul_t(jnp.concatenate([gi_k, gi_v], axis=1), qkv_side[:, lin + rank :])
     input_grad = g_mid + r1 * e1 - resid * (
         r1 * r1 * r1 * jnp.mean(e1 * resid, axis=-1, keepdims=True)
     )
     input_grad = input_grad.astype(low).reshape(rows, length, width)
-    g_qkv = t_mul(unit1, g_lin).astype(low)
-    gr_qkv = jnp.concatenate(
-        [t_mul(q_inner, g_q), t_mul(k_inner, g_k), t_mul(v_inner, g_v)], axis=1
-    ).astype(low)
-    qkv_pack = jnp.concatenate(
-        [g_qkv.reshape(n_f, own_rows, lin), gr_qkv.reshape(n_f, rank_rows, lin)], axis=1
-    )
-    qkv_pack, o_pack, grad_down_weight, grad_down_down, input_grad, far, own_branch = tie(
-        (), (qkv_pack, o_pack, grad_down_weight, grad_down_down, input_grad, far, sums[0])
-    )
-    for first, second in zip(far_first, far, strict=True):
-        own_branch = own_branch + jnp.concatenate([first, second], axis=0).astype(wide)
-    outputs = (mid + active * own_branch).astype(low).reshape(rows, length, width)
+    kv_pack = jnp.concatenate(
+        [
+            t_mul(unit1, g_kv).astype(low).reshape(n_f, own_rows, 2 * kv),
+            jnp.concatenate([t_mul(k_inner, g_k), t_mul(v_inner, g_v)], axis=1)
+            .astype(low)
+            .reshape(n_f, rank_rows, 2 * kv),
+        ],
+        axis=1,
+    )
+    kv_pack, input_grad, sums = tie((), (kv_pack, input_grad, sums))
 
     g_slab = slab_sums.done(wide)
     unit_grad = g_slab[rank_rows:]
@@ -1499,39 +1579,40 @@
         ],
         axis=1,
     ).astype(low)
+    far = group.send([block[middle:] for block in sums])
     packs, slab_pieces, mlp_small = scatter_whole(
-        (qkv_pack, o_pack), g_slab.astype(low), mlp_small, 6, n_seq
-    )
-    qkv_pack, o_pack = (pack.astype(wide) for pack in packs)
+        (o_pack, q_pack, kv_pack), g_slab.astype(low), mlp_small, 6, n_seq
+    )
+    packs, slab_pieces, mlp_small, far = tie((), (packs, slab_pieces, mlp_small, far))
+    own_branch = sums[0]
+    for first, second in zip(far_first, far, strict=True):
+        own_branch = own_branch + jnp.concatenate([first, second], axis=0).astype(wide)
+    outputs = (mid + active * own_branch).astype(low).reshape(rows, length, width)
+    o_pack, q_pack, kv_pack = (pack.astype(wide) for pack in packs)
 
     grad_o_weight = o_pack[:o_rows]
     grad_o_up = o_pack[o_rows : o_rows + rank_rows]
     grad_down_up = o_pack[o_rows + rank_rows :]
-    grad_o_down = mul_t(packs[1][:o_rows], o_raise)
-    unit_grad = qkv_pack[:own_rows]
-    grad_lin = unit_grad * gain1
-    grad_q_weight, grad_k_weight, grad_v_weight = (
-        grad_lin[:, :hq],
-        grad_lin[:, hq : hq + kv],
-        grad_lin[:, hq + kv :],
-    )
-    grad_q_up, grad_k_up, grad_v_up = (
-        qkv_pack[own_rows:, :hq],
-        qkv_pack[own_rows:, hq : hq + kv],
-        qkv_pack[own_rows:, hq + kv :],
-    )
+    grad_o_down = mul_t(packs[0][:o_rows], o_raise)
+    grad_q_weight = q_pack[:own_rows] * gain1
+    grad_kv = kv_pack[:own_rows] * gain1
+    grad_k_weight, grad_v_weight = grad_kv[:, :kv], grad_kv[:, kv:]
+    grad_q_up = q_pack[own_rows:]
+    grad_k_up, grad_v_up = kv_pack[own_rows:, :kv], kv_pack[own_rows:, kv:]
     grad_q_down = mul_t(grad_q_weight.astype(low), q_raise)
     grad_k_down = mul_t(grad_k_weight.astype(low), k_raise)
     grad_v_down = mul_t(grad_v_weight.astype(low), v_raise)
-    own_lin = jnp.concatenate(
+    own_q = q_weight.astype(wide) + mul(q_down, q_raise)
+    own_kv = jnp.concatenate(
         [
-            q_weight.astype(wide) + mul(q_down, q_raise),
             k_weight.astype(wide) + mul(k_down, k_raise),
             v_weight.astype(wide) + mul(v_down, v_raise),
         ],
         axis=1,
     )
-    grad_attn_gain = jnp.sum(unit_grad * own_lin, axis=1)
+    grad_attn_gain = jnp.sum(q_pack[:own_rows] * own_q, axis=1) + jnp.sum(
+        kv_pack[:own_rows] * own_kv, axis=1
+    )
 
     grad_gate_down, grad_up_down = mlp_small[:, :rank], mlp_small[:, rank : 2 * rank]
     grad_mlp_gain = mlp_small[:, 2 * rank]

time: 629 us -> 619 us (0.984)
  Pallas kernels: 276 us -> 296 us
  waiting for transfers between devices: 72.4 us -> 57.8 us
  other arithmetic: 40.5 us -> 31.2 us
  matrix products: 128 us -> 121 us
    pallas_call x0 -> x4, Pallas kernels: none -> 20.7 us  [the longest x1 8.26 us: query_gradients(): pl.pallas_call(body, out_shape=(jax.ShapeDtypeStruct((tokens, width), wid...]
    ppermute x4, waiting for transfers between devices: 23 us -> 10.3 us  [send(): lax.ppermute(sums[k].astype(low), 'seq', self.shift(k))]
    dot_general x10 -> x6, matrix products: 29.5 us -> 23.6 us  [mul(): return jnp.dot(left, right, preferred_element_type=wide)]
    unnamed x254 -> x256, local copies, waits for them, and re-layouts: 17.4 us -> 22.9 us
    dot_general x12 -> x9, matrix products: 42.5 us -> 41 us  [t_mul(): lax.dot_general(left, right, (((0,), (0,)), ((), ())), preferred_element_...]
  transfers between devices with their start and end apart: 56 -> 56, of which waited for: 16 -> 13; matrix products, arithmetic and copies ran while one was open for 26% -> 24% of each run, Pallas kernels for 32% -> 47%
where the time goes in v4:
time: 619 us; the launch traced here: 609 us
  Pallas kernels  296 us (48%)
  matrix products  121 us (20%)
  waiting for transfers between devices  57.8 us (9%)
  starting transfers between devices  52.4 us (8%)
  local copies, waits for them, and re-layouts  47.8 us (8%)
  other arithmetic  31.2 us (5%)
    pallas_call x1, Pallas kernels, scatter_whole(): pl.pallas_call(body, out_shape=tuple((jax.ShapeDtypeStruct(pack.shape[1:]...  62.2 us
    pallas_call x1, Pallas kernels, gather_whole(): pl.pallas_call(body, out_shape=tuple((jax.ShapeDtypeStruct((n_f,) + b.sha...  62 us
    dot_general x17, matrix products, mul_t(): lax.dot_general(left, right, (((1,), (1,)), ((), ())), preferred_element_...  56.6 us
    pallas_call x2, Pallas kernels, gather_group(): pl.pallas_call(body, out_shape=jax.ShapeDtypeStruct((n_seq,) + block.shap...  54.4 us
    dot_general x9, matrix products, t_mul(): lax.dot_general(left, right, (((0,), (0,)), ((), ())), preferred_element_...  41 us
    pallas_call x2, Pallas kernels, mlp_forward(): pl.pallas_call(body, grid=(stop - first,), out_shape=(jax.ShapeDtypeStruc...  40.5 us
    ppermute x32, starting transfers between devices, hop(): return lax.ppermute(block, 'fsdp', self.up if way > 0 else self.down)  35.4 us
    ppermute x32, waiting for transfers between devices, hop(): return lax.ppermute(block, 'fsdp', self.up if way > 0 else self.down)  28.4 us
  transfers between devices with their start and end apart: 56, of which 13 were waited for; matrix products, arithmetic and copies ran while one was open for 24% of the time, Pallas kernels for 47%

profile of v4, /device:TPU:0, one launch (start us, length us, event | category | flops | bytes accessed | tf_op | source)
XLA Modules:
  0.0 609.4 jit_solution(3476562652343337788)
XLA Ops:
  8.0 3.0 collective-permute-start
  11.1 2.0 collective-permute-start.2
  16.7 2.0 pad_maximum_fusion.refs_0_
  20.2 3.1 fusion.12
  27.3 62.0 %shard_map.477 = (bf16[8,144,2304]{2,1,0:T(8,128)(2,1)}, bf16[8,32,1536]{2,1,0:T(8,128)(2,1)}, bf16[8,128,1536]{2,1,0:T(8,128)(2,1)}, bf16[8,32,2560]{2,1,0:T(8,128)(2,1)}, bf16[8,144,512]{2,1,0:T(8,128)(2,1)}) custom-call(bf16[144,2304]{1,0:T(8,128)(2,1)} %copy-done.27, bf16[32,1536]{1,0:T(8,128)(2,1)} %copy-done.45, bf16[128,1536]{1,0:T(8,128)(2,1)} %copy-done.32, ...), custom_call_target="tpu_custom_call" | custom-call | tf_op jit(solution)/shard_map/pallas_call | solution.py:250
  89.3 1.6 collective-permute-start.3
  93.4 6.1 %shard_map.478 = (bf16[512,1024]{1,0:T(8,128)(2,1)S(1)}, bf16[512,512]{1,0:T(8,128)(2,1)S(1)}, bf16[512,768]{1,0:T(8,128)(2,1)S(1)}) custom-call(bf16[512,1152]{1,0:T(8,128)(2,1)S(1)} %fusion.14.x, bf16[1152,2304]{1,0:T(8,128)(2,1)} %bitcast.154, bf16[256,1536]{1,0:T(8,128)(2,1)S(1)} %bitcast.139, f32[512,128]{1,0:T(8,128)S(1)} %get-tuple-element.302.cos, ...), custom_call_target="tpu_custom_call" | custom-call | flops 2000000000 | bytes 2000000 | tf_op jit(solution)/shard_map/pallas_call | solution.py:935
  100.3 17.3 %shard_map.479.kv = bf16[4,512,512]{2,1,0:T(8,128)(2,1)} custom-call(bf16[512,512]{1,0:T(8,128)(2,1)} %copy-done.29), custom_call_target="tpu_custom_call" | custom-call | tf_op jit(solution)/shard_map/pallas_call | solution.py:319
  117.6 1.8 and_select_fusion.hidden
  121.1 1.6 collective-permute-start.7
  124.2 5.1 shard_map.480
  129.4 4.4 fusion.10
  134.5 1.8 multiply_reduce_fusion.1
  137.8 12.5 %collective-permute-done.9 = bf16[512,1152]{1,0:T(8,128)(2,1)S(1)} collective-permute-done((bf16[512,1152]{1,0:T(8,128)(2,1)}, bf16[512,1152]{1,0:T(8,128)(2,1)S(1)}, u32[]{:S(2)}, u32[]{:S(2)}) %collective-permute-start.9) | collective-permute-done | bytes 1179680 | tf_op jit(solution)/shard_map/ppermute | solution.py:769
  152.8 1.6 collective-permute-start.10
  159.2 37.1 %shard_map.481 = bf16[4,512,1152]{2,1,0:T(8,128)(2,1)} custom-call(bf16[512,1152]{1,0:T(8,128)(2,1)} %multiply_convert_fusion.1.x), custom_call_target="tpu_custom_call" | custom-call | tf_op jit(solution)/shard_map/pallas_call | solution.py:319
  200.1 1.7 fusion.34
  201.8 1.9 slice.257.raised
  203.8 1.7 fusion.35
  206.2 22.3 %shard_map.482 = (bf16[2048,1792]{1,0:T(8,128)(2,1)}, bf16[2048,1792]{1,0:T(8,128)(2,1)}, bf16[2048,1792]{1,0:T(8,128)(2,1)}, bf16[8,144,1792]{2,1,0:T(8,128)(2,...) custom-call(bf16[2048,1152]{1,0:T(8,128)(2,1)} %bitcast.148, ...), custom_call_target="tpu_custom_call" | custom-call | flops 3000000000 | bytes 3000000 | tf_op jit(solution)/shard_map/pallas_call | solution.py:1186
  228.6 1.6 collective-permute-start.18
  231.1 18.2 %shard_map.483 = (bf16[2048,1792]{1,0:T(8,128)(2,1)}, bf16[2048,1792]{1,0:T(8,128)(2,1)}, bf16[2048,1792]{1,0:T(8,128)(2,1)}, bf16[8,144,1792]{2,1,0:T(8,128)(2,...) custom-call(bf16[2048,1152]{1,0:T(8,128)(2,1)} %bitcast.149, ...), custom_call_target="tpu_custom_call", output_to_operand_aliasing={{0}: (12, {}), {1}: (13, {}), {2}: (14, {}), {3}: (15, {}),... | custom-call | flops 3000000000 | bytes 3000000 | tf_op jit(solution)/shard_map/pallas_call | solution.py:1186
  249.3 1.9 dynamic-slice_bitcast_fusion
  251.1 1.9 dynamic-slice_bitcast_fusion.1
  253.0 1.8 constant_dynamic-update-slice_fusion.3
  256.4 1.6 collective-permute-start.21
  259.4 10.3 %convolution_convert_fusion = bf16[1792,1152]{1,0:T(8,128)(2,1)S(1)} fusion(bf16[2048,1792]{1,0:T(8,128)(2,1)S(1)} %copy-done.68, bf16[2048,1152]{1,0:T(8,128)(2,1)S(1)} %constant_dynamic-update-slice_fusion.g), kind=kOutput, calls=%fused_computation | convolution fusion | flops 8457781248 | bytes 16187392 | tf_op jit(solution)/shard_map/dot_general | solution.py:29
  269.8 1.6 collective-permute-start.26
  271.9 1.6 collective-permute-start.25
  274.1 22.9 %shard_map.485 = (bf16[2048,1792]{1,0:T(8,128)(2,1)}, bf16[2048,1792]{1,0:T(8,128)(2,1)}, bf16[1792,1152]{1,0:T(8,128)(2,1)}) custom-call(bf16[2048,1152]{1,0:T(8,128)(2,1)} %copy-done.67, bf16[256,1152]{1,0:T(8,128)(2,1)} %slice.257.raised, bf16[2048,1792]{1,0:T(8,128)(2,1)} %get-tuple-element.411.mul_g, bf16[2048,1792]{1,0:T(8,128)(2,1)} %get-tuple-element.412.mul_u, ...), custom_call_target="tpu_custom_call" | custom-call | flops 3000000000 | bytes 3000000 | tf_op jit(solution)/shard_map/pallas_call | solution.py:1248
  300.0 13.0 %convolution_convert_fusion.3 = bf16[1152,1792]{1,0:T(8,128)(2,1)S(1)} fusion(bf16[2048,1152]{1,0:T(8,128)(2,1)} %bitcast.150, bf16[2048,1792]{1,0:T(8,128)(2,1)} %get-tuple-element.459), kind=kOutput, calls=%fused_computation.3 | convolution fusion | flops 8457781248 | bytes 16187392 | tf_op jit(solution)/shard_map/dot_general | solution.py:29
  312.9 1.6 collective-permute-start.29
  316.6 2.7 collective-permute-start.55
  320.6 1.6 collective-permute-start.31
  322.2 12.4 %convolution_convert_fusion.2 = bf16[1152,1792]{1,0:T(8,128)(2,1)S(1)} fusion(bf16[2048,1152]{1,0:T(8,128)(2,1)S(1)} %bitcast.153, bf16[2048,1792]{1,0:T(8,128)(2,1)} %get-tuple-element.460), kind=kOutput, calls=%fused_computation.2 | convolution fusion | flops 8457781248 | bytes 16187392 | tf_op jit(solution)/shard_map/dot_general | solution.py:29
  337.5 2.0 collective-permute-start.35
  341.1 1.6 collective-permute-start.33
  342.7 9.3 %fusion.3 = f32[1024,1152]{1,0:T(8,128)} fusion(bf16[1152,1792]{1,0:T(8,128)(2,1)S(1)} %bitcast.167, bf16[2048,1792]{1,0:T(8,128)(2,1)} %get-tuple-element.460), kind=kOutput, calls=%fused_computation.9 | convolution fusion | flops 4227858432 | bytes 12517376 | tf_op jit(solution)/shard_map/dot_general | solution.py:25
  352.0 9.7 %add_convert_fusion.1 = bf16[1024,1152]{1,0:T(8,128)(2,1)} fusion(f32[1024,1152]{1,0:T(8,128)} %fusion.3, bf16[1152,1792]{1,0:T(8,128)(2,1)S(1)} %bitcast.166, bf16[2048,1792]{1,0:T(8,128)(2,1)} %get-tuple-element.459), kind=kOutput, calls=%fused_computation.5 | convolution fusion | flops 4230217728 | bytes 14876672 | tf_op jit(solution)/shard_map/dot_general | solution.py:25
  367.0 1.6 collective-permute-start.37
  368.7 9.3 %fusion = f32[1024,1152]{1,0:T(8,128)} fusion(bf16[1152,1792]{1,0:T(8,128)(2,1)S(1)} %bitcast.168, bf16[2048,1792]{1,0:T(8,128)(2,1)} %get-tuple-element.460), kind=kOutput, calls=%fused_computation.6 | convolution fusion | flops 4227858432 | bytes 12517376 | tf_op jit(solution)/shard_map/dot_general | solution.py:25
  379.6 11.2 %add_convert_fusion = bf16[1024,1152]{1,0:T(8,128)(2,1)} fusion(f32[1024,1152]{1,0:T(8,128)} %fusion, bf16[1152,1792]{1,0:T(8,128)(2,1)} %bitcast.165, bf16[2048,1792]{1,0:T(8,128)(2,1)} %get-tuple-element.459), kind=kOutput, calls=%fused_computation.4 | convolution fusion | flops 4230217728 | bytes 14876672 | tf_op jit(solution)/shard_map/dot_general | solution.py:25
  390.8 4.8 collective-permute-done.39.refs_2_
  400.9 13.6 %convolution_convert_fusion.1 = bf16[2048,1152]{1,0:T(8,128)(2,1)} fusion(bf16[2048,1792]{1,0:T(8,128)(2,1)S(1)} %bitcast.160, bf16[1792,1152]{1,0:T(8,128)(2,1)} %get-tuple-element.468), kind=kOutput, calls=%fused_computation.1 | convolution fusion | flops 8458076160 | bytes 16187392 | tf_op jit(solution)/shard_map/dot_general | solution.py:21
  414.5 10.3 %collective-permute-done.42 = bf16[512,1152]{1,0:T(8,128)(2,1)S(1)} collective-permute-done((bf16[512,1152]{1,0:T(8,128)(2,1)S(1)}, bf16[512,1152]{1,0:T(8,128)(2,1)S(1)}, u32[]{:S(2)}, u32[]{:S(2)}) %collective-permute-start.42) | collective-permute-done | bytes 1179680 | tf_op jit(solution)/shard_map/ppermute | solution.py:788
  424.8 2.9 collective-permute-done.40.refs_4_
  428.6 1.8 fusion.77
  431.8 1.6 collective-permute-start.44
  434.1 2.4 multiply_convert_fusion
  436.5 1.6 convolution_convert_fusion.10
  438.1 2.8 fusion.19.g
  440.9 20.8 %collective-permute-done.44.refs_4_ = bf16[176,3584]{1,0:T(8,128)(2,1)S(1)} collective-permute-done((bf16[176,3584]{1,0:T(8,128)(2,1)S(1)}, bf16[176,3584]{1,0:T(8,128)(2,1)S(1)}, u32[]{:S(2)}, u32[]{:S(2)}) %collective-permute-start.44) | collective-permute-done | bytes 1261600 | tf_op jit(solution)/shard_map/ppermute | solution.py:658
  467.1 11.3 %shard_map.494 = (bf16[512,1024]{1,0:T(8,128)(2,1)}, bf16[4,512,512]{2,1,0:T(8,128)(2,1)}) custom-call(bf16[512,1024]{1,0:T(8,128)(2,1)} %copy-done.54, bf16[4,512,512]{2,1,0:T(8,128)(2,1)} %shard_map.479.kv, f32[2,256,1024]{2,1,0:T(8,128)} %and_select_fusion.hidden, f32[2,4,256,1]{3,2,1,0:T(8,128)} %copy-done.57, bf16[512,1024]{1,0:T(8,128)(2,1)} %copy-done.55, ...), custom_call_target="tpu_custom_call" | custom-call | flops 3000000000 | bytes 3000000 | tf_op jit(solution)/shard_map/pallas_call | solution.py:1010
  480.6 1.9 shard_map.495
  482.6 1.6 convert_add_fusion.2
  491.8 4.4 shard_map.497
  496.2 8.3 %shard_map.496 = (f32[512,1152]{1,0:T(8,128)S(1)}, bf16[8,176,1024]{2,1,0:T(8,128)(2,1)}) custom-call(bf16[512,1152]{1,0:T(8,128)(2,1)S(1)} %copy-done.12, bf16[512,256]{1,0:T(8,128)(2,1)S(1)} %copy-done.25, bf16[512,1024]{1,0:T(8,128)(2,1)S(1)} %copy-done.26, bf16[256,1536]{1,0:T(8,128)(2,1)S(1)} %bitcast.140, bf16[1152,2304]{1,0:T(8,128)(2,1)} %bitcast.155), custom_call_target="tpu_custom_call" | custom-call | flops 2000000000 | bytes 2000000 | tf_op jit(solution)/shard_map/pallas_call | solution.py:1056
  506.1 2.1 fusion.32
  510.7 2.8 fusion.15
  519.5 2.2 pad.4.refs_0_
  521.7 62.2 %shard_map.499 = (bf16[192,1280]{1,0:T(8,128)(2,1)}, bf16[176,1024]{1,0:T(8,128)(2,1)}, bf16[176,512]{1,0:T(8,128)(2,1)}, bf16[4,176,3584]{2,1,0:T(8,128)(2,1)}, f32[144,640]{1,0:T(8,128)}) custom-call(bf16[8,192,1280]{2,1,0:T(8,128)(2,1)} %pad.4.refs_0_, bf16[8,176,1024]{2,1,0:T(8,128)(2,1)} %get-tuple-element.515.refs_1_, ...), custom_call_target="tpu_custom_call" | custom-call | tf_op jit(solution)/shard_map/pallas_call | solution.py:561
  586.6 2.1 fusion.45
  593.9 8.3 %shard_map.500 = (f32[144,6912]{1,0:T(8,128)}, f32[144,6912]{1,0:T(8,128)}, f32[32,6912]{1,0:T(8,128)}, f32[32,6912]{1,0:T(8,128)}) custom-call(f32[144,1]{1,0:T(8,128)} %copy-done.24, bf16[4,176,3584]{2,1,0:T(8,128)(2,1)} %get-tuple-element.533.x), custom_call_target="tpu_custom_call" | custom-call | tf_op jit(solution)/shard_map/pallas_call | solution.py:890
  605.7 3.2 add_convert_fusion.2
  (450 shorter events, 103.2 us)
Async XLA Ops:
  8.0 81.3 %collective-permute-start = (bf16[176,3584]{1,0:T(8,128)(2,1)S(1)}, bf16[176,3584]{1,0:T(8,128)(2,1)}, u32[]{:S(2)}, u32[]{:S(2)}) collective-permute-start(bf16[176,3584]{1,0:T(8,128)(2,1)S(1)} %shard_map.475.refs_0_), channel_id=1, source_target_pairs={{0,1},{1,3},{3,5},{5,7},{7,6},{6,4},{4,2},{2,0},{8,9},{9,11},{11,1... | collective-permute-start | bytes 3784712 | tf_op jit(solution)/shard_map/ppermute | solution.py:658
  11.0 78.3 %collective-permute-start.1 = (bf16[176,3584]{1,0:T(8,128)(2,1)S(1)}, bf16[176,3584]{1,0:T(8,128)(2,1)}, u32[]{:S(2)}, u32[]{:S(2)}) collective-permute-start(bf16[176,3584]{1,0:T(8,128)(2,1)S(1)} %shard_map.475.refs_0_), channel_id=1, source_target_pairs={{1,0},{3,1},{5,3},{7,5},{6,7},{4,6},{2,4},{0,2},{9,8},{11,9},{13,1... | collective-permute-start | bytes 3784712 | tf_op jit(solution)/shard_map/ppermute | solution.py:658
  11.1 78.1 %collective-permute-start.2 = (bf16[2,256]{1,0:T(2,128)(2,1)S(1)}, bf16[2,256]{1,0:T(2,128)(2,1)S(1)}, u32[]{:S(2)}, u32[]{:S(2)}) collective-permute-start(bf16[2,256]{1,0:T(2,128)(2,1)S(1)} %convert_element_type.223), channel_id=1, source_target_pairs={{0,16},{8,24},{16,0},{24,8},{1,17},{9,25},{17,1},{25,9},{2,18},{10... | collective-permute-start | bytes 3080 | tf_op jit(solution)/shard_map/ppermute | solution.py:769
  19.7 72.5 %copy-start.15 = (f32[512,128]{1,0:T(8,128)}, f32[512,128]{1,0:T(8,128)S(1)}, u32[]{:S(2)}) copy-start(f32[512,128]{1,0:T(8,128)S(1)} %get-tuple-element.303.sin) | copy-start | bytes 786436
  19.7 72.5 %copy-start.17 = (f32[512,128]{1,0:T(8,128)}, f32[512,128]{1,0:T(8,128)S(1)}, u32[]{:S(2)}) copy-start(f32[512,128]{1,0:T(8,128)S(1)} %get-tuple-element.302.cos) | copy-start | bytes 786436
  19.7 114.8 %copy-start.108 = (f32[512]{0:T(512)}, f32[512]{0:T(512)S(1)}, u32[]{:S(2)}) copy-start(f32[512]{0:T(512)S(1)} %compare_convert_fusion) | copy-start | bytes 6148
  20.2 72.0 %copy-start.11 = (bf16[512,1152]{1,0:T(8,128)(2,1)}, bf16[512,1152]{1,0:T(8,128)(2,1)S(1)}, u32[]{:S(2)}) copy-start(bf16[512,1152]{1,0:T(8,128)(2,1)S(1)} %fusion.14.x) | copy-start | bytes 3538948
  89.3 30.5 %collective-permute-start.3 = (bf16[176,3584]{1,0:T(8,128)(2,1)}, bf16[176,3584]{1,0:T(8,128)(2,1)}, u32[]{:S(2)}, u32[]{:S(2)}) collective-permute-start(bf16[176,3584]{1,0:T(8,128)(2,1)} %collective-permute-done.refs_1_), channel_id=1, source_target_pairs={{0,1},{1,3},{3,5},{5,7},{7,6},{6,4},{4,2},{2,0},{8,9},{9,11},{11,1... | collective-permute-start | bytes 3784712 | tf_op jit(solution)/shard_map/ppermute | solution.py:658
  90.9 30.2 %collective-permute-start.4 = (bf16[176,3584]{1,0:T(8,128)(2,1)}, bf16[176,3584]{1,0:T(8,128)(2,1)}, u32[]{:S(2)}, u32[]{:S(2)}) collective-permute-start(bf16[176,3584]{1,0:T(8,128)(2,1)} %collective-permute-done.1.refs_2_), channel_id=1, source_target_pairs={{1,0},{3,1},{5,3},{7,5},{6,7},{4,6},{2,4},{0,2},{9,8},{11,9},{13,1... | collective-permute-start | bytes 3784712 | tf_op jit(solution)/shard_map/ppermute | solution.py:658
  91.7 26.0 %collective-permute-start.5 = (bf16[2,256]{1,0:T(2,128)(2,1)S(1)}, bf16[2,256]{1,0:T(2,128)(2,1)S(1)}, u32[]{:S(2)}, u32[]{:S(2)}) collective-permute-start(bf16[2,256]{1,0:T(2,128)(2,1)S(1)} %convert_element_type.223), channel_id=1, source_target_pairs={{0,8},{8,0},{16,24},{24,16},{1,9},{9,1},{17,25},{25,17},{2,10},{10... | collective-permute-start | bytes 3080 | tf_op jit(solution)/shard_map/ppermute | solution.py:775
  91.7 25.9 %collective-permute-start.6 = (bf16[2,256]{1,0:T(2,128)(2,1)S(1)}, bf16[2,256]{1,0:T(2,128)(2,1)S(1)}, u32[]{:S(2)}, u32[]{:S(2)}) collective-permute-start(bf16[2,256]{1,0:T(2,128)(2,1)S(1)} %collective-permute-done.2), channel_id=1, source_target_pairs={{0,8},{8,0},{16,24},{24,16},{1,9},{9,1},{17,25},{25,17},{2,10},{10... | collective-permute-start | bytes 3080 | tf_op jit(solution)/shard_map/ppermute | solution.py:775
  100.3 105.2 %copy-start.33 = (bf16[512,768]{1,0:T(8,128)(2,1)}, bf16[512,768]{1,0:T(8,128)(2,1)S(1)}, u32[]{:S(2)}) copy-start(bf16[512,768]{1,0:T(8,128)(2,1)S(1)} %get-tuple-element.496) | copy-start | bytes 2359300
  121.1 29.3 %collective-permute-start.7 = (bf16[176,3584]{1,0:T(8,128)(2,1)}, bf16[176,3584]{1,0:T(8,128)(2,1)S(1)}, u32[]{:S(2)}, u32[]{:S(2)}) collective-permute-start(bf16[176,3584]{1,0:T(8,128)(2,1)} %collective-permute-done.3.refs_3_), channel_id=1, source_target_pairs={{0,1},{1,3},{3,5},{5,7},{7,6},{6,4},{4,2},{2,0},{8,9},{9,11},{11,1... | collective-permute-start | bytes 3784712 | tf_op jit(solution)/shard_map/ppermute | solution.py:658
  122.7 29.2 %collective-permute-start.8 = (bf16[176,3584]{1,0:T(8,128)(2,1)}, bf16[176,3584]{1,0:T(8,128)(2,1)S(1)}, u32[]{:S(2)}, u32[]{:S(2)}) collective-permute-start(bf16[176,3584]{1,0:T(8,128)(2,1)} %collective-permute-done.4.refs_4_), channel_id=1, source_target_pairs={{1,0},{3,1},{5,3},{7,5},{6,7},{4,6},{2,4},{0,2},{9,8},{11,9},{13,1... | collective-permute-start | bytes 3784712 | tf_op jit(solution)/shard_map/ppermute | solution.py:658
  123.3 27.0 %collective-permute-start.9 = (bf16[512,1152]{1,0:T(8,128)(2,1)}, bf16[512,1152]{1,0:T(8,128)(2,1)S(1)}, u32[]{:S(2)}, u32[]{:S(2)}) collective-permute-start(bf16[512,1152]{1,0:T(8,128)(2,1)} %fusion.12), channel_id=1, source_target_pairs={{0,16},{8,24},{16,0},{24,8},{1,17},{9,25},{17,1},{25,9},{2,18},{10... | collective-permute-start | bytes 3538952 | tf_op jit(solution)/shard_map/ppermute | solution.py:769
  152.8 43.5 %collective-permute-start.10 = (bf16[176,1792]{1,0:T(8,128)(2,1)}, bf16[176,1792]{1,0:T(8,128)(2,1)S(1)}, u32[]{:S(2)}, u32[]{:S(2)}) collective-permute-start(bf16[176,1792]{1,0:T(8,128)(2,1)} %slice.194), channel_id=1, source_target_pairs={{0,1},{1,3},{3,5},{5,7},{7,6},{6,4},{4,2},{2,0},{8,9},{9,11},{11,1... | collective-permute-start | bytes 1892360 | tf_op jit(solution)/shard_map/ppermute | solution.py:658
  155.3 41.1 %collective-permute-start.11 = (bf16[176,1792]{1,0:T(8,128)(2,1)}, bf16[176,1792]{1,0:T(8,128)(2,1)}, u32[]{:S(2)}, u32[]{:S(2)}) collective-permute-start(bf16[176,1792]{1,0:T(8,128)(2,1)} %slice.195), channel_id=1, source_target_pairs={{1,0},{3,1},{5,3},{7,5},{6,7},{4,6},{2,4},{0,2},{9,8},{11,9},{13,1... | collective-permute-start | bytes 1892360 | tf_op jit(solution)/shard_map/ppermute | solution.py:658
  155.7 40.6 %collective-permute-start.12 = (bf16[216,1408]{1,0:T(8,128)(2,1)}, bf16[216,1408]{1,0:T(8,128)(2,1)}, u32[]{:S(2)}, u32[]{:S(2)}) collective-permute-start(bf16[216,1408]{1,0:T(8,128)(2,1)} %pad_maximum_fusion.refs_0_), channel_id=1, source_target_pairs={{0,1},{1,3},{3,5},{5,7},{7,6},{6,4},{4,2},{2,0},{8,9},{9,11},{11,1... | collective-permute-start | bytes 1824776 | tf_op jit(solution)/shard_map/ppermute | solution.py:658
  157.3 39.1 %collective-permute-start.13 = (bf16[216,1408]{1,0:T(8,128)(2,1)}, bf16[216,1408]{1,0:T(8,128)(2,1)}, u32[]{:S(2)}, u32[]{:S(2)}) collective-permute-start(bf16[216,1408]{1,0:T(8,128)(2,1)} %pad_maximum_fusion.refs_0_), channel_id=1, source_target_pairs={{1,0},{3,1},{5,3},{7,5},{6,7},{4,6},{2,4},{0,2},{9,8},{11,9},{13,1... | collective-permute-start | bytes 1824776 | tf_op jit(solution)/shard_map/ppermute | solution.py:658
  158.0 1.1 collective-permute-start.20
  196.4 32.2 %collective-permute-start.16 = (bf16[512,1152]{1,0:T(8,128)(2,1)}, bf16[512,1152]{1,0:T(8,128)(2,1)S(1)}, u32[]{:S(2)}, u32[]{:S(2)}) collective-permute-start(bf16[512,1152]{1,0:T(8,128)(2,1)} %fusion.12), channel_id=1, source_target_pairs={{0,8},{8,0},{16,24},{24,16},{1,9},{9,1},{17,25},{25,17},{2,10},{10... | collective-permute-start | bytes 3538952 | tf_op jit(solution)/shard_map/ppermute | solution.py:775
  196.7 31.9 %collective-permute-start.17 = (bf16[512,1152]{1,0:T(8,128)(2,1)S(1)}, bf16[512,1152]{1,0:T(8,128)(2,1)S(1)}, u32[]{:S(2)}, u32[]{:S(2)}) collective-permute-start(bf16[512,1152]{1,0:T(8,128)(2,1)S(1)} %copy-done.89), channel_id=1, source_target_pairs={{0,8},{8,0},{16,24},{24,16},{1,9},{9,1},{17,25},{25,17},{2,10},{10... | collective-permute-start | bytes 3538952 | tf_op jit(solution)/shard_map/ppermute | solution.py:775
  198.0 30.5 %collective-permute-start.14 = (bf16[216,1408]{1,0:T(8,128)(2,1)}, bf16[216,1408]{1,0:T(8,128)(2,1)S(1)}, u32[]{:S(2)}, u32[]{:S(2)}) collective-permute-start(bf16[216,1408]{1,0:T(8,128)(2,1)} %collective-permute-done.12.refs_1_), channel_id=1, source_target_pairs={{0,1},{1,3},{3,5},{5,7},{7,6},{6,4},{4,2},{2,0},{8,9},{9,11},{11,1... | collective-permute-start | bytes 1824776 | tf_op jit(solution)/shard_map/ppermute | solution.py:658
  199.6 28.9 %collective-permute-start.15 = (bf16[216,1408]{1,0:T(8,128)(2,1)}, bf16[216,1408]{1,0:T(8,128)(2,1)S(1)}, u32[]{:S(2)}, u32[]{:S(2)}) collective-permute-start(bf16[216,1408]{1,0:T(8,128)(2,1)} %collective-permute-done.13.refs_2_), channel_id=1, source_target_pairs={{1,0},{3,1},{5,3},{7,5},{6,7},{4,6},{2,4},{0,2},{9,8},{11,9},{13,1... | collective-permute-start | bytes 1824776 | tf_op jit(solution)/shard_map/ppermute | solution.py:658
  228.6 24.4 %collective-permute-start.18 = (bf16[216,1408]{1,0:T(8,128)(2,1)S(1)}, bf16[216,1408]{1,0:T(8,128)(2,1)S(1)}, u32[]{:S(2)}, u32[]{:S(2)}) collective-permute-start(bf16[216,1408]{1,0:T(8,128)(2,1)S(1)} %collective-permute-done.14.refs_3_), channel_id=1, source_target_pairs={{0,1},{1,3},{3,5},{5,7},{7,6},{6,4},{4,2},{2,0},{8,9},{9,11},{11,1... | collective-permute-start | bytes 1824776 | tf_op jit(solution)/shard_map/ppermute | solution.py:658
  230.2 22.8 %collective-permute-start.19 = (bf16[216,1408]{1,0:T(8,128)(2,1)S(1)}, bf16[216,1408]{1,0:T(8,128)(2,1)S(1)}, u32[]{:S(2)}, u32[]{:S(2)}) collective-permute-start(bf16[216,1408]{1,0:T(8,128)(2,1)S(1)} %collective-permute-done.15.refs_4_), channel_id=1, source_target_pairs={{1,0},{3,1},{5,3},{7,5},{6,7},{4,6},{2,4},{0,2},{9,8},{11,9},{13,1... | collective-permute-start | bytes 1824776 | tf_op jit(solution)/shard_map/ppermute | solution.py:658
  254.8 14.9 %collective-permute-start.23 = (f32[6]{0:T(128)S(1)}, f32[6]{0:T(128)S(1)}, u32[]{:S(2)}, u32[]{:S(2)}) collective-permute-start(f32[6]{0:T(128)S(1)} %fusion.111), channel_id=1, source_target_pairs={{0,16},{8,24},{16,0},{24,8},{1,17},{9,25},{17,1},{25,9},{2,18},{10... | collective-permute-start | bytes 80 | tf_op jit(solution)/shard_map/ppermute | solution.py:817
  255.8 14.0 %collective-permute-start.22 = (bf16[216,768]{1,0:T(8,128)(2,1)S(1)}, bf16[216,768]{1,0:T(8,128)(2,1)S(1)}, u32[]{:S(2)}, u32[]{:S(2)}) collective-permute-start(bf16[216,768]{1,0:T(8,128)(2,1)S(1)} %slice.199), channel_id=1, source_target_pairs={{1,0},{3,1},{5,3},{7,5},{6,7},{4,6},{2,4},{0,2},{9,8},{11,9},{13,1... | collective-permute-start | bytes 995336 | tf_op jit(solution)/shard_map/ppermute | solution.py:658
  256.4 13.4 %collective-permute-start.21 = (bf16[216,640]{1,0:T(8,128)(2,1)S(1)}, bf16[216,640]{1,0:T(8,128)(2,1)S(1)}, u32[]{:S(2)}, u32[]{:S(2)}) collective-permute-start(bf16[216,640]{1,0:T(8,128)(2,1)S(1)} %slice.198), channel_id=1, source_target_pairs={{0,1},{1,3},{3,5},{5,7},{7,6},{6,4},{4,2},{2,0},{8,9},{9,11},{11,1... | collective-permute-start | bytes 829448 | tf_op jit(solution)/shard_map/ppermute | solution.py:658
  269.8 27.2 %collective-permute-start.26 = (f32[6]{0:T(128)S(1)}, f32[6]{0:T(128)S(1)}, u32[]{:S(2)}, u32[]{:S(2)}) collective-permute-start(f32[6]{0:T(128)S(1)} %add.212), channel_id=1, source_target_pairs={{0,1},{1,0},{2,3},{3,2},{4,5},{5,4},{6,7},{7,6},{8,9},{9,8},{10,11... | collective-permute-start | bytes 80 | tf_op jit(solution)/shard_map/ppermute | solution.py:817
  271.9 25.1 %collective-permute-start.25 = (bf16[216,640]{1,0:T(8,128)(2,1)S(1)}, bf16[216,640]{1,0:T(8,128)(2,1)S(1)}, u32[]{:S(2)}, u32[]{:S(2)}) collective-permute-start(bf16[216,640]{1,0:T(8,128)(2,1)S(1)} %get-tuple-element.408), channel_id=1, source_target_pairs={{1,0},{3,1},{5,3},{7,5},{6,7},{4,6},{2,4},{0,2},{9,8},{11,9},{13,1... | collective-permute-start | bytes 829448 | tf_op jit(solution)/shard_map/ppermute | solution.py:658
  273.5 23.5 %collective-permute-start.24 = (bf16[216,512]{1,0:T(8,128)(2,1)S(1)}, bf16[216,512]{1,0:T(8,128)(2,1)S(1)}, u32[]{:S(2)}, u32[]{:S(2)}) collective-permute-start(bf16[216,512]{1,0:T(8,128)(2,1)S(1)} %get-tuple-element.407), channel_id=1, source_target_pairs={{0,1},{1,3},{3,5},{5,7},{7,6},{6,4},{4,2},{2,0},{8,9},{9,11},{11,1... | collective-permute-start | bytes 663560 | tf_op jit(solution)/shard_map/ppermute | solution.py:658
  297.9 18.7 %collective-permute-start.27 = (bf16[216,1152]{1,0:T(8,128)(2,1)S(1)}, bf16[216,1152]{1,0:T(8,128)(2,1)S(1)}, u32[]{:S(2)}, u32[]{:S(2)}) collective-permute-start(bf16[216,1152]{1,0:T(8,128)(2,1)S(1)} %get-tuple-element.427), channel_id=1, source_target_pairs={{0,1},{1,3},{3,5},{5,7},{7,6},{6,4},{4,2},{2,0},{8,9},{9,11},{11,1... | collective-permute-start | bytes 1493000 | tf_op jit(solution)/shard_map/ppermute | solution.py:658
  298.4 18.1 %collective-permute-start.28 = (bf16[216,1152]{1,0:T(8,128)(2,1)S(1)}, bf16[216,1152]{1,0:T(8,128)(2,1)S(1)}, u32[]{:S(2)}, u32[]{:S(2)}) collective-permute-start(bf16[216,1152]{1,0:T(8,128)(2,1)S(1)} %get-tuple-element.428), channel_id=1, source_target_pairs={{1,0},{3,1},{5,3},{7,5},{6,7},{4,6},{2,4},{0,2},{9,8},{11,9},{13,1... | collective-permute-start | bytes 1493000 | tf_op jit(solution)/shard_map/ppermute | solution.py:658
  312.9 3.6 collective-permute-start.29
  316.0 114.9 %copy-start.4 = (bf16[256,1792]{1,0:T(8,128)(2,1)}, bf16[256,1792]{1,0:T(8,128)(2,1)S(1)}, u32[]{:S(2)}) copy-start(bf16[256,1792]{1,0:T(8,128)(2,1)S(1)} %convolution_convert_fusion.7) | copy-start | bytes 2752516
  316.6 19.5 %collective-permute-start.55 = (f32[6]{0:T(128)S(1)}, f32[6]{0:T(128)S(1)}, u32[]{:S(2)}, u32[]{:S(2)}) collective-permute-start(f32[6]{0:T(128)S(1)} %add.214), channel_id=1, source_target_pairs={{0,4},{1,5},{2,6},{3,7},{4,0},{5,1},{6,2},{7,3},{8,12},{9,13},{10,... | collective-permute-start | bytes 80 | tf_op jit(solution)/shard_map/ppermute | solution.py:817
  320.1 16.0 %collective-permute-start.30 = (bf16[216,1152]{1,0:T(8,128)(2,1)S(1)}, bf16[216,1152]{1,0:T(8,128)(2,1)S(1)}, u32[]{:S(2)}, u32[]{:S(2)}) collective-permute-start(bf16[216,1152]{1,0:T(8,128)(2,1)S(1)} %get-tuple-element.434), channel_id=1, source_target_pairs={{0,1},{1,3},{3,5},{5,7},{7,6},{6,4},{4,2},{2,0},{8,9},{9,11},{11,1... | collective-permute-start | bytes 1493000 | tf_op jit(solution)/shard_map/ppermute | solution.py:658
  320.6 15.5 %collective-permute-start.31 = (bf16[216,1152]{1,0:T(8,128)(2,1)S(1)}, bf16[216,1152]{1,0:T(8,128)(2,1)S(1)}, u32[]{:S(2)}, u32[]{:S(2)}) collective-permute-start(bf16[216,1152]{1,0:T(8,128)(2,1)S(1)} %get-tuple-element.435), channel_id=1, source_target_pairs={{1,0},{3,1},{5,3},{7,5},{6,7},{4,6},{2,4},{0,2},{9,8},{11,9},{13,1... | collective-permute-start | bytes 1493000 | tf_op jit(solution)/shard_map/ppermute | solution.py:658
  334.7 96.2 %copy-start.2 = (bf16[1152,1792]{1,0:T(8,128)(2,1)}, bf16[1152,1792]{1,0:T(8,128)(2,1)S(1)}, u32[]{:S(2)}) copy-start(bf16[1152,1792]{1,0:T(8,128)(2,1)S(1)} %convolution_convert_fusion.2) | copy-start | bytes 12386308
  336.1 94.8 %copy-start.6 = (bf16[256,1792]{1,0:T(8,128)(2,1)}, bf16[256,1792]{1,0:T(8,128)(2,1)S(1)}, u32[]{:S(2)}) copy-start(bf16[256,1792]{1,0:T(8,128)(2,1)S(1)} %convolution_convert_fusion.6) | copy-start | bytes 2752516
  337.1 24.7 %collective-permute-start.34 = (bf16[216,1152]{1,0:T(8,128)(2,1)S(1)}, bf16[216,1152]{1,0:T(8,128)(2,1)S(1)}, u32[]{:S(2)}, u32[]{:S(2)}) collective-permute-start(bf16[216,1152]{1,0:T(8,128)(2,1)S(1)} %get-tuple-element.453), channel_id=1, source_target_pairs={{0,1},{1,3},{3,5},{5,7},{7,6},{6,4},{4,2},{2,0},{8,9},{9,11},{11,1... | collective-permute-start | bytes 1493000 | tf_op jit(solution)/shard_map/ppermute | solution.py:658
  337.5 24.3 %collective-permute-start.35 = (bf16[216,1152]{1,0:T(8,128)(2,1)S(1)}, bf16[216,1152]{1,0:T(8,128)(2,1)S(1)}, u32[]{:S(2)}, u32[]{:S(2)}) collective-permute-start(bf16[216,1152]{1,0:T(8,128)(2,1)S(1)} %get-tuple-element.454), channel_id=1, source_target_pairs={{1,0},{3,1},{5,3},{7,5},{6,7},{4,6},{2,4},{0,2},{9,8},{11,9},{13,1... | collective-permute-start | bytes 1493000 | tf_op jit(solution)/shard_map/ppermute | solution.py:658
  340.7 25.2 %collective-permute-start.32 = (bf16[176,1792]{1,0:T(8,128)(2,1)S(1)}, bf16[176,1792]{1,0:T(8,128)(2,1)S(1)}, u32[]{:S(2)}, u32[]{:S(2)}) collective-permute-start(bf16[176,1792]{1,0:T(8,128)(2,1)S(1)} %get-tuple-element.445), channel_id=1, source_target_pairs={{0,1},{1,3},{3,5},{5,7},{7,6},{6,4},{4,2},{2,0},{8,9},{9,11},{11,1... | collective-permute-start | bytes 1892360 | tf_op jit(solution)/shard_map/ppermute | solution.py:658
  341.1 24.7 %collective-permute-start.33 = (bf16[176,1792]{1,0:T(8,128)(2,1)S(1)}, bf16[176,1792]{1,0:T(8,128)(2,1)S(1)}, u32[]{:S(2)}, u32[]{:S(2)}) collective-permute-start(bf16[176,1792]{1,0:T(8,128)(2,1)S(1)} %get-tuple-element.446), channel_id=1, source_target_pairs={{1,0},{3,1},{5,3},{7,5},{6,7},{4,6},{2,4},{0,2},{9,8},{11,9},{13,1... | collective-permute-start | bytes 1892360 | tf_op jit(solution)/shard_map/ppermute | solution.py:658
  366.6 29.0 %collective-permute-start.36 = (bf16[176,3584]{1,0:T(8,128)(2,1)S(1)}, bf16[176,3584]{1,0:T(8,128)(2,1)S(1)}, u32[]{:S(2)}, u32[]{:S(2)}) collective-permute-start(bf16[176,3584]{1,0:T(8,128)(2,1)S(1)} %get-tuple-element.457), channel_id=1, source_target_pairs={{0,1},{1,3},{3,5},{5,7},{7,6},{6,4},{4,2},{2,0},{8,9},{9,11},{11,1... | collective-permute-start | bytes 3784712 | tf_op jit(solution)/shard_map/ppermute | solution.py:658
  367.0 28.5 %collective-permute-start.37 = (bf16[176,3584]{1,0:T(8,128)(2,1)S(1)}, bf16[176,3584]{1,0:T(8,128)(2,1)S(1)}, u32[]{:S(2)}, u32[]{:S(2)}) collective-permute-start(bf16[176,3584]{1,0:T(8,128)(2,1)S(1)} %get-tuple-element.458), channel_id=1, source_target_pairs={{1,0},{3,1},{5,3},{7,5},{6,7},{4,6},{2,4},{0,2},{9,8},{11,9},{13,1... | collective-permute-start | bytes 3784712 | tf_op jit(solution)/shard_map/ppermute | solution.py:658
  379.1 16.5 %collective-permute-start.38 = (bf16[512,1152]{1,0:T(8,128)(2,1)}, bf16[512,1152]{1,0:T(8,128)(2,1)S(1)}, u32[]{:S(2)}, u32[]{:S(2)}) collective-permute-start(bf16[512,1152]{1,0:T(8,128)(2,1)} %slice.206), channel_id=1, source_target_pairs={{0,8},{8,0},{16,24},{24,16},{1,9},{9,1},{17,25},{25,17},{2,10},{10... | collective-permute-start | bytes 3538952 | tf_op jit(solution)/shard_map/ppermute | solution.py:779
  379.1 16.5 %collective-permute-start.39 = (bf16[216,1408]{1,0:T(8,128)(2,1)}, bf16[216,1408]{1,0:T(8,128)(2,1)}, u32[]{:S(2)}, u32[]{:S(2)}) collective-permute-start(bf16[216,1408]{1,0:T(8,128)(2,1)} %pad_maximum_fusion.1.refs_0_), channel_id=1, source_target_pairs={{0,16},{8,24},{16,0},{24,8},{1,17},{9,25},{17,1},{25,9},{2,18},{10... | collective-permute-start | bytes 1824776 | tf_op jit(solution)/shard_map/ppermute | solution.py:769
  397.1 27.7 %collective-permute-start.42 = (bf16[512,1152]{1,0:T(8,128)(2,1)S(1)}, bf16[512,1152]{1,0:T(8,128)(2,1)S(1)}, u32[]{:S(2)}, u32[]{:S(2)}) collective-permute-start(bf16[512,1152]{1,0:T(8,128)(2,1)S(1)} %add_convert_fusion.3), channel_id=1, source_target_pairs={{0,16},{8,24},{16,0},{24,8},{1,17},{9,25},{17,1},{25,9},{2,18},{10... | collective-permute-start | bytes 3538952 | tf_op jit(solution)/shard_map/ppermute | solution.py:788
  398.6 29.1 %collective-permute-start.40 = (bf16[176,3584]{1,0:T(8,128)(2,1)S(1)}, bf16[176,3584]{1,0:T(8,128)(2,1)S(1)}, u32[]{:S(2)}, u32[]{:S(2)}) collective-permute-start(bf16[176,3584]{1,0:T(8,128)(2,1)S(1)} %get-tuple-element.465), channel_id=1, source_target_pairs={{0,1},{1,3},{3,5},{5,7},{7,6},{6,4},{4,2},{2,0},{8,9},{9,11},{11,1... | collective-permute-start | bytes 3784712 | tf_op jit(solution)/shard_map/ppermute | solution.py:658
  399.1 28.8 %collective-permute-start.41 = (bf16[176,3584]{1,0:T(8,128)(2,1)S(1)}, bf16[176,3584]{1,0:T(8,128)(2,1)S(1)}, u32[]{:S(2)}, u32[]{:S(2)}) collective-permute-start(bf16[176,3584]{1,0:T(8,128)(2,1)S(1)} %get-tuple-element.466), channel_id=1, source_target_pairs={{1,0},{3,1},{5,3},{7,5},{6,7},{4,6},{2,4},{0,2},{9,8},{11,9},{13,1... | collective-permute-start | bytes 3784712 | tf_op jit(solution)/shard_map/ppermute | solution.py:658
  400.8 24.0 %collective-permute-start.43 = (bf16[512,1152]{1,0:T(8,128)(2,1)S(1)}, bf16[512,1152]{1,0:T(8,128)(2,1)S(1)}, u32[]{:S(2)}, u32[]{:S(2)}) collective-permute-start(bf16[512,1152]{1,0:T(8,128)(2,1)S(1)} %slice.208), channel_id=1, source_target_pairs={{0,8},{8,0},{16,24},{24,16},{1,9},{9,1},{17,25},{25,17},{2,10},{10... | collective-permute-start | bytes 3538952 | tf_op jit(solution)/shard_map/ppermute | solution.py:779
  430.3 10.6 %collective-permute-start.46 = (bf16[512,1152]{1,0:T(8,128)(2,1)}, bf16[512,1152]{1,0:T(8,128)(2,1)S(1)}, u32[]{:S(2)}, u32[]{:S(2)}) collective-permute-start(bf16[512,1152]{1,0:T(8,128)(2,1)} %get-tuple-element.547), channel_id=1, source_target_pairs={{0,8},{8,0},{16,24},{24,16},{1,9},{9,1},{17,25},{25,17},{2,10},{10... | collective-permute-start | bytes 3538952 | tf_op jit(solution)/shard_map/ppermute | solution.py:783
  430.3 10.6 %collective-permute-start.47 = (bf16[512,1152]{1,0:T(8,128)(2,1)S(1)}, bf16[512,1152]{1,0:T(8,128)(2,1)S(1)}, u32[]{:S(2)}, u32[]{:S(2)}) collective-permute-start(bf16[512,1152]{1,0:T(8,128)(2,1)S(1)} %get-tuple-element.545), channel_id=1, source_target_pairs={{0,8},{8,0},{16,24},{24,16},{1,9},{9,1},{17,25},{25,17},{2,10},{10... | collective-permute-start | bytes 3538952 | tf_op jit(solution)/shard_map/ppermute | solution.py:783
  431.8 29.9 %collective-permute-start.44 = (bf16[176,3584]{1,0:T(8,128)(2,1)S(1)}, bf16[176,3584]{1,0:T(8,128)(2,1)S(1)}, u32[]{:S(2)}, u32[]{:S(2)}) collective-permute-start(bf16[176,3584]{1,0:T(8,128)(2,1)S(1)} %get-tuple-element.473), channel_id=1, source_target_pairs={{0,1},{1,3},{3,5},{5,7},{7,6},{6,4},{4,2},{2,0},{8,9},{9,11},{11,1... | collective-permute-start | bytes 3784712 | tf_op jit(solution)/shard_map/ppermute | solution.py:658
  433.5 29.4 %collective-permute-start.45 = (bf16[176,3584]{1,0:T(8,128)(2,1)S(1)}, bf16[176,3584]{1,0:T(8,128)(2,1)S(1)}, u32[]{:S(2)}, u32[]{:S(2)}) collective-permute-start(bf16[176,3584]{1,0:T(8,128)(2,1)S(1)} %get-tuple-element.474), channel_id=1, source_target_pairs={{1,0},{3,1},{5,3},{7,5},{6,7},{4,6},{2,4},{0,2},{9,8},{11,9},{13,1... | collective-permute-start | bytes 3784712 | tf_op jit(solution)/shard_map/ppermute | solution.py:658
  465.1 19.2 %collective-permute-start.50 = (bf16[256,1152]{1,0:T(8,128)(2,1)}, bf16[256,1152]{1,0:T(8,128)(2,1)}, u32[]{:S(2)}, u32[]{:S(2)}) collective-permute-start(bf16[256,1152]{1,0:T(8,128)(2,1)} %slice.366), channel_id=1, source_target_pairs={{0,16},{8,24},{16,0},{24,8},{1,17},{9,25},{17,1},{25,9},{2,18},{10... | collective-permute-start | bytes 1769480 | tf_op jit(solution)/shard_map/ppermute | solution.py:788
  466.6 17.7 %collective-permute-start.48 = (bf16[216,1408]{1,0:T(8,128)(2,1)}, bf16[216,1408]{1,0:T(8,128)(2,1)}, u32[]{:S(2)}, u32[]{:S(2)}) collective-permute-start(bf16[216,1408]{1,0:T(8,128)(2,1)} %pad_maximum_fusion.1.refs_0_), channel_id=1, source_target_pairs={{0,8},{8,0},{16,24},{24,16},{1,9},{9,1},{17,25},{25,17},{2,10},{10... | collective-permute-start | bytes 1824776 | tf_op jit(solution)/shard_map/ppermute | solution.py:775
  466.6 17.7 %collective-permute-start.49 = (bf16[216,1408]{1,0:T(8,128)(2,1)}, bf16[216,1408]{1,0:T(8,128)(2,1)}, u32[]{:S(2)}, u32[]{:S(2)}) collective-permute-start(bf16[216,1408]{1,0:T(8,128)(2,1)} %collective-permute-done.39.refs_2_), channel_id=1, source_target_pairs={{0,8},{8,0},{16,24},{24,16},{1,9},{9,1},{17,25},{25,17},{2,10},{10... | collective-permute-start | bytes 1824776 | tf_op jit(solution)/shard_map/ppermute | solution.py:775
  485.6 4.5 collective-permute-start.51
  485.7 4.4 collective-permute-start.53
  490.4 14.0 %collective-permute-start.52 = (bf16[512,512]{1,0:T(8,128)(2,1)S(1)}, bf16[512,512]{1,0:T(8,128)(2,1)S(1)}, u32[]{:S(2)}, u32[]{:S(2)}) collective-permute-start(bf16[512,512]{1,0:T(8,128)(2,1)S(1)} %get-tuple-element.552), channel_id=1, source_target_pairs={{0,16},{8,24},{16,0},{24,8},{1,17},{9,25},{17,1},{25,9},{2,18},{10... | collective-permute-start | bytes 1572872 | tf_op jit(solution)/shard_map/ppermute | solution.py:788
  516.9 68.1 %collective-permute-start.54 = (bf16[256,1152]{1,0:T(8,128)(2,1)S(1)}, bf16[256,1152]{1,0:T(8,128)(2,1)S(1)}, u32[]{:S(2)}, u32[]{:S(2)}) collective-permute-start(bf16[256,1152]{1,0:T(8,128)(2,1)S(1)} %slice.365), channel_id=1, source_target_pairs={{0,16},{8,24},{16,0},{24,8},{1,17},{9,25},{17,1},{25,9},{2,18},{10... | collective-permute-start | bytes 1769480 | tf_op jit(solution)/shard_map/ppermute | solution.py:788
  (116 other events, 897.9 us)

commit v5 on v4

--- a/solution.py
+++ b/solution.py
@@ -1027,16 +1027,20 @@
 
 def output_gradients(attn, inner, g_branch, ready, n_f):
     columns = g_branch.shape[1]
+    wide_columns = columns + -columns % (128 * CORES)
     sizes = [part.shape[-2] if part.ndim == 3 else part.shape[1] // n_f for part in (attn, inner, ready)]
 
     def body(a, b, g, done, out):
-        first = by_owner(out, 0, t_mul(a[...], g[...]), n_f)
-        first = by_owner(out, first, t_mul(b[...], g[...]), n_f)
-        out[:, first:, :] = done[...]
+        main = out.at[:, :, :columns]
+        first = by_owner(main, 0, t_mul(a[...], g[...]), n_f)
+        first = by_owner(main, first, t_mul(b[...], g[...]), n_f)
+        out[:, first:, :columns] = done[...]
+        if columns < wide_columns:
+            out[:, :, columns:] = jnp.zeros((n_f, sum(sizes), wide_columns - columns), low)
 
     return pl.pallas_call(
         body,
-        out_shape=jax.ShapeDtypeStruct((n_f, sum(sizes), columns), low),
+        out_shape=jax.ShapeDtypeStruct((n_f, sum(sizes), wide_columns), low),
         cost_estimate=brief(2),
         compiler_params=pltpu.CompilerParams(vmem_limit_bytes=40 * 2**20),
     )(attn, inner, g_branch, ready)
@@ -1124,7 +1128,6 @@
             low_end, high_end = max(start, column), min(end, column + block.shape[1])
             if low_end < high_end:
                 wanted.append((at, offset, low_end - column, high_end - column, side, low_end - start))
-    adapters = [a.reshape(n_f, own_rows, rank) for a in adapters]
 
     def body(x, lower_g, lower_u, *refs):
         blocks, refs = refs[: len(items)], refs[len(items) + len(before) :]
@@ -1392,8 +1395,20 @@
     mid = resid + active * (projected[:, :width] + mul(o_inner, o_raise))
     r2 = lax.rsqrt(jnp.mean(mid * mid, axis=-1, keepdims=True) + epsilon)
     unit2 = (mid * r2).astype(low)
-    unit2, mid, r2, g_mlp, attn_low, o_inner, log_total = tie(
-        (slabs,), (unit2, mid, r2, g_mlp, attn_low, o_inner, log_total)
+    unit2, mid, r2, g_mlp, attn_low, o_inner, log_total, gate_adapter, up_adapter, d_raise = tie(
+        (slabs,),
+        (
+            unit2,
+            mid,
+            r2,
+            g_mlp,
+            attn_low,
+            o_inner,
+            log_total,
+            gate_adapter.reshape(n_f, own_rows, rank),
+            up_adapter.reshape(n_f, own_rows, rank),
+            d_raise,
+        ),
     )
 
     slabs.advance()
@@ -1447,13 +1462,13 @@
     down_sums.advance()
     counted.advance()
     gg = t_mul(unit2, g_gate).astype(low)
-    gg_raise = t_mul(gate_adapter, gg).astype(low)
+    gg_raise = t_mul(gate_adapter.reshape(width, rank), gg).astype(low)
     gg, gg_raise, g_gate, g_up, unit2 = tie(
         (down_sums, counted), (gg, gg_raise, g_gate, g_up, unit2)
     )
     down_sums.advance()
     gu = t_mul(unit2, g_up).astype(low)
-    gu_raise = t_mul(up_adapter, gu).astype(low)
+    gu_raise = t_mul(up_adapter.reshape(width, rank), gu).astype(low)
     gg, gu, gg_raise, gu_raise, g_gate, g_up = tie(
         (down_sums,), (gg, gu, gg_raise, gu_raise, g_gate, g_up)
     )
@@ -1507,8 +1522,22 @@
     g_branch = (active * g_mid).astype(low)
     g_inner = mul_t(g_branch, o_raise).astype(low)
     g_attn = mul_t(jnp.concatenate([g_branch, g_inner], axis=1), side_o).astype(low)
-    g_attn, terms, near, g_mid, g_branch, down_rows = tie(
-        (slab_sums,), (g_attn, terms, near, g_mid, g_branch, down_rows)
+    own_full = [
+        lax.dynamic_index_in_dim(full, lax.axis_index("fsdp"), 0, False)
+        for full in (gate_full, up_full)
+    ]
+    merged = jnp.concatenate(own_full, axis=1)
+    own_q = q_weight.astype(wide) + mul(q_down, q_raise)
+    own_kv = jnp.concatenate(
+        [
+            k_weight.astype(wide) + mul(k_down, k_raise),
+            v_weight.astype(wide) + mul(v_down, v_raise),
+        ],
+        axis=1,
+    )
+    g_attn, terms, near, g_mid, g_branch, down_rows, merged, own_q, own_kv = tie(
+        (slab_sums,),
+        (g_attn, terms, near, g_mid, g_branch, down_rows, merged, own_q, own_kv),
     )
 
     down_rows = group.across(down_rows)
@@ -1563,18 +1592,13 @@
 
     g_slab = slab_sums.done(wide)
     unit_grad = g_slab[rank_rows:]
-    own_full = [
-        lax.dynamic_index_in_dim(full, lax.axis_index("fsdp"), 0, False)
-        for full in (gate_full, up_full)
-    ]
-    merged = jnp.concatenate(own_full, axis=1).astype(wide)
     weight_grad = (unit_grad * gain2).astype(low)
     mlp_small = jnp.concatenate(
         [
             mul_t(weight_grad[:, :slab], g_raise),
             mul_t(weight_grad[:, slab:], u_raise),
             jnp.broadcast_to(
-                jnp.sum(unit_grad * merged, axis=1, keepdims=True) / gain2, (own_rows, 128)
+                jnp.sum(unit_grad * merged.astype(wide), axis=1, keepdims=True) / gain2, (own_rows, 128)
             ),
         ],
         axis=1,
@@ -1588,6 +1612,7 @@
     for first, second in zip(far_first, far, strict=True):
         own_branch = own_branch + jnp.concatenate([first, second], axis=0).astype(wide)
     outputs = (mid + active * own_branch).astype(low).reshape(rows, length, width)
+    packs[0] = packs[0][:, :width]
     o_pack, q_pack, kv_pack = (pack.astype(wide) for pack in packs)
 
     grad_o_weight = o_pack[:o_rows]
@@ -1602,14 +1627,6 @@
     grad_q_down = mul_t(grad_q_weight.astype(low), q_raise)
     grad_k_down = mul_t(grad_k_weight.astype(low), k_raise)
     grad_v_down = mul_t(grad_v_weight.astype(low), v_raise)
-    own_q = q_weight.astype(wide) + mul(q_down, q_raise)
-    own_kv = jnp.concatenate(
-        [
-            k_weight.astype(wide) + mul(k_down, k_raise),
-            v_weight.astype(wide) + mul(v_down, v_raise),
-        ],
-        axis=1,
-    )
     grad_attn_gain = jnp.sum(q_pack[:own_rows] * own_q, axis=1) + jnp.sum(
         kv_pack[:own_rows] * own_kv, axis=1
     )

time: 619 us -> 609 us (0.984)
    unnamed x256 -> x276, local copies, waits for them, and re-layouts: 22.9 us -> 21.2 us
  transfers between devices with their start and end apart: 56 -> 56, of which waited for: 13 -> 10; matrix products, arithmetic and copies ran while one was open for 24% -> 24% of each run, Pallas kernels for 47% -> 47%
where the time goes in v5:
time: 609 us; the launch traced here: 600 us
  Pallas kernels  295 us (48%)
  matrix products  118 us (19%)
  waiting for transfers between devices  54.8 us (9%)
  starting transfers between devices  53.1 us (9%)
  local copies, waits for them, and re-layouts  42.2 us (7%)
  other arithmetic  34.4 us (6%)
    pallas_call x1, Pallas kernels, scatter_whole(): pl.pallas_call(body, out_shape=tuple((jax.ShapeDtypeStruct(pack.shape[1:]...  62.7 us
    pallas_call x1, Pallas kernels, gather_whole(): pl.pallas_call(body, out_shape=tuple((jax.ShapeDtypeStruct((n_f,) + b.sha...  60 us
    dot_general x17, matrix products, mul_t(): lax.dot_general(left, right, (((1,), (1,)), ((), ())), preferred_element_...  55.6 us
    pallas_call x2, Pallas kernels, gather_group(): pl.pallas_call(body, out_shape=jax.ShapeDtypeStruct((n_seq,) + block.shap...  54.4 us
    dot_general x9, matrix products, t_mul(): lax.dot_general(left, right, (((0,), (0,)), ((), ())), preferred_element_...  40.9 us
    pallas_call x2, Pallas kernels, mlp_forward(): pl.pallas_call(body, grid=(stop - first,), out_shape=(jax.ShapeDtypeStruc...  40.4 us
    ppermute x32, starting transfers between devices, hop(): return lax.ppermute(block, 'fsdp', self.up if way > 0 else self.down)  35.5 us
    ppermute x32, waiting for transfers between devices, hop(): return lax.ppermute(block, 'fsdp', self.up if way > 0 else self.down)  26.7 us
  transfers between devices with their start and end apart: 56, of which 10 were waited for; matrix products, arithmetic and copies ran while one was open for 24% of the time, Pallas kernels for 47%

profile of v5, /device:TPU:0, one launch (start us, length us, event | category | flops | bytes accessed | tf_op | source)
XLA Modules:
  0.0 599.9 jit_solution(4068832697341043131)
XLA Ops:
  3.7 1.6 copy-done.20
  8.0 3.0 collective-permute-start
  11.2 2.0 collective-permute-start.2
  14.9 1.6 fusion.18
  16.5 1.9 pad_maximum_fusion.1.refs_0_
  18.4 1.7 multiply_sine_fusion
  20.6 1.7 fusion.14.x
  22.3 3.0 fusion.12
  29.2 60.0 %shard_map.477 = (bf16[8,144,2304]{2,1,0:T(8,128)(2,1)}, bf16[8,32,1536]{2,1,0:T(8,128)(2,1)}, bf16[8,128,1536]{2,1,0:T(8,128)(2,1)}, bf16[8,32,2560]{2,1,0:T(8,128)(2,1)}, bf16[8,144,512]{2,1,0:T(8,128)(2,1)}) custom-call(bf16[144,2304]{1,0:T(8,128)(2,1)} %copy-done.27, bf16[32,1536]{1,0:T(8,128)(2,1)} %copy-done.49, bf16[128,1536]{1,0:T(8,128)(2,1)} %copy-done.32, ...), custom_call_target="tpu_custom_call" | custom-call | tf_op jit(solution)/shard_map/pallas_call | solution.py:250
  89.3 1.6 collective-permute-start.3
  92.2 2.3 fusion.72
  94.5 6.2 %shard_map.478 = (bf16[512,1024]{1,0:T(8,128)(2,1)S(1)}, bf16[512,512]{1,0:T(8,128)(2,1)S(1)}, bf16[512,768]{1,0:T(8,128)(2,1)S(1)}) custom-call(bf16[512,1152]{1,0:T(8,128)(2,1)S(1)} %fusion.14.x, bf16[1152,2304]{1,0:T(8,128)(2,1)} %bitcast.155, bf16[256,1536]{1,0:T(8,128)(2,1)S(1)} %bitcast.138, f32[512,128]{1,0:T(8,128)S(1)} %copy-done.16, ...), custom_call_target="tpu_custom_call" | custom-call | flops 2000000000 | bytes 2000000 | tf_op jit(solution)/shard_map/pallas_call | solution.py:935
  101.5 17.3 %shard_map.479.kv = bf16[4,512,512]{2,1,0:T(8,128)(2,1)} custom-call(bf16[512,512]{1,0:T(8,128)(2,1)} %copy-done.29), custom_call_target="tpu_custom_call" | custom-call | tf_op jit(solution)/shard_map/pallas_call | solution.py:319
  118.8 2.1 slice.258.raised
  120.9 1.8 and_select_fusion.hidden
  126.4 5.1 shard_map.480
  131.5 4.4 fusion.10
  136.7 1.8 multiply_reduce_fusion.1
  140.0 12.3 %collective-permute-done.9 = bf16[512,1152]{1,0:T(8,128)(2,1)S(1)} collective-permute-done((bf16[512,1152]{1,0:T(8,128)(2,1)S(1)}, bf16[512,1152]{1,0:T(8,128)(2,1)S(1)}, u32[]{:S(2)}, u32[]{:S(2)}) %collective-permute-start.9) | collective-permute-done | bytes 1179680 | tf_op jit(solution)/shard_map/ppermute | solution.py:769
  155.0 1.6 collective-permute-start.10
  157.9 1.6 collective-permute-start.12
  160.3 37.1 %shard_map.481 = bf16[4,512,1152]{2,1,0:T(8,128)(2,1)} custom-call(bf16[512,1152]{1,0:T(8,128)(2,1)} %multiply_convert_fusion.1.x), custom_call_target="tpu_custom_call" | custom-call | tf_op jit(solution)/shard_map/pallas_call | solution.py:319
  198.6 1.6 collective-permute-start.14
  203.2 22.3 %shard_map.482 = (bf16[2048,1792]{1,0:T(8,128)(2,1)}, bf16[2048,1792]{1,0:T(8,128)(2,1)}, bf16[2048,1792]{1,0:T(8,128)(2,1)}, bf16[8,144,1792]{2,1,0:T(8,128)(2,...) custom-call(bf16[2048,1152]{1,0:T(8,128)(2,1)} %bitcast.149, ...), custom_call_target="tpu_custom_call" | custom-call | flops 3000000000 | bytes 3000000 | tf_op jit(solution)/shard_map/pallas_call | solution.py:1189
  225.6 1.6 collective-permute-start.18
  228.0 18.1 %shard_map.483 = (bf16[2048,1792]{1,0:T(8,128)(2,1)}, bf16[2048,1792]{1,0:T(8,128)(2,1)}, bf16[2048,1792]{1,0:T(8,128)(2,1)}, bf16[8,144,1792]{2,1,0:T(8,128)(2,...) custom-call(bf16[2048,1152]{1,0:T(8,128)(2,1)} %bitcast.150, ...), custom_call_target="tpu_custom_call", output_to_operand_aliasing={{0}: (12, {}), {1}: (13, {}), {2}: (14, {}), {3}: (15, {}),... | custom-call | flops 3000000000 | bytes 3000000 | tf_op jit(solution)/shard_map/pallas_call | solution.py:1189
  254.8 10.4 %convolution_convert_fusion = bf16[1792,1152]{1,0:T(8,128)(2,1)S(1)} fusion(bf16[2048,1792]{1,0:T(8,128)(2,1)S(1)} %bitcast.161, bf16[2048,1152]{1,0:T(8,128)(2,1)S(1)} %constant_dynamic-update-slice_fusion.g), kind=kOutput, calls=%fused_computation | convolution fusion | flops 8457781248 | bytes 16187392 | tf_op jit(solution)/shard_map/dot_general | solution.py:29
  265.2 1.6 collective-permute-start.26
  267.4 1.6 collective-permute-start.25
  269.6 22.9 %shard_map.485 = (bf16[2048,1792]{1,0:T(8,128)(2,1)}, bf16[2048,1792]{1,0:T(8,128)(2,1)}, bf16[1792,1152]{1,0:T(8,128)(2,1)}) custom-call(bf16[2048,1152]{1,0:T(8,128)(2,1)} %copy-done.71, bf16[256,1152]{1,0:T(8,128)(2,1)} %slice.258.raised, bf16[2048,1792]{1,0:T(8,128)(2,1)} %get-tuple-element.420.mul_g, bf16[2048,1792]{1,0:T(8,128)(2,1)} %get-tuple-element.421.mul_u, ...), custom_call_target="tpu_custom_call" | custom-call | flops 3000000000 | bytes 3000000 | tf_op jit(solution)/shard_map/pallas_call | solution.py:1251
  293.9 1.6 collective-permute-start.28
  295.4 12.9 %convolution_convert_fusion.3 = bf16[1152,1792]{1,0:T(8,128)(2,1)S(1)} fusion(bf16[2048,1152]{1,0:T(8,128)(2,1)} %bitcast.151, bf16[2048,1792]{1,0:T(8,128)(2,1)} %get-tuple-element.468), kind=kOutput, calls=%fused_computation.3 | convolution fusion | flops 8457781248 | bytes 16187392 | tf_op jit(solution)/shard_map/dot_general | solution.py:29
  308.3 1.7 collective-permute-start.29
  311.9 2.7 collective-permute-start.55
  316.0 1.7 collective-permute-start.31
  317.6 12.4 %convolution_convert_fusion.2 = bf16[1152,1792]{1,0:T(8,128)(2,1)S(1)} fusion(bf16[2048,1152]{1,0:T(8,128)(2,1)S(1)} %bitcast.154, bf16[2048,1792]{1,0:T(8,128)(2,1)} %get-tuple-element.469), kind=kOutput, calls=%fused_computation.2 | convolution fusion | flops 8457781248 | bytes 16187392 | tf_op jit(solution)/shard_map/dot_general | solution.py:29
  332.9 2.0 collective-permute-start.35
  336.5 1.7 collective-permute-start.33
  338.1 9.3 %fusion.3 = f32[1024,1152]{1,0:T(8,128)} fusion(bf16[1152,1792]{1,0:T(8,128)(2,1)S(1)} %bitcast.170, bf16[2048,1792]{1,0:T(8,128)(2,1)} %get-tuple-element.469), kind=kOutput, calls=%fused_computation.9 | convolution fusion | flops 4227858432 | bytes 12517376 | tf_op jit(solution)/shard_map/dot_general | solution.py:25
  347.5 9.7 %add_convert_fusion.1 = bf16[1024,1152]{1,0:T(8,128)(2,1)} fusion(f32[1024,1152]{1,0:T(8,128)} %fusion.3, bf16[1152,1792]{1,0:T(8,128)(2,1)S(1)} %bitcast.169, bf16[2048,1792]{1,0:T(8,128)(2,1)} %get-tuple-element.468), kind=kOutput, calls=%fused_computation.5 | convolution fusion | flops 4230217728 | bytes 14876672 | tf_op jit(solution)/shard_map/dot_general | solution.py:25
  361.9 1.7 collective-permute-start.37
  363.6 9.3 %fusion = f32[1024,1152]{1,0:T(8,128)} fusion(bf16[1152,1792]{1,0:T(8,128)(2,1)S(1)} %bitcast.171, bf16[2048,1792]{1,0:T(8,128)(2,1)} %get-tuple-element.469), kind=kOutput, calls=%fused_computation.6 | convolution fusion | flops 4227858432 | bytes 12517376 | tf_op jit(solution)/shard_map/dot_general | solution.py:25
  374.5 11.2 %add_convert_fusion = bf16[1024,1152]{1,0:T(8,128)(2,1)} fusion(f32[1024,1152]{1,0:T(8,128)} %fusion, bf16[1152,1792]{1,0:T(8,128)(2,1)} %bitcast.168, bf16[2048,1792]{1,0:T(8,128)(2,1)} %get-tuple-element.468), kind=kOutput, calls=%fused_computation.4 | convolution fusion | flops 4230217728 | bytes 14876672 | tf_op jit(solution)/shard_map/dot_general | solution.py:25
  385.7 4.8 collective-permute-done.39.refs_2_
  393.9 1.7 collective-permute-start.41
  395.8 13.6 %convolution_convert_fusion.1 = bf16[2048,1152]{1,0:T(8,128)(2,1)} fusion(bf16[2048,1792]{1,0:T(8,128)(2,1)S(1)} %bitcast.163, bf16[1792,1152]{1,0:T(8,128)(2,1)} %get-tuple-element.477), kind=kOutput, calls=%fused_computation.1 | convolution fusion | flops 8458076160 | bytes 16187392 | tf_op jit(solution)/shard_map/dot_general | solution.py:21
  409.4 10.3 %collective-permute-done.42 = bf16[512,1152]{1,0:T(8,128)(2,1)S(1)} collective-permute-done((bf16[512,1152]{1,0:T(8,128)(2,1)S(1)}, bf16[512,1152]{1,0:T(8,128)(2,1)S(1)}, u32[]{:S(2)}, u32[]{:S(2)}) %collective-permute-start.42) | collective-permute-done | bytes 1179680 | tf_op jit(solution)/shard_map/ppermute | solution.py:788
  419.7 2.9 collective-permute-done.40.refs_4_
  423.3 1.8 fusion.71
  428.9 2.4 multiply_convert_fusion
  431.3 1.6 convolution_convert_fusion.10
  432.9 2.8 fusion.19.g
  435.7 20.9 %collective-permute-done.44.refs_4_ = bf16[176,3584]{1,0:T(8,128)(2,1)S(1)} collective-permute-done((bf16[176,3584]{1,0:T(8,128)(2,1)S(1)}, bf16[176,3584]{1,0:T(8,128)(2,1)S(1)}, u32[]{:S(2)}, u32[]{:S(2)}) %collective-permute-start.44) | collective-permute-done | bytes 1261600 | tf_op jit(solution)/shard_map/ppermute | solution.py:658
  461.7 11.3 %shard_map.494 = (bf16[512,1024]{1,0:T(8,128)(2,1)}, bf16[4,512,512]{2,1,0:T(8,128)(2,1)}) custom-call(bf16[512,1024]{1,0:T(8,128)(2,1)} %copy-done.58, bf16[4,512,512]{2,1,0:T(8,128)(2,1)} %shard_map.479.kv, f32[2,256,1024]{2,1,0:T(8,128)} %and_select_fusion.hidden, f32[2,4,256,1]{3,2,1,0:T(8,128)} %copy-done.61, bf16[512,1024]{1,0:T(8,128)(2,1)} %copy-done.59, ...), custom_call_target="tpu_custom_call" | custom-call | flops 3000000000 | bytes 3000000 | tf_op jit(solution)/shard_map/pallas_call | solution.py:1010
  475.3 1.9 shard_map.495.refs_0_
  477.3 1.6 convert_add_fusion.2
  486.7 4.4 shard_map.497
  491.1 8.3 %shard_map.496 = (f32[512,1152]{1,0:T(8,128)S(1)}, bf16[8,176,1024]{2,1,0:T(8,128)(2,1)}) custom-call(bf16[512,1152]{1,0:T(8,128)(2,1)S(1)} %copy-done.12, bf16[512,256]{1,0:T(8,128)(2,1)S(1)} %copy-done.25, bf16[512,1024]{1,0:T(8,128)(2,1)S(1)} %copy-done.26, bf16[256,1536]{1,0:T(8,128)(2,1)S(1)} %bitcast.142, bf16[1152,2304]{1,0:T(8,128)(2,1)} %bitcast.156), custom_call_target="tpu_custom_call" | custom-call | flops 2000000000 | bytes 2000000 | tf_op jit(solution)/shard_map/pallas_call | solution.py:1060
  501.0 2.1 fusion.30
  505.6 2.8 fusion.15
  514.4 62.7 %shard_map.499 = (bf16[192,1280]{1,0:T(8,128)(2,1)}, bf16[176,1024]{1,0:T(8,128)(2,1)}, bf16[176,512]{1,0:T(8,128)(2,1)}, bf16[4,176,3584]{2,1,0:T(8,128)(2,1)}, f32[144,640]{1,0:T(8,128)}) custom-call(bf16[8,192,1280]{2,1,0:T(8,128)(2,1)} %copy-done.13, bf16[8,176,1024]{2,1,0:T(8,128)(2,1)} %get-tuple-element.524.refs_1_, ...), custom_call_target="tpu_custom_call" | custom-call | tf_op jit(solution)/shard_map/pallas_call | solution.py:561
  577.1 2.2 fusion.43
  584.8 8.3 %shard_map.500 = (f32[144,6912]{1,0:T(8,128)}, f32[144,6912]{1,0:T(8,128)}, f32[32,6912]{1,0:T(8,128)}, f32[32,6912]{1,0:T(8,128)}) custom-call(f32[144,1]{1,0:T(8,128)} %copy-done.23, bf16[4,176,3584]{2,1,0:T(8,128)(2,1)} %get-tuple-element.545.x), custom_call_target="tpu_custom_call" | custom-call | tf_op jit(solution)/shard_map/pallas_call | solution.py:890
  596.8 2.5 add_convert_fusion.2
  (472 shorter events, 96.6 us)
Async XLA Ops:
  8.0 81.3 %collective-permute-start = (bf16[176,3584]{1,0:T(8,128)(2,1)S(1)}, bf16[176,3584]{1,0:T(8,128)(2,1)}, u32[]{:S(2)}, u32[]{:S(2)}) collective-permute-start(bf16[176,3584]{1,0:T(8,128)(2,1)S(1)} %shard_map.475.refs_0_), channel_id=1, source_target_pairs={{0,1},{1,3},{3,5},{5,7},{7,6},{6,4},{4,2},{2,0},{8,9},{9,11},{11,1... | collective-permute-start | bytes 3784712 | tf_op jit(solution)/shard_map/ppermute | solution.py:658
  11.0 78.3 %collective-permute-start.1 = (bf16[176,3584]{1,0:T(8,128)(2,1)S(1)}, bf16[176,3584]{1,0:T(8,128)(2,1)}, u32[]{:S(2)}, u32[]{:S(2)}) collective-permute-start(bf16[176,3584]{1,0:T(8,128)(2,1)S(1)} %shard_map.475.refs_0_), channel_id=1, source_target_pairs={{1,0},{3,1},{5,3},{7,5},{6,7},{4,6},{2,4},{0,2},{9,8},{11,9},{13,1... | collective-permute-start | bytes 3784712 | tf_op jit(solution)/shard_map/ppermute | solution.py:658
  11.2 78.1 %collective-permute-start.2 = (bf16[2,256]{1,0:T(2,128)(2,1)S(1)}, bf16[2,256]{1,0:T(2,128)(2,1)S(1)}, u32[]{:S(2)}, u32[]{:S(2)}) collective-permute-start(bf16[2,256]{1,0:T(2,128)(2,1)S(1)} %convert_element_type.221), channel_id=1, source_target_pairs={{0,16},{8,24},{16,0},{24,8},{1,17},{9,25},{17,1},{25,9},{2,18},{10... | collective-permute-start | bytes 3080 | tf_op jit(solution)/shard_map/ppermute | solution.py:769
  14.9 121.8 %copy-start.116 = (f32[512]{0:T(512)}, f32[512]{0:T(512)S(1)}, u32[]{:S(2)}) copy-start(f32[512]{0:T(512)S(1)} %compare_convert_fusion) | copy-start | bytes 6148
  20.2 74.3 %copy-start.14 = (f32[512,128]{1,0:T(8,128)}, f32[512,128]{1,0:T(8,128)S(1)}, u32[]{:S(2)}) copy-start(f32[512,128]{1,0:T(8,128)S(1)} %get-tuple-element.309.sin) | copy-start | bytes 786436
  22.3 72.2 %copy-start.11 = (bf16[512,1152]{1,0:T(8,128)(2,1)}, bf16[512,1152]{1,0:T(8,128)(2,1)S(1)}, u32[]{:S(2)}) copy-start(bf16[512,1152]{1,0:T(8,128)(2,1)S(1)} %fusion.14.x) | copy-start | bytes 3538948
  29.2 65.3 %copy-start.16 = (f32[512,128]{1,0:T(8,128)S(1)}, f32[512,128]{1,0:T(8,128)}, u32[]{:S(2)}) copy-start(f32[512,128]{1,0:T(8,128)} %get-tuple-element.308.cos) | copy-start | bytes 786436
  89.3 33.3 %collective-permute-start.3 = (bf16[176,3584]{1,0:T(8,128)(2,1)}, bf16[176,3584]{1,0:T(8,128)(2,1)}, u32[]{:S(2)}, u32[]{:S(2)}) collective-permute-start(bf16[176,3584]{1,0:T(8,128)(2,1)} %collective-permute-done.refs_1_), channel_id=1, source_target_pairs={{0,1},{1,3},{3,5},{5,7},{7,6},{6,4},{4,2},{2,0},{8,9},{9,11},{11,1... | collective-permute-start | bytes 3784712 | tf_op jit(solution)/shard_map/ppermute | solution.py:658
  90.9 31.8 %collective-permute-start.4 = (bf16[176,3584]{1,0:T(8,128)(2,1)}, bf16[176,3584]{1,0:T(8,128)(2,1)}, u32[]{:S(2)}, u32[]{:S(2)}) collective-permute-start(bf16[176,3584]{1,0:T(8,128)(2,1)} %collective-permute-done.1.refs_2_), channel_id=1, source_target_pairs={{1,0},{3,1},{5,3},{7,5},{6,7},{4,6},{2,4},{0,2},{9,8},{11,9},{13,1... | collective-permute-start | bytes 3784712 | tf_op jit(solution)/shard_map/ppermute | solution.py:658
  91.6 29.3 %collective-permute-start.5 = (bf16[2,256]{1,0:T(2,128)(2,1)S(1)}, bf16[2,256]{1,0:T(2,128)(2,1)S(1)}, u32[]{:S(2)}, u32[]{:S(2)}) collective-permute-start(bf16[2,256]{1,0:T(2,128)(2,1)S(1)} %convert_element_type.221), channel_id=1, source_target_pairs={{0,8},{8,0},{16,24},{24,16},{1,9},{9,1},{17,25},{25,17},{2,10},{10... | collective-permute-start | bytes 3080 | tf_op jit(solution)/shard_map/ppermute | solution.py:775
  91.7 29.2 %collective-permute-start.6 = (bf16[2,256]{1,0:T(2,128)(2,1)S(1)}, bf16[2,256]{1,0:T(2,128)(2,1)S(1)}, u32[]{:S(2)}, u32[]{:S(2)}) collective-permute-start(bf16[2,256]{1,0:T(2,128)(2,1)S(1)} %collective-permute-done.2), channel_id=1, source_target_pairs={{0,8},{8,0},{16,24},{24,16},{1,9},{9,1},{17,25},{25,17},{2,10},{10... | collective-permute-start | bytes 3080 | tf_op jit(solution)/shard_map/ppermute | solution.py:775
  101.5 101.0 %copy-start.33 = (bf16[512,768]{1,0:T(8,128)(2,1)}, bf16[512,768]{1,0:T(8,128)(2,1)S(1)}, u32[]{:S(2)}) copy-start(bf16[512,768]{1,0:T(8,128)(2,1)S(1)} %get-tuple-element.505) | copy-start | bytes 2359300
  122.7 29.9 %collective-permute-start.7 = (bf16[176,3584]{1,0:T(8,128)(2,1)}, bf16[176,3584]{1,0:T(8,128)(2,1)S(1)}, u32[]{:S(2)}, u32[]{:S(2)}) collective-permute-start(bf16[176,3584]{1,0:T(8,128)(2,1)} %collective-permute-done.3.refs_3_), channel_id=1, source_target_pairs={{0,1},{1,3},{3,5},{5,7},{7,6},{6,4},{4,2},{2,0},{8,9},{9,11},{11,1... | collective-permute-start | bytes 3784712 | tf_op jit(solution)/shard_map/ppermute | solution.py:658
  124.2 29.8 %collective-permute-start.8 = (bf16[176,3584]{1,0:T(8,128)(2,1)}, bf16[176,3584]{1,0:T(8,128)(2,1)S(1)}, u32[]{:S(2)}, u32[]{:S(2)}) collective-permute-start(bf16[176,3584]{1,0:T(8,128)(2,1)} %collective-permute-done.4.refs_4_), channel_id=1, source_target_pairs={{1,0},{3,1},{5,3},{7,5},{6,7},{4,6},{2,4},{0,2},{9,8},{11,9},{13,1... | collective-permute-start | bytes 3784712 | tf_op jit(solution)/shard_map/ppermute | solution.py:658
  124.9 27.4 %collective-permute-start.9 = (bf16[512,1152]{1,0:T(8,128)(2,1)S(1)}, bf16[512,1152]{1,0:T(8,128)(2,1)S(1)}, u32[]{:S(2)}, u32[]{:S(2)}) collective-permute-start(bf16[512,1152]{1,0:T(8,128)(2,1)S(1)} %copy-done.83), channel_id=1, source_target_pairs={{0,16},{8,24},{16,0},{24,8},{1,17},{9,25},{17,1},{25,9},{2,18},{10... | collective-permute-start | bytes 3538952 | tf_op jit(solution)/shard_map/ppermute | solution.py:769
  155.0 42.5 %collective-permute-start.10 = (bf16[176,1792]{1,0:T(8,128)(2,1)}, bf16[176,1792]{1,0:T(8,128)(2,1)S(1)}, u32[]{:S(2)}, u32[]{:S(2)}) collective-permute-start(bf16[176,1792]{1,0:T(8,128)(2,1)} %slice.198), channel_id=1, source_target_pairs={{0,1},{1,3},{3,5},{5,7},{7,6},{6,4},{4,2},{2,0},{8,9},{9,11},{11,1... | collective-permute-start | bytes 1892360 | tf_op jit(solution)/shard_map/ppermute | solution.py:658
  157.4 40.0 %collective-permute-start.11 = (bf16[176,1792]{1,0:T(8,128)(2,1)}, bf16[176,1792]{1,0:T(8,128)(2,1)S(1)}, u32[]{:S(2)}, u32[]{:S(2)}) collective-permute-start(bf16[176,1792]{1,0:T(8,128)(2,1)} %slice.199), channel_id=1, source_target_pairs={{1,0},{3,1},{5,3},{7,5},{6,7},{4,6},{2,4},{0,2},{9,8},{11,9},{13,1... | collective-permute-start | bytes 1892360 | tf_op jit(solution)/shard_map/ppermute | solution.py:658
  157.9 39.5 %collective-permute-start.12 = (bf16[216,1408]{1,0:T(8,128)(2,1)}, bf16[216,1408]{1,0:T(8,128)(2,1)}, u32[]{:S(2)}, u32[]{:S(2)}) collective-permute-start(bf16[216,1408]{1,0:T(8,128)(2,1)} %pad_maximum_fusion.1.refs_0_), channel_id=1, source_target_pairs={{0,1},{1,3},{3,5},{5,7},{7,6},{6,4},{4,2},{2,0},{8,9},{9,11},{11,1... | collective-permute-start | bytes 1824776 | tf_op jit(solution)/shard_map/ppermute | solution.py:658
  159.5 38.0 %collective-permute-start.13 = (bf16[216,1408]{1,0:T(8,128)(2,1)}, bf16[216,1408]{1,0:T(8,128)(2,1)}, u32[]{:S(2)}, u32[]{:S(2)}) collective-permute-start(bf16[216,1408]{1,0:T(8,128)(2,1)} %pad_maximum_fusion.1.refs_0_), channel_id=1, source_target_pairs={{1,0},{3,1},{5,3},{7,5},{6,7},{4,6},{2,4},{0,2},{9,8},{11,9},{13,1... | collective-permute-start | bytes 1824776 | tf_op jit(solution)/shard_map/ppermute | solution.py:658
  160.2 38.0 %collective-permute-start.20 = (f32[6]{0:T(128)S(1)}, f32[6]{0:T(128)S(1)}, u32[]{:S(2)}, u32[]{:S(2)}) collective-permute-start(f32[6]{0:T(128)S(1)} %pad_maximum_fusion.11), channel_id=1, source_target_pairs={{0,8},{8,0},{16,24},{24,16},{1,9},{9,1},{17,25},{25,17},{2,10},{10... | collective-permute-start | bytes 80 | tf_op jit(solution)/shard_map/ppermute | solution.py:817
  197.5 28.1 %collective-permute-start.16 = (bf16[512,1152]{1,0:T(8,128)(2,1)S(1)}, bf16[512,1152]{1,0:T(8,128)(2,1)}, u32[]{:S(2)}, u32[]{:S(2)}) collective-permute-start(bf16[512,1152]{1,0:T(8,128)(2,1)S(1)} %copy-done.84), channel_id=1, source_target_pairs={{0,8},{8,0},{16,24},{24,16},{1,9},{9,1},{17,25},{25,17},{2,10},{10... | collective-permute-start | bytes 3538952 | tf_op jit(solution)/shard_map/ppermute | solution.py:775
  198.0 27.5 %collective-permute-start.17 = (bf16[512,1152]{1,0:T(8,128)(2,1)S(1)}, bf16[512,1152]{1,0:T(8,128)(2,1)S(1)}, u32[]{:S(2)}, u32[]{:S(2)}) collective-permute-start(bf16[512,1152]{1,0:T(8,128)(2,1)S(1)} %copy-done.97), channel_id=1, source_target_pairs={{0,8},{8,0},{16,24},{24,16},{1,9},{9,1},{17,25},{25,17},{2,10},{10... | collective-permute-start | bytes 3538952 | tf_op jit(solution)/shard_map/ppermute | solution.py:775
  198.6 27.0 %collective-permute-start.14 = (bf16[216,1408]{1,0:T(8,128)(2,1)}, bf16[216,1408]{1,0:T(8,128)(2,1)S(1)}, u32[]{:S(2)}, u32[]{:S(2)}) collective-permute-start(bf16[216,1408]{1,0:T(8,128)(2,1)} %collective-permute-done.12.refs_1_), channel_id=1, source_target_pairs={{0,1},{1,3},{3,5},{5,7},{7,6},{6,4},{4,2},{2,0},{8,9},{9,11},{11,1... | collective-permute-start | bytes 1824776 | tf_op jit(solution)/shard_map/ppermute | solution.py:658
  200.2 25.4 %collective-permute-start.15 = (bf16[216,1408]{1,0:T(8,128)(2,1)}, bf16[216,1408]{1,0:T(8,128)(2,1)}, u32[]{:S(2)}, u32[]{:S(2)}) collective-permute-start(bf16[216,1408]{1,0:T(8,128)(2,1)} %collective-permute-done.13.refs_2_), channel_id=1, source_target_pairs={{1,0},{3,1},{5,3},{7,5},{6,7},{4,6},{2,4},{0,2},{9,8},{11,9},{13,1... | collective-permute-start | bytes 1824776 | tf_op jit(solution)/shard_map/ppermute | solution.py:658
  225.6 24.1 %collective-permute-start.18 = (bf16[216,1408]{1,0:T(8,128)(2,1)S(1)}, bf16[216,1408]{1,0:T(8,128)(2,1)S(1)}, u32[]{:S(2)}, u32[]{:S(2)}) collective-permute-start(bf16[216,1408]{1,0:T(8,128)(2,1)S(1)} %collective-permute-done.14.refs_3_), channel_id=1, source_target_pairs={{0,1},{1,3},{3,5},{5,7},{7,6},{6,4},{4,2},{2,0},{8,9},{9,11},{11,1... | collective-permute-start | bytes 1824776 | tf_op jit(solution)/shard_map/ppermute | solution.py:658
  227.2 22.5 %collective-permute-start.19 = (bf16[216,1408]{1,0:T(8,128)(2,1)}, bf16[216,1408]{1,0:T(8,128)(2,1)S(1)}, u32[]{:S(2)}, u32[]{:S(2)}) collective-permute-start(bf16[216,1408]{1,0:T(8,128)(2,1)} %collective-permute-done.15.refs_4_), channel_id=1, source_target_pairs={{1,0},{3,1},{5,3},{7,5},{6,7},{4,6},{2,4},{0,2},{9,8},{11,9},{13,1... | collective-permute-start | bytes 1824776 | tf_op jit(solution)/shard_map/ppermute | solution.py:658
  249.8 15.3 %collective-permute-start.23 = (f32[6]{0:T(128)S(1)}, f32[6]{0:T(128)S(1)}, u32[]{:S(2)}, u32[]{:S(2)}) collective-permute-start(f32[6]{0:T(128)S(1)} %fusion.108), channel_id=1, source_target_pairs={{0,16},{8,24},{16,0},{24,8},{1,17},{9,25},{17,1},{25,9},{2,18},{10... | collective-permute-start | bytes 80 | tf_op jit(solution)/shard_map/ppermute | solution.py:817
  250.8 14.4 %collective-permute-start.22 = (bf16[216,768]{1,0:T(8,128)(2,1)S(1)}, bf16[216,768]{1,0:T(8,128)(2,1)S(1)}, u32[]{:S(2)}, u32[]{:S(2)}) collective-permute-start(bf16[216,768]{1,0:T(8,128)(2,1)S(1)} %slice.201), channel_id=1, source_target_pairs={{1,0},{3,1},{5,3},{7,5},{6,7},{4,6},{2,4},{0,2},{9,8},{11,9},{13,1... | collective-permute-start | bytes 995336 | tf_op jit(solution)/shard_map/ppermute | solution.py:658
  252.1 13.1 %collective-permute-start.21 = (bf16[216,640]{1,0:T(8,128)(2,1)S(1)}, bf16[216,640]{1,0:T(8,128)(2,1)S(1)}, u32[]{:S(2)}, u32[]{:S(2)}) collective-permute-start(bf16[216,640]{1,0:T(8,128)(2,1)S(1)} %slice.200), channel_id=1, source_target_pairs={{0,1},{1,3},{3,5},{5,7},{7,6},{6,4},{4,2},{2,0},{8,9},{9,11},{11,1... | collective-permute-start | bytes 829448 | tf_op jit(solution)/shard_map/ppermute | solution.py:658
  265.2 27.2 %collective-permute-start.26 = (f32[6]{0:T(128)S(1)}, f32[6]{0:T(128)S(1)}, u32[]{:S(2)}, u32[]{:S(2)}) collective-permute-start(f32[6]{0:T(128)S(1)} %add.210), channel_id=1, source_target_pairs={{0,1},{1,0},{2,3},{3,2},{4,5},{5,4},{6,7},{7,6},{8,9},{9,8},{10,11... | collective-permute-start | bytes 80 | tf_op jit(solution)/shard_map/ppermute | solution.py:817
  267.4 25.2 %collective-permute-start.25 = (bf16[216,640]{1,0:T(8,128)(2,1)S(1)}, bf16[216,640]{1,0:T(8,128)(2,1)S(1)}, u32[]{:S(2)}, u32[]{:S(2)}) collective-permute-start(bf16[216,640]{1,0:T(8,128)(2,1)S(1)} %get-tuple-element.416), channel_id=1, source_target_pairs={{1,0},{3,1},{5,3},{7,5},{6,7},{4,6},{2,4},{0,2},{9,8},{11,9},{13,1... | collective-permute-start | bytes 829448 | tf_op jit(solution)/shard_map/ppermute | solution.py:658
  269.0 23.5 %collective-permute-start.24 = (bf16[216,512]{1,0:T(8,128)(2,1)S(1)}, bf16[216,512]{1,0:T(8,128)(2,1)S(1)}, u32[]{:S(2)}, u32[]{:S(2)}) collective-permute-start(bf16[216,512]{1,0:T(8,128)(2,1)S(1)} %get-tuple-element.415), channel_id=1, source_target_pairs={{0,1},{1,3},{3,5},{5,7},{7,6},{6,4},{4,2},{2,0},{8,9},{9,11},{11,1... | collective-permute-start | bytes 663560 | tf_op jit(solution)/shard_map/ppermute | solution.py:658
  293.4 18.6 %collective-permute-start.27 = (bf16[216,1152]{1,0:T(8,128)(2,1)S(1)}, bf16[216,1152]{1,0:T(8,128)(2,1)S(1)}, u32[]{:S(2)}, u32[]{:S(2)}) collective-permute-start(bf16[216,1152]{1,0:T(8,128)(2,1)S(1)} %get-tuple-element.436), channel_id=1, source_target_pairs={{0,1},{1,3},{3,5},{5,7},{7,6},{6,4},{4,2},{2,0},{8,9},{9,11},{11,1... | collective-permute-start | bytes 1493000 | tf_op jit(solution)/shard_map/ppermute | solution.py:658
  293.9 18.1 %collective-permute-start.28 = (bf16[216,1152]{1,0:T(8,128)(2,1)S(1)}, bf16[216,1152]{1,0:T(8,128)(2,1)S(1)}, u32[]{:S(2)}, u32[]{:S(2)}) collective-permute-start(bf16[216,1152]{1,0:T(8,128)(2,1)S(1)} %get-tuple-element.437), channel_id=1, source_target_pairs={{1,0},{3,1},{5,3},{7,5},{6,7},{4,6},{2,4},{0,2},{9,8},{11,9},{13,1... | collective-permute-start | bytes 1493000 | tf_op jit(solution)/shard_map/ppermute | solution.py:658
  308.3 3.6 collective-permute-start.29
  311.4 114.3 %copy-start.4 = (bf16[256,1792]{1,0:T(8,128)(2,1)}, bf16[256,1792]{1,0:T(8,128)(2,1)S(1)}, u32[]{:S(2)}) copy-start(bf16[256,1792]{1,0:T(8,128)(2,1)S(1)} %convolution_convert_fusion.7) | copy-start | bytes 2752516
  311.9 19.5 %collective-permute-start.55 = (f32[6]{0:T(128)S(1)}, f32[6]{0:T(128)S(1)}, u32[]{:S(2)}, u32[]{:S(2)}) collective-permute-start(f32[6]{0:T(128)S(1)} %add.212), channel_id=1, source_target_pairs={{0,4},{1,5},{2,6},{3,7},{4,0},{5,1},{6,2},{7,3},{8,12},{9,13},{10,... | collective-permute-start | bytes 80 | tf_op jit(solution)/shard_map/ppermute | solution.py:817
  315.5 16.0 %collective-permute-start.30 = (bf16[216,1152]{1,0:T(8,128)(2,1)S(1)}, bf16[216,1152]{1,0:T(8,128)(2,1)S(1)}, u32[]{:S(2)}, u32[]{:S(2)}) collective-permute-start(bf16[216,1152]{1,0:T(8,128)(2,1)S(1)} %get-tuple-element.443), channel_id=1, source_target_pairs={{0,1},{1,3},{3,5},{5,7},{7,6},{6,4},{4,2},{2,0},{8,9},{9,11},{11,1... | collective-permute-start | bytes 1493000 | tf_op jit(solution)/shard_map/ppermute | solution.py:658
  316.0 15.6 %collective-permute-start.31 = (bf16[216,1152]{1,0:T(8,128)(2,1)S(1)}, bf16[216,1152]{1,0:T(8,128)(2,1)S(1)}, u32[]{:S(2)}, u32[]{:S(2)}) collective-permute-start(bf16[216,1152]{1,0:T(8,128)(2,1)S(1)} %get-tuple-element.444), channel_id=1, source_target_pairs={{1,0},{3,1},{5,3},{7,5},{6,7},{4,6},{2,4},{0,2},{9,8},{11,9},{13,1... | collective-permute-start | bytes 1493000 | tf_op jit(solution)/shard_map/ppermute | solution.py:658
  330.1 95.6 %copy-start.2 = (bf16[1152,1792]{1,0:T(8,128)(2,1)}, bf16[1152,1792]{1,0:T(8,128)(2,1)S(1)}, u32[]{:S(2)}) copy-start(bf16[1152,1792]{1,0:T(8,128)(2,1)S(1)} %convolution_convert_fusion.2) | copy-start | bytes 12386308
  331.5 94.2 %copy-start.6 = (bf16[256,1792]{1,0:T(8,128)(2,1)}, bf16[256,1792]{1,0:T(8,128)(2,1)S(1)}, u32[]{:S(2)}) copy-start(bf16[256,1792]{1,0:T(8,128)(2,1)S(1)} %convolution_convert_fusion.6) | copy-start | bytes 2752516
  332.5 24.7 %collective-permute-start.34 = (bf16[216,1152]{1,0:T(8,128)(2,1)S(1)}, bf16[216,1152]{1,0:T(8,128)(2,1)S(1)}, u32[]{:S(2)}, u32[]{:S(2)}) collective-permute-start(bf16[216,1152]{1,0:T(8,128)(2,1)S(1)} %get-tuple-element.462), channel_id=1, source_target_pairs={{0,1},{1,3},{3,5},{5,7},{7,6},{6,4},{4,2},{2,0},{8,9},{9,11},{11,1... | collective-permute-start | bytes 1493000 | tf_op jit(solution)/shard_map/ppermute | solution.py:658
  332.9 24.3 %collective-permute-start.35 = (bf16[216,1152]{1,0:T(8,128)(2,1)S(1)}, bf16[216,1152]{1,0:T(8,128)(2,1)S(1)}, u32[]{:S(2)}, u32[]{:S(2)}) collective-permute-start(bf16[216,1152]{1,0:T(8,128)(2,1)S(1)} %get-tuple-element.463), channel_id=1, source_target_pairs={{1,0},{3,1},{5,3},{7,5},{6,7},{4,6},{2,4},{0,2},{9,8},{11,9},{13,1... | collective-permute-start | bytes 1493000 | tf_op jit(solution)/shard_map/ppermute | solution.py:658
  336.1 24.7 %collective-permute-start.32 = (bf16[176,1792]{1,0:T(8,128)(2,1)S(1)}, bf16[176,1792]{1,0:T(8,128)(2,1)S(1)}, u32[]{:S(2)}, u32[]{:S(2)}) collective-permute-start(bf16[176,1792]{1,0:T(8,128)(2,1)S(1)} %get-tuple-element.454), channel_id=1, source_target_pairs={{0,1},{1,3},{3,5},{5,7},{7,6},{6,4},{4,2},{2,0},{8,9},{9,11},{11,1... | collective-permute-start | bytes 1892360 | tf_op jit(solution)/shard_map/ppermute | solution.py:658
  336.5 24.2 %collective-permute-start.33 = (bf16[176,1792]{1,0:T(8,128)(2,1)S(1)}, bf16[176,1792]{1,0:T(8,128)(2,1)S(1)}, u32[]{:S(2)}, u32[]{:S(2)}) collective-permute-start(bf16[176,1792]{1,0:T(8,128)(2,1)S(1)} %get-tuple-element.455), channel_id=1, source_target_pairs={{1,0},{3,1},{5,3},{7,5},{6,7},{4,6},{2,4},{0,2},{9,8},{11,9},{13,1... | collective-permute-start | bytes 1892360 | tf_op jit(solution)/shard_map/ppermute | solution.py:658
  361.5 29.0 %collective-permute-start.36 = (bf16[176,3584]{1,0:T(8,128)(2,1)S(1)}, bf16[176,3584]{1,0:T(8,128)(2,1)S(1)}, u32[]{:S(2)}, u32[]{:S(2)}) collective-permute-start(bf16[176,3584]{1,0:T(8,128)(2,1)S(1)} %get-tuple-element.466), channel_id=1, source_target_pairs={{0,1},{1,3},{3,5},{5,7},{7,6},{6,4},{4,2},{2,0},{8,9},{9,11},{11,1... | collective-permute-start | bytes 3784712 | tf_op jit(solution)/shard_map/ppermute | solution.py:658
  361.9 28.5 %collective-permute-start.37 = (bf16[176,3584]{1,0:T(8,128)(2,1)S(1)}, bf16[176,3584]{1,0:T(8,128)(2,1)S(1)}, u32[]{:S(2)}, u32[]{:S(2)}) collective-permute-start(bf16[176,3584]{1,0:T(8,128)(2,1)S(1)} %get-tuple-element.467), channel_id=1, source_target_pairs={{1,0},{3,1},{5,3},{7,5},{6,7},{4,6},{2,4},{0,2},{9,8},{11,9},{13,1... | collective-permute-start | bytes 3784712 | tf_op jit(solution)/shard_map/ppermute | solution.py:658
  374.0 16.5 %collective-permute-start.38 = (bf16[512,1152]{1,0:T(8,128)(2,1)}, bf16[512,1152]{1,0:T(8,128)(2,1)S(1)}, u32[]{:S(2)}, u32[]{:S(2)}) collective-permute-start(bf16[512,1152]{1,0:T(8,128)(2,1)} %slice.207), channel_id=1, source_target_pairs={{0,8},{8,0},{16,24},{24,16},{1,9},{9,1},{17,25},{25,17},{2,10},{10... | collective-permute-start | bytes 3538952 | tf_op jit(solution)/shard_map/ppermute | solution.py:779
  374.0 16.5 %collective-permute-start.39 = (bf16[216,1408]{1,0:T(8,128)(2,1)}, bf16[216,1408]{1,0:T(8,128)(2,1)}, u32[]{:S(2)}, u32[]{:S(2)}) collective-permute-start(bf16[216,1408]{1,0:T(8,128)(2,1)} %pad_maximum_fusion.2.refs_0_), channel_id=1, source_target_pairs={{0,16},{8,24},{16,0},{24,8},{1,17},{9,25},{17,1},{25,9},{2,18},{10... | collective-permute-start | bytes 1824776 | tf_op jit(solution)/shard_map/ppermute | solution.py:769
  392.0 27.7 %collective-permute-start.42 = (bf16[512,1152]{1,0:T(8,128)(2,1)S(1)}, bf16[512,1152]{1,0:T(8,128)(2,1)S(1)}, u32[]{:S(2)}, u32[]{:S(2)}) collective-permute-start(bf16[512,1152]{1,0:T(8,128)(2,1)S(1)} %add_convert_fusion.3), channel_id=1, source_target_pairs={{0,16},{8,24},{16,0},{24,8},{1,17},{9,25},{17,1},{25,9},{2,18},{10... | collective-permute-start | bytes 3538952 | tf_op jit(solution)/shard_map/ppermute | solution.py:788
  393.5 29.1 %collective-permute-start.40 = (bf16[176,3584]{1,0:T(8,128)(2,1)S(1)}, bf16[176,3584]{1,0:T(8,128)(2,1)S(1)}, u32[]{:S(2)}, u32[]{:S(2)}) collective-permute-start(bf16[176,3584]{1,0:T(8,128)(2,1)S(1)} %get-tuple-element.474), channel_id=1, source_target_pairs={{0,1},{1,3},{3,5},{5,7},{7,6},{6,4},{4,2},{2,0},{8,9},{9,11},{11,1... | collective-permute-start | bytes 3784712 | tf_op jit(solution)/shard_map/ppermute | solution.py:658
  393.9 28.8 %collective-permute-start.41 = (bf16[176,3584]{1,0:T(8,128)(2,1)S(1)}, bf16[176,3584]{1,0:T(8,128)(2,1)S(1)}, u32[]{:S(2)}, u32[]{:S(2)}) collective-permute-start(bf16[176,3584]{1,0:T(8,128)(2,1)S(1)} %get-tuple-element.475), channel_id=1, source_target_pairs={{1,0},{3,1},{5,3},{7,5},{6,7},{4,6},{2,4},{0,2},{9,8},{11,9},{13,1... | collective-permute-start | bytes 3784712 | tf_op jit(solution)/shard_map/ppermute | solution.py:658
  395.7 24.0 %collective-permute-start.43 = (bf16[512,1152]{1,0:T(8,128)(2,1)S(1)}, bf16[512,1152]{1,0:T(8,128)(2,1)S(1)}, u32[]{:S(2)}, u32[]{:S(2)}) collective-permute-start(bf16[512,1152]{1,0:T(8,128)(2,1)S(1)} %slice.209), channel_id=1, source_target_pairs={{0,8},{8,0},{16,24},{24,16},{1,9},{9,1},{17,25},{25,17},{2,10},{10... | collective-permute-start | bytes 3538952 | tf_op jit(solution)/shard_map/ppermute | solution.py:779
  425.1 10.6 %collective-permute-start.46 = (bf16[512,1152]{1,0:T(8,128)(2,1)}, bf16[512,1152]{1,0:T(8,128)(2,1)S(1)}, u32[]{:S(2)}, u32[]{:S(2)}) collective-permute-start(bf16[512,1152]{1,0:T(8,128)(2,1)} %get-tuple-element.559), channel_id=1, source_target_pairs={{0,8},{8,0},{16,24},{24,16},{1,9},{9,1},{17,25},{25,17},{2,10},{10... | collective-permute-start | bytes 3538952 | tf_op jit(solution)/shard_map/ppermute | solution.py:783
  425.1 10.6 %collective-permute-start.47 = (bf16[512,1152]{1,0:T(8,128)(2,1)S(1)}, bf16[512,1152]{1,0:T(8,128)(2,1)S(1)}, u32[]{:S(2)}, u32[]{:S(2)}) collective-permute-start(bf16[512,1152]{1,0:T(8,128)(2,1)S(1)} %get-tuple-element.557), channel_id=1, source_target_pairs={{0,8},{8,0},{16,24},{24,16},{1,9},{9,1},{17,25},{25,17},{2,10},{10... | collective-permute-start | bytes 3538952 | tf_op jit(solution)/shard_map/ppermute | solution.py:783
  426.6 29.9 %collective-permute-start.44 = (bf16[176,3584]{1,0:T(8,128)(2,1)S(1)}, bf16[176,3584]{1,0:T(8,128)(2,1)S(1)}, u32[]{:S(2)}, u32[]{:S(2)}) collective-permute-start(bf16[176,3584]{1,0:T(8,128)(2,1)S(1)} %get-tuple-element.482), channel_id=1, source_target_pairs={{0,1},{1,3},{3,5},{5,7},{7,6},{6,4},{4,2},{2,0},{8,9},{9,11},{11,1... | collective-permute-start | bytes 3784712 | tf_op jit(solution)/shard_map/ppermute | solution.py:658
  428.2 29.4 %collective-permute-start.45 = (bf16[176,3584]{1,0:T(8,128)(2,1)S(1)}, bf16[176,3584]{1,0:T(8,128)(2,1)S(1)}, u32[]{:S(2)}, u32[]{:S(2)}) collective-permute-start(bf16[176,3584]{1,0:T(8,128)(2,1)S(1)} %get-tuple-element.483), channel_id=1, source_target_pairs={{1,0},{3,1},{5,3},{7,5},{6,7},{4,6},{2,4},{0,2},{9,8},{11,9},{13,1... | collective-permute-start | bytes 3784712 | tf_op jit(solution)/shard_map/ppermute | solution.py:658
  459.7 19.2 %collective-permute-start.50 = (bf16[256,1152]{1,0:T(8,128)(2,1)}, bf16[256,1152]{1,0:T(8,128)(2,1)}, u32[]{:S(2)}, u32[]{:S(2)}) collective-permute-start(bf16[256,1152]{1,0:T(8,128)(2,1)} %slice.362), channel_id=1, source_target_pairs={{0,16},{8,24},{16,0},{24,8},{1,17},{9,25},{17,1},{25,9},{2,18},{10... | collective-permute-start | bytes 1769480 | tf_op jit(solution)/shard_map/ppermute | solution.py:788
  461.2 17.7 %collective-permute-start.48 = (bf16[216,1408]{1,0:T(8,128)(2,1)}, bf16[216,1408]{1,0:T(8,128)(2,1)}, u32[]{:S(2)}, u32[]{:S(2)}) collective-permute-start(bf16[216,1408]{1,0:T(8,128)(2,1)} %pad_maximum_fusion.2.refs_0_), channel_id=1, source_target_pairs={{0,8},{8,0},{16,24},{24,16},{1,9},{9,1},{17,25},{25,17},{2,10},{10... | collective-permute-start | bytes 1824776 | tf_op jit(solution)/shard_map/ppermute | solution.py:775
  461.2 17.7 %collective-permute-start.49 = (bf16[216,1408]{1,0:T(8,128)(2,1)}, bf16[216,1408]{1,0:T(8,128)(2,1)}, u32[]{:S(2)}, u32[]{:S(2)}) collective-permute-start(bf16[216,1408]{1,0:T(8,128)(2,1)} %collective-permute-done.39.refs_2_), channel_id=1, source_target_pairs={{0,8},{8,0},{16,24},{24,16},{1,9},{9,1},{17,25},{25,17},{2,10},{10... | collective-permute-start | bytes 1824776 | tf_op jit(solution)/shard_map/ppermute | solution.py:775
  480.5 4.5 collective-permute-start.51
  480.6 4.4 collective-permute-start.53
  485.3 14.0 %collective-permute-start.52 = (bf16[512,512]{1,0:T(8,128)(2,1)S(1)}, bf16[512,512]{1,0:T(8,128)(2,1)S(1)}, u32[]{:S(2)}, u32[]{:S(2)}) collective-permute-start(bf16[512,512]{1,0:T(8,128)(2,1)S(1)} %get-tuple-element.564), channel_id=1, source_target_pairs={{0,16},{8,24},{16,0},{24,8},{1,17},{9,25},{17,1},{25,9},{2,18},{10... | collective-permute-start | bytes 1572872 | tf_op jit(solution)/shard_map/ppermute | solution.py:788
  511.8 65.3 %collective-permute-start.54 = (bf16[256,1152]{1,0:T(8,128)(2,1)S(1)}, bf16[256,1152]{1,0:T(8,128)(2,1)S(1)}, u32[]{:S(2)}, u32[]{:S(2)}) collective-permute-start(bf16[256,1152]{1,0:T(8,128)(2,1)S(1)} %slice.361), channel_id=1, source_target_pairs={{0,16},{8,24},{16,0},{24,8},{1,17},{9,25},{17,1},{25,9},{2,18},{10... | collective-permute-start | bytes 1769480 | tf_op jit(solution)/shard_map/ppermute | solution.py:788
  (126 other events, 1051.2 us)

commit v6 on v5

--- a/solution.py
+++ b/solution.py
@@ -1355,10 +1355,21 @@
     unit1 = (resid * r1).astype(low)
 
     slabs.advance()
-    seg_pieces = group.over(segments.astype(low))
+    seg_pieces = group.across(group.over(segments.astype(low)))
+    key_seg = jnp.concatenate(seg_pieces, axis=1).astype(jnp.int32)
+    key_place = jnp.concatenate(
+        [
+            group.index(k, c) * length + jnp.arange(length, dtype=jnp.int32)
+            for k, c in group.order
+        ]
+    )
+    allowed = (segments[:, :, None] == key_seg[:, None, :]) & (
+        key_place[None, None, :] <= places[None, :, None]
+    )
+    mask = jnp.where(allowed, 0.0, -1e30).astype(wide)
     whole = gather_whole(small_blocks, (False, False, True, True, True), 0, n_f, n_seq)
-    whole, seg_pieces, unit1, cosine, sine, g_mlp = tie(
-        (slabs, downs), (whole, seg_pieces, unit1, cosine, sine, g_mlp)
+    whole, mask, unit1, cosine, sine, g_mlp = tie(
+        (slabs, downs), (whole, mask, unit1, cosine, sine, g_mlp)
     )
     qkv_side, ups, side_o, ups2, adapters = (part.reshape(-1, part.shape[2]) for part in whole)
     kv = HD
@@ -1369,21 +1380,9 @@
     o_raise, d_raise = ups2[:, :width], ups2[:, width : 2 * width]
 
     slabs.advance()
-    seg_pieces = group.across(seg_pieces)
     half = HD // 2
     queries, both, inner = project(unit1, qkv_side, ups, cosine, sine, hq, rank)
     both = gather_group(both, 2, n_seq)
-    key_seg = jnp.concatenate(seg_pieces, axis=1).astype(jnp.int32)
-    key_place = jnp.concatenate(
-        [
-            group.index(k, c) * length + jnp.arange(length, dtype=jnp.int32)
-            for k, c in group.order
-        ]
-    )
-    allowed = (segments[:, :, None] == key_seg[:, None, :]) & (
-        key_place[None, None, :] <= places[None, :, None]
-    )
-    mask = jnp.where(allowed, 0.0, -1e30).astype(wide)
     both, queries, mask, inner, g_mlp = tie((slabs,), (both, queries, mask, inner, g_mlp))
     q_inner, k_inner, v_inner = inner[:, :rank], inner[:, rank : 2 * rank], inner[:, 2 * rank :]
 

time: 609 us -> 611 us (level)
    unnamed x276 -> x284, local copies, waits for them, and re-layouts: 21.2 us -> 28.5 us
  transfers between devices with their start and end apart: 56 -> 56, of which waited for: 10 -> 12; matrix products, arithmetic and copies ran while one was open for 24% -> 23% of each run, Pallas kernels for 47% -> 47%
where the time goes in v6:
time: 611 us; the launch traced here: 602 us
  Pallas kernels  294 us (48%)
  matrix products  118 us (19%)
  waiting for transfers between devices  54.9 us (9%)
  starting transfers between devices  52.9 us (9%)
  local copies, waits for them, and re-layouts  47.6 us (8%)
  other arithmetic  31.6 us (5%)
    pallas_call x1, Pallas kernels, scatter_whole(): pl.pallas_call(body, out_shape=tuple((jax.ShapeDtypeStruct(pack.shape[1:]...  63 us
    pallas_call x1, Pallas kernels, gather_whole(): pl.pallas_call(body, out_shape=tuple((jax.ShapeDtypeStruct((n_f,) + b.sha...  59.3 us
    dot_general x17, matrix products, mul_t(): lax.dot_general(left, right, (((1,), (1,)), ((), ())), preferred_element_...  55.4 us
    pallas_call x2, Pallas kernels, gather_group(): pl.pallas_call(body, out_shape=jax.ShapeDtypeStruct((n_seq,) + block.shap...  54.4 us
    dot_general x9, matrix products, t_mul(): lax.dot_general(left, right, (((0,), (0,)), ((), ())), preferred_element_...  40.9 us
    pallas_call x2, Pallas kernels, mlp_forward(): pl.pallas_call(body, grid=(stop - first,), out_shape=(jax.ShapeDtypeStruc...  40.4 us
    ppermute x32, starting transfers between devices, hop(): return lax.ppermute(block, 'fsdp', self.up if way > 0 else self.down)  34.4 us
    unnamed x284, local copies, waits for them, and re-layouts  28.5 us
  transfers between devices with their start and end apart: 56, of which 12 were waited for; matrix products, arithmetic and copies ran while one was open for 23% of the time, Pallas kernels for 47%

profile of v6, /device:TPU:0, one launch (start us, length us, event | category | flops | bytes accessed | tf_op | source)
XLA Modules:
  0.0 601.8 jit_solution(13472129476808595219)
XLA Ops:
  1.5 3.0 collective-permute-start.3
  5.8 1.5 copy-done.19
  7.4 1.6 copy-done.20
  14.9 1.6 fusion.18
  18.4 1.7 multiply_sine_fusion
  33.6 59.3 %shard_map.477 = (bf16[8,144,2304]{2,1,0:T(8,128)(2,1)}, bf16[8,32,1536]{2,1,0:T(8,128)(2,1)}, bf16[8,128,1536]{2,1,0:T(8,128)(2,1)}, bf16[8,32,2560]{2,1,0:T(8,128)(2,1)}, bf16[8,144,512]{2,1,0:T(8,128)(2,1)}) custom-call(bf16[144,2304]{1,0:T(8,128)(2,1)} %copy-done.27, bf16[32,1536]{1,0:T(8,128)(2,1)} %copy-done.49, bf16[128,1536]{1,0:T(8,128)(2,1)} %copy-done.32, ...), custom_call_target="tpu_custom_call" | custom-call | tf_op jit(solution)/shard_map/pallas_call | solution.py:250
  93.0 1.8 and_select_fusion.hidden
  95.3 1.6 collective-permute-start.6
  96.9 6.2 %shard_map.478 = (bf16[512,1024]{1,0:T(8,128)(2,1)S(1)}, bf16[512,512]{1,0:T(8,128)(2,1)S(1)}, bf16[512,768]{1,0:T(8,128)(2,1)S(1)}) custom-call(bf16[512,1152]{1,0:T(8,128)(2,1)S(1)} %fusion.14.x, bf16[1152,2304]{1,0:T(8,128)(2,1)} %bitcast.155, bf16[256,1536]{1,0:T(8,128)(2,1)S(1)} %bitcast.138, f32[512,128]{1,0:T(8,128)S(1)} %copy-done.16, ...), custom_call_target="tpu_custom_call" | custom-call | flops 2000000000 | bytes 2000000 | tf_op jit(solution)/shard_map/pallas_call | solution.py:935
  103.8 17.3 %shard_map.479.kv = bf16[4,512,512]{2,1,0:T(8,128)(2,1)} custom-call(bf16[512,512]{1,0:T(8,128)(2,1)} %copy-done.29), custom_call_target="tpu_custom_call" | custom-call | tf_op jit(solution)/shard_map/pallas_call | solution.py:319
  121.1 2.1 slice.258.raised
  128.2 5.1 shard_map.480
  133.4 4.4 fusion.10
  138.5 1.8 multiply_reduce_fusion.1
  141.8 12.8 %collective-permute-done.9 = bf16[512,1152]{1,0:T(8,128)(2,1)S(1)} collective-permute-done((bf16[512,1152]{1,0:T(8,128)(2,1)S(1)}, bf16[512,1152]{1,0:T(8,128)(2,1)S(1)}, u32[]{:S(2)}, u32[]{:S(2)}) %collective-permute-start.9) | collective-permute-done | bytes 1179680 | tf_op jit(solution)/shard_map/ppermute | solution.py:769
  157.1 1.6 collective-permute-start.10
  160.0 1.6 collective-permute-start.12
  162.4 37.1 %shard_map.481 = bf16[4,512,1152]{2,1,0:T(8,128)(2,1)} custom-call(bf16[512,1152]{1,0:T(8,128)(2,1)} %multiply_convert_fusion.1.x), custom_call_target="tpu_custom_call" | custom-call | tf_op jit(solution)/shard_map/pallas_call | solution.py:319
  200.7 1.6 collective-permute-start.14
  205.3 22.3 %shard_map.482 = (bf16[2048,1792]{1,0:T(8,128)(2,1)}, bf16[2048,1792]{1,0:T(8,128)(2,1)}, bf16[2048,1792]{1,0:T(8,128)(2,1)}, bf16[8,144,1792]{2,1,0:T(8,128)(2,...) custom-call(bf16[2048,1152]{1,0:T(8,128)(2,1)} %bitcast.149, ...), custom_call_target="tpu_custom_call" | custom-call | flops 3000000000 | bytes 3000000 | tf_op jit(solution)/shard_map/pallas_call | solution.py:1189
  227.6 1.6 collective-permute-start.18
  230.1 18.1 %shard_map.483 = (bf16[2048,1792]{1,0:T(8,128)(2,1)}, bf16[2048,1792]{1,0:T(8,128)(2,1)}, bf16[2048,1792]{1,0:T(8,128)(2,1)}, bf16[8,144,1792]{2,1,0:T(8,128)(2,...) custom-call(bf16[2048,1152]{1,0:T(8,128)(2,1)} %bitcast.150, ...), custom_call_target="tpu_custom_call", output_to_operand_aliasing={{0}: (12, {}), {1}: (13, {}), {2}: (14, {}), {3}: (15, {}),... | custom-call | flops 3000000000 | bytes 3000000 | tf_op jit(solution)/shard_map/pallas_call | solution.py:1189
  256.5 10.4 %convolution_convert_fusion = bf16[1792,1152]{1,0:T(8,128)(2,1)S(1)} fusion(bf16[2048,1792]{1,0:T(8,128)(2,1)S(1)} %bitcast.161, bf16[2048,1152]{1,0:T(8,128)(2,1)S(1)} %constant_dynamic-update-slice_fusion.g), kind=kOutput, calls=%fused_computation | convolution fusion | flops 8457781248 | bytes 16187392 | tf_op jit(solution)/shard_map/dot_general | solution.py:29
  266.9 1.6 collective-permute-start.26
  269.0 1.6 collective-permute-start.25
  271.2 22.9 %shard_map.485 = (bf16[2048,1792]{1,0:T(8,128)(2,1)}, bf16[2048,1792]{1,0:T(8,128)(2,1)}, bf16[1792,1152]{1,0:T(8,128)(2,1)}) custom-call(bf16[2048,1152]{1,0:T(8,128)(2,1)} %copy-done.72, bf16[256,1152]{1,0:T(8,128)(2,1)} %slice.258.raised, bf16[2048,1792]{1,0:T(8,128)(2,1)} %get-tuple-element.418.mul_g, bf16[2048,1792]{1,0:T(8,128)(2,1)} %get-tuple-element.419.mul_u, ...), custom_call_target="tpu_custom_call" | custom-call | flops 3000000000 | bytes 3000000 | tf_op jit(solution)/shard_map/pallas_call | solution.py:1251
  295.5 1.6 collective-permute-start.28
  297.1 12.9 %convolution_convert_fusion.3 = bf16[1152,1792]{1,0:T(8,128)(2,1)S(1)} fusion(bf16[2048,1152]{1,0:T(8,128)(2,1)} %bitcast.151, bf16[2048,1792]{1,0:T(8,128)(2,1)} %get-tuple-element.466), kind=kOutput, calls=%fused_computation.3 | convolution fusion | flops 8457781248 | bytes 16187392 | tf_op jit(solution)/shard_map/dot_general | solution.py:29
  309.9 1.6 collective-permute-start.29
  313.6 2.7 collective-permute-start.55
  317.6 1.7 collective-permute-start.31
  319.2 12.4 %convolution_convert_fusion.2 = bf16[1152,1792]{1,0:T(8,128)(2,1)S(1)} fusion(bf16[2048,1152]{1,0:T(8,128)(2,1)S(1)} %bitcast.154, bf16[2048,1792]{1,0:T(8,128)(2,1)} %get-tuple-element.467), kind=kOutput, calls=%fused_computation.2 | convolution fusion | flops 8457781248 | bytes 16187392 | tf_op jit(solution)/shard_map/dot_general | solution.py:29
  334.5 2.0 collective-permute-start.35
  338.1 1.7 collective-permute-start.33
  339.8 9.3 %fusion.3 = f32[1024,1152]{1,0:T(8,128)} fusion(bf16[1152,1792]{1,0:T(8,128)(2,1)S(1)} %bitcast.170, bf16[2048,1792]{1,0:T(8,128)(2,1)} %get-tuple-element.467), kind=kOutput, calls=%fused_computation.9 | convolution fusion | flops 4227858432 | bytes 12517376 | tf_op jit(solution)/shard_map/dot_general | solution.py:25
  349.1 9.7 %add_convert_fusion.1 = bf16[1024,1152]{1,0:T(8,128)(2,1)} fusion(f32[1024,1152]{1,0:T(8,128)} %fusion.3, bf16[1152,1792]{1,0:T(8,128)(2,1)S(1)} %bitcast.169, bf16[2048,1792]{1,0:T(8,128)(2,1)} %get-tuple-element.466), kind=kOutput, calls=%fused_computation.5 | convolution fusion | flops 4230217728 | bytes 14876672 | tf_op jit(solution)/shard_map/dot_general | solution.py:25
  363.5 1.7 collective-permute-start.37
  365.2 9.3 %fusion = f32[1024,1152]{1,0:T(8,128)} fusion(bf16[1152,1792]{1,0:T(8,128)(2,1)S(1)} %bitcast.171, bf16[2048,1792]{1,0:T(8,128)(2,1)} %get-tuple-element.467), kind=kOutput, calls=%fused_computation.6 | convolution fusion | flops 4227858432 | bytes 12517376 | tf_op jit(solution)/shard_map/dot_general | solution.py:25
  375.6 1.6 collective-permute-start.39
  377.2 11.0 %add_convert_fusion = bf16[1024,1152]{1,0:T(8,128)(2,1)} fusion(f32[1024,1152]{1,0:T(8,128)} %fusion, bf16[1152,1792]{1,0:T(8,128)(2,1)} %bitcast.168, bf16[2048,1792]{1,0:T(8,128)(2,1)} %get-tuple-element.466), kind=kOutput, calls=%fused_computation.4 | convolution fusion | flops 4230217728 | bytes 14876672 | tf_op jit(solution)/shard_map/dot_general | solution.py:25
  388.2 3.9 collective-permute-done.39.refs_2_
  392.1 1.5 add_convert_fusion.3
  393.6 1.7 collective-permute-start.42
  396.6 1.7 collective-permute-start.41
  398.5 13.6 %convolution_convert_fusion.1 = bf16[2048,1152]{1,0:T(8,128)(2,1)} fusion(bf16[2048,1792]{1,0:T(8,128)(2,1)S(1)} %bitcast.163, bf16[1792,1152]{1,0:T(8,128)(2,1)} %get-tuple-element.475), kind=kOutput, calls=%fused_computation.1 | convolution fusion | flops 8458076160 | bytes 16187392 | tf_op jit(solution)/shard_map/dot_general | solution.py:21
  412.1 9.2 %collective-permute-done.42 = bf16[512,1152]{1,0:T(8,128)(2,1)S(1)} collective-permute-done((bf16[512,1152]{1,0:T(8,128)(2,1)S(1)}, bf16[512,1152]{1,0:T(8,128)(2,1)S(1)}, u32[]{:S(2)}, u32[]{:S(2)}) %collective-permute-start.42) | collective-permute-done | bytes 1179680 | tf_op jit(solution)/shard_map/ppermute | solution.py:788
  421.3 4.1 collective-permute-done.40.refs_4_
  426.1 1.8 fusion.71
  431.6 2.4 multiply_convert_fusion
  434.0 1.6 convolution_convert_fusion.10
  435.6 2.8 fusion.19.g
  438.4 20.9 %collective-permute-done.44.refs_4_ = bf16[176,3584]{1,0:T(8,128)(2,1)S(1)} collective-permute-done((bf16[176,3584]{1,0:T(8,128)(2,1)S(1)}, bf16[176,3584]{1,0:T(8,128)(2,1)S(1)}, u32[]{:S(2)}, u32[]{:S(2)}) %collective-permute-start.44) | collective-permute-done | bytes 1261600 | tf_op jit(solution)/shard_map/ppermute | solution.py:658
  462.9 11.3 %shard_map.494 = (bf16[512,1024]{1,0:T(8,128)(2,1)}, bf16[4,512,512]{2,1,0:T(8,128)(2,1)}) custom-call(bf16[512,1024]{1,0:T(8,128)(2,1)} %copy-done.58, bf16[4,512,512]{2,1,0:T(8,128)(2,1)} %shard_map.479.kv, f32[2,256,1024]{2,1,0:T(8,128)} %and_select_fusion.hidden, f32[2,4,256,1]{3,2,1,0:T(8,128)} %copy-done.61, bf16[512,1024]{1,0:T(8,128)(2,1)} %copy-done.59, ...), custom_call_target="tpu_custom_call" | custom-call | flops 3000000000 | bytes 3000000 | tf_op jit(solution)/shard_map/pallas_call | solution.py:1010
  476.6 1.9 shard_map.495.refs_0_
  478.6 1.6 convert_add_fusion.2
  486.6 1.6 collective-permute-start.52
  488.7 4.4 shard_map.497
  493.1 8.3 %shard_map.496 = (f32[512,1152]{1,0:T(8,128)S(1)}, bf16[8,176,1024]{2,1,0:T(8,128)(2,1)}) custom-call(bf16[512,1152]{1,0:T(8,128)(2,1)S(1)} %copy-done.12, bf16[512,256]{1,0:T(8,128)(2,1)S(1)} %copy-done.25, bf16[512,1024]{1,0:T(8,128)(2,1)S(1)} %copy-done.26, bf16[256,1536]{1,0:T(8,128)(2,1)S(1)} %bitcast.142, bf16[1152,2304]{1,0:T(8,128)(2,1)} %bitcast.156), custom_call_target="tpu_custom_call" | custom-call | flops 2000000000 | bytes 2000000 | tf_op jit(solution)/shard_map/pallas_call | solution.py:1060
  503.1 2.1 fusion.30
  507.7 2.8 fusion.15
  515.9 63.0 %shard_map.499 = (bf16[192,1280]{1,0:T(8,128)(2,1)}, bf16[176,1024]{1,0:T(8,128)(2,1)}, bf16[176,512]{1,0:T(8,128)(2,1)}, bf16[4,176,3584]{2,1,0:T(8,128)(2,1)}, f32[144,640]{1,0:T(8,128)}) custom-call(bf16[8,192,1280]{2,1,0:T(8,128)(2,1)} %copy-done.13, bf16[8,176,1024]{2,1,0:T(8,128)(2,1)} %get-tuple-element.522.refs_1_, ...), custom_call_target="tpu_custom_call" | custom-call | tf_op jit(solution)/shard_map/pallas_call | solution.py:561
  579.0 2.2 fusion.43
  586.7 8.3 %shard_map.500 = (f32[144,6912]{1,0:T(8,128)}, f32[144,6912]{1,0:T(8,128)}, f32[32,6912]{1,0:T(8,128)}, f32[32,6912]{1,0:T(8,128)}) custom-call(f32[144,1]{1,0:T(8,128)} %copy-done.23, bf16[4,176,3584]{2,1,0:T(8,128)(2,1)} %get-tuple-element.543.x), custom_call_target="tpu_custom_call" | custom-call | tf_op jit(solution)/shard_map/pallas_call | solution.py:890
  598.8 2.5 add_convert_fusion.2
  (480 shorter events, 102.5 us)
Async XLA Ops:
  1.5 21.0 %collective-permute-start.3 = (bf16[2,256]{1,0:T(2,128)(2,1)S(1)}, bf16[2,256]{1,0:T(2,128)(2,1)S(1)}, u32[]{:S(2)}, u32[]{:S(2)}) collective-permute-start(bf16[2,256]{1,0:T(2,128)(2,1)S(1)} %convert_element_type.221), channel_id=1, source_target_pairs={{0,16},{8,24},{16,0},{24,8},{1,17},{9,25},{17,1},{25,9},{2,18},{10... | collective-permute-start | bytes 3080 | tf_op jit(solution)/shard_map/ppermute | solution.py:769
  4.5 88.5 %collective-permute-start.2 = (bf16[2,256]{1,0:T(2,128)(2,1)S(1)}, bf16[2,256]{1,0:T(2,128)(2,1)S(1)}, u32[]{:S(2)}, u32[]{:S(2)}) collective-permute-start(bf16[2,256]{1,0:T(2,128)(2,1)S(1)} %convert_element_type.221), channel_id=1, source_target_pairs={{0,8},{8,0},{16,24},{24,16},{1,9},{9,1},{17,25},{25,17},{2,10},{10... | collective-permute-start | bytes 3080 | tf_op jit(solution)/shard_map/ppermute | solution.py:775
  11.6 83.1 %collective-permute-start = (bf16[176,3584]{1,0:T(8,128)(2,1)S(1)}, bf16[176,3584]{1,0:T(8,128)(2,1)}, u32[]{:S(2)}, u32[]{:S(2)}) collective-permute-start(bf16[176,3584]{1,0:T(8,128)(2,1)S(1)} %shard_map.475.refs_0_), channel_id=1, source_target_pairs={{0,1},{1,3},{3,5},{5,7},{7,6},{6,4},{4,2},{2,0},{8,9},{9,11},{11,1... | collective-permute-start | bytes 3784712 | tf_op jit(solution)/shard_map/ppermute | solution.py:658
  13.2 81.6 %collective-permute-start.1 = (bf16[176,3584]{1,0:T(8,128)(2,1)S(1)}, bf16[176,3584]{1,0:T(8,128)(2,1)}, u32[]{:S(2)}, u32[]{:S(2)}) collective-permute-start(bf16[176,3584]{1,0:T(8,128)(2,1)S(1)} %shard_map.475.refs_0_), channel_id=1, source_target_pairs={{1,0},{3,1},{5,3},{7,5},{6,7},{4,6},{2,4},{0,2},{9,8},{11,9},{13,1... | collective-permute-start | bytes 3784712 | tf_op jit(solution)/shard_map/ppermute | solution.py:658
  14.9 123.6 %copy-start.120 = (f32[512]{0:T(512)}, f32[512]{0:T(512)S(1)}, u32[]{:S(2)}) copy-start(f32[512]{0:T(512)S(1)} %compare_convert_fusion) | copy-start | bytes 6148
  17.4 79.5 %copy-start.11 = (bf16[512,1152]{1,0:T(8,128)(2,1)}, bf16[512,1152]{1,0:T(8,128)(2,1)S(1)}, u32[]{:S(2)}) copy-start(bf16[512,1152]{1,0:T(8,128)(2,1)S(1)} %fusion.14.x) | copy-start | bytes 3538948
  20.1 76.7 %copy-start.14 = (f32[512,128]{1,0:T(8,128)}, f32[512,128]{1,0:T(8,128)S(1)}, u32[]{:S(2)}) copy-start(f32[512,128]{1,0:T(8,128)S(1)} %get-tuple-element.308.sin) | copy-start | bytes 786436
  22.5 74.3 %copy-start.16 = (f32[512,128]{1,0:T(8,128)S(1)}, f32[512,128]{1,0:T(8,128)}, u32[]{:S(2)}) copy-start(f32[512,128]{1,0:T(8,128)} %get-tuple-element.307.cos) | copy-start | bytes 786436
  22.6 70.4 %collective-permute-start.4 = (bf16[2,256]{1,0:T(2,128)(2,1)S(1)}, bf16[2,256]{1,0:T(2,128)(2,1)S(1)}, u32[]{:S(2)}, u32[]{:S(2)}) collective-permute-start(bf16[2,256]{1,0:T(2,128)(2,1)S(1)} %collective-permute-done.3), channel_id=1, source_target_pairs={{0,8},{8,0},{16,24},{24,16},{1,9},{9,1},{17,25},{25,17},{2,10},{10... | collective-permute-start | bytes 3080 | tf_op jit(solution)/shard_map/ppermute | solution.py:775
  94.8 30.5 %collective-permute-start.5 = (bf16[176,3584]{1,0:T(8,128)(2,1)}, bf16[176,3584]{1,0:T(8,128)(2,1)}, u32[]{:S(2)}, u32[]{:S(2)}) collective-permute-start(bf16[176,3584]{1,0:T(8,128)(2,1)} %collective-permute-done.refs_1_), channel_id=1, source_target_pairs={{0,1},{1,3},{3,5},{5,7},{7,6},{6,4},{4,2},{2,0},{8,9},{9,11},{11,1... | collective-permute-start | bytes 3784712 | tf_op jit(solution)/shard_map/ppermute | solution.py:658
  95.3 30.2 %collective-permute-start.6 = (bf16[176,3584]{1,0:T(8,128)(2,1)}, bf16[176,3584]{1,0:T(8,128)(2,1)}, u32[]{:S(2)}, u32[]{:S(2)}) collective-permute-start(bf16[176,3584]{1,0:T(8,128)(2,1)} %collective-permute-done.1.refs_2_), channel_id=1, source_target_pairs={{1,0},{3,1},{5,3},{7,5},{6,7},{4,6},{2,4},{0,2},{9,8},{11,9},{13,1... | collective-permute-start | bytes 3784712 | tf_op jit(solution)/shard_map/ppermute | solution.py:658
  103.8 100.8 %copy-start.33 = (bf16[512,768]{1,0:T(8,128)(2,1)}, bf16[512,768]{1,0:T(8,128)(2,1)S(1)}, u32[]{:S(2)}) copy-start(bf16[512,768]{1,0:T(8,128)(2,1)S(1)} %get-tuple-element.503) | copy-start | bytes 2359300
  125.5 29.4 %collective-permute-start.7 = (bf16[176,3584]{1,0:T(8,128)(2,1)}, bf16[176,3584]{1,0:T(8,128)(2,1)S(1)}, u32[]{:S(2)}, u32[]{:S(2)}) collective-permute-start(bf16[176,3584]{1,0:T(8,128)(2,1)} %collective-permute-done.5.refs_3_), channel_id=1, source_target_pairs={{0,1},{1,3},{3,5},{5,7},{7,6},{6,4},{4,2},{2,0},{8,9},{9,11},{11,1... | collective-permute-start | bytes 3784712 | tf_op jit(solution)/shard_map/ppermute | solution.py:658
  127.0 29.2 %collective-permute-start.8 = (bf16[176,3584]{1,0:T(8,128)(2,1)}, bf16[176,3584]{1,0:T(8,128)(2,1)S(1)}, u32[]{:S(2)}, u32[]{:S(2)}) collective-permute-start(bf16[176,3584]{1,0:T(8,128)(2,1)} %collective-permute-done.6.refs_4_), channel_id=1, source_target_pairs={{1,0},{3,1},{5,3},{7,5},{6,7},{4,6},{2,4},{0,2},{9,8},{11,9},{13,1... | collective-permute-start | bytes 3784712 | tf_op jit(solution)/shard_map/ppermute | solution.py:658
  127.7 26.9 %collective-permute-start.9 = (bf16[512,1152]{1,0:T(8,128)(2,1)S(1)}, bf16[512,1152]{1,0:T(8,128)(2,1)S(1)}, u32[]{:S(2)}, u32[]{:S(2)}) collective-permute-start(bf16[512,1152]{1,0:T(8,128)(2,1)S(1)} %copy-done.84), channel_id=1, source_target_pairs={{0,16},{8,24},{16,0},{24,8},{1,17},{9,25},{17,1},{25,9},{2,18},{10... | collective-permute-start | bytes 3538952 | tf_op jit(solution)/shard_map/ppermute | solution.py:769
  157.1 42.5 %collective-permute-start.10 = (bf16[176,1792]{1,0:T(8,128)(2,1)}, bf16[176,1792]{1,0:T(8,128)(2,1)S(1)}, u32[]{:S(2)}, u32[]{:S(2)}) collective-permute-start(bf16[176,1792]{1,0:T(8,128)(2,1)} %slice.198), channel_id=1, source_target_pairs={{0,1},{1,3},{3,5},{5,7},{7,6},{6,4},{4,2},{2,0},{8,9},{9,11},{11,1... | collective-permute-start | bytes 1892360 | tf_op jit(solution)/shard_map/ppermute | solution.py:658
  159.6 40.0 %collective-permute-start.11 = (bf16[176,1792]{1,0:T(8,128)(2,1)}, bf16[176,1792]{1,0:T(8,128)(2,1)S(1)}, u32[]{:S(2)}, u32[]{:S(2)}) collective-permute-start(bf16[176,1792]{1,0:T(8,128)(2,1)} %slice.199), channel_id=1, source_target_pairs={{1,0},{3,1},{5,3},{7,5},{6,7},{4,6},{2,4},{0,2},{9,8},{11,9},{13,1... | collective-permute-start | bytes 1892360 | tf_op jit(solution)/shard_map/ppermute | solution.py:658
  160.0 39.5 %collective-permute-start.12 = (bf16[216,1408]{1,0:T(8,128)(2,1)}, bf16[216,1408]{1,0:T(8,128)(2,1)}, u32[]{:S(2)}, u32[]{:S(2)}) collective-permute-start(bf16[216,1408]{1,0:T(8,128)(2,1)} %pad_maximum_fusion.1.refs_0_), channel_id=1, source_target_pairs={{0,1},{1,3},{3,5},{5,7},{7,6},{6,4},{4,2},{2,0},{8,9},{9,11},{11,1... | collective-permute-start | bytes 1824776 | tf_op jit(solution)/shard_map/ppermute | solution.py:658
  161.6 38.0 %collective-permute-start.13 = (bf16[216,1408]{1,0:T(8,128)(2,1)}, bf16[216,1408]{1,0:T(8,128)(2,1)}, u32[]{:S(2)}, u32[]{:S(2)}) collective-permute-start(bf16[216,1408]{1,0:T(8,128)(2,1)} %pad_maximum_fusion.1.refs_0_), channel_id=1, source_target_pairs={{1,0},{3,1},{5,3},{7,5},{6,7},{4,6},{2,4},{0,2},{9,8},{11,9},{13,1... | collective-permute-start | bytes 1824776 | tf_op jit(solution)/shard_map/ppermute | solution.py:658
  162.3 38.0 %collective-permute-start.20 = (f32[6]{0:T(128)S(1)}, f32[6]{0:T(128)S(1)}, u32[]{:S(2)}, u32[]{:S(2)}) collective-permute-start(f32[6]{0:T(128)S(1)} %pad_maximum_fusion.11), channel_id=1, source_target_pairs={{0,8},{8,0},{16,24},{24,16},{1,9},{9,1},{17,25},{25,17},{2,10},{10... | collective-permute-start | bytes 80 | tf_op jit(solution)/shard_map/ppermute | solution.py:817
  199.6 28.0 %collective-permute-start.16 = (bf16[512,1152]{1,0:T(8,128)(2,1)S(1)}, bf16[512,1152]{1,0:T(8,128)(2,1)}, u32[]{:S(2)}, u32[]{:S(2)}) collective-permute-start(bf16[512,1152]{1,0:T(8,128)(2,1)S(1)} %copy-done.85), channel_id=1, source_target_pairs={{0,8},{8,0},{16,24},{24,16},{1,9},{9,1},{17,25},{25,17},{2,10},{10... | collective-permute-start | bytes 3538952 | tf_op jit(solution)/shard_map/ppermute | solution.py:775
  200.2 27.5 %collective-permute-start.17 = (bf16[512,1152]{1,0:T(8,128)(2,1)S(1)}, bf16[512,1152]{1,0:T(8,128)(2,1)S(1)}, u32[]{:S(2)}, u32[]{:S(2)}) collective-permute-start(bf16[512,1152]{1,0:T(8,128)(2,1)S(1)} %copy-done.99), channel_id=1, source_target_pairs={{0,8},{8,0},{16,24},{24,16},{1,9},{9,1},{17,25},{25,17},{2,10},{10... | collective-permute-start | bytes 3538952 | tf_op jit(solution)/shard_map/ppermute | solution.py:775
  200.7 26.9 %collective-permute-start.14 = (bf16[216,1408]{1,0:T(8,128)(2,1)}, bf16[216,1408]{1,0:T(8,128)(2,1)S(1)}, u32[]{:S(2)}, u32[]{:S(2)}) collective-permute-start(bf16[216,1408]{1,0:T(8,128)(2,1)} %collective-permute-done.12.refs_1_), channel_id=1, source_target_pairs={{0,1},{1,3},{3,5},{5,7},{7,6},{6,4},{4,2},{2,0},{8,9},{9,11},{11,1... | collective-permute-start | bytes 1824776 | tf_op jit(solution)/shard_map/ppermute | solution.py:658
  202.3 25.3 %collective-permute-start.15 = (bf16[216,1408]{1,0:T(8,128)(2,1)}, bf16[216,1408]{1,0:T(8,128)(2,1)}, u32[]{:S(2)}, u32[]{:S(2)}) collective-permute-start(bf16[216,1408]{1,0:T(8,128)(2,1)} %collective-permute-done.13.refs_2_), channel_id=1, source_target_pairs={{1,0},{3,1},{5,3},{7,5},{6,7},{4,6},{2,4},{0,2},{9,8},{11,9},{13,1... | collective-permute-start | bytes 1824776 | tf_op jit(solution)/shard_map/ppermute | solution.py:658
  227.6 24.1 %collective-permute-start.18 = (bf16[216,1408]{1,0:T(8,128)(2,1)S(1)}, bf16[216,1408]{1,0:T(8,128)(2,1)S(1)}, u32[]{:S(2)}, u32[]{:S(2)}) collective-permute-start(bf16[216,1408]{1,0:T(8,128)(2,1)S(1)} %collective-permute-done.14.refs_3_), channel_id=1, source_target_pairs={{0,1},{1,3},{3,5},{5,7},{7,6},{6,4},{4,2},{2,0},{8,9},{9,11},{11,1... | collective-permute-start | bytes 1824776 | tf_op jit(solution)/shard_map/ppermute | solution.py:658
  229.3 22.5 %collective-permute-start.19 = (bf16[216,1408]{1,0:T(8,128)(2,1)}, bf16[216,1408]{1,0:T(8,128)(2,1)S(1)}, u32[]{:S(2)}, u32[]{:S(2)}) collective-permute-start(bf16[216,1408]{1,0:T(8,128)(2,1)} %collective-permute-done.15.refs_4_), channel_id=1, source_target_pairs={{1,0},{3,1},{5,3},{7,5},{6,7},{4,6},{2,4},{0,2},{9,8},{11,9},{13,1... | collective-permute-start | bytes 1824776 | tf_op jit(solution)/shard_map/ppermute | solution.py:658
  251.9 15.0 %collective-permute-start.23 = (f32[6]{0:T(128)S(1)}, f32[6]{0:T(128)S(1)}, u32[]{:S(2)}, u32[]{:S(2)}) collective-permute-start(f32[6]{0:T(128)S(1)} %fusion.108), channel_id=1, source_target_pairs={{0,16},{8,24},{16,0},{24,8},{1,17},{9,25},{17,1},{25,9},{2,18},{10... | collective-permute-start | bytes 80 | tf_op jit(solution)/shard_map/ppermute | solution.py:817
  252.4 14.4 %collective-permute-start.22 = (bf16[216,768]{1,0:T(8,128)(2,1)S(1)}, bf16[216,768]{1,0:T(8,128)(2,1)S(1)}, u32[]{:S(2)}, u32[]{:S(2)}) collective-permute-start(bf16[216,768]{1,0:T(8,128)(2,1)S(1)} %slice.201), channel_id=1, source_target_pairs={{1,0},{3,1},{5,3},{7,5},{6,7},{4,6},{2,4},{0,2},{9,8},{11,9},{13,1... | collective-permute-start | bytes 995336 | tf_op jit(solution)/shard_map/ppermute | solution.py:658
  253.3 13.5 %collective-permute-start.21 = (bf16[216,640]{1,0:T(8,128)(2,1)S(1)}, bf16[216,640]{1,0:T(8,128)(2,1)S(1)}, u32[]{:S(2)}, u32[]{:S(2)}) collective-permute-start(bf16[216,640]{1,0:T(8,128)(2,1)S(1)} %slice.200), channel_id=1, source_target_pairs={{0,1},{1,3},{3,5},{5,7},{7,6},{6,4},{4,2},{2,0},{8,9},{9,11},{11,1... | collective-permute-start | bytes 829448 | tf_op jit(solution)/shard_map/ppermute | solution.py:658
  266.9 27.2 %collective-permute-start.26 = (f32[6]{0:T(128)S(1)}, f32[6]{0:T(128)S(1)}, u32[]{:S(2)}, u32[]{:S(2)}) collective-permute-start(f32[6]{0:T(128)S(1)} %add.210), channel_id=1, source_target_pairs={{0,1},{1,0},{2,3},{3,2},{4,5},{5,4},{6,7},{7,6},{8,9},{9,8},{10,11... | collective-permute-start | bytes 80 | tf_op jit(solution)/shard_map/ppermute | solution.py:817
  269.0 25.2 %collective-permute-start.25 = (bf16[216,640]{1,0:T(8,128)(2,1)S(1)}, bf16[216,640]{1,0:T(8,128)(2,1)S(1)}, u32[]{:S(2)}, u32[]{:S(2)}) collective-permute-start(bf16[216,640]{1,0:T(8,128)(2,1)S(1)} %get-tuple-element.414), channel_id=1, source_target_pairs={{1,0},{3,1},{5,3},{7,5},{6,7},{4,6},{2,4},{0,2},{9,8},{11,9},{13,1... | collective-permute-start | bytes 829448 | tf_op jit(solution)/shard_map/ppermute | solution.py:658
  270.6 23.5 %collective-permute-start.24 = (bf16[216,512]{1,0:T(8,128)(2,1)S(1)}, bf16[216,512]{1,0:T(8,128)(2,1)S(1)}, u32[]{:S(2)}, u32[]{:S(2)}) collective-permute-start(bf16[216,512]{1,0:T(8,128)(2,1)S(1)} %get-tuple-element.413), channel_id=1, source_target_pairs={{0,1},{1,3},{3,5},{5,7},{7,6},{6,4},{4,2},{2,0},{8,9},{9,11},{11,1... | collective-permute-start | bytes 663560 | tf_op jit(solution)/shard_map/ppermute | solution.py:658
  295.0 18.6 %collective-permute-start.27 = (bf16[216,1152]{1,0:T(8,128)(2,1)S(1)}, bf16[216,1152]{1,0:T(8,128)(2,1)S(1)}, u32[]{:S(2)}, u32[]{:S(2)}) collective-permute-start(bf16[216,1152]{1,0:T(8,128)(2,1)S(1)} %get-tuple-element.434), channel_id=1, source_target_pairs={{0,1},{1,3},{3,5},{5,7},{7,6},{6,4},{4,2},{2,0},{8,9},{9,11},{11,1... | collective-permute-start | bytes 1493000 | tf_op jit(solution)/shard_map/ppermute | solution.py:658
  295.5 18.1 %collective-permute-start.28 = (bf16[216,1152]{1,0:T(8,128)(2,1)S(1)}, bf16[216,1152]{1,0:T(8,128)(2,1)S(1)}, u32[]{:S(2)}, u32[]{:S(2)}) collective-permute-start(bf16[216,1152]{1,0:T(8,128)(2,1)S(1)} %get-tuple-element.435), channel_id=1, source_target_pairs={{1,0},{3,1},{5,3},{7,5},{6,7},{4,6},{2,4},{0,2},{9,8},{11,9},{13,1... | collective-permute-start | bytes 1493000 | tf_op jit(solution)/shard_map/ppermute | solution.py:658
  309.9 3.6 collective-permute-start.29
  313.0 115.4 %copy-start.4 = (bf16[256,1792]{1,0:T(8,128)(2,1)}, bf16[256,1792]{1,0:T(8,128)(2,1)S(1)}, u32[]{:S(2)}) copy-start(bf16[256,1792]{1,0:T(8,128)(2,1)S(1)} %convolution_convert_fusion.7) | copy-start | bytes 2752516
  313.6 19.5 %collective-permute-start.55 = (f32[6]{0:T(128)S(1)}, f32[6]{0:T(128)S(1)}, u32[]{:S(2)}, u32[]{:S(2)}) collective-permute-start(f32[6]{0:T(128)S(1)} %add.212), channel_id=1, source_target_pairs={{0,4},{1,5},{2,6},{3,7},{4,0},{5,1},{6,2},{7,3},{8,12},{9,13},{10,... | collective-permute-start | bytes 80 | tf_op jit(solution)/shard_map/ppermute | solution.py:817
  317.1 16.0 %collective-permute-start.30 = (bf16[216,1152]{1,0:T(8,128)(2,1)S(1)}, bf16[216,1152]{1,0:T(8,128)(2,1)S(1)}, u32[]{:S(2)}, u32[]{:S(2)}) collective-permute-start(bf16[216,1152]{1,0:T(8,128)(2,1)S(1)} %get-tuple-element.441), channel_id=1, source_target_pairs={{0,1},{1,3},{3,5},{5,7},{7,6},{6,4},{4,2},{2,0},{8,9},{9,11},{11,1... | collective-permute-start | bytes 1493000 | tf_op jit(solution)/shard_map/ppermute | solution.py:658
  317.6 15.6 %collective-permute-start.31 = (bf16[216,1152]{1,0:T(8,128)(2,1)S(1)}, bf16[216,1152]{1,0:T(8,128)(2,1)S(1)}, u32[]{:S(2)}, u32[]{:S(2)}) collective-permute-start(bf16[216,1152]{1,0:T(8,128)(2,1)S(1)} %get-tuple-element.442), channel_id=1, source_target_pairs={{1,0},{3,1},{5,3},{7,5},{6,7},{4,6},{2,4},{0,2},{9,8},{11,9},{13,1... | collective-permute-start | bytes 1493000 | tf_op jit(solution)/shard_map/ppermute | solution.py:658
  331.7 96.7 %copy-start.2 = (bf16[1152,1792]{1,0:T(8,128)(2,1)}, bf16[1152,1792]{1,0:T(8,128)(2,1)S(1)}, u32[]{:S(2)}) copy-start(bf16[1152,1792]{1,0:T(8,128)(2,1)S(1)} %convolution_convert_fusion.2) | copy-start | bytes 12386308
  333.1 95.3 %copy-start.6 = (bf16[256,1792]{1,0:T(8,128)(2,1)}, bf16[256,1792]{1,0:T(8,128)(2,1)S(1)}, u32[]{:S(2)}) copy-start(bf16[256,1792]{1,0:T(8,128)(2,1)S(1)} %convolution_convert_fusion.6) | copy-start | bytes 2752516
  334.1 24.7 %collective-permute-start.34 = (bf16[216,1152]{1,0:T(8,128)(2,1)S(1)}, bf16[216,1152]{1,0:T(8,128)(2,1)S(1)}, u32[]{:S(2)}, u32[]{:S(2)}) collective-permute-start(bf16[216,1152]{1,0:T(8,128)(2,1)S(1)} %get-tuple-element.460), channel_id=1, source_target_pairs={{0,1},{1,3},{3,5},{5,7},{7,6},{6,4},{4,2},{2,0},{8,9},{9,11},{11,1... | collective-permute-start | bytes 1493000 | tf_op jit(solution)/shard_map/ppermute | solution.py:658
  334.5 24.3 %collective-permute-start.35 = (bf16[216,1152]{1,0:T(8,128)(2,1)S(1)}, bf16[216,1152]{1,0:T(8,128)(2,1)S(1)}, u32[]{:S(2)}, u32[]{:S(2)}) collective-permute-start(bf16[216,1152]{1,0:T(8,128)(2,1)S(1)} %get-tuple-element.461), channel_id=1, source_target_pairs={{1,0},{3,1},{5,3},{7,5},{6,7},{4,6},{2,4},{0,2},{9,8},{11,9},{13,1... | collective-permute-start | bytes 1493000 | tf_op jit(solution)/shard_map/ppermute | solution.py:658
  337.7 24.7 %collective-permute-start.32 = (bf16[176,1792]{1,0:T(8,128)(2,1)S(1)}, bf16[176,1792]{1,0:T(8,128)(2,1)S(1)}, u32[]{:S(2)}, u32[]{:S(2)}) collective-permute-start(bf16[176,1792]{1,0:T(8,128)(2,1)S(1)} %get-tuple-element.452), channel_id=1, source_target_pairs={{0,1},{1,3},{3,5},{5,7},{7,6},{6,4},{4,2},{2,0},{8,9},{9,11},{11,1... | collective-permute-start | bytes 1892360 | tf_op jit(solution)/shard_map/ppermute | solution.py:658
  338.1 24.2 %collective-permute-start.33 = (bf16[176,1792]{1,0:T(8,128)(2,1)S(1)}, bf16[176,1792]{1,0:T(8,128)(2,1)S(1)}, u32[]{:S(2)}, u32[]{:S(2)}) collective-permute-start(bf16[176,1792]{1,0:T(8,128)(2,1)S(1)} %get-tuple-element.453), channel_id=1, source_target_pairs={{1,0},{3,1},{5,3},{7,5},{6,7},{4,6},{2,4},{0,2},{9,8},{11,9},{13,1... | collective-permute-start | bytes 1892360 | tf_op jit(solution)/shard_map/ppermute | solution.py:658
  363.1 29.0 %collective-permute-start.36 = (bf16[176,3584]{1,0:T(8,128)(2,1)S(1)}, bf16[176,3584]{1,0:T(8,128)(2,1)S(1)}, u32[]{:S(2)}, u32[]{:S(2)}) collective-permute-start(bf16[176,3584]{1,0:T(8,128)(2,1)S(1)} %get-tuple-element.464), channel_id=1, source_target_pairs={{0,1},{1,3},{3,5},{5,7},{7,6},{6,4},{4,2},{2,0},{8,9},{9,11},{11,1... | collective-permute-start | bytes 3784712 | tf_op jit(solution)/shard_map/ppermute | solution.py:658
  363.5 28.5 %collective-permute-start.37 = (bf16[176,3584]{1,0:T(8,128)(2,1)S(1)}, bf16[176,3584]{1,0:T(8,128)(2,1)S(1)}, u32[]{:S(2)}, u32[]{:S(2)}) collective-permute-start(bf16[176,3584]{1,0:T(8,128)(2,1)S(1)} %get-tuple-element.465), channel_id=1, source_target_pairs={{1,0},{3,1},{5,3},{7,5},{6,7},{4,6},{2,4},{0,2},{9,8},{11,9},{13,1... | collective-permute-start | bytes 3784712 | tf_op jit(solution)/shard_map/ppermute | solution.py:658
  375.6 16.5 %collective-permute-start.38 = (bf16[512,1152]{1,0:T(8,128)(2,1)}, bf16[512,1152]{1,0:T(8,128)(2,1)S(1)}, u32[]{:S(2)}, u32[]{:S(2)}) collective-permute-start(bf16[512,1152]{1,0:T(8,128)(2,1)} %slice.207), channel_id=1, source_target_pairs={{0,8},{8,0},{16,24},{24,16},{1,9},{9,1},{17,25},{25,17},{2,10},{10... | collective-permute-start | bytes 3538952 | tf_op jit(solution)/shard_map/ppermute | solution.py:779
  375.6 16.5 %collective-permute-start.39 = (bf16[216,1408]{1,0:T(8,128)(2,1)}, bf16[216,1408]{1,0:T(8,128)(2,1)}, u32[]{:S(2)}, u32[]{:S(2)}) collective-permute-start(bf16[216,1408]{1,0:T(8,128)(2,1)} %pad_maximum_fusion.2.refs_0_), channel_id=1, source_target_pairs={{0,16},{8,24},{16,0},{24,8},{1,17},{9,25},{17,1},{25,9},{2,18},{10... | collective-permute-start | bytes 1824776 | tf_op jit(solution)/shard_map/ppermute | solution.py:769
  393.6 27.7 %collective-permute-start.42 = (bf16[512,1152]{1,0:T(8,128)(2,1)S(1)}, bf16[512,1152]{1,0:T(8,128)(2,1)S(1)}, u32[]{:S(2)}, u32[]{:S(2)}) collective-permute-start(bf16[512,1152]{1,0:T(8,128)(2,1)S(1)} %add_convert_fusion.3), channel_id=1, source_target_pairs={{0,16},{8,24},{16,0},{24,8},{1,17},{9,25},{17,1},{25,9},{2,18},{10... | collective-permute-start | bytes 3538952 | tf_op jit(solution)/shard_map/ppermute | solution.py:788
  396.2 29.1 %collective-permute-start.40 = (bf16[176,3584]{1,0:T(8,128)(2,1)S(1)}, bf16[176,3584]{1,0:T(8,128)(2,1)S(1)}, u32[]{:S(2)}, u32[]{:S(2)}) collective-permute-start(bf16[176,3584]{1,0:T(8,128)(2,1)S(1)} %get-tuple-element.472), channel_id=1, source_target_pairs={{0,1},{1,3},{3,5},{5,7},{7,6},{6,4},{4,2},{2,0},{8,9},{9,11},{11,1... | collective-permute-start | bytes 3784712 | tf_op jit(solution)/shard_map/ppermute | solution.py:658
  396.6 28.8 %collective-permute-start.41 = (bf16[176,3584]{1,0:T(8,128)(2,1)S(1)}, bf16[176,3584]{1,0:T(8,128)(2,1)S(1)}, u32[]{:S(2)}, u32[]{:S(2)}) collective-permute-start(bf16[176,3584]{1,0:T(8,128)(2,1)S(1)} %get-tuple-element.473), channel_id=1, source_target_pairs={{1,0},{3,1},{5,3},{7,5},{6,7},{4,6},{2,4},{0,2},{9,8},{11,9},{13,1... | collective-permute-start | bytes 3784712 | tf_op jit(solution)/shard_map/ppermute | solution.py:658
  398.4 22.9 %collective-permute-start.43 = (bf16[512,1152]{1,0:T(8,128)(2,1)S(1)}, bf16[512,1152]{1,0:T(8,128)(2,1)S(1)}, u32[]{:S(2)}, u32[]{:S(2)}) collective-permute-start(bf16[512,1152]{1,0:T(8,128)(2,1)S(1)} %slice.209), channel_id=1, source_target_pairs={{0,8},{8,0},{16,24},{24,16},{1,9},{9,1},{17,25},{25,17},{2,10},{10... | collective-permute-start | bytes 3538952 | tf_op jit(solution)/shard_map/ppermute | solution.py:779
  427.8 10.6 %collective-permute-start.46 = (bf16[512,1152]{1,0:T(8,128)(2,1)}, bf16[512,1152]{1,0:T(8,128)(2,1)S(1)}, u32[]{:S(2)}, u32[]{:S(2)}) collective-permute-start(bf16[512,1152]{1,0:T(8,128)(2,1)} %get-tuple-element.557), channel_id=1, source_target_pairs={{0,8},{8,0},{16,24},{24,16},{1,9},{9,1},{17,25},{25,17},{2,10},{10... | collective-permute-start | bytes 3538952 | tf_op jit(solution)/shard_map/ppermute | solution.py:783
  427.8 10.6 %collective-permute-start.47 = (bf16[512,1152]{1,0:T(8,128)(2,1)S(1)}, bf16[512,1152]{1,0:T(8,128)(2,1)S(1)}, u32[]{:S(2)}, u32[]{:S(2)}) collective-permute-start(bf16[512,1152]{1,0:T(8,128)(2,1)S(1)} %get-tuple-element.555), channel_id=1, source_target_pairs={{0,8},{8,0},{16,24},{24,16},{1,9},{9,1},{17,25},{25,17},{2,10},{10... | collective-permute-start | bytes 3538952 | tf_op jit(solution)/shard_map/ppermute | solution.py:783
  429.3 29.9 %collective-permute-start.44 = (bf16[176,3584]{1,0:T(8,128)(2,1)S(1)}, bf16[176,3584]{1,0:T(8,128)(2,1)S(1)}, u32[]{:S(2)}, u32[]{:S(2)}) collective-permute-start(bf16[176,3584]{1,0:T(8,128)(2,1)S(1)} %get-tuple-element.480), channel_id=1, source_target_pairs={{0,1},{1,3},{3,5},{5,7},{7,6},{6,4},{4,2},{2,0},{8,9},{9,11},{11,1... | collective-permute-start | bytes 3784712 | tf_op jit(solution)/shard_map/ppermute | solution.py:658
  430.4 29.4 %collective-permute-start.45 = (bf16[176,3584]{1,0:T(8,128)(2,1)S(1)}, bf16[176,3584]{1,0:T(8,128)(2,1)S(1)}, u32[]{:S(2)}, u32[]{:S(2)}) collective-permute-start(bf16[176,3584]{1,0:T(8,128)(2,1)S(1)} %get-tuple-element.481), channel_id=1, source_target_pairs={{1,0},{3,1},{5,3},{7,5},{6,7},{4,6},{2,4},{0,2},{9,8},{11,9},{13,1... | collective-permute-start | bytes 3784712 | tf_op jit(solution)/shard_map/ppermute | solution.py:658
  462.0 18.2 %collective-permute-start.50 = (bf16[256,1152]{1,0:T(8,128)(2,1)}, bf16[256,1152]{1,0:T(8,128)(2,1)}, u32[]{:S(2)}, u32[]{:S(2)}) collective-permute-start(bf16[256,1152]{1,0:T(8,128)(2,1)} %slice.362), channel_id=1, source_target_pairs={{0,16},{8,24},{16,0},{24,8},{1,17},{9,25},{17,1},{25,9},{2,18},{10... | collective-permute-start | bytes 1769480 | tf_op jit(solution)/shard_map/ppermute | solution.py:788
  462.4 17.8 %collective-permute-start.48 = (bf16[216,1408]{1,0:T(8,128)(2,1)}, bf16[216,1408]{1,0:T(8,128)(2,1)}, u32[]{:S(2)}, u32[]{:S(2)}) collective-permute-start(bf16[216,1408]{1,0:T(8,128)(2,1)} %pad_maximum_fusion.2.refs_0_), channel_id=1, source_target_pairs={{0,8},{8,0},{16,24},{24,16},{1,9},{9,1},{17,25},{25,17},{2,10},{10... | collective-permute-start | bytes 1824776 | tf_op jit(solution)/shard_map/ppermute | solution.py:775
  462.4 17.8 %collective-permute-start.49 = (bf16[216,1408]{1,0:T(8,128)(2,1)}, bf16[216,1408]{1,0:T(8,128)(2,1)}, u32[]{:S(2)}, u32[]{:S(2)}) collective-permute-start(bf16[216,1408]{1,0:T(8,128)(2,1)} %collective-permute-done.39.refs_2_), channel_id=1, source_target_pairs={{0,8},{8,0},{16,24},{24,16},{1,9},{9,1},{17,25},{25,17},{2,10},{10... | collective-permute-start | bytes 1824776 | tf_op jit(solution)/shard_map/ppermute | solution.py:775
  481.8 4.5 collective-permute-start.51
  481.9 4.4 collective-permute-start.53
  486.6 14.8 %collective-permute-start.52 = (bf16[512,512]{1,0:T(8,128)(2,1)S(1)}, bf16[512,512]{1,0:T(8,128)(2,1)S(1)}, u32[]{:S(2)}, u32[]{:S(2)}) collective-permute-start(bf16[512,512]{1,0:T(8,128)(2,1)S(1)} %get-tuple-element.562), channel_id=1, source_target_pairs={{0,16},{8,24},{16,0},{24,8},{1,17},{9,25},{17,1},{25,9},{2,18},{10... | collective-permute-start | bytes 1572872 | tf_op jit(solution)/shard_map/ppermute | solution.py:788
  513.8 65.2 %collective-permute-start.54 = (bf16[256,1152]{1,0:T(8,128)(2,1)S(1)}, bf16[256,1152]{1,0:T(8,128)(2,1)S(1)}, u32[]{:S(2)}, u32[]{:S(2)}) collective-permute-start(bf16[256,1152]{1,0:T(8,128)(2,1)S(1)} %slice.361), channel_id=1, source_target_pairs={{0,16},{8,24},{16,0},{24,8},{1,17},{9,25},{17,1},{25,9},{2,18},{10... | collective-permute-start | bytes 1769480 | tf_op jit(solution)/shard_map/ppermute | solution.py:788
  (130 other events, 1226.4 us)
